TPU v7x, 32 devices: a whole 2x2x4 slice. The times are simulated.
32 devices in a mesh: ctx: 16 (over z, x, core), tp: 2 (over y).
Axes of the slice: x: 2, y: 2, z: 4, core: 2. Of those that a mesh axis runs over, the one named last changes fastest.
Arguments:
- inputs: bfloat16 [8192, 5376], P('ctx', 'tp')
- in_gain: float32 [5376], replicated, may hold values from 0.1 to 1.9
- q_weight: bfloat16 [5376, 4096], P('ctx', 'tp')
- key_matrix: bfloat16 [5376, 2048], P('ctx', 'tp')
- value_matrix: bfloat16 [5376, 2048], P('ctx', 'tp'), may hold values from -0.078125 to 0.078125
- q_gain: float32 [128], replicated
- key_norm_gain: float32 [128], replicated
- out_weight: bfloat16 [4096, 5376], P('tp', 'ctx')
- post_gain: float32 [5376], P('tp'), may hold values from 0.1 to 1.9
- segment_ids: int32 [8192], P('ctx'), may hold values from 0 to 10, as said below
- positions: int32 [8192], P('ctx'), may hold values from 0 to 1535, as said below
Outputs:
- outputs: bfloat16 [8192, 5376], P('ctx', 'tp')
Inputs may be any that keep to these rules, and one draw needn't show every extreme that they name: segment_ids start at 0 and rise by 0 or 1 from each token to the next. positions are 0 at the first token of each document and rise by 1 within it; no document has more than 1536 tokens, and the last document has exactly 1536.
All inputs are finite; a program needn't handle non-finite values.
Results may differ from a plain program's by a relative error of at most 0.013.
The roundings to bfloat16 on the way count: a program that leaves them out, or rounds other values in their place, can miss the bound.
Values may be sent and summed in bfloat16 or wider, within the bound.
No kernel may reach another device: no remote copies, remote signals or barrier semaphores. Data moves between devices by JAX's collectives and lax.ppermute only.
A program may use at most 192 MiB of HBM per device.

v0:
```python
import jax
import jax.numpy as jnp
from jax import lax
from jax.sharding import PartitionSpec as P

MODEL_WIDTH = 5376
QUERY_HEADS = 32
HEAD_SIZE = 128
VISIBLE_SPAN = 1024


EPS = 1e-06
ROPE_BASE = 10000.0
MASKED = -1e30


def from_behind(x, axis, by):
    size = lax.axis_size(axis)
    pairs = [(i, i + by) for i in range(size) if 0 <= i + by < size]
    return lax.ppermute(x, axis, pairs)


def rms_scale(values, gain):
    return values * lax.rsqrt(jnp.mean(values * values, axis=-1, keepdims=True) + EPS) * gain


def rotate(values, position):
    half_dim = values.shape[-1] // 2
    frequency = ROPE_BASE ** (-jnp.arange(half_dim, dtype=jnp.float32) / half_dim)
    angles = position.astype(jnp.float32)[:, None] * frequency[None, :]
    cosine = jnp.cos(angles)[:, None, :]
    sine = jnp.sin(angles)[:, None, :]
    first = values[..., :half_dim]
    second = values[..., half_dim:]
    return jnp.concatenate(
        [first * cosine - second * sine, second * cosine + first * sine], axis=-1
    )


def prepare_heads(projected, gain, position, heads, factor):
    shaped = projected.reshape(projected.shape[0], heads, HEAD_SIZE)
    return (rotate(rms_scale(shaped, gain), position) * factor).astype(jnp.bfloat16)


def block_scores(grouped, keys_block):
    return jnp.einsum("qhgd,khd->hgqk", grouped, keys_block, preferred_element_type=jnp.float32)


def block_mix(weights_block, values_block):
    return jnp.einsum(
        "hgqk,khd->qhgd", weights_block, values_block, preferred_element_type=jnp.float32
    )


def local(
    inputs,
    in_gain,
    q_weight,
    key_matrix,
    value_matrix,
    q_gain,
    key_norm_gain,
    out_weight,
    post_gain,
    segment_ids,
    positions,
):
    tok_rows = inputs.shape[0]
    gathered = lax.all_gather(inputs, "tp", axis=1, tiled=True)
    normalized = rms_scale(gathered.astype(jnp.float32), in_gain).astype(jnp.bfloat16)
    q_cols = q_weight.shape[1]
    kv_cols = key_matrix.shape[1]

    def add_rows(piece):
        return jnp.dot(normalized, piece, preferred_element_type=jnp.float32)

    q_raw = add_rows(lax.all_gather(q_weight, "ctx", axis=0, tiled=True))
    k_raw = add_rows(lax.all_gather(key_matrix, "ctx", axis=0, tiled=True))
    v_raw = add_rows(lax.all_gather(value_matrix, "ctx", axis=0, tiled=True))
    q_heads = q_cols // HEAD_SIZE
    kv_heads = kv_cols // HEAD_SIZE
    query_heads_all = prepare_heads(
        q_raw, q_gain, positions, q_heads, (MODEL_WIDTH // QUERY_HEADS) ** (-0.5)
    )
    keys_own = prepare_heads(k_raw, key_norm_gain, positions, kv_heads, 1.0)
    values_own = v_raw.reshape(tok_rows, kv_heads, HEAD_SIZE).astype(jnp.bfloat16)
    reach = (VISIBLE_SPAN - 1) // tok_rows + 1
    key_list = [keys_own]
    value_list = [values_own]
    segment_list = [segment_ids]
    for distance in range(1, reach + 1):
        far_keys, far_values, far_segments = from_behind(
            (keys_own, values_own, segment_ids), "ctx", distance
        )
        key_list.insert(0, far_keys)
        value_list.insert(0, far_values)
        segment_list.insert(0, far_segments)
    key_all = jnp.concatenate(key_list, axis=0)
    value_all = jnp.concatenate(value_list, axis=0)
    segment_all = jnp.concatenate(segment_list, axis=0)
    my_start = lax.axis_index("ctx") * tok_rows
    key_index = my_start - reach * tok_rows + jnp.arange((reach + 1) * tok_rows, dtype=jnp.int32)
    query_index = my_start + jnp.arange(tok_rows, dtype=jnp.int32)
    gap = query_index[:, None] - key_index[None, :]
    allowed = (
        (segment_ids[:, None] == segment_all[None, :])
        & (gap >= 0)
        & (gap < VISIBLE_SPAN)
        & (key_index[None, :] >= 0)
    )
    head_group = q_heads // kv_heads
    grouped = query_heads_all.reshape(tok_rows, kv_heads, head_group, HEAD_SIZE)
    scores = block_scores(grouped, key_all)
    scores = jnp.where(allowed[None, None], scores, MASKED)
    expo = jnp.exp(scores - jnp.max(scores, axis=-1, keepdims=True))
    weights = (expo / jnp.sum(expo, axis=-1, keepdims=True)).astype(jnp.bfloat16)
    mixed = block_mix(weights, value_all)
    attended = mixed.reshape(tok_rows, q_cols).astype(jnp.bfloat16)
    partial_terms = jnp.dot(
        attended,
        lax.all_gather(out_weight, "ctx", axis=1, tiled=True),
        preferred_element_type=jnp.float32,
    )
    share = lax.psum_scatter(
        partial_terms.astype(jnp.bfloat16), "tp", scatter_dimension=1, tiled=True
    ).astype(jnp.float32)
    squares = lax.psum(jnp.sum(share * share, axis=-1), "tp")
    branch = share * lax.rsqrt(squares[:, None] / MODEL_WIDTH + EPS) * post_gain
    return (inputs.astype(jnp.float32) + branch).astype(jnp.bfloat16)


def solution(mesh):
    return jax.shard_map(
        local,
        mesh=mesh,
        in_specs=(
            P("ctx", "tp"),
            P(),
            P("ctx", "tp"),
            P("ctx", "tp"),
            P("ctx", "tp"),
            P(),
            P(),
            P("tp", "ctx"),
            P("tp"),
            P("ctx"),
            P("ctx"),
        ),
        out_specs=P("ctx", "tp"),
        check_vma=False,
    )
```

profile of v0, /device:TPU:2, one launch (start us, length us, event | category | flops | bytes accessed | tf_op | source)
XLA Modules:
  0.0 667.4 jit_solution(12490937769247324131)
XLA Ops:
  6.5 0.7 all-gather.6.cloned.1.call-update
  7.3 0.7 all-gather.10.cloned.1.call-update
  8.1 0.7 all-gather.8.cloned.1.call-update
  8.8 0.5 all-gather.12.cloned.1.call-update
  9.4 0.5 all-gather.14.cloned.1.call-update
  10.0 3.5 collective-permute-start.2
  13.4 1.9 collective-permute-start.3
  15.4 1.0 multiply_cosine_fusion
  16.5 1.9 collective-permute-done.3
  18.4 2.5 fusion.21
  20.9 60.8 %all-gather.6.cloned.1.call-done = bf16[512,5376]{1,0:T(8,128)(2,1)} async-done(((bf16[512,2688]{1,0:T(8,128)(2,1)}), bf16[512,5376]{1,0:T(8,128)(2,1)}) %all-gather.6.cloned.1.call-update) | async-done | bytes 5505040 | tf_op jit(solution)/shard_map/all_gather | solution.py:69
  81.7 3.7 fusion.7
  85.4 88.8 %all-gather.10.cloned.1.call-done = bf16[5376,1024]{1,0:T(8,128)(2,1)} async-done(((bf16[336,1024]{1,0:T(8,128)(2,1)}), bf16[5376,1024]{1,0:T(8,128)(2,1)}) %all-gather.10.cloned.1.call-update) | async-done | bytes 11010064 | tf_op jit(solution)/shard_map/all_gather | solution.py:78
  174.2 10.3 %fusion.32 = f32[512,1024]{1,0:T(8,128)S(1)} fusion(bf16[5376,1024]{1,0:T(8,128)(2,1)} %all-gather.10.cloned.1.call-done, bf16[512,5376]{1,0:T(8,128)(2,1)} %all-gather.6.cloned.1.call-done, f32[5376]{0:T(1024)S(1)} %copy-done.7, f32[512]{0:T(512)S(1)} %add_rsqrt_fusion.3), kind=kOutput, calls=%fused_computation.63 | convolution fusion | flops 5648154624 | bytes 18635776 | tf_op jit(solution)/shard_map/dot_general | solution.py:75
  184.5 0.5 copy.53
  185.0 0.6 multiply_reduce_fusion.1
  185.6 0.1 copy.39
  185.8 0.7 fusion.22
  186.5 0.8 subtract_convert_fusion
  187.2 1.5 pad_maximum_fusion
  188.8 3.2 collective-permute-start.4
  192.0 1.9 collective-permute-start.5
  193.9 91.4 %all-gather.8.cloned.1.call-done = bf16[5376,1024]{1,0:T(8,128)(2,1)} async-done(((bf16[336,1024]{1,0:T(8,128)(2,1)}), bf16[5376,1024]{1,0:T(8,128)(2,1)}) %all-gather.8.cloned.1.call-update) | async-done | bytes 11010064 | tf_op jit(solution)/shard_map/all_gather | solution.py:79
  285.3 11.2 %convolution_convert_fusion.1 = bf16[512,1024]{1,0:T(8,128)(2,1)} fusion(bf16[5376,1024]{1,0:T(8,128)(2,1)} %all-gather.8.cloned.1.call-done, bf16[512,5376]{1,0:T(8,128)(2,1)} %all-gather.6.cloned.1.call-done, f32[5376]{0:T(1024)S(1)} %copy-done.7, f32[512]{0:T(512)S(1)} %add_rsqrt_fusion.3), kind=kOutput, calls=%fused_computation.45 | convolution fusion | flops 5648678912 | bytes 17587200 | tf_op jit(solution)/shard_map/dot_general | solution.py:75
  296.5 2.4 copy.51
  298.8 4.4 collective-permute-start
  303.2 2.1 collective-permute-start.1
  305.4 130.3 %all-gather.12.cloned.1.call-done = bf16[5376,2048]{1,0:T(8,128)(2,1)} async-done(((bf16[336,2048]{1,0:T(8,128)(2,1)}), bf16[5376,2048]{1,0:T(8,128)(2,1)}) %all-gather.12.cloned.1.call-update) | async-done | bytes 22020112 | tf_op jit(solution)/shard_map/all_gather | solution.py:77
  435.7 16.5 %convolution_bitcast_fusion = f32[64,8,16,128]{3,1,2,0:T(8,128)S(1)} fusion(bf16[5376,2048]{1,0:T(8,128)(2,1)} %all-gather.12.cloned.1.call-done, bf16[512,5376]{1,0:T(8,128)(2,1)} %all-gather.6.cloned.1.call-done, f32[5376]{0:T(1024)S(1)} %copy-done.7, f32[512]{0:T(512)S(1)} %add_rsqrt_fusion.3), kind=kOutput, calls=%fused_computation.38 | convolution fusion | flops 11285299200 | bytes 31742976 | tf_op jit(solution)/shard_map/dot_general | solution.py:75
  452.2 0.9 copy.54
  453.1 1.9 copy-done
  455.1 1.2 multiply_reduce_fusion
  456.2 0.1 copy.41
  456.3 0.1 copy.42
  456.5 4.1 multiply_multiply_fusion
  460.6 1.5 multiply_subtract_fusion
  462.1 3.4 copy.43
  465.5 3.3 copy.44
  468.9 26.4 %fusion.35 = (f32[8,2,512]{2,1,0:T(2,128)S(1)}, f32[8,2,512,1536]{2,3,1,0:T(8,128)}) fusion(pred[512,1536]{0,1:T(8,128)(4,1)} %fusion.21, bf16[512,8,64]{2,0,1:T(8,128)(2,1)S(1)} %get-tuple-element.8, bf16[512,8,64]{2,0,1:T(8,128)(2,1)S(1)} %get-tuple-element.7, bf16[512,8,128]{2,0,1:T(8,128)(2,1)} %collective-permute-done.5, ...), kind=kOutput, calls=%fused_computation.64 | convolution fusion | flops 3274704384 | bytes 58490880 | tf_op jit(solution)/shard_map/sub | solution.py:115
  495.3 19.4 %fusion.23 = bf16[8,128,2,512]{3,1,2,0:T(8,128)(2,1)S(1)} fusion(f32[8,2,512,1536]{2,3,1,0:T(8,128)} %get-tuple-element.12, f32[8,2,512]{2,1,0:T(2,128)S(1)} %get-tuple-element.11, bf16[512,8,128]{0,2,1:T(8,128)(2,1)S(1)} %bitcast.67, bf16[512,8,128]{0,2,1:T(8,128)(2,1)} %collective-permute-done.1, bf16[512,8,128]{0,2,1:T(8,128)(2,1)} %collective-permute-done), kind=kOutput, calls=%fused_computation.44 | convolution fusion | flops 3256877056 | bytes 55607296 | tf_op jit(solution)/shard_map/hgqk,khd->qhgd/dot_general | solution.py:50
  514.7 37.2 %all-gather.14.cloned.1.call-done = bf16[2048,5376]{0,1:T(8,128)(2,1)} async-done(((bf16[2048,336]{0,1:T(8,128)(2,1)}), bf16[2048,5376]{0,1:T(8,128)(2,1)}) %all-gather.14.cloned.1.call-update) | async-done | bytes 22020112 | tf_op jit(solution)/shard_map/all_gather | solution.py:121
  551.9 18.1 %convolution_convert_fusion = bf16[512,5376]{1,0:T(8,128)(2,1)} fusion(bf16[512,2048]{0,1:T(8,128)(2,1)S(1)} %bitcast.68, bf16[2048,5376]{0,1:T(8,128)(2,1)} %all-gather.14.cloned.1.call-done), kind=kOutput, calls=%fused_computation.14 | convolution fusion | flops 11277041664 | bytes 29622272 | tf_op jit(solution)/shard_map/dot_general | solution.py:119
  569.9 8.3 %copy.49 = bf16[512,5376]{0,1:T(8,128)(2,1)} copy(bf16[512,5376]{1,0:T(8,128)(2,1)} %convolution_convert_fusion) | data formatting | bytes 11010048
  578.2 68.9 %reduce-scatter.4.cloned.1.call-done = bf16[2688,512]{1,0:T(8,128)(2,1)} async-done(((bf16[5376,512]{1,0:T(8,128)(2,1)}), bf16[2688,512]{1,0:T(8,128)(2,1)}) %reduce-scatter.4.cloned.1.call-update) | async-done | bytes 2752528
  647.1 3.3 copy.50
  650.4 0.6 fusion.10
  651.0 4.9 psum.7
  656.0 4.6 fusion.13
  (37 shorter events, 0.4 us)
Async XLA Ops:
  6.5 3.4 copy-start.3
  6.5 8.8 %copy-start.4 = (s32[512]{0:T(512)S(1)}, s32[512]{0:T(512)}, u32[]{:S(2)}) copy-start(s32[512]{0:T(512)} %param.21) | copy-start | bytes 6148
  6.5 75.1 %all-gather.6.cloned.1.call-start = ((), (), s32[]{:S(2)}) async-start(), calls=%async_computation.1 | async-start | bytes 8257536 | tf_op jit(solution)/shard_map/all_gather | solution.py:69
  7.3 166.9 %all-gather.10.cloned.1.call-start = ((), (), s32[]{:S(2)}) async-start(), calls=%async_computation.3 | async-start | bytes 11698176 | tf_op jit(solution)/shard_map/all_gather | solution.py:78
  8.0 277.3 %all-gather.8.cloned.1.call-start = ((), (), s32[]{:S(2)}) async-start(), calls=%async_computation.2 | async-start | bytes 11698176 | tf_op jit(solution)/shard_map/all_gather | solution.py:79
  8.7 426.9 %all-gather.12.cloned.1.call-start = ((), (), s32[]{:S(2)}) async-start(), calls=%async_computation.4 | async-start | bytes 23396352 | tf_op jit(solution)/shard_map/all_gather | solution.py:77
  9.3 164.9 %copy-start.7 = (f32[5376]{0:T(1024)S(1)}, f32[5376]{0:T(1024)}, u32[]{:S(2)}) copy-start(f32[5376]{0:T(1024)} %param.12) | copy-start | bytes 64516
  9.3 542.5 %all-gather.14.cloned.1.call-start = ((), (), s32[]{:S(2)}) async-start(), calls=%async_computation.5 | async-start | bytes 23396352 | tf_op jit(solution)/shard_map/all_gather | solution.py:121
  9.9 637.2 %reduce-scatter.4.cloned.1.call-start = ((), (), s32[]{:S(2)}) async-start(), calls=%async_computation.6 | async-start | bytes 8257536
  10.0 6.5 collective-permute-start.2
  13.4 4.9 collective-permute-start.3
  184.5 1.2 copy-start.5
  188.8 280.1 %collective-permute-start.4 = (bf16[512,8,128]{2,0,1:T(8,128)(2,1)}, bf16[512,8,128]{2,0,1:T(8,128)(2,1)}, u32[]{:S(2)}, u32[]{:S(2)}) collective-permute-start(bf16[512,8,128]{2,0,1:T(8,128)(2,1)} %pad_maximum_fusion), channel_id=1, source_target_pairs={{0,4},{2,6},{4,8},{6,10},{8,12},{10,14},{12,16},{14,18},{16,20},{1... | collective-permute-start | bytes 3145736 | tf_op jit(solution)/shard_map/ppermute | solution.py:20
  192.0 276.8 %collective-permute-start.5 = (bf16[512,8,128]{2,0,1:T(8,128)(2,1)}, bf16[512,8,128]{2,0,1:T(8,128)(2,1)}, u32[]{:S(2)}, u32[]{:S(2)}) collective-permute-start(bf16[512,8,128]{2,0,1:T(8,128)(2,1)} %pad_maximum_fusion), channel_id=1, source_target_pairs={{0,2},{2,4},{4,6},{6,8},{8,10},{10,12},{12,14},{14,16},{16,18},{18... | collective-permute-start | bytes 3145736 | tf_op jit(solution)/shard_map/ppermute | solution.py:20
  298.8 196.4 %collective-permute-start = (bf16[512,8,128]{0,2,1:T(8,128)(2,1)}, bf16[512,8,128]{0,2,1:T(8,128)(2,1)}, u32[]{:S(2)}, u32[]{:S(2)}) collective-permute-start(bf16[512,8,128]{0,2,1:T(8,128)(2,1)} %bitcast.65), channel_id=1, source_target_pairs={{0,4},{2,6},{4,8},{6,10},{8,12},{10,14},{12,16},{14,18},{16,20},{1... | collective-permute-start | bytes 3145736 | tf_op jit(solution)/shard_map/ppermute | solution.py:20
  303.2 192.0 %collective-permute-start.1 = (bf16[512,8,128]{0,2,1:T(8,128)(2,1)}, bf16[512,8,128]{0,2,1:T(8,128)(2,1)}, u32[]{:S(2)}, u32[]{:S(2)}) collective-permute-start(bf16[512,8,128]{0,2,1:T(8,128)(2,1)} %bitcast.66), channel_id=1, source_target_pairs={{0,2},{2,4},{4,6},{6,8},{8,10},{10,12},{12,14},{14,16},{16,18},{18... | collective-permute-start | bytes 3145736 | tf_op jit(solution)/shard_map/ppermute | solution.py:20
  453.1 2.0 copy-start
  453.1 3.4 copy-start.6
  468.9 26.4 %copy-start.1 = (bf16[512,1024]{0,1:T(8,128)(2,1)S(1)}, bf16[512,1024]{0,1:T(8,128)(2,1)}, u32[]{:S(2)}) copy-start(bf16[512,1024]{0,1:T(8,128)(2,1)} %copy.51) | copy-start | bytes 3145732
  578.2 77.8 %copy-start.2 = (f32[2688]{0:T(1024)S(1)}, f32[2688]{0:T(1024)}, u32[]{:S(2)}) copy-start(f32[2688]{0:T(1024)} %param.19) | copy-start | bytes 32260
Sparse Core Ops, SparseCore 0:
  8.9 72.7 all-gather.5
  84.0 90.1 all-gather.9
  176.5 108.7 all-gather.7
  286.8 148.8 all-gather.11
  437.1 114.6 all-gather.13
  578.4 68.7 reduce-scatter.3
where the time goes:
time: 670 us; the launch traced here: 667 us
  waiting for transfers between devices  482 us (72%)
  matrix products  102 us (15%)
  local copies, waits for them, and re-layouts  24.3 us (4%)
  other arithmetic  22.9 us (3%)
  starting transfers between devices  17.2 us (3%)
  between operations  13.8 us (2%)
    all_gather x1, waiting for transfers between devices, local(): q_raw = add_rows(lax.all_gather(q_weight, 'ctx', axis=0, tiled=True))  130 us
    all_gather x1, waiting for transfers between devices, local(): v_raw = add_rows(lax.all_gather(value_matrix, 'ctx', axis=0, tiled=True))  91.4 us
    all_gather x1, waiting for transfers between devices, local(): k_raw = add_rows(lax.all_gather(key_matrix, 'ctx', axis=0, tiled=True))  88.8 us
    unnamed x7, waiting for transfers between devices  72.1 us
    all_gather x1, waiting for transfers between devices, local(): gathered = lax.all_gather(inputs, 'tp', axis=1, tiled=True)  60.8 us
    dot_general x3, matrix products, add_rows(): return jnp.dot(normalized, piece, preferred_element_type=jnp.float32)  38 us
    all_gather x1, waiting for transfers between devices, local(): lax.all_gather(out_weight, 'ctx', axis=1, tiled=True)  37.2 us
    sub x1, matrix products, local(): expo = jnp.exp(scores - jnp.max(scores, axis=-1, keepdims=True))  26.4 us
  transfers between devices with their start and end apart: 12, of which 7 were waited for; matrix products, arithmetic and copies ran while one was open for 17% of the time, Pallas kernels for 0%

commit v1 on v0

--- a/solution.py
+++ b/solution.py
@@ -52,6 +52,34 @@
     )
 
 
+def gather_features(inputs):
+    if lax.axis_size("tp") != 2:
+        return lax.all_gather(inputs, "tp", axis=1, tiled=True)
+    other = lax.ppermute(inputs, "tp", [(0, 1), (1, 0)])
+    first = lax.axis_index("tp") == 0
+    return jnp.concatenate(
+        [jnp.where(first, inputs, other), jnp.where(first, other, inputs)], axis=1
+    )
+
+
+def project_out(attended, out_full):
+    if lax.axis_size("tp") != 2:
+        partial_terms = jnp.dot(attended, out_full, preferred_element_type=jnp.float32)
+        return lax.psum_scatter(
+            partial_terms.astype(jnp.bfloat16), "tp", scatter_dimension=1, tiled=True
+        ).astype(jnp.float32)
+    here = lax.axis_index("tp")
+    cols = out_full.shape[1] // 2
+
+    def half(which):
+        weight = lax.dynamic_slice_in_dim(out_full, which * cols, cols, axis=1)
+        return jnp.dot(attended, weight, preferred_element_type=jnp.float32).astype(jnp.bfloat16)
+
+    theirs = half(1 - here)
+    arrived = lax.ppermute(theirs, "tp", [(0, 1), (1, 0)])
+    return half(here).astype(jnp.float32) + arrived.astype(jnp.float32)
+
+
 def local(
     inputs,
     in_gain,
@@ -66,17 +94,17 @@
     positions,
 ):
     tok_rows = inputs.shape[0]
-    gathered = lax.all_gather(inputs, "tp", axis=1, tiled=True)
-    normalized = rms_scale(gathered.astype(jnp.float32), in_gain).astype(jnp.bfloat16)
     q_cols = q_weight.shape[1]
     kv_cols = key_matrix.shape[1]
-
-    def add_rows(piece):
-        return jnp.dot(normalized, piece, preferred_element_type=jnp.float32)
-
-    q_raw = add_rows(lax.all_gather(q_weight, "ctx", axis=0, tiled=True))
-    k_raw = add_rows(lax.all_gather(key_matrix, "ctx", axis=0, tiled=True))
-    v_raw = add_rows(lax.all_gather(value_matrix, "ctx", axis=0, tiled=True))
+    stacked = jnp.concatenate([key_matrix, value_matrix, q_weight], axis=1)
+    weights_full = lax.all_gather(stacked, "ctx", axis=0, tiled=True)
+    out_full = lax.all_gather(out_weight, "ctx", axis=1, tiled=True)
+    gathered = gather_features(inputs)
+    normalized = rms_scale(gathered.astype(jnp.float32), in_gain).astype(jnp.bfloat16)
+    raw = jnp.dot(normalized, weights_full, preferred_element_type=jnp.float32)
+    k_raw = raw[:, :kv_cols]
+    v_raw = raw[:, kv_cols : 2 * kv_cols]
+    q_raw = raw[:, 2 * kv_cols :]
     q_heads = q_cols // HEAD_SIZE
     kv_heads = kv_cols // HEAD_SIZE
     query_heads_all = prepare_heads(
@@ -116,14 +144,7 @@
     weights = (expo / jnp.sum(expo, axis=-1, keepdims=True)).astype(jnp.bfloat16)
     mixed = block_mix(weights, value_all)
     attended = mixed.reshape(tok_rows, q_cols).astype(jnp.bfloat16)
-    partial_terms = jnp.dot(
-        attended,
-        lax.all_gather(out_weight, "ctx", axis=1, tiled=True),
-        preferred_element_type=jnp.float32,
-    )
-    share = lax.psum_scatter(
-        partial_terms.astype(jnp.bfloat16), "tp", scatter_dimension=1, tiled=True
-    ).astype(jnp.float32)
+    share = project_out(attended, out_full)
     squares = lax.psum(jnp.sum(share * share, axis=-1), "tp")
     branch = share * lax.rsqrt(squares[:, None] / MODEL_WIDTH + EPS) * post_gain
     return (inputs.astype(jnp.float32) + branch).astype(jnp.bfloat16)

time: 670 us -> 532 us (0.79)
  waiting for transfers between devices: 482 us -> 345 us
    all_gather x5 -> x2, waiting for transfers between devices: 408 us -> 151 us  [the longest x1 151 us: local(): weights_full = lax.all_gather(stacked, 'ctx', axis=0, tiled=True)]
    ppermute x0 -> x2, waiting for transfers between devices: none -> 109 us  [the longest x1 59.5 us: project_out(): arrived = lax.ppermute(theirs, 'tp', [(0, 1), (1, 0)])]
    ppermute x6, waiting for transfers between devices: 1.9 us -> 85 us  [from_behind(): return lax.ppermute(x, axis, pairs)]
    unnamed x7 -> x2, waiting for transfers between devices: 72.1 us -> 0.71 us
    unnamed x20 -> x36, local copies, waits for them, and re-layouts: 14.9 us -> 10.2 us
    dot_general x4 -> x3, matrix products: 56 us -> 54.6 us  [the longest x1 29.3 us: local(): raw = jnp.dot(normalized, weights_full, preferred_element_type=jnp.float32)]
  transfers between devices with their start and end apart: 12 -> 10, of which waited for: 7 -> 7; matrix products, arithmetic and copies ran while one was open for 17% -> 20% of each run, Pallas kernels for 0% -> 0%
where the time goes in v1:
time: 532 us; the launch traced here: 531 us
  waiting for transfers between devices  345 us (65%)
  matrix products  98.6 us (19%)
  other arithmetic  26.9 us (5%)
  starting transfers between devices  21.3 us (4%)
  local copies, waits for them, and re-layouts  20.3 us (4%)
  between operations  13.8 us (3%)
    all_gather x1, waiting for transfers between devices, local(): weights_full = lax.all_gather(stacked, 'ctx', axis=0, tiled=True)  151 us
    ppermute x6, waiting for transfers between devices, from_behind(): return lax.ppermute(x, axis, pairs)  85 us
    ppermute x1, waiting for transfers between devices, project_out(): arrived = lax.ppermute(theirs, 'tp', [(0, 1), (1, 0)])  59.5 us
    ppermute x1, waiting for transfers between devices, gather_features(): other = lax.ppermute(inputs, 'tp', [(0, 1), (1, 0)])  49.1 us
    dot_general x1, matrix products, local(): raw = jnp.dot(normalized, weights_full, preferred_element_type=jnp.float32)  29.3 us
    sub x1, matrix products, local(): expo = jnp.exp(scores - jnp.max(scores, axis=-1, keepdims=True))  25.7 us
    dot_general x2, matrix products, half(): jnp.dot(attended, weight, preferred_element_type=jnp.float32)  25.3 us
    dot_general x1, matrix products, block_mix(): jnp.einsum('hgqk,khd->qhgd', weights_block, values_block, preferred_eleme...  18.3 us
  transfers between devices with their start and end apart: 10, of which 7 were waited for; matrix products, arithmetic and copies ran while one was open for 20% of the time, Pallas kernels for 0%

profile of v1, /device:TPU:2, one launch (start us, length us, event | category | flops | bytes accessed | tf_op | source)
XLA Modules:
  0.0 531.1 jit_solution(10345726557326241141)
XLA Ops:
  6.5 3.7 pad_maximum_fusion.2
  10.3 0.7 all-gather.5.cloned.1.call-update
  11.0 1.6 collective-permute-start
  12.6 3.4 collective-permute-start.3
  16.1 1.9 collective-permute-start.4
  18.1 1.0 multiply_cosine_fusion
  19.1 1.9 collective-permute-done.4
  21.0 2.5 fusion.31
  23.5 49.1 %collective-permute-done = bf16[512,2688]{1,0:T(8,128)(2,1)} collective-permute-done((bf16[512,2688]{1,0:T(8,128)(2,1)S(1)}, bf16[512,2688]{1,0:T(8,128)(2,1)}, u32[]{:S(2)}, u32[]{:S(2)}) %collective-permute-start) | collective-permute-done | bytes 2752544 | tf_op jit(solution)/shard_map/ppermute | solution.py:58
  72.6 2.4 broadcast_select_fusion.1
  75.1 1.5 copy-done.3
  76.5 1.2 fusion.7
  77.7 151.0 %all-gather.3.cloned.1.call-done = bf16[5376,4096]{1,0:T(8,128)(2,1)} async-done(((bf16[336,4096]{1,0:T(8,128)(2,1)}), bf16[5376,4096]{1,0:T(8,128)(2,1)}) %all-gather.3.cloned.1.call-update) | async-done | bytes 44040208 | tf_op jit(solution)/shard_map/all_gather | solution.py:100
  228.7 29.3 %fusion.14 = f32[512,4096]{1,0:T(8,128)S(1)} fusion(bf16[5376,4096]{1,0:T(8,128)(2,1)} %all-gather.3.cloned.1.call-done, f32[5376]{0:T(1024)S(1)} %copy-done.14, f32[512]{0:T(512)S(1)} %add_rsqrt_fusion.3, bf16[512,2688]{1,0:T(8,128)(2,1)} %copy-done.4, bf16[512,2688]{1,0:T(8,128)(2,1)} %copy-done.3), kind=kOutput, calls=%fused_computation.18 | convolution fusion | flops 22567845888 | bytes 57957376 | tf_op jit(solution)/shard_map/dot_general | solution.py:104
  258.0 0.3 slice_bitcast_fusion.2
  258.3 0.5 copy.51
  258.7 2.4 copy-done.5
  261.2 0.6 multiply_reduce_fusion.2
  261.9 0.6 fusion.32
  262.6 0.8 subtract_convert_fusion
  263.3 1.5 pad_maximum_fusion.3
  264.9 3.8 collective-permute-start.5
  268.7 1.9 collective-permute-start.6
  270.6 1.8 slice.48
  272.4 1.4 copy.49
  273.8 2.9 collective-permute-start.1
  276.7 3.9 collective-permute-start.2
  280.7 2.6 slice_bitcast_fusion
  283.3 0.9 copy.52
  284.2 1.9 copy-done
  286.2 1.2 multiply_reduce_fusion.1
  287.3 0.1 copy.41
  287.4 0.1 copy.42
  287.6 4.2 multiply_multiply_fusion
  291.8 1.5 multiply_subtract_fusion
  293.3 3.4 copy.43
  296.7 3.3 copy.44
  300.0 15.5 %collective-permute-done.5 = bf16[512,8,128]{2,0,1:T(8,128)(2,1)} collective-permute-done((bf16[512,8,128]{2,0,1:T(8,128)(2,1)}, bf16[512,8,128]{2,0,1:T(8,128)(2,1)}, u32[]{:S(2)}, u32[]{:S(2)}) %collective-permute-start.5) | collective-permute-done | bytes 1048608 | tf_op jit(solution)/shard_map/ppermute | solution.py:20
  315.5 44.0 %collective-permute-done.6 = bf16[512,8,128]{2,0,1:T(8,128)(2,1)} collective-permute-done((bf16[512,8,128]{2,0,1:T(8,128)(2,1)}, bf16[512,8,128]{2,0,1:T(8,128)(2,1)}, u32[]{:S(2)}, u32[]{:S(2)}) %collective-permute-start.6) | collective-permute-done | bytes 1048608 | tf_op jit(solution)/shard_map/ppermute | solution.py:20
  359.5 25.7 %fusion.44 = (f32[8,2,512]{2,1,0:T(2,128)S(1)}, f32[8,2,512,1536]{2,3,1,0:T(8,128)}) fusion(pred[512,1536]{0,1:T(8,128)(4,1)} %fusion.31, bf16[512,8,64]{2,0,1:T(8,128)(2,1)S(1)} %get-tuple-element.12, bf16[512,8,64]{2,0,1:T(8,128)(2,1)S(1)} %get-tuple-element.11, bf16[512,8,128]{2,0,1:T(8,128)(2,1)} %collective-permute-done.6, ...), kind=kOutput, calls=%fused_computation.77 | convolution fusion | flops 3274704384 | bytes 58490880 | tf_op jit(solution)/shard_map/sub | solution.py:143
  385.3 23.6 %collective-permute-done.2 = bf16[512,8,128]{0,2,1:T(8,128)(2,1)} collective-permute-done((bf16[512,8,128]{0,2,1:T(8,128)(2,1)}, bf16[512,8,128]{0,2,1:T(8,128)(2,1)}, u32[]{:S(2)}, u32[]{:S(2)}) %collective-permute-start.2) | collective-permute-done | bytes 1048608 | tf_op jit(solution)/shard_map/ppermute | solution.py:20
  408.8 18.3 %fusion.33 = bf16[8,128,2,512]{3,1,2,0:T(8,128)(2,1)S(1)} fusion(f32[8,2,512,1536]{2,3,1,0:T(8,128)} %get-tuple-element.16, f32[8,2,512]{2,1,0:T(2,128)S(1)} %get-tuple-element.15, bf16[512,8,128]{0,2,1:T(8,128)(2,1)S(1)} %bitcast.60, bf16[512,8,128]{0,2,1:T(8,128)(2,1)} %collective-permute-done.2, bf16[512,8,128]{0,2,1:T(8,128)(2,1)} %collective-permute-done.1), kind=kOutput, calls=%fused_computation.56 | convolution fusion | flops 3256877056 | bytes 55607296 | tf_op jit(solution)/shard_map/hgqk,khd->qhgd/dot_general | solution.py:50
  427.2 12.5 %fusion.21 = bf16[512,2688]{1,0:T(8,128)(2,1)} fusion(bf16[512,2048]{0,1:T(8,128)(2,1)S(1)} %bitcast.61, bf16[2048,5376]{0,1:T(8,128)(2,1)} %all-gather.5.cloned.1.call-done, s32[]{:T(128)S(6)} %select_n.27), kind=kOutput, calls=%fused_computation.28 | convolution fusion | flops 5638520832 | bytes 15859716 | tf_op jit(solution)/shard_map/dot_general | solution.py:76
  439.7 1.7 collective-permute-start.7
  441.5 59.5 %collective-permute-done.7 = bf16[512,2688]{1,0:T(8,128)(2,1)} collective-permute-done((bf16[512,2688]{1,0:T(8,128)(2,1)}, bf16[512,2688]{1,0:T(8,128)(2,1)}, u32[]{:S(2)}, u32[]{:S(2)}) %collective-permute-start.7) | collective-permute-done | bytes 2752544 | tf_op jit(solution)/shard_map/ppermute | solution.py:79
  501.0 12.7 %multiply_reduce_fusion = (f32[512]{0:T(512)S(1)}, bf16[512,2688]{1,0:T(8,128)(2,1)}) fusion(bf16[512,2688]{1,0:T(8,128)(2,1)} %collective-permute-done.7, bf16[512,2048]{0,1:T(8,128)(2,1)} %bitcast.62, bf16[2048,5376]{0,1:T(8,128)(2,1)} %all-gather.5.cloned.1.call-done, s32[]{:T(128)S(6)} %select_n.26), kind=kOutput, calls=%fused_computation.21 | convolution fusion | flops 5645401600 | bytes 18614276 | tf_op jit(solution)/shard_map/dot_general | solution.py:76
  513.7 4.9 psum.7
  518.7 5.7 %add_convert_fusion = bf16[512,2688]{1,0:T(8,128)(2,1)} fusion(bf16[512,2688]{1,0:T(8,128)(2,1)S(1)} %copy-done.2, bf16[512,2688]{1,0:T(8,128)(2,1)} %collective-permute-done.7, bf16[512,2688]{1,0:T(8,128)(2,1)} %get-tuple-element.18, f32[2688]{0:T(1024)S(1)} %copy-done.9, f32[512]{0:T(512)S(1)} %add_rsqrt_fusion.2), kind=kLoop, calls=%fused_computation.20 | loop fusion | flops 11010048 | bytes 11022848 | tf_op jit(solution)/shard_map/convert_element_type | solution.py:150
  (46 shorter events, 0.3 us)
Async XLA Ops:
  6.5 4.5 copy-start.1
  6.5 6.1 %copy-start.10 = (s32[512]{0:T(512)S(1)}, s32[512]{0:T(512)}, u32[]{:S(2)}) copy-start(s32[512]{0:T(512)} %param.20) | copy-start | bytes 6148
  6.5 11.5 %copy-start.11 = (s32[512]{0:T(512)S(1)}, s32[512]{0:T(512)}, u32[]{:S(2)}) copy-start(s32[512]{0:T(512)} %param.21) | copy-start | bytes 6148
  6.5 222.1 %all-gather.3.cloned.1.call-start = ((), (), s32[]{:S(2)}) async-start(), calls=%async_computation | async-start | bytes 46792704 | tf_op jit(solution)/shard_map/all_gather | solution.py:100
  10.3 416.9 %all-gather.5.cloned.1.call-start = ((), (), s32[]{:S(2)}) async-start(), calls=%async_computation.1 | async-start | bytes 23396352 | tf_op jit(solution)/shard_map/all_gather | solution.py:101
  11.0 61.6 %collective-permute-start = (bf16[512,2688]{1,0:T(8,128)(2,1)S(1)}, bf16[512,2688]{1,0:T(8,128)(2,1)}, u32[]{:S(2)}, u32[]{:S(2)}) collective-permute-start(bf16[512,2688]{1,0:T(8,128)(2,1)S(1)} %copy-done.1), channel_id=1, source_target_pairs={{0,1},{1,0},{2,3},{3,2},{4,5},{5,4},{6,7},{7,6},{8,9},{9,8},{10,11... | collective-permute-start | bytes 8257544 | tf_op jit(solution)/shard_map/ppermute | solution.py:58
  12.6 6.5 %collective-permute-start.3 = (s32[512]{0:T(512)S(1)}, s32[512]{0:T(512)S(1)}, u32[]{:S(2)}, u32[]{:S(2)}) collective-permute-start(s32[512]{0:T(512)S(1)} %copy-done.10), channel_id=1, source_target_pairs={{0,4},{2,6},{4,8},{6,10},{8,12},{10,14},{12,16},{14,18},{16,20},{1... | collective-permute-start | bytes 6152 | tf_op jit(solution)/shard_map/ppermute | solution.py:20
  16.1 4.9 collective-permute-start.4
  19.1 243.5 %copy-start.6 = (f32[512,64]{1,0:T(8,128)}, f32[512,64]{1,0:T(8,128)S(1)}, u32[]{:S(2)}) copy-start(f32[512,64]{1,0:T(8,128)S(1)} %get-tuple-element.14) | copy-start | bytes 393220
  75.0 1.5 copy-start.3
  75.0 2.6 copy-start.4
  75.0 153.6 %copy-start.14 = (f32[5376]{0:T(1024)S(1)}, f32[5376]{0:T(1024)}, u32[]{:S(2)}) copy-start(f32[5376]{0:T(1024)} %param.12) | copy-start | bytes 64516
  258.0 3.2 copy-start.5
  258.2 3.7 copy-start.12
  264.9 50.7 %collective-permute-start.5 = (bf16[512,8,128]{2,0,1:T(8,128)(2,1)}, bf16[512,8,128]{2,0,1:T(8,128)(2,1)}, u32[]{:S(2)}, u32[]{:S(2)}) collective-permute-start(bf16[512,8,128]{2,0,1:T(8,128)(2,1)} %pad_maximum_fusion.3), channel_id=1, source_target_pairs={{0,4},{2,6},{4,8},{6,10},{8,12},{10,14},{12,16},{14,18},{16,20},{1... | collective-permute-start | bytes 3145736 | tf_op jit(solution)/shard_map/ppermute | solution.py:20
  268.7 90.8 %collective-permute-start.6 = (bf16[512,8,128]{2,0,1:T(8,128)(2,1)}, bf16[512,8,128]{2,0,1:T(8,128)(2,1)}, u32[]{:S(2)}, u32[]{:S(2)}) collective-permute-start(bf16[512,8,128]{2,0,1:T(8,128)(2,1)} %pad_maximum_fusion.3), channel_id=1, source_target_pairs={{0,2},{2,4},{4,6},{6,8},{8,10},{10,12},{12,14},{14,16},{16,18},{18... | collective-permute-start | bytes 3145736 | tf_op jit(solution)/shard_map/ppermute | solution.py:20
  273.8 111.5 %collective-permute-start.1 = (bf16[512,8,128]{0,2,1:T(8,128)(2,1)}, bf16[512,8,128]{0,2,1:T(8,128)(2,1)}, u32[]{:S(2)}, u32[]{:S(2)}) collective-permute-start(bf16[512,8,128]{0,2,1:T(8,128)(2,1)} %bitcast.58), channel_id=1, source_target_pairs={{0,4},{2,6},{4,8},{6,10},{8,12},{10,14},{12,16},{14,18},{16,20},{1... | collective-permute-start | bytes 3145736 | tf_op jit(solution)/shard_map/ppermute | solution.py:20
  276.7 132.1 %collective-permute-start.2 = (bf16[512,8,128]{0,2,1:T(8,128)(2,1)}, bf16[512,8,128]{0,2,1:T(8,128)(2,1)}, u32[]{:S(2)}, u32[]{:S(2)}) collective-permute-start(bf16[512,8,128]{0,2,1:T(8,128)(2,1)} %bitcast.59), channel_id=1, source_target_pairs={{0,2},{2,4},{4,6},{6,8},{8,10},{10,12},{12,14},{14,16},{16,18},{18... | collective-permute-start | bytes 3145736 | tf_op jit(solution)/shard_map/ppermute | solution.py:20
  284.2 2.0 copy-start
  284.2 3.4 copy-start.13
  287.6 4.2 copy-start.7
  359.5 49.3 %copy-start.8 = (bf16[512,1024]{0,1:T(8,128)(2,1)S(1)}, bf16[512,1024]{0,1:T(8,128)(2,1)}, u32[]{:S(2)}) copy-start(bf16[512,1024]{0,1:T(8,128)(2,1)} %copy.49) | copy-start | bytes 3145732
  427.2 12.6 %copy-start.15 = (bf16[8,128,2,512]{3,1,2,0:T(8,128)(2,1)}, bf16[8,128,2,512]{3,1,2,0:T(8,128)(2,1)S(1)}, u32[]{:S(2)}) copy-start(bf16[8,128,2,512]{3,1,2,0:T(8,128)(2,1)S(1)} %fusion.33) | copy-start | bytes 6291460
  439.7 61.2 %collective-permute-start.7 = (bf16[512,2688]{1,0:T(8,128)(2,1)}, bf16[512,2688]{1,0:T(8,128)(2,1)}, u32[]{:S(2)}, u32[]{:S(2)}) collective-permute-start(bf16[512,2688]{1,0:T(8,128)(2,1)} %fusion.21), channel_id=1, source_target_pairs={{0,1},{1,0},{2,3},{3,2},{4,5},{5,4},{6,7},{7,6},{8,9},{9,8},{10,11... | collective-permute-start | bytes 8257544 | tf_op jit(solution)/shard_map/ppermute | solution.py:79
  441.5 77.2 %copy-start.2 = (bf16[512,2688]{1,0:T(8,128)(2,1)S(1)}, bf16[512,2688]{1,0:T(8,128)(2,1)}, u32[]{:S(2)}) copy-start(bf16[512,2688]{1,0:T(8,128)(2,1)} %param.11) | copy-start | bytes 8257540
  441.5 77.2 %copy-start.9 = (f32[2688]{0:T(1024)S(1)}, f32[2688]{0:T(1024)}, u32[]{:S(2)}) copy-start(f32[2688]{0:T(1024)} %param.19) | copy-start | bytes 32260
Sparse Core Ops, SparseCore 0:
  10.4 218.2 all-gather.2
  230.2 171.3 all-gather.4

commit v2 on v1

--- a/solution.py
+++ b/solution.py
@@ -1,6 +1,10 @@
+import functools
+
 import jax
 import jax.numpy as jnp
 from jax import lax
+from jax.experimental import pallas as pl
+from jax.experimental.pallas import tpu as pltpu
 from jax.sharding import PartitionSpec as P
 
 MODEL_WIDTH = 5376
@@ -13,33 +17,302 @@
 ROPE_BASE = 10000.0
 MASKED = -1e30
 
+INNER = 4
+QUERY_BLOCK = 256
+
+
+def rms_scale(values, gain):
+    return values * lax.rsqrt(jnp.mean(values * values, axis=-1, keepdims=True) + EPS) * gain
+
+
+def angles_of(position, half_dim):
+    frequency = ROPE_BASE ** (-jnp.arange(half_dim, dtype=jnp.float32) / half_dim)
+    angles = position.astype(jnp.float32)[:, None] * frequency[None, :]
+    return jnp.cos(angles)[:, None, :], jnp.sin(angles)[:, None, :]
+
+
+def rotate(values, cosine, sine):
+    half_dim = values.shape[-1] // 2
+    first = values[..., :half_dim]
+    second = values[..., half_dim:]
+    return jnp.concatenate(
+        [first * cosine - second * sine, second * cosine + first * sine], axis=-1
+    )
+
+
+def prepare_heads(projected, gain, turn, factor):
+    shaped = projected.reshape(projected.shape[0], -1, HEAD_SIZE)
+    turned = rotate(rms_scale(shaped, gain), *turn) * factor
+    return turned.astype(jnp.bfloat16).reshape(projected.shape)
+
+
+def swap(x, mask):
+    size = lax.axis_size("ctx")
+    return lax.ppermute(x, "ctx", [(c, c ^ mask) for c in range(size)])
+
+
+def swap_tp(x):
+    return lax.ppermute(x, "tp", [(0, 1), (1, 0)])
+
+
+def ring_step(x, by=1):
+    size = lax.axis_size("ctx")
+    return lax.ppermute(x, "ctx", [(c, (c + by * INNER) % size) for c in range(size)])
+
+
+def after(x, *others):
+    return lax.optimization_barrier((x, *others))[0]
+
+
+def placed(blocks, places):
+    whole = jnp.zeros((len(blocks), *blocks[0].shape), blocks[0].dtype)
+    for block, place in zip(blocks, places):
+        whole = lax.dynamic_update_index_in_dim(whole, block, place, 0)
+    return whole
+
+
+def attend_kernel(pos_ref, q_ref, k_ref, v_ref, o_ref):
+    start = pl.multiple_of(pl.program_id(0) * QUERY_BLOCK, QUERY_BLOCK)
+    window = VISIBLE_SPAN + QUERY_BLOCK
+    keys = k_ref[pl.ds(start, window), :]
+    values = v_ref[pl.ds(start, window), :]
+    shape = (QUERY_BLOCK, window)
+    last = lax.broadcasted_iota(jnp.int32, shape, 0) + VISIBLE_SPAN
+    column = lax.broadcasted_iota(jnp.int32, shape, 1)
+    first = last - jnp.minimum(pos_ref[...], VISIBLE_SPAN - 1)
+    allowed = (column <= last) & (column >= first)
+    for head in range(q_ref.shape[1] // HEAD_SIZE):
+        span = slice(head * HEAD_SIZE, (head + 1) * HEAD_SIZE)
+        scores = lax.dot_general(
+            q_ref[:, span], keys, (((1,), (1,)), ((), ())), preferred_element_type=jnp.float32
+        )
+        scores = jnp.where(allowed, scores, MASKED)
+        expo = jnp.exp(scores - jnp.max(scores, axis=-1, keepdims=True))
+        weights = (expo / jnp.sum(expo, axis=-1, keepdims=True)).astype(jnp.bfloat16)
+        mixed = jnp.dot(weights, values, preferred_element_type=jnp.float32)
+        o_ref[:, span] = mixed.astype(jnp.bfloat16)
+
+
+def attend(position, queries, keys, values):
+    tokens, cols = queries.shape
+    window = VISIBLE_SPAN + QUERY_BLOCK
+    heads = cols // HEAD_SIZE
+    return pl.pallas_call(
+        attend_kernel,
+        grid=(tokens // QUERY_BLOCK,),
+        in_specs=[
+            pl.BlockSpec((QUERY_BLOCK, 1), lambda b: (b, 0)),
+            pl.BlockSpec((QUERY_BLOCK, cols), lambda b: (b, 0)),
+            pl.BlockSpec(keys.shape, lambda b: (0, 0)),
+            pl.BlockSpec(values.shape, lambda b: (0, 0)),
+        ],
+        out_specs=pl.BlockSpec((QUERY_BLOCK, cols), lambda b: (b, 0)),
+        out_shape=jax.ShapeDtypeStruct((tokens, cols), jnp.bfloat16),
+        compiler_params=pltpu.CompilerParams(vmem_limit_bytes=40 * 2**20),
+        cost_estimate=pl.CostEstimate(
+            flops=4 * tokens * window * cols,
+            bytes_accessed=4 * tokens * cols + 4 * keys.shape[0] * HEAD_SIZE,
+            transcendentals=heads * tokens * window,
+        ),
+    )(position, queries, keys, values)
+
+
+def group_kernel(inner, pieces, place_ref, *refs):
+    lefts, weight_ref, o_ref = refs[: inner * pieces], refs[-2], refs[-1]
+    place = place_ref[0]
+    depth = lefts[0].shape[1]
+    total = None
+    for m in range(inner):
+        for piece in range(pieces):
+            row = pl.multiple_of(((place ^ m) * pieces + piece) * depth, depth)
+            term = jnp.dot(
+                lefts[m * pieces + piece][...],
+                weight_ref[pl.ds(row, depth), :],
+                preferred_element_type=jnp.float32,
+            )
+            total = term if total is None else total + term
+    o_ref[...] = total.astype(jnp.bfloat16)
+
+
+def group_product(place, attended, weight):
+    lefts = [piece for pieces in attended for piece in pieces]
+    tokens, depth = lefts[0].shape
+    rows, cols = weight.shape
+    block = 512
+    return pl.pallas_call(
+        functools.partial(group_kernel, len(attended), len(attended[0])),
+        grid=(tokens // block,),
+        in_specs=[pl.BlockSpec(memory_space=pltpu.SMEM)]
+        + [pl.BlockSpec((block, depth), lambda b: (b, 0)) for _ in lefts]
+        + [pl.BlockSpec((rows, cols), lambda b: (0, 0))],
+        out_specs=pl.BlockSpec((block, cols), lambda b: (b, 0)),
+        out_shape=jax.ShapeDtypeStruct((tokens, cols), jnp.bfloat16),
+        compiler_params=pltpu.CompilerParams(vmem_limit_bytes=40 * 2**20),
+        cost_estimate=pl.CostEstimate(
+            flops=2 * tokens * rows * cols,
+            bytes_accessed=2 * (tokens * rows + rows * cols + tokens * cols),
+            transcendentals=0,
+        ),
+    )(jnp.reshape(place, (1,)), *lefts, weight)
+
+
+def plane_inputs(inputs, in_gain, place, side):
+    rows = inputs.shape[0]
+    half = rows // 2
+    a, b = inputs[:half], inputs[half:]
+    a_y, b_x = swap_tp(a), swap(b, 2)
+    a_x, a_xy = swap(a, 2), swap(a_y, 2)
+    b_y, b_xy = swap_tp(b), swap_tp(b_x)
+    mine = {(0, 0): (a, a_y), (0, 2): (a_x, a_xy), (1, 0): (b, b_y), (1, 2): (b_x, b_xy)}
+    normed = jnp.zeros((INNER * rows, 2 * inputs.shape[1]), jnp.bfloat16)
+    for core in (0, 1):
+        for (part, mask), (near, far) in mine.items():
+            if core:
+                near, far = swap(near, 1), swap(far, 1)
+            low = jnp.where(side == 0, near, far)
+            high = jnp.where(side == 0, far, near)
+            tokens = jnp.concatenate([low, high], axis=1).astype(jnp.float32)
+            block = rms_scale(tokens, in_gain).astype(jnp.bfloat16)
+            row = (place ^ mask ^ core) * rows + part * half
+            normed = lax.dynamic_update_slice_in_dim(normed, block, row, 0)
+    return normed
+
+
+def quarter(weights, which):
+    cut = [
+        lax.dynamic_slice_in_dim(w, which * (w.shape[1] // INNER), w.shape[1] // INNER, axis=1)
+        for w in weights
+    ]
+    return jnp.concatenate(cut, axis=1) if len(cut) > 1 else cut[0]
+
+
+def plane_rows(weights, place):
+    blocks = [quarter(weights, place)]
+    for mask in range(1, INNER):
+        blocks.append(swap(quarter(weights, place ^ mask), mask))
+    whole = placed(blocks, [place ^ mask for mask in range(INNER)])
+    return whole.reshape(-1, whole.shape[-1])
+
+
+def by_planes(
+    inputs,
+    in_gain,
+    q_weight,
+    key_matrix,
+    value_matrix,
+    q_gain,
+    key_norm_gain,
+    out_weight,
+    post_gain,
+    segment_ids,
+    positions,
+):
+    tok_rows = inputs.shape[0]
+    planes = lax.axis_size("ctx") // INNER
+    me = lax.axis_index("ctx")
+    place, plane = me % INNER, me // INNER
+    side = lax.axis_index("tp")
+    plane_tokens = INNER * tok_rows
+
+    kv_start = plane_rows([key_matrix, value_matrix], place)
+    q_start = plane_rows([q_weight], place)
+    q_half = q_start.shape[1] // 2
+    hops = {}
+
+    def ring(name, block):
+        hops[name] = [block]
+
+    def hop(name, *others):
+        block = hops[name][-1]
+        hops[name].append(ring_step(after(block, *others) if others else block))
+        return hops[name][-1]
+
+    kv_half = kv_start.shape[1] // 2
+    ring("k", kv_start[:, :kv_half])
+    ring("v", kv_start[:, kv_half:])
+    ring("qa", q_start[:, :q_half])
+    ring("qb", q_start[:, q_half:])
+    ring("o", out_weight)
+    steps = planes - 1
+    previous = []
+    order = []
+    for _ in range(steps):
+        order += ["k", "v"]
+    for _ in range(steps):
+        order += ["qa"]
+    for _ in range(steps):
+        order += ["qb"]
+    for _ in range(steps):
+        order += ["o"]
+    for name in order:
+        previous.append(hop(name, *previous[-2:-1]))
+
+    source = [(plane - d) % planes for d in range(planes)]
+
+    def whole_rows(name):
+        return placed(hops[name], source).reshape(MODEL_WIDTH, -1)
+
+    normed = plane_inputs(inputs, in_gain, place, side)
+    position_blocks = [positions] + [swap(positions, mask) for mask in range(1, INNER)]
+    position = placed(position_blocks, [place ^ mask for mask in range(INNER)]).reshape(-1)
+    turn = angles_of(position, HEAD_SIZE // 2)
+    turn = lax.optimization_barrier(turn)
+
+    def project(name):
+        return jnp.dot(normed, whole_rows(name), preferred_element_type=jnp.float32)
+
+    size = lax.axis_size("ctx")
+    up = [(c, c + INNER) for c in range(size - INNER)]
+
+    def with_halo(own):
+        far = lax.ppermute(own[plane_tokens - VISIBLE_SPAN :], "ctx", up)
+        return jnp.concatenate([far, own], axis=0)
+
+    keys = with_halo(prepare_heads(project("k"), key_norm_gain, turn, 1.0))
+    values = with_halo(project("v").astype(jnp.bfloat16))
+    factor = (MODEL_WIDTH // QUERY_HEADS) ** (-0.5)
+    attended = [[] for _ in range(INNER)]
+    for index, name in enumerate(("qa", "qb")):
+        queries = prepare_heads(project(name), q_gain, turn, factor)
+        span = slice(index * HEAD_SIZE, (index + 1) * HEAD_SIZE)
+        own = attend(position[:, None], queries, keys[:, span], values[:, span])
+        far = swap(own, 2)
+        for mask, piece in zip(range(INNER), (own, swap(own, 1), far, swap(far, 1))):
+            attended[mask].append(piece)
+
+    both = ("ctx", "tp")
+    cols = out_weight.shape[1]
+    per_side = planes // 2
+    arrived, places = [], []
+    for d in range(planes):
+        term = group_product(place, attended, hops["o"][d])
+        pairs, inside = [], []
+        for c in range(size):
+            home = ((c // INNER - d) % planes) // per_side
+            pairs.append((2 * c + 1 - home, 2 * c + home))
+            inside.append(2 * c + home)
+        other = lax.ppermute(term, both, pairs)
+        total = (term.astype(jnp.float32) + other.astype(jnp.float32)).astype(jnp.bfloat16)
+        for mask in range(INNER):
+            row = (place ^ mask) * tok_rows
+            block = lax.dynamic_slice_in_dim(total, row, tok_rows, axis=0)
+            if mask:
+                block = lax.ppermute(block, both, [(n, n ^ (2 * mask)) for n in inside])
+            arrived.append(block)
+            places.append(source[d] * INNER + (place ^ mask))
+    slots = placed(arrived, places)
+    mine = lax.dynamic_slice_in_dim(slots, side * per_side * INNER, per_side * INNER, axis=0)
+    share = mine.transpose(1, 0, 2).reshape(tok_rows, -1).astype(jnp.float32)
+    own_squares = jnp.sum(share * share, axis=-1)
+    squares = own_squares + swap_tp(own_squares)
+    branch = share * lax.rsqrt(squares[:, None] / MODEL_WIDTH + EPS) * post_gain
+    return (inputs.astype(jnp.float32) + branch).astype(jnp.bfloat16)
+
 
 def from_behind(x, axis, by):
     size = lax.axis_size(axis)
     pairs = [(i, i + by) for i in range(size) if 0 <= i + by < size]
     return lax.ppermute(x, axis, pairs)
-
-
-def rms_scale(values, gain):
-    return values * lax.rsqrt(jnp.mean(values * values, axis=-1, keepdims=True) + EPS) * gain
-
-
-def rotate(values, position):
-    half_dim = values.shape[-1] // 2
-    frequency = ROPE_BASE ** (-jnp.arange(half_dim, dtype=jnp.float32) / half_dim)
-    angles = position.astype(jnp.float32)[:, None] * frequency[None, :]
-    cosine = jnp.cos(angles)[:, None, :]
-    sine = jnp.sin(angles)[:, None, :]
-    first = values[..., :half_dim]
-    second = values[..., half_dim:]
-    return jnp.concatenate(
-        [first * cosine - second * sine, second * cosine + first * sine], axis=-1
-    )
-
-
-def prepare_heads(projected, gain, position, heads, factor):
-    shaped = projected.reshape(projected.shape[0], heads, HEAD_SIZE)
-    return (rotate(rms_scale(shaped, gain), position) * factor).astype(jnp.bfloat16)
 
 
 def block_scores(grouped, keys_block):
@@ -80,7 +353,7 @@
     return half(here).astype(jnp.float32) + arrived.astype(jnp.float32)
 
 
-def local(
+def by_devices(
     inputs,
     in_gain,
     q_weight,
@@ -107,10 +380,12 @@
     q_raw = raw[:, 2 * kv_cols :]
     q_heads = q_cols // HEAD_SIZE
     kv_heads = kv_cols // HEAD_SIZE
+    turn = angles_of(positions, HEAD_SIZE // 2)
     query_heads_all = prepare_heads(
-        q_raw, q_gain, positions, q_heads, (MODEL_WIDTH // QUERY_HEADS) ** (-0.5)
-    )
-    keys_own = prepare_heads(k_raw, key_norm_gain, positions, kv_heads, 1.0)
+        q_raw, q_gain, turn, (MODEL_WIDTH // QUERY_HEADS) ** (-0.5)
+    )
+    keys_own = prepare_heads(k_raw, key_norm_gain, turn, 1.0)
+    keys_own = keys_own.reshape(tok_rows, kv_heads, HEAD_SIZE)
     values_own = v_raw.reshape(tok_rows, kv_heads, HEAD_SIZE).astype(jnp.bfloat16)
     reach = (VISIBLE_SPAN - 1) // tok_rows + 1
     key_list = [keys_own]
@@ -150,9 +425,14 @@
     return (inputs.astype(jnp.float32) + branch).astype(jnp.bfloat16)
 
 
+def fits_planes(sizes):
+    return sizes["tp"] == 2 and sizes["ctx"] == 16
+
+
 def solution(mesh):
+    sizes = mesh.shape
     return jax.shard_map(
-        local,
+        by_planes if fits_planes(sizes) else by_devices,
         mesh=mesh,
         in_specs=(
             P("ctx", "tp"),

time: 532 us -> 656 us (1.23); the launches traced: 531 us -> 645 us
  local copies, waits for them, and re-layouts: 20.3 us -> 152 us
  waiting for transfers between devices: 345 us -> 267 us
  Pallas kernels: 0 us -> 55.7 us
  matrix products: 98.6 us -> 44.9 us
  starting transfers between devices: 21.3 us -> 63.5 us
  other arithmetic: 26.9 us -> 59.6 us
  between operations: 13.8 us -> 1.74 us
    all_gather x2 -> x0, waiting for transfers between devices: 151 us -> none  [the longest x1 151 us: local(): weights_full = lax.all_gather(stacked, 'ctx', axis=0, tiled=True)]
    ppermute x8 -> x63, waiting for transfers between devices: 194 us -> 267 us  [the longest x15 136 us: ring_step(): lax.ppermute(x, 'ctx', [(c, (c + by * INNER) % size) for c in range(size)])]
    pallas_call x0 -> x6, Pallas kernels: none -> 55.7 us  [the longest x2 30.2 us: attend(): pl.pallas_call(attend_kernel, grid=(tokens // QUERY_BLOCK,), in_specs=[pl...]
    ppermute x8 -> x63, starting transfers between devices: 21.3 us -> 63.5 us  [the longest x12 22.7 us: by_planes(): block = lax.ppermute(block, both, [(n, n ^ 2 * mask) for n in inside])]
    dynamic_update_slice x0 -> x42, local copies, waits for them, and re-layouts: none -> 39.7 us  [placed(): whole = lax.dynamic_update_index_in_dim(whole, block, place, 0)]
    dot_general x4, matrix products: 72.9 us -> 44.9 us  [project(): return jnp.dot(normed, whole_rows(name), preferred_element_type=jnp.float32)]
    sub x1 -> x0, matrix products: 25.7 us -> none  [local(): expo = jnp.exp(scores - jnp.max(scores, axis=-1, keepdims=True))]
    broadcast_in_dim x0 -> x15, local copies, waits for them, and re-layouts: none -> 24.1 us  [the longest x12 13.7 us: placed(): whole = lax.dynamic_update_index_in_dim(whole, block, place, 0)]
  transfers between devices with their start and end apart: 10 -> 63, of which waited for: 7 -> 24; matrix products, arithmetic and copies ran while one was open for 20% -> 36% of each run, Pallas kernels for 0% -> 9%
where the time goes in v2:
time: 656 us; the launch traced here: 645 us
  waiting for transfers between devices  267 us (41%)
  local copies, waits for them, and re-layouts  152 us (23%)
  starting transfers between devices  63.5 us (10%)
  other arithmetic  59.6 us (9%)
  Pallas kernels  55.7 us (8%)
  matrix products  44.9 us (7%)
    ppermute x15, waiting for transfers between devices, ring_step(): lax.ppermute(x, 'ctx', [(c, (c + by * INNER) % size) for c in range(size)])  136 us
    ppermute x26, waiting for transfers between devices, swap(): return lax.ppermute(x, 'ctx', [(c, c ^ mask) for c in range(size)])  68.4 us
    dot_general x4, matrix products, project(): return jnp.dot(normed, whole_rows(name), preferred_element_type=jnp.float32)  44.9 us
    dynamic_update_slice x42, local copies, waits for them, and re-layouts, placed(): whole = lax.dynamic_update_index_in_dim(whole, block, place, 0)  39.7 us
    pallas_call x2, Pallas kernels, attend(): pl.pallas_call(attend_kernel, grid=(tokens // QUERY_BLOCK,), in_specs=[pl...  30.2 us
    pallas_call x4, Pallas kernels, group_product(): pl.pallas_call(functools.partial(group_kernel, len(attended), len(attende...  25.5 us
    ppermute x4, waiting for transfers between devices, swap_tp(): return lax.ppermute(x, 'tp', [(0, 1), (1, 0)])  24.6 us
    ppermute x4, waiting for transfers between devices, by_planes(): other = lax.ppermute(term, both, pairs)  24.4 us
  transfers between devices with their start and end apart: 63, of which 24 were waited for; matrix products, arithmetic and copies ran while one was open for 36% of the time, Pallas kernels for 9%

profile of v2, /device:TPU:2, one launch (start us, length us, event | category | flops | bytes accessed | tf_op | source)
XLA Modules:
  0.0 644.7 jit_solution(7974967872277493476)
XLA Ops:
  0.0 2.7 slice.58
  12.7 23.5 %collective-permute-done.1 = s32[512]{0:T(512)S(1)} collective-permute-done((s32[512]{0:T(512)S(1)}, s32[512]{0:T(512)S(1)}, u32[]{:S(2)}, u32[]{:S(2)}) %collective-permute-start.1) | collective-permute-done | bytes 2080 | tf_op jit(solution)/shard_map/ppermute | solution.py:51
  41.8 5.7 collective-permute-done.21
  54.8 4.6 collective-permute-done.22
  59.3 6.2 collective-permute-done.19
  82.7 3.4 collective-permute-done.23
  86.1 14.7 %collective-permute-done.27 = bf16[1344,256]{1,0:T(8,128)(2,1)S(1)} collective-permute-done((bf16[1344,256]{1,0:T(8,128)(2,1)S(1)}, bf16[1344,256]{1,0:T(8,128)(2,1)S(1)}, u32[]{:S(2)}, u32[]{:S(2)}) %collective-permute-start.27) | collective-permute-done | bytes 688160 | tf_op jit(solution)/shard_map/ppermute | solution.py:60
  102.6 2.8 broadcast_select_fusion.11
  106.5 9.0 %collective-permute-done.24 = bf16[1344,256]{1,0:T(8,128)(2,1)S(1)} collective-permute-done((bf16[1344,256]{1,0:T(8,128)(2,1)S(1)}, bf16[1344,256]{1,0:T(8,128)(2,1)S(1)}, u32[]{:S(2)}, u32[]{:S(2)}) %collective-permute-start.24) | collective-permute-done | bytes 688160 | tf_op jit(solution)/shard_map/ppermute | solution.py:60
  115.6 14.7 %collective-permute-done.28 = bf16[1344,256]{1,0:T(8,128)(2,1)S(1)} collective-permute-done((bf16[1344,256]{1,0:T(8,128)(2,1)S(1)}, bf16[1344,256]{1,0:T(8,128)(2,1)S(1)}, u32[]{:S(2)}, u32[]{:S(2)}) %collective-permute-start.28) | collective-permute-done | bytes 688160 | tf_op jit(solution)/shard_map/ppermute | solution.py:60
  132.1 27.7 %collective-permute-done.29 = bf16[1344,256]{1,0:T(8,128)(2,1)S(1)} collective-permute-done((bf16[1344,256]{1,0:T(8,128)(2,1)S(1)}, bf16[1344,256]{1,0:T(8,128)(2,1)S(1)}, u32[]{:S(2)}, u32[]{:S(2)}) %collective-permute-start.29) | collective-permute-done | bytes 688160 | tf_op jit(solution)/shard_map/ppermute | solution.py:60
  163.9 4.6 copy.124
  171.3 23.8 %collective-permute-done.8 = bf16[256,2688]{1,0:T(8,128)(2,1)S(1)} collective-permute-done((bf16[256,2688]{1,0:T(8,128)(2,1)}, bf16[256,2688]{1,0:T(8,128)(2,1)S(1)}, u32[]{:S(2)}, u32[]{:S(2)}) %collective-permute-start.8) | collective-permute-done | bytes 1376288 | tf_op jit(solution)/shard_map/ppermute | solution.py:55
  197.2 7.5 %broadcast_in_dim.179 = bf16[2048,5376]{1,0:T(8,128)(2,1)} broadcast(bf16[]{:T(256)} %constant.183.clone.1), dimensions={} | broadcast | bytes 22020098 | tf_op jit(solution)/shard_map/broadcast_in_dim | solution.py:167
  210.8 15.6 %collective-permute-done.26 = bf16[1344,256]{1,0:T(8,128)(2,1)S(1)} collective-permute-done((bf16[1344,256]{1,0:T(8,128)(2,1)S(1)}, bf16[1344,256]{1,0:T(8,128)(2,1)S(1)}, u32[]{:S(2)}, u32[]{:S(2)}) %collective-permute-start.26) | collective-permute-done | bytes 688160 | tf_op jit(solution)/shard_map/ppermute | solution.py:60
  227.3 17.4 %collective-permute-done.30 = bf16[1344,256]{1,0:T(8,128)(2,1)S(1)} collective-permute-done((bf16[1344,256]{1,0:T(8,128)(2,1)S(1)}, bf16[1344,256]{1,0:T(8,128)(2,1)S(1)}, u32[]{:S(2)}, u32[]{:S(2)}) %collective-permute-start.30) | collective-permute-done | bytes 688160 | tf_op jit(solution)/shard_map/ppermute | solution.py:60
  263.3 5.7 collective-permute-done.31
  269.0 14.4 %collective-permute-done.34 = bf16[1344,256]{1,0:T(8,128)(2,1)} collective-permute-done((bf16[1344,256]{1,0:T(8,128)(2,1)S(1)}, bf16[1344,256]{1,0:T(8,128)(2,1)}, u32[]{:S(2)}, u32[]{:S(2)}) %collective-permute-start.34) | collective-permute-done | bytes 688160 | tf_op jit(solution)/shard_map/ppermute | solution.py:60
  284.3 4.5 copy.122
  290.8 11.7 %collective-permute-done.35 = bf16[1344,256]{1,0:T(8,128)(2,1)} collective-permute-done((bf16[1344,256]{1,0:T(8,128)(2,1)}, bf16[1344,256]{1,0:T(8,128)(2,1)}, u32[]{:S(2)}, u32[]{:S(2)}) %collective-permute-start.35) | collective-permute-done | bytes 688160 | tf_op jit(solution)/shard_map/ppermute | solution.py:60
  314.5 12.0 %multiply_reduce_fusion.3 = (f32[2048,2]{0,1:T(2,128)S(1)}, f32[2048,2,128]{0,2,1:T(8,128)}) fusion(bf16[2,128,5376]{2,1,0:T(8,128)(2,1)S(1)} %bitcast.145, bf16[2048,5376]{1,0:T(8,128)(2,1)} %fusion.33), kind=kOutput, calls=%fused_computation.83 | convolution fusion | flops 5638189056 | bytes 26886144 | tf_op jit(solution)/shard_map/dot_general | solution.py:262
  326.5 11.2 %convolution_convert_fusion = bf16[2048,256]{1,0:T(8,128)(2,1)S(1)} fusion(bf16[2048,5376]{1,0:T(8,128)(2,1)} %fusion.33, bf16[5376,256]{1,0:T(8,128)(2,1)} %bitcast.39), kind=kOutput, calls=%fused_computation.72 | convolution fusion | flops 5637668864 | bytes 25821184 | tf_op jit(solution)/shard_map/dot_general | solution.py:262
  338.7 3.3 collective-permute-start.33
  342.0 10.3 %multiply_reduce_fusion.2 = (f32[2048,2]{0,1:T(2,128)S(1)}, f32[2048,2,128]{0,2,1:T(8,128)S(1)}) fusion(bf16[2,128,5376]{2,1,0:T(8,128)(2,1)S(1)} %bitcast.144, bf16[2048,5376]{1,0:T(8,128)(2,1)} %fusion.33), kind=kOutput, calls=%fused_computation.81 | convolution fusion | flops 5638189056 | bytes 26886144 | tf_op jit(solution)/shard_map/dot_general | solution.py:262
  354.3 6.4 collective-permute-start.32
  364.0 4.5 copy.127
  368.5 11.3 %multiply_reduce_fusion.1 = (f32[2048,2]{0,1:T(2,128)S(1)}, f32[2048,2,128]{0,2,1:T(8,128)S(1)}) fusion(bf16[2,128,5376]{2,1,0:T(8,128)(2,1)} %bitcast.146, bf16[2048,5376]{1,0:T(8,128)(2,1)} %fusion.33), kind=kOutput, calls=%fused_computation.79 | convolution fusion | flops 5638189056 | bytes 26886144 | tf_op jit(solution)/shard_map/dot_general | solution.py:262
  392.7 15.1 %shard_map.101.refs_1_ = bf16[2048,256]{1,0:T(8,128)(2,1)S(1)} custom-call(s32[2048,1]{1,0:T(8,128)S(1)} %bitcast.131, bf16[2048,256]{1,0:T(8,128)(2,1)S(1)} %copy.128.q_ref, bf16[3072,128]{1,0:T(8,128)(2,1)S(1)} %get-tuple-element.76.k_ref, bf16[3072,128]{1,0:T(8,128)(2,1)S(1)} %get-tuple-element.74.v_ref), custom_call_target="tpu_custom_call" | custom-call | flops 2684354560 | bytes 3670016 | tf_op jit(solution)/shard_map/pallas_call | solution.py:100
  409.4 15.1 %shard_map.100.refs_0_ = bf16[2048,256]{1,0:T(8,128)(2,1)S(1)} custom-call(s32[2048,1]{1,0:T(8,128)S(1)} %bitcast.132, bf16[2048,256]{1,0:T(8,128)(2,1)S(1)} %copy-done.14, bf16[3072,128]{1,0:T(8,128)(2,1)S(1)} %get-tuple-element.77.k_ref, bf16[3072,128]{1,0:T(8,128)(2,1)S(1)} %get-tuple-element.75.v_ref), custom_call_target="tpu_custom_call" | custom-call | flops 2684354560 | bytes 3670016 | tf_op jit(solution)/shard_map/pallas_call | solution.py:100
  426.8 7.2 %collective-permute-done.40.refs_5_ = bf16[2048,256]{1,0:T(8,128)(2,1)S(1)} collective-permute-done((bf16[2048,256]{1,0:T(8,128)(2,1)S(1)}, bf16[2048,256]{1,0:T(8,128)(2,1)S(1)}, u32[]{:S(2)}, u32[]{:S(2)}) %collective-permute-start.40) | collective-permute-done | bytes 1048608 | tf_op jit(solution)/shard_map/ppermute | solution.py:51
  434.0 19.3 %collective-permute-done.39.refs_4_ = bf16[2048,256]{1,0:T(8,128)(2,1)} collective-permute-done((bf16[2048,256]{1,0:T(8,128)(2,1)S(1)}, bf16[2048,256]{1,0:T(8,128)(2,1)}, u32[]{:S(2)}, u32[]{:S(2)}) %collective-permute-start.39) | collective-permute-done | bytes 1048608 | tf_op jit(solution)/shard_map/ppermute | solution.py:51
  459.2 6.4 shard_map.102
  474.5 6.4 shard_map.103
  484.6 6.9 %collective-permute-start.48 = (bf16[2048,336]{0,1:T(8,128)(2,1)}, bf16[2048,336]{0,1:T(8,128)(2,1)}, u32[]{:S(2)}, u32[]{:S(2)}) collective-permute-start(bf16[2048,336]{0,1:T(8,128)(2,1)} %copy.101), channel_id=1, source_target_pairs={{0,1},{2,3},{4,5},{6,7},{9,8},{11,10},{13,12},{15,14},{17,16},{19,... | collective-permute-start | bytes 4128776 | tf_op jit(solution)/shard_map/ppermute | solution.py:294
  491.7 4.5 copy.83
  500.2 6.4 shard_map.104
  512.7 2.6 copy.114.refs_8_
  516.7 6.4 shard_map.105
  524.3 2.7 copy.115
  534.5 3.4 collective-permute-start.46
  542.8 5.3 collective-permute-done.53
  558.7 2.9 broadcast_in_dim.173
  586.7 19.1 %collective-permute-done.58 = bf16[2048,336]{0,1:T(8,128)(2,1)} collective-permute-done((bf16[2048,336]{0,1:T(8,128)(2,1)S(1)}, bf16[2048,336]{0,1:T(8,128)(2,1)}, u32[]{:S(2)}, u32[]{:S(2)}) %collective-permute-start.58) | collective-permute-done | bytes 1376288 | tf_op jit(solution)/shard_map/ppermute | solution.py:294
  612.6 3.5 collective-permute-start.61
  618.0 6.1 collective-permute-done.60
  624.3 7.1 %collective-permute-done.61 = bf16[512,336]{1,0:T(8,128)(2,1)S(1)} collective-permute-done((bf16[512,336]{1,0:T(8,128)(2,1)S(1)}, bf16[512,336]{1,0:T(8,128)(2,1)S(1)}, u32[]{:S(2)}, u32[]{:S(2)}) %collective-permute-start.61) | collective-permute-done | bytes 344096 | tf_op jit(solution)/shard_map/ppermute | solution.py:300
  636.5 2.7 dynamic-slice_convert_fusion
  641.4 2.9 copy.121
  (362 shorter events, 211.6 us)
Async XLA Ops:
  2.7 100.0 %collective-permute-start.6 = (bf16[256,2688]{1,0:T(8,128)(2,1)}, bf16[256,2688]{1,0:T(8,128)(2,1)}, u32[]{:S(2)}, u32[]{:S(2)}) collective-permute-start(bf16[256,2688]{1,0:T(8,128)(2,1)} %slice.58), channel_id=1, source_target_pairs={{0,1},{1,0},{2,3},{3,2},{4,5},{5,4},{6,7},{7,6},{8,9},{9,8},{10,11... | collective-permute-start | bytes 4128776 | tf_op jit(solution)/shard_map/ppermute | solution.py:55
  4.2 158.1 %collective-permute-start.7 = (bf16[256,2688]{1,0:T(8,128)(2,1)}, bf16[256,2688]{1,0:T(8,128)(2,1)}, u32[]{:S(2)}, u32[]{:S(2)}) collective-permute-start(bf16[256,2688]{1,0:T(8,128)(2,1)} %slice.58), channel_id=1, source_target_pairs={{0,4},{2,6},{4,0},{6,2},{8,12},{10,14},{12,8},{14,10},{16,20},{18,... | collective-permute-start | bytes 4128776 | tf_op jit(solution)/shard_map/ppermute | solution.py:51
  4.7 31.5 %collective-permute-start.1 = (s32[512]{0:T(512)S(1)}, s32[512]{0:T(512)S(1)}, u32[]{:S(2)}, u32[]{:S(2)}) collective-permute-start(s32[512]{0:T(512)S(1)} %copy-done.53), channel_id=1, source_target_pairs={{0,4},{2,6},{4,0},{6,2},{8,12},{10,14},{12,8},{14,10},{16,20},{18,... | collective-permute-start | bytes 6152 | tf_op jit(solution)/shard_map/ppermute | solution.py:51
  6.2 30.5 %collective-permute-start.2 = (s32[512]{0:T(512)S(1)}, s32[512]{0:T(512)S(1)}, u32[]{:S(2)}, u32[]{:S(2)}) collective-permute-start(s32[512]{0:T(512)S(1)} %copy-done.53), channel_id=1, source_target_pairs={{0,6},{2,4},{4,2},{6,0},{8,14},{10,12},{12,10},{14,8},{16,22},{18,... | collective-permute-start | bytes 6152 | tf_op jit(solution)/shard_map/ppermute | solution.py:51
  12.3 26.9 %collective-permute-start.20 = (bf16[336,512]{1,0:T(8,128)(2,1)}, bf16[336,512]{1,0:T(8,128)(2,1)}, u32[]{:S(2)}, u32[]{:S(2)}) collective-permute-start(bf16[336,512]{1,0:T(8,128)(2,1)} %pad_maximum_fusion.10), channel_id=1, source_target_pairs={{0,2},{2,0},{4,6},{6,4},{8,10},{10,8},{12,14},{14,12},{16,18},{18,... | collective-permute-start | bytes 1032200 | tf_op jit(solution)/shard_map/ppermute | solution.py:51
  54.0 153.0 %collective-permute-start.13 = (bf16[256,2688]{1,0:T(8,128)(2,1)}, bf16[256,2688]{1,0:T(8,128)(2,1)}, u32[]{:S(2)}, u32[]{:S(2)}) collective-permute-start(bf16[256,2688]{1,0:T(8,128)(2,1)} %slice.58), channel_id=1, source_target_pairs={{0,2},{2,0},{4,6},{6,4},{8,10},{10,8},{12,14},{14,12},{16,18},{18,... | collective-permute-start | bytes 4128776 | tf_op jit(solution)/shard_map/ppermute | solution.py:51
  66.4 19.7 %collective-permute-start.23 = (bf16[1344,256]{1,0:T(8,128)(2,1)S(1)}, bf16[1344,256]{1,0:T(8,128)(2,1)S(1)}, u32[]{:S(2)}, u32[]{:S(2)}) collective-permute-start(bf16[1344,256]{1,0:T(8,128)(2,1)S(1)} %get-tuple-element.81), channel_id=1, source_target_pairs={{0,8},{2,10},{4,12},{6,14},{8,16},{10,18},{12,20},{14,22},{16,24},... | collective-permute-start | bytes 2064392 | tf_op jit(solution)/shard_map/ppermute | solution.py:60
  70.5 30.3 %collective-permute-start.27 = (bf16[1344,256]{1,0:T(8,128)(2,1)S(1)}, bf16[1344,256]{1,0:T(8,128)(2,1)S(1)}, u32[]{:S(2)}, u32[]{:S(2)}) collective-permute-start(bf16[1344,256]{1,0:T(8,128)(2,1)S(1)} %get-tuple-element.80), channel_id=1, source_target_pairs={{0,8},{2,10},{4,12},{6,14},{8,16},{10,18},{12,20},{14,22},{16,24},... | collective-permute-start | bytes 2064392 | tf_op jit(solution)/shard_map/ppermute | solution.py:60
  86.1 29.5 %collective-permute-start.24 = (bf16[1344,256]{1,0:T(8,128)(2,1)S(1)}, bf16[1344,256]{1,0:T(8,128)(2,1)S(1)}, u32[]{:S(2)}, u32[]{:S(2)}) collective-permute-start(bf16[1344,256]{1,0:T(8,128)(2,1)S(1)} %collective-permute-done.23), channel_id=1, source_target_pairs={{0,8},{2,10},{4,12},{6,14},{8,16},{10,18},{12,20},{14,22},{16,24},... | collective-permute-start | bytes 2064392 | tf_op jit(solution)/shard_map/ppermute | solution.py:60
  100.8 29.5 %collective-permute-start.28 = (bf16[1344,256]{1,0:T(8,128)(2,1)S(1)}, bf16[1344,256]{1,0:T(8,128)(2,1)S(1)}, u32[]{:S(2)}, u32[]{:S(2)}) collective-permute-start(bf16[1344,256]{1,0:T(8,128)(2,1)S(1)} %collective-permute-done.27), channel_id=1, source_target_pairs={{0,8},{2,10},{4,12},{6,14},{8,16},{10,18},{12,20},{14,22},{16,24},... | collective-permute-start | bytes 2064392 | tf_op jit(solution)/shard_map/ppermute | solution.py:60
  105.4 63.1 %collective-permute-start.3 = (bf16[256,2688]{1,0:T(8,128)(2,1)}, bf16[256,2688]{1,0:T(8,128)(2,1)}, u32[]{:S(2)}, u32[]{:S(2)}) collective-permute-start(bf16[256,2688]{1,0:T(8,128)(2,1)} %get-tuple-element.55), channel_id=1, source_target_pairs={{0,1},{1,0},{2,3},{3,2},{4,5},{5,4},{6,7},{7,6},{8,9},{9,8},{10,11... | collective-permute-start | bytes 4128776 | tf_op jit(solution)/shard_map/ppermute | solution.py:55
  115.6 46.7 %collective-permute-start.25 = (bf16[1344,256]{1,0:T(8,128)(2,1)S(1)}, bf16[1344,256]{1,0:T(8,128)(2,1)S(1)}, u32[]{:S(2)}, u32[]{:S(2)}) collective-permute-start(bf16[1344,256]{1,0:T(8,128)(2,1)S(1)} %collective-permute-done.24), channel_id=1, source_target_pairs={{0,8},{2,10},{4,12},{6,14},{8,16},{10,18},{12,20},{14,22},{16,24},... | collective-permute-start | bytes 2064392 | tf_op jit(solution)/shard_map/ppermute | solution.py:60
  130.3 29.5 %collective-permute-start.29 = (bf16[1344,256]{1,0:T(8,128)(2,1)S(1)}, bf16[1344,256]{1,0:T(8,128)(2,1)S(1)}, u32[]{:S(2)}, u32[]{:S(2)}) collective-permute-start(bf16[1344,256]{1,0:T(8,128)(2,1)S(1)} %collective-permute-done.28), channel_id=1, source_target_pairs={{0,8},{2,10},{4,12},{6,14},{8,16},{10,18},{12,20},{14,22},{16,24},... | collective-permute-start | bytes 2064392 | tf_op jit(solution)/shard_map/ppermute | solution.py:60
  159.8 85.8 %collective-permute-start.4 = (bf16[256,2688]{1,0:T(8,128)(2,1)}, bf16[256,2688]{1,0:T(8,128)(2,1)}, u32[]{:S(2)}, u32[]{:S(2)}) collective-permute-start(bf16[256,2688]{1,0:T(8,128)(2,1)} %get-tuple-element.55), channel_id=1, source_target_pairs={{0,4},{2,6},{4,0},{6,2},{8,12},{10,14},{12,8},{14,10},{16,20},{18,... | collective-permute-start | bytes 4128776 | tf_op jit(solution)/shard_map/ppermute | solution.py:51
  162.3 86.6 %collective-permute-start.9 = (bf16[256,2688]{1,0:T(8,128)(2,1)}, bf16[256,2688]{1,0:T(8,128)(2,1)}, u32[]{:S(2)}, u32[]{:S(2)}) collective-permute-start(bf16[256,2688]{1,0:T(8,128)(2,1)} %get-tuple-element.55), channel_id=1, source_target_pairs={{0,2},{2,0},{4,6},{6,4},{8,10},{10,8},{12,14},{14,12},{16,18},{18,... | collective-permute-start | bytes 4128776 | tf_op jit(solution)/shard_map/ppermute | solution.py:51
  162.3 32.8 %collective-permute-start.8 = (bf16[256,2688]{1,0:T(8,128)(2,1)}, bf16[256,2688]{1,0:T(8,128)(2,1)S(1)}, u32[]{:S(2)}, u32[]{:S(2)}) collective-permute-start(bf16[256,2688]{1,0:T(8,128)(2,1)} %collective-permute-done.7), channel_id=1, source_target_pairs={{0,1},{1,0},{2,3},{3,2},{4,5},{5,4},{6,7},{7,6},{8,9},{9,8},{10,11... | collective-permute-start | bytes 4128776 | tf_op jit(solution)/shard_map/ppermute | solution.py:55
  168.5 38.7 %collective-permute-start.14 = (bf16[256,2688]{1,0:T(8,128)(2,1)}, bf16[256,2688]{1,0:T(8,128)(2,1)S(1)}, u32[]{:S(2)}, u32[]{:S(2)}) collective-permute-start(bf16[256,2688]{1,0:T(8,128)(2,1)} %collective-permute-done.6), channel_id=1, source_target_pairs={{0,2},{2,0},{4,6},{6,4},{8,10},{10,8},{12,14},{14,12},{16,18},{18,... | collective-permute-start | bytes 4128776 | tf_op jit(solution)/shard_map/ppermute | solution.py:51
  195.1 65.9 %collective-permute-start.15 = (bf16[256,2688]{1,0:T(8,128)(2,1)}, bf16[256,2688]{1,0:T(8,128)(2,1)S(1)}, u32[]{:S(2)}, u32[]{:S(2)}) collective-permute-start(bf16[256,2688]{1,0:T(8,128)(2,1)} %collective-permute-done.7), channel_id=1, source_target_pairs={{0,2},{2,0},{4,6},{6,4},{8,10},{10,8},{12,14},{14,12},{16,18},{18,... | collective-permute-start | bytes 4128776 | tf_op jit(solution)/shard_map/ppermute | solution.py:51
  207.0 19.4 %collective-permute-start.26 = (bf16[1344,256]{1,0:T(8,128)(2,1)S(1)}, bf16[1344,256]{1,0:T(8,128)(2,1)S(1)}, u32[]{:S(2)}, u32[]{:S(2)}) collective-permute-start(bf16[1344,256]{1,0:T(8,128)(2,1)S(1)} %copy-done.50), channel_id=1, source_target_pairs={{0,8},{2,10},{4,12},{6,14},{8,16},{10,18},{12,20},{14,22},{16,24},... | collective-permute-start | bytes 2064392 | tf_op jit(solution)/shard_map/ppermute | solution.py:60
  207.2 39.0 %collective-permute-start.5 = (bf16[256,2688]{1,0:T(8,128)(2,1)}, bf16[256,2688]{1,0:T(8,128)(2,1)}, u32[]{:S(2)}, u32[]{:S(2)}) collective-permute-start(bf16[256,2688]{1,0:T(8,128)(2,1)} %collective-permute-done.3), channel_id=1, source_target_pairs={{0,4},{2,6},{4,0},{6,2},{8,12},{10,14},{12,8},{14,10},{16,20},{18,... | collective-permute-start | bytes 4128776 | tf_op jit(solution)/shard_map/ppermute | solution.py:51
  226.4 18.4 %collective-permute-start.30 = (bf16[1344,256]{1,0:T(8,128)(2,1)S(1)}, bf16[1344,256]{1,0:T(8,128)(2,1)S(1)}, u32[]{:S(2)}, u32[]{:S(2)}) collective-permute-start(bf16[1344,256]{1,0:T(8,128)(2,1)S(1)} %collective-permute-done.26), channel_id=1, source_target_pairs={{0,8},{2,10},{4,12},{6,14},{8,16},{10,18},{12,20},{14,22},{16,24},... | collective-permute-start | bytes 2064392 | tf_op jit(solution)/shard_map/ppermute | solution.py:60
  246.2 58.7 %collective-permute-start.11 = (bf16[256,2688]{1,0:T(8,128)(2,1)}, bf16[256,2688]{1,0:T(8,128)(2,1)}, u32[]{:S(2)}, u32[]{:S(2)}) collective-permute-start(bf16[256,2688]{1,0:T(8,128)(2,1)} %collective-permute-done.4), channel_id=1, source_target_pairs={{0,2},{2,0},{4,6},{6,4},{8,10},{10,8},{12,14},{14,12},{16,18},{18,... | collective-permute-start | bytes 4128776 | tf_op jit(solution)/shard_map/ppermute | solution.py:51
  248.9 20.1 %collective-permute-start.31 = (bf16[1344,256]{1,0:T(8,128)(2,1)S(1)}, bf16[1344,256]{1,0:T(8,128)(2,1)S(1)}, u32[]{:S(2)}, u32[]{:S(2)}) collective-permute-start(bf16[1344,256]{1,0:T(8,128)(2,1)S(1)} %collective-permute-done.30), channel_id=1, source_target_pairs={{0,8},{2,10},{4,12},{6,14},{8,16},{10,18},{12,20},{14,22},{16,24},... | collective-permute-start | bytes 2064392 | tf_op jit(solution)/shard_map/ppermute | solution.py:60
  249.3 34.0 %collective-permute-start.34 = (bf16[1344,256]{1,0:T(8,128)(2,1)S(1)}, bf16[1344,256]{1,0:T(8,128)(2,1)}, u32[]{:S(2)}, u32[]{:S(2)}) collective-permute-start(bf16[1344,256]{1,0:T(8,128)(2,1)S(1)} %copy-done.49), channel_id=1, source_target_pairs={{0,8},{2,10},{4,12},{6,14},{8,16},{10,18},{12,20},{14,22},{16,24},... | collective-permute-start | bytes 2064392 | tf_op jit(solution)/shard_map/ppermute | solution.py:60
  261.0 43.9 %collective-permute-start.12 = (bf16[256,2688]{1,0:T(8,128)(2,1)}, bf16[256,2688]{1,0:T(8,128)(2,1)}, u32[]{:S(2)}, u32[]{:S(2)}) collective-permute-start(bf16[256,2688]{1,0:T(8,128)(2,1)} %collective-permute-done.5), channel_id=1, source_target_pairs={{0,2},{2,0},{4,6},{6,4},{8,10},{10,8},{12,14},{14,12},{16,18},{18,... | collective-permute-start | bytes 4128776 | tf_op jit(solution)/shard_map/ppermute | solution.py:51
  283.4 19.1 %collective-permute-start.35 = (bf16[1344,256]{1,0:T(8,128)(2,1)}, bf16[1344,256]{1,0:T(8,128)(2,1)}, u32[]{:S(2)}, u32[]{:S(2)}) collective-permute-start(bf16[1344,256]{1,0:T(8,128)(2,1)} %collective-permute-done.34), channel_id=1, source_target_pairs={{0,8},{2,10},{4,12},{6,14},{8,16},{10,18},{12,20},{14,22},{16,24},... | collective-permute-start | bytes 2064392 | tf_op jit(solution)/shard_map/ppermute | solution.py:60
  302.5 59.5 %collective-permute-start.36 = (bf16[1344,256]{1,0:T(8,128)(2,1)}, bf16[1344,256]{1,0:T(8,128)(2,1)}, u32[]{:S(2)}, u32[]{:S(2)}) collective-permute-start(bf16[1344,256]{1,0:T(8,128)(2,1)} %collective-permute-done.35), channel_id=1, source_target_pairs={{0,8},{2,10},{4,12},{6,14},{8,16},{10,18},{12,20},{14,22},{16,24},... | collective-permute-start | bytes 2064392 | tf_op jit(solution)/shard_map/ppermute | solution.py:60
  302.5 123.8 %collective-permute-start.47 = (bf16[2048,336]{0,1:T(8,128)(2,1)}, bf16[2048,336]{0,1:T(8,128)(2,1)}, u32[]{:S(2)}, u32[]{:S(2)}) collective-permute-start(bf16[2048,336]{0,1:T(8,128)(2,1)} %param.18), channel_id=1, source_target_pairs={{0,8},{2,10},{4,12},{6,14},{8,16},{10,18},{12,20},{14,22},{16,24},... | collective-permute-start | bytes 4128776 | tf_op jit(solution)/shard_map/ppermute | solution.py:60
  338.7 51.4 %collective-permute-start.33 = (bf16[1024,256]{1,0:T(8,128)(2,1)}, bf16[1024,256]{1,0:T(8,128)(2,1)}, u32[]{:S(2)}, u32[]{:S(2)}) collective-permute-start(bf16[1024,256]{1,0:T(8,128)(2,1)} %slice.86), channel_id=1, source_target_pairs={{0,8},{2,10},{4,12},{6,14},{8,16},{10,18},{12,20},{14,22},{16,24},... | collective-permute-start | bytes 1572872 | tf_op jit(solution)/shard_map/ppermute | solution.py:268
  354.3 37.3 %collective-permute-start.32 = (bf16[1024,256]{1,0:T(8,128)(2,1)}, bf16[1024,256]{1,0:T(8,128)(2,1)}, u32[]{:S(2)}, u32[]{:S(2)}) collective-permute-start(bf16[1024,256]{1,0:T(8,128)(2,1)} %copy.125), channel_id=1, source_target_pairs={{0,8},{2,10},{4,12},{6,14},{8,16},{10,18},{12,20},{14,22},{16,24},... | collective-permute-start | bytes 1572872 | tf_op jit(solution)/shard_map/ppermute | solution.py:268
  407.8 26.2 %collective-permute-start.40 = (bf16[2048,256]{1,0:T(8,128)(2,1)S(1)}, bf16[2048,256]{1,0:T(8,128)(2,1)S(1)}, u32[]{:S(2)}, u32[]{:S(2)}) collective-permute-start(bf16[2048,256]{1,0:T(8,128)(2,1)S(1)} %shard_map.101.refs_1_), channel_id=1, source_target_pairs={{0,4},{2,6},{4,0},{6,2},{8,12},{10,14},{12,8},{14,10},{16,20},{18,... | collective-permute-start | bytes 3145736 | tf_op jit(solution)/shard_map/ppermute | solution.py:51
  424.5 28.8 %collective-permute-start.39 = (bf16[2048,256]{1,0:T(8,128)(2,1)S(1)}, bf16[2048,256]{1,0:T(8,128)(2,1)}, u32[]{:S(2)}, u32[]{:S(2)}) collective-permute-start(bf16[2048,256]{1,0:T(8,128)(2,1)S(1)} %shard_map.100.refs_0_), channel_id=1, source_target_pairs={{0,4},{2,6},{4,0},{6,2},{8,12},{10,14},{12,8},{14,10},{16,20},{18,... | collective-permute-start | bytes 3145736 | tf_op jit(solution)/shard_map/ppermute | solution.py:51
  426.3 31.4 %collective-permute-start.52 = (bf16[2048,336]{0,1:T(8,128)(2,1)}, bf16[2048,336]{0,1:T(8,128)(2,1)}, u32[]{:S(2)}, u32[]{:S(2)}) collective-permute-start(bf16[2048,336]{0,1:T(8,128)(2,1)} %collective-permute-done.47), channel_id=1, source_target_pairs={{0,8},{2,10},{4,12},{6,14},{8,16},{10,18},{12,20},{14,22},{16,24},... | collective-permute-start | bytes 4128776 | tf_op jit(solution)/shard_map/ppermute | solution.py:60
  426.3 31.4 %collective-permute-start.38 = (bf16[2048,256]{1,0:T(8,128)(2,1)S(1)}, bf16[2048,256]{1,0:T(8,128)(2,1)}, u32[]{:S(2)}, u32[]{:S(2)}) collective-permute-start(bf16[2048,256]{1,0:T(8,128)(2,1)S(1)} %shard_map.101.refs_1_), channel_id=1, source_target_pairs={{0,2},{2,0},{4,6},{6,4},{8,10},{10,8},{12,14},{14,12},{16,18},{18,... | collective-permute-start | bytes 3145736 | tf_op jit(solution)/shard_map/ppermute | solution.py:51
  426.3 31.4 %collective-permute-start.37 = (bf16[2048,256]{1,0:T(8,128)(2,1)S(1)}, bf16[2048,256]{1,0:T(8,128)(2,1)}, u32[]{:S(2)}, u32[]{:S(2)}) collective-permute-start(bf16[2048,256]{1,0:T(8,128)(2,1)S(1)} %shard_map.100.refs_0_), channel_id=1, source_target_pairs={{0,2},{2,0},{4,6},{6,4},{8,10},{10,8},{12,14},{14,12},{16,18},{18,... | collective-permute-start | bytes 3145736 | tf_op jit(solution)/shard_map/ppermute | solution.py:51
  434.0 23.8 %collective-permute-start.42 = (bf16[2048,256]{1,0:T(8,128)(2,1)S(1)}, bf16[2048,256]{1,0:T(8,128)(2,1)}, u32[]{:S(2)}, u32[]{:S(2)}) collective-permute-start(bf16[2048,256]{1,0:T(8,128)(2,1)S(1)} %collective-permute-done.40.refs_5_), channel_id=1, source_target_pairs={{0,2},{2,0},{4,6},{6,4},{8,10},{10,8},{12,14},{14,12},{16,18},{18,... | collective-permute-start | bytes 3145736 | tf_op jit(solution)/shard_map/ppermute | solution.py:51
  457.7 54.9 %collective-permute-start.57 = (bf16[2048,336]{0,1:T(8,128)(2,1)}, bf16[2048,336]{0,1:T(8,128)(2,1)}, u32[]{:S(2)}, u32[]{:S(2)}) collective-permute-start(bf16[2048,336]{0,1:T(8,128)(2,1)} %collective-permute-done.52), channel_id=1, source_target_pairs={{0,8},{2,10},{4,12},{6,14},{8,16},{10,18},{12,20},{14,22},{16,24},... | collective-permute-start | bytes 4128776 | tf_op jit(solution)/shard_map/ppermute | solution.py:60
  469.3 57.6 %collective-permute-start.43 = (bf16[2048,336]{0,1:T(8,128)(2,1)}, bf16[2048,336]{0,1:T(8,128)(2,1)}, u32[]{:S(2)}, u32[]{:S(2)}) collective-permute-start(bf16[2048,336]{0,1:T(8,128)(2,1)} %copy.94), channel_id=1, source_target_pairs={{1,0},{3,2},{5,4},{7,6},{9,8},{11,10},{13,12},{15,14},{16,17},{18,... | collective-permute-start | bytes 4128776 | tf_op jit(solution)/shard_map/ppermute | solution.py:294
  484.6 53.3 %collective-permute-start.48 = (bf16[2048,336]{0,1:T(8,128)(2,1)}, bf16[2048,336]{0,1:T(8,128)(2,1)}, u32[]{:S(2)}, u32[]{:S(2)}) collective-permute-start(bf16[2048,336]{0,1:T(8,128)(2,1)} %copy.101), channel_id=1, source_target_pairs={{0,1},{2,3},{4,5},{6,7},{9,8},{11,10},{13,12},{15,14},{17,16},{19,... | collective-permute-start | bytes 4128776 | tf_op jit(solution)/shard_map/ppermute | solution.py:294
  510.3 37.8 %collective-permute-start.53 = (bf16[2048,336]{0,1:T(8,128)(2,1)}, bf16[2048,336]{0,1:T(8,128)(2,1)}, u32[]{:S(2)}, u32[]{:S(2)}) collective-permute-start(bf16[2048,336]{0,1:T(8,128)(2,1)} %copy.108), channel_id=1, source_target_pairs={{0,1},{2,3},{4,5},{6,7},{8,9},{10,11},{12,13},{14,15},{17,16},{19,... | collective-permute-start | bytes 4128776 | tf_op jit(solution)/shard_map/ppermute | solution.py:294
  530.3 23.3 %collective-permute-start.44 = (bf16[512,336]{1,0:T(8,128)(2,1)}, bf16[512,336]{1,0:T(8,128)(2,1)}, u32[]{:S(2)}, u32[]{:S(2)}) collective-permute-start(bf16[512,336]{1,0:T(8,128)(2,1)} %get-tuple-element.72), channel_id=1, source_target_pairs={{0,2},{2,0},{4,6},{6,4},{8,10},{10,8},{12,14},{14,12},{17,19},{19,... | collective-permute-start | bytes 1032200 | tf_op jit(solution)/shard_map/ppermute | solution.py:300
  532.2 22.1 %collective-permute-start.45 = (bf16[512,336]{1,0:T(8,128)(2,1)}, bf16[512,336]{1,0:T(8,128)(2,1)}, u32[]{:S(2)}, u32[]{:S(2)}) collective-permute-start(bf16[512,336]{1,0:T(8,128)(2,1)} %get-tuple-element.71), channel_id=1, source_target_pairs={{0,4},{2,6},{4,0},{6,2},{8,12},{10,14},{12,8},{14,10},{17,21},{19,... | collective-permute-start | bytes 1032200 | tf_op jit(solution)/shard_map/ppermute | solution.py:300
  534.5 21.3 %collective-permute-start.46 = (bf16[512,336]{1,0:T(8,128)(2,1)}, bf16[512,336]{1,0:T(8,128)(2,1)}, u32[]{:S(2)}, u32[]{:S(2)}) collective-permute-start(bf16[512,336]{1,0:T(8,128)(2,1)} %get-tuple-element.70), channel_id=1, source_target_pairs={{0,6},{2,4},{4,2},{6,0},{8,14},{10,12},{12,10},{14,8},{17,23},{19,... | collective-permute-start | bytes 1032200 | tf_op jit(solution)/shard_map/ppermute | solution.py:300
  554.3 17.7 %collective-permute-start.54 = (bf16[512,336]{1,0:T(8,128)(2,1)}, bf16[512,336]{1,0:T(8,128)(2,1)}, u32[]{:S(2)}, u32[]{:S(2)}) collective-permute-start(bf16[512,336]{1,0:T(8,128)(2,1)} %get-tuple-element.64), channel_id=1, source_target_pairs={{1,3},{3,1},{5,7},{7,5},{9,11},{11,9},{13,15},{15,13},{16,18},{18,... | collective-permute-start | bytes 1032200 | tf_op jit(solution)/shard_map/ppermute | solution.py:300
  555.7 18.1 %collective-permute-start.55 = (bf16[512,336]{1,0:T(8,128)(2,1)}, bf16[512,336]{1,0:T(8,128)(2,1)}, u32[]{:S(2)}, u32[]{:S(2)}) collective-permute-start(bf16[512,336]{1,0:T(8,128)(2,1)} %get-tuple-element.63), channel_id=1, source_target_pairs={{1,5},{3,7},{5,1},{7,3},{9,13},{11,15},{13,9},{15,11},{16,20},{18,... | collective-permute-start | bytes 1032200 | tf_op jit(solution)/shard_map/ppermute | solution.py:300
  557.1 18.7 %collective-permute-start.56 = (bf16[512,336]{1,0:T(8,128)(2,1)}, bf16[512,336]{1,0:T(8,128)(2,1)}, u32[]{:S(2)}, u32[]{:S(2)}) collective-permute-start(bf16[512,336]{1,0:T(8,128)(2,1)} %get-tuple-element.62), channel_id=1, source_target_pairs={{1,7},{3,5},{5,3},{7,1},{9,15},{11,13},{13,11},{15,9},{16,22},{18,... | collective-permute-start | bytes 1032200 | tf_op jit(solution)/shard_map/ppermute | solution.py:300
  563.6 42.3 %collective-permute-start.58 = (bf16[2048,336]{0,1:T(8,128)(2,1)S(1)}, bf16[2048,336]{0,1:T(8,128)(2,1)}, u32[]{:S(2)}, u32[]{:S(2)}) collective-permute-start(bf16[2048,336]{0,1:T(8,128)(2,1)S(1)} %copy-done.39), channel_id=1, source_target_pairs={{1,0},{3,2},{5,4},{7,6},{8,9},{10,11},{12,13},{14,15},{16,17},{18,... | collective-permute-start | bytes 4128776 | tf_op jit(solution)/shard_map/ppermute | solution.py:294
  612.6 18.9 %collective-permute-start.61 = (bf16[512,336]{1,0:T(8,128)(2,1)S(1)}, bf16[512,336]{1,0:T(8,128)(2,1)S(1)}, u32[]{:S(2)}, u32[]{:S(2)}) collective-permute-start(bf16[512,336]{1,0:T(8,128)(2,1)S(1)} %get-tuple-element.58), channel_id=1, source_target_pairs={{0,6},{2,4},{4,2},{6,0},{9,15},{11,13},{13,11},{15,9},{17,23},{19,... | collective-permute-start | bytes 1032200 | tf_op jit(solution)/shard_map/ppermute | solution.py:300
  (71 other events, 1521.9 us)

commit v3 on v2

--- a/solution.py
+++ b/solution.py
@@ -19,6 +19,8 @@
 
 INNER = 4
 QUERY_BLOCK = 256
+TOKEN_BLOCK = 512
+VMEM = 48 * 2**20
 
 
 def rms_scale(values, gain):
@@ -47,28 +49,106 @@
 
 
 def swap(x, mask):
-    size = lax.axis_size("ctx")
-    return lax.ppermute(x, "ctx", [(c, c ^ mask) for c in range(size)])
+    return lax.ppermute(x, "i", [(c, c ^ mask) for c in range(INNER)])
 
 
 def swap_tp(x):
     return lax.ppermute(x, "tp", [(0, 1), (1, 0)])
 
 
-def ring_step(x, by=1):
-    size = lax.axis_size("ctx")
-    return lax.ppermute(x, "ctx", [(c, (c + by * INNER) % size) for c in range(size)])
+def ring_step(x):
+    size = lax.axis_size("z")
+    return lax.ppermute(x, "z", [(c, (c + 1) % size) for c in range(size)])
 
 
 def after(x, *others):
     return lax.optimization_barrier((x, *others))[0]
 
 
-def placed(blocks, places):
-    whole = jnp.zeros((len(blocks), *blocks[0].shape), blocks[0].dtype)
-    for block, place in zip(blocks, places):
-        whole = lax.dynamic_update_index_in_dim(whole, block, place, 0)
-    return whole
+def in_order(first, mine, other):
+    return jnp.where(first, jnp.stack([mine, other]), jnp.stack([other, mine]))
+
+
+def norm_kernel(x_ref, gain_ref, o_ref):
+    sides = [x_ref[0, side].astype(jnp.float32) for side in range(2)]
+    squares = sum(jnp.sum(x * x, axis=-1, keepdims=True) for x in sides)
+    scale = lax.rsqrt(squares / MODEL_WIDTH + EPS)
+    per_side = o_ref.shape[0] // 2
+    cols = o_ref.shape[2]
+    for side, x in enumerate(sides):
+        normed = (x * scale * gain_ref[side]).astype(jnp.bfloat16)
+        for part in range(per_side):
+            o_ref[side * per_side + part] = normed[:, part * cols : (part + 1) * cols]
+
+
+def norm_by_blocks(gathered, in_gain, blocks):
+    inner, sides, rows, cols = gathered.shape
+    width = sides * cols // blocks
+    step = 256
+    per_place = rows // step
+    return pl.pallas_call(
+        norm_kernel,
+        grid=(inner, per_place),
+        in_specs=[
+            pl.BlockSpec((1, sides, step, cols), lambda i, r: (i, 0, r, 0)),
+            pl.BlockSpec((sides, 1, cols), lambda i, r: (0, 0, 0)),
+        ],
+        out_specs=pl.BlockSpec((blocks, step, width), lambda i, r: (0, i * per_place + r, 0)),
+        out_shape=jax.ShapeDtypeStruct((blocks, inner * rows, width), jnp.bfloat16),
+        compiler_params=pltpu.CompilerParams(vmem_limit_bytes=VMEM),
+        cost_estimate=pl.CostEstimate(
+            flops=5 * gathered.size, bytes_accessed=4 * gathered.size, transcendentals=0
+        ),
+    )(gathered, in_gain.reshape(sides, 1, cols))
+
+
+def project_kernel(factor, source_ref, x_ref, *refs):
+    blocks = x_ref.shape[0]
+    weights, rest, o_ref = refs[:blocks], refs[blocks:-1], refs[-1]
+    total = None
+    for d in range(blocks):
+        term = jnp.dot(x_ref[source_ref[d]], weights[d][...], preferred_element_type=jnp.float32)
+        total = term if total is None else total + term
+    if not rest:
+        o_ref[...] = total.astype(jnp.bfloat16)
+        return
+    gain_ref, cos_ref, sin_ref = rest
+    for head in range(total.shape[1] // HEAD_SIZE):
+        span = slice(head * HEAD_SIZE, (head + 1) * HEAD_SIZE)
+        values = total[:, span]
+        values = rms_scale(values, gain_ref[...])
+        turned = pltpu.roll(values, HEAD_SIZE // 2, 1)
+        values = values * cos_ref[...] + turned * sin_ref[...]
+        o_ref[:, span] = (values * factor).astype(jnp.bfloat16)
+
+
+def project(normed, source, weights, gain=None, turn=None, factor=1.0):
+    blocks, tokens, width = normed.shape
+    cols = weights[0].shape[1]
+    extra, extra_specs = [], []
+    if gain is not None:
+        extra = [gain.reshape(1, HEAD_SIZE), *turn]
+        extra_specs = [pl.BlockSpec((1, HEAD_SIZE), lambda b: (0, 0))] + [
+            pl.BlockSpec((TOKEN_BLOCK, HEAD_SIZE), lambda b: (b, 0))
+        ] * 2
+    return pl.pallas_call(
+        functools.partial(project_kernel, factor),
+        grid=(tokens // TOKEN_BLOCK,),
+        in_specs=[
+            pl.BlockSpec(memory_space=pltpu.SMEM),
+            pl.BlockSpec((blocks, TOKEN_BLOCK, width), lambda b: (0, b, 0)),
+        ]
+        + [pl.BlockSpec((width, cols), lambda b: (0, 0))] * blocks
+        + extra_specs,
+        out_specs=pl.BlockSpec((TOKEN_BLOCK, cols), lambda b: (b, 0)),
+        out_shape=jax.ShapeDtypeStruct((tokens, cols), jnp.bfloat16),
+        compiler_params=pltpu.CompilerParams(vmem_limit_bytes=VMEM),
+        cost_estimate=pl.CostEstimate(
+            flops=2 * normed.size * cols,
+            bytes_accessed=2 * (normed.size + blocks * width * cols + tokens * cols),
+            transcendentals=0,
+        ),
+    )(source, normed, *weights, *extra)
 
 
 def attend_kernel(pos_ref, q_ref, k_ref, v_ref, o_ref):
@@ -108,7 +188,7 @@
         ],
         out_specs=pl.BlockSpec((QUERY_BLOCK, cols), lambda b: (b, 0)),
         out_shape=jax.ShapeDtypeStruct((tokens, cols), jnp.bfloat16),
-        compiler_params=pltpu.CompilerParams(vmem_limit_bytes=40 * 2**20),
+        compiler_params=pltpu.CompilerParams(vmem_limit_bytes=VMEM),
         cost_estimate=pl.CostEstimate(
             flops=4 * tokens * window * cols,
             bytes_accessed=4 * tokens * cols + 4 * keys.shape[0] * HEAD_SIZE,
@@ -125,9 +205,10 @@
     for m in range(inner):
         for piece in range(pieces):
             row = pl.multiple_of(((place ^ m) * pieces + piece) * depth, depth)
-            term = jnp.dot(
+            term = lax.dot_general(
+                weight_ref[:, pl.ds(row, depth)],
                 lefts[m * pieces + piece][...],
-                weight_ref[pl.ds(row, depth), :],
+                (((1,), (1,)), ((), ())),
                 preferred_element_type=jnp.float32,
             )
             total = term if total is None else total + term
@@ -137,17 +218,16 @@
 def group_product(place, attended, weight):
     lefts = [piece for pieces in attended for piece in pieces]
     tokens, depth = lefts[0].shape
-    rows, cols = weight.shape
-    block = 512
+    cols, rows = weight.shape
     return pl.pallas_call(
         functools.partial(group_kernel, len(attended), len(attended[0])),
-        grid=(tokens // block,),
+        grid=(tokens // TOKEN_BLOCK,),
         in_specs=[pl.BlockSpec(memory_space=pltpu.SMEM)]
-        + [pl.BlockSpec((block, depth), lambda b: (b, 0)) for _ in lefts]
-        + [pl.BlockSpec((rows, cols), lambda b: (0, 0))],
-        out_specs=pl.BlockSpec((block, cols), lambda b: (b, 0)),
-        out_shape=jax.ShapeDtypeStruct((tokens, cols), jnp.bfloat16),
-        compiler_params=pltpu.CompilerParams(vmem_limit_bytes=40 * 2**20),
+        + [pl.BlockSpec((TOKEN_BLOCK, depth), lambda b: (b, 0)) for _ in lefts]
+        + [pl.BlockSpec((cols, rows), lambda b: (0, 0))],
+        out_specs=pl.BlockSpec((cols, TOKEN_BLOCK), lambda b: (0, b)),
+        out_shape=jax.ShapeDtypeStruct((cols, tokens), jnp.bfloat16),
+        compiler_params=pltpu.CompilerParams(vmem_limit_bytes=VMEM),
         cost_estimate=pl.CostEstimate(
             flops=2 * tokens * rows * cols,
             bytes_accessed=2 * (tokens * rows + rows * cols + tokens * cols),
@@ -156,42 +236,29 @@
     )(jnp.reshape(place, (1,)), *lefts, weight)
 
 
-def plane_inputs(inputs, in_gain, place, side):
-    rows = inputs.shape[0]
-    half = rows // 2
-    a, b = inputs[:half], inputs[half:]
-    a_y, b_x = swap_tp(a), swap(b, 2)
-    a_x, a_xy = swap(a, 2), swap(a_y, 2)
-    b_y, b_xy = swap_tp(b), swap_tp(b_x)
-    mine = {(0, 0): (a, a_y), (0, 2): (a_x, a_xy), (1, 0): (b, b_y), (1, 2): (b_x, b_xy)}
-    normed = jnp.zeros((INNER * rows, 2 * inputs.shape[1]), jnp.bfloat16)
-    for core in (0, 1):
-        for (part, mask), (near, far) in mine.items():
-            if core:
-                near, far = swap(near, 1), swap(far, 1)
-            low = jnp.where(side == 0, near, far)
-            high = jnp.where(side == 0, far, near)
-            tokens = jnp.concatenate([low, high], axis=1).astype(jnp.float32)
-            block = rms_scale(tokens, in_gain).astype(jnp.bfloat16)
-            row = (place ^ mask ^ core) * rows + part * half
-            normed = lax.dynamic_update_slice_in_dim(normed, block, row, 0)
-    return normed
-
-
-def quarter(weights, which):
-    cut = [
-        lax.dynamic_slice_in_dim(w, which * (w.shape[1] // INNER), w.shape[1] // INNER, axis=1)
-        for w in weights
-    ]
-    return jnp.concatenate(cut, axis=1) if len(cut) > 1 else cut[0]
-
-
-def plane_rows(weights, place):
-    blocks = [quarter(weights, place)]
-    for mask in range(1, INNER):
-        blocks.append(swap(quarter(weights, place ^ mask), mask))
-    whole = placed(blocks, [place ^ mask for mask in range(INNER)])
-    return whole.reshape(-1, whole.shape[-1])
+def shuffle_start(weights, place):
+    def cut(which):
+        parts = []
+        for core in range(2):
+            cols = [w.shape[1] // INNER for w in weights]
+            spans = [
+                lax.dynamic_slice_in_dim(w, (which * 2 + core) * n, n, axis=1)
+                for w, n in zip(weights, cols)
+            ]
+            parts.append(jnp.concatenate(spans, axis=1) if len(spans) > 1 else spans[0])
+        return jnp.stack(parts)
+
+    side = place // 2
+    return cut(side), swap(cut(1 - side), 2)
+
+
+def shuffle_end(mine, theirs, place):
+    core = place % 2
+    rows = in_order(place // 2 == 0, mine, theirs)
+    keep = lax.dynamic_index_in_dim(rows, core, 1, keepdims=False)
+    give = lax.dynamic_index_in_dim(rows, 1 - core, 1, keepdims=False)
+    whole = in_order(core == 0, keep, swap(give, 1))
+    return whole.transpose(1, 0, 2, 3).reshape(-1, whole.shape[-1])
 
 
 def by_planes(
@@ -208,105 +275,95 @@
     positions,
 ):
     tok_rows = inputs.shape[0]
-    planes = lax.axis_size("ctx") // INNER
-    me = lax.axis_index("ctx")
-    place, plane = me % INNER, me // INNER
-    side = lax.axis_index("tp")
+    planes = lax.axis_size("z")
+    place, plane, side = lax.axis_index("i"), lax.axis_index("z"), lax.axis_index("tp")
     plane_tokens = INNER * tok_rows
-
-    kv_start = plane_rows([key_matrix, value_matrix], place)
-    q_start = plane_rows([q_weight], place)
-    q_half = q_start.shape[1] // 2
-    hops = {}
-
-    def ring(name, block):
-        hops[name] = [block]
+    source = ((plane - jnp.arange(planes)) % planes).astype(jnp.int32)
+
+    gathered = lax.all_gather(inputs, ("i", "tp"), axis=0, tiled=False)
+    gathered = gathered.reshape(INNER, 2, *inputs.shape)
+
+    kv_on_way = shuffle_start([key_matrix, value_matrix], place)
+    out_rows = out_weight.T
+    hops = {"o": [out_rows]}
+    previous = []
 
     def hop(name, *others):
         block = hops[name][-1]
         hops[name].append(ring_step(after(block, *others) if others else block))
-        return hops[name][-1]
-
-    kv_half = kv_start.shape[1] // 2
-    ring("k", kv_start[:, :kv_half])
-    ring("v", kv_start[:, kv_half:])
-    ring("qa", q_start[:, :q_half])
-    ring("qb", q_start[:, q_half:])
-    ring("o", out_weight)
-    steps = planes - 1
-    previous = []
-    order = []
-    for _ in range(steps):
-        order += ["k", "v"]
-    for _ in range(steps):
-        order += ["qa"]
-    for _ in range(steps):
-        order += ["qb"]
-    for _ in range(steps):
-        order += ["o"]
+        previous.append(hops[name][-1])
+
+    hop("o")
+    pos_x = in_order(place // 2 == 0, positions, swap(positions, 2))
+    q_on_way = shuffle_start([after(q_weight, kv_on_way[0])], place)
+    kv = shuffle_end(*kv_on_way, place)
+    kv_half = kv.shape[1] // 2
+    hops["k"], hops["v"] = [kv[:, :kv_half]], [kv[:, kv_half:]]
+    pos = in_order(place % 2 == 0, pos_x, swap(pos_x, 1)).transpose(1, 0, 2).reshape(-1)
+    hop("k")
+    hop("v")
+    q = shuffle_end(*q_on_way, place)
+    q_half = q.shape[1] // 2
+    hops["qa"], hops["qb"] = [q[:, :q_half]], [q[:, q_half:]]
+    order = ["k", "v"] * (planes - 2) + ["qa", "qb"] * (planes - 1) + ["o"] * (planes - 2)
     for name in order:
-        previous.append(hop(name, *previous[-2:-1]))
-
-    source = [(plane - d) % planes for d in range(planes)]
-
-    def whole_rows(name):
-        return placed(hops[name], source).reshape(MODEL_WIDTH, -1)
-
-    normed = plane_inputs(inputs, in_gain, place, side)
-    position_blocks = [positions] + [swap(positions, mask) for mask in range(1, INNER)]
-    position = placed(position_blocks, [place ^ mask for mask in range(INNER)]).reshape(-1)
-    turn = angles_of(position, HEAD_SIZE // 2)
-    turn = lax.optimization_barrier(turn)
-
-    def project(name):
-        return jnp.dot(normed, whole_rows(name), preferred_element_type=jnp.float32)
-
-    size = lax.axis_size("ctx")
-    up = [(c, c + INNER) for c in range(size - INNER)]
-
-    def with_halo(own):
-        far = lax.ppermute(own[plane_tokens - VISIBLE_SPAN :], "ctx", up)
-        return jnp.concatenate([far, own], axis=0)
-
-    keys = with_halo(prepare_heads(project("k"), key_norm_gain, turn, 1.0))
-    values = with_halo(project("v").astype(jnp.bfloat16))
+        hop(name, previous[-2])
+
+    half = HEAD_SIZE // 2
+    frequency = ROPE_BASE ** (-jnp.arange(half, dtype=jnp.float32) / half)
+    angles = pos.astype(jnp.float32)[:, None] * frequency[None, :]
+    cosine, sine = jnp.cos(angles), jnp.sin(angles)
+    turn = (
+        jnp.concatenate([cosine, cosine], axis=1),
+        jnp.concatenate([-sine, sine], axis=1),
+    )
+
+    normed = norm_by_blocks(gathered, in_gain, planes)
+    keys = project(normed, source, hops["k"], key_norm_gain, turn)
+    values = project(normed, source, hops["v"])
+    up = [(c, c + 1) for c in range(planes - 1)]
+    own_kv = jnp.concatenate([keys, values], axis=1)
+    halo = lax.ppermute(own_kv[plane_tokens - VISIBLE_SPAN :], "z", up)
+    all_kv = jnp.concatenate([halo, own_kv], axis=0)
+
     factor = (MODEL_WIDTH // QUERY_HEADS) ** (-0.5)
     attended = [[] for _ in range(INNER)]
     for index, name in enumerate(("qa", "qb")):
-        queries = prepare_heads(project(name), q_gain, turn, factor)
-        span = slice(index * HEAD_SIZE, (index + 1) * HEAD_SIZE)
-        own = attend(position[:, None], queries, keys[:, span], values[:, span])
+        queries = project(normed, source, hops[name], q_gain, turn, factor)
+        spans = [
+            slice(n * HEAD_SIZE, (n + 1) * HEAD_SIZE) for n in (index, index + kv_half // HEAD_SIZE)
+        ]
+        own = attend(pos[:, None], queries, all_kv[:, spans[0]], all_kv[:, spans[1]])
         far = swap(own, 2)
         for mask, piece in zip(range(INNER), (own, swap(own, 1), far, swap(far, 1))):
             attended[mask].append(piece)
 
-    both = ("ctx", "tp")
-    cols = out_weight.shape[1]
+    axes = ("z", "i", "tp")
+    cols = out_rows.shape[0]
     per_side = planes // 2
-    arrived, places = [], []
+    slots = jnp.zeros((planes, INNER, cols, tok_rows), jnp.bfloat16)
     for d in range(planes):
         term = group_product(place, attended, hops["o"][d])
-        pairs, inside = [], []
-        for c in range(size):
+        across, inside = [], []
+        for c in range(planes * INNER):
             home = ((c // INNER - d) % planes) // per_side
-            pairs.append((2 * c + 1 - home, 2 * c + home))
+            across.append((2 * c + 1 - home, 2 * c + home))
             inside.append(2 * c + home)
-        other = lax.ppermute(term, both, pairs)
+        other = lax.ppermute(term, axes, across)
         total = (term.astype(jnp.float32) + other.astype(jnp.float32)).astype(jnp.bfloat16)
         for mask in range(INNER):
-            row = (place ^ mask) * tok_rows
-            block = lax.dynamic_slice_in_dim(total, row, tok_rows, axis=0)
+            block = lax.dynamic_slice_in_dim(total, (place ^ mask) * tok_rows, tok_rows, axis=1)
             if mask:
-                block = lax.ppermute(block, both, [(n, n ^ (2 * mask)) for n in inside])
-            arrived.append(block)
-            places.append(source[d] * INNER + (place ^ mask))
-    slots = placed(arrived, places)
-    mine = lax.dynamic_slice_in_dim(slots, side * per_side * INNER, per_side * INNER, axis=0)
-    share = mine.transpose(1, 0, 2).reshape(tok_rows, -1).astype(jnp.float32)
-    own_squares = jnp.sum(share * share, axis=-1)
+                block = lax.ppermute(block, axes, [(n, n ^ (2 * mask)) for n in inside])
+            slots = lax.dynamic_update_slice(
+                slots, block[None, None], (source[d], place ^ mask, 0, 0)
+            )
+    mine = lax.dynamic_slice_in_dim(slots, side * per_side, per_side, axis=0)
+    share = mine.reshape(-1, tok_rows).astype(jnp.float32)
+    own_squares = jnp.sum(share * share, axis=0)
     squares = own_squares + swap_tp(own_squares)
-    branch = share * lax.rsqrt(squares[:, None] / MODEL_WIDTH + EPS) * post_gain
-    return (inputs.astype(jnp.float32) + branch).astype(jnp.bfloat16)
+    branch = share * lax.rsqrt(squares / MODEL_WIDTH + EPS)[None, :] * post_gain[:, None]
+    return (inputs.astype(jnp.float32) + branch.T).astype(jnp.bfloat16)
 
 
 def from_behind(x, axis, by):
@@ -425,28 +482,29 @@
     return (inputs.astype(jnp.float32) + branch).astype(jnp.bfloat16)
 
 
-def fits_planes(sizes):
-    return sizes["tp"] == 2 and sizes["ctx"] == 16
-
-
 def solution(mesh):
-    sizes = mesh.shape
+    ctx, tp = mesh.shape["ctx"], mesh.shape["tp"]
+    whole_planes = tp == 2 and ctx % (2 * INNER) == 0
+    if whole_planes:
+        devices = mesh.devices.reshape(ctx // INNER, INNER, tp)
+        mesh = jax.sharding.Mesh(devices, ("z", "i", "tp"))
+    tokens = ("z", "i") if whole_planes else "ctx"
     return jax.shard_map(
-        by_planes if fits_planes(sizes) else by_devices,
+        by_planes if whole_planes else by_devices,
         mesh=mesh,
         in_specs=(
-            P("ctx", "tp"),
+            P(tokens, "tp"),
             P(),
-            P("ctx", "tp"),
-            P("ctx", "tp"),
-            P("ctx", "tp"),
+            P(tokens, "tp"),
+            P(tokens, "tp"),
+            P(tokens, "tp"),
             P(),
             P(),
-            P("tp", "ctx"),
+            P("tp", tokens),
             P("tp"),
-            P("ctx"),
-            P("ctx"),
+            P(tokens),
+            P(tokens),
         ),
-        out_specs=P("ctx", "tp"),
+        out_specs=P(tokens, "tp"),
         check_vma=False,
     )

time: 656 us -> 519 us (0.79)
  the two profiles are of different devices: /device:TPU:2 before, /device:TPU:24 now
where the time goes in v3:
time: 519 us; the launch traced here: 517 us
  waiting for transfers between devices  258 us (50%)
  Pallas kernels  130 us (25%)
  starting transfers between devices  70.9 us (14%)
  between operations  22.1 us (4%)
  local copies, waits for them, and re-layouts  20.9 us (4%)
  other arithmetic  15.9 us (3%)
    ppermute x15, waiting for transfers between devices, ring_step(): return lax.ppermute(x, 'z', [(c, (c + 1) % size) for c in range(size)])  117 us
    ppermute x12, waiting for transfers between devices, swap(): return lax.ppermute(x, 'i', [(c, c ^ mask) for c in range(INNER)])  73.5 us
    pallas_call x4, Pallas kernels, project(): pl.pallas_call(functools.partial(project_kernel, factor), grid=(tokens //...  51.4 us
    ppermute x4, waiting for transfers between devices, by_planes(): other = lax.ppermute(term, axes, across)  45.2 us
    ppermute x15, starting transfers between devices, ring_step(): return lax.ppermute(x, 'z', [(c, (c + 1) % size) for c in range(size)])  31 us
    pallas_call x2, Pallas kernels, attend(): pl.pallas_call(attend_kernel, grid=(tokens // QUERY_BLOCK,), in_specs=[pl...  30.3 us
    pallas_call x4, Pallas kernels, group_product(): pl.pallas_call(functools.partial(group_kernel, len(attended), len(attende...  26.4 us
    pallas_call x1, Pallas kernels, norm_by_blocks(): pl.pallas_call(norm_kernel, grid=(inner, per_place), in_specs=[pl.BlockSp...  21.5 us
  transfers between devices with their start and end apart: 46, of which 21 were waited for; matrix products, arithmetic and copies ran while one was open for 5% of the time, Pallas kernels for 25%

profile of v3, /device:TPU:24, one launch (start us, length us, event | category | flops | bytes accessed | tf_op | source)
XLA Modules:
  0.0 517.2 jit_solution(5128717718465473181)
XLA Ops:
  9.9 19.2 %collective-permute-done.4 = bf16[2,336,512]{2,1,0:T(8,128)(2,1)S(1)} collective-permute-done((bf16[2,336,512]{2,1,0:T(8,128)(2,1)S(1)}, bf16[2,336,512]{2,1,0:T(8,128)(2,1)S(1)}, u32[]{:S(2)}, u32[]{:S(2)}) %collective-permute-start.4) | collective-permute-done | bytes 688160 | tf_op jit(solution)/shard_map/ppermute | solution.py:52
  30.6 2.5 collective-permute-start.2
  36.5 27.4 %collective-permute-done.2 = bf16[2,336,512]{2,1,0:T(8,128)(2,1)} collective-permute-done((bf16[2,336,512]{2,1,0:T(8,128)(2,1)S(1)}, bf16[2,336,512]{2,1,0:T(8,128)(2,1)}, u32[]{:S(2)}, u32[]{:S(2)}) %collective-permute-start.2) | collective-permute-done | bytes 688160 | tf_op jit(solution)/shard_map/ppermute | solution.py:52
  66.2 2.1 collective-permute-start.7
  68.5 28.1 %collective-permute-done.7.refs_2_ = bf16[1344,256]{1,0:T(8,128)(2,1)S(1)} collective-permute-done((bf16[1344,256]{1,0:T(8,128)(2,1)S(1)}, bf16[1344,256]{1,0:T(8,128)(2,1)S(1)}, u32[]{:S(2)}, u32[]{:S(2)}) %collective-permute-start.7) | collective-permute-done | bytes 688160 | tf_op jit(solution)/shard_map/ppermute | solution.py:61
  96.6 2.1 collective-permute-start.8
  99.6 15.4 %collective-permute-done.8.refs_3_ = bf16[1344,256]{1,0:T(8,128)(2,1)S(1)} collective-permute-done((bf16[1344,256]{1,0:T(8,128)(2,1)S(1)}, bf16[1344,256]{1,0:T(8,128)(2,1)S(1)}, u32[]{:S(2)}, u32[]{:S(2)}) %collective-permute-start.8) | collective-permute-done | bytes 688160 | tf_op jit(solution)/shard_map/ppermute | solution.py:61
  115.9 3.9 collective-permute-start.9
  119.8 10.0 %collective-permute-done.14.refs_3_ = bf16[1344,256]{1,0:T(8,128)(2,1)S(1)} collective-permute-done((bf16[1344,256]{1,0:T(8,128)(2,1)S(1)}, bf16[1344,256]{1,0:T(8,128)(2,1)S(1)}, u32[]{:S(2)}, u32[]{:S(2)}) %collective-permute-start.14) | collective-permute-done | bytes 688160 | tf_op jit(solution)/shard_map/ppermute | solution.py:61
  130.6 3.9 collective-permute-start.16
  141.3 3.3 collective-permute-done.9.refs_1_
  144.6 3.9 collective-permute-start.10
  148.5 10.9 %collective-permute-done.16.refs_1_ = bf16[1344,256]{1,0:T(8,128)(2,1)} collective-permute-done((bf16[1344,256]{1,0:T(8,128)(2,1)S(1)}, bf16[1344,256]{1,0:T(8,128)(2,1)}, u32[]{:S(2)}, u32[]{:S(2)}) %collective-permute-start.16) | collective-permute-done | bytes 688160 | tf_op jit(solution)/shard_map/ppermute | solution.py:61
  159.3 3.9 collective-permute-start.17
  163.2 3.7 fusion.2
  167.6 36.0 %collective-permute-done.10.refs_2_ = bf16[1344,256]{1,0:T(8,128)(2,1)} collective-permute-done((bf16[1344,256]{1,0:T(8,128)(2,1)}, bf16[1344,256]{1,0:T(8,128)(2,1)}, u32[]{:S(2)}, u32[]{:S(2)}) %collective-permute-start.10) | collective-permute-done | bytes 688160 | tf_op jit(solution)/shard_map/ppermute | solution.py:61
  203.6 3.9 collective-permute-start.11
  207.5 10.9 %collective-permute-done.17.refs_2_ = bf16[1344,256]{1,0:T(8,128)(2,1)} collective-permute-done((bf16[1344,256]{1,0:T(8,128)(2,1)}, bf16[1344,256]{1,0:T(8,128)(2,1)}, u32[]{:S(2)}, u32[]{:S(2)}) %collective-permute-start.17) | collective-permute-done | bytes 688160 | tf_op jit(solution)/shard_map/ppermute | solution.py:61
  218.3 3.9 collective-permute-start.18
  222.2 21.5 %shard_map.100.x_ref = bf16[4,2048,1344]{2,1,0:T(8,128)(2,1)} custom-call(bf16[4,2,512,2688]{3,2,1,0:T(8,128)(2,1)} %bitcast.102, f32[2,1,2688]{2,1,0:T(1,128)S(1)} %reshape.106.gain_ref), custom_call_target="tpu_custom_call" | custom-call | flops 55050240 | bytes 44040192 | tf_op jit(solution)/shard_map/pallas_call | solution.py:89
  243.8 11.1 %shard_map.103 = bf16[2048,256]{1,0:T(8,128)(2,1)S(1)} custom-call(s32[4]{0:T(128)S(1)} %and_select_fusion.source_ref, bf16[4,2048,1344]{2,1,0:T(8,128)(2,1)} %shard_map.100.x_ref, bf16[1344,256]{1,0:T(8,128)(2,1)S(1)} %get-tuple-element.51.refs_0_, bf16[1344,256]{1,0:T(8,128)(2,1)S(1)} %copy-done.10, bf16[1344,256]{1,0:T(8,128)(2,1)S(1)} %copy-done.12, ...), custom_call_target="tpu_custom_call" | custom-call | flops 5637144576 | bytes 25821184 | tf_op jit(solution)/shard_map/pallas_call | solution.py:134
  254.9 13.0 %shard_map.102 = bf16[2048,256]{1,0:T(8,128)(2,1)S(1)} custom-call(s32[4]{0:T(128)S(1)} %and_select_fusion.source_ref, bf16[4,2048,1344]{2,1,0:T(8,128)(2,1)} %shard_map.100.x_ref, bf16[1344,256]{1,0:T(8,128)(2,1)S(1)} %get-tuple-element.52.refs_0_, bf16[1344,256]{1,0:T(8,128)(2,1)S(1)} %copy-done.16, bf16[1344,256]{1,0:T(8,128)(2,1)S(1)} %copy-done.18, ...), custom_call_target="tpu_custom_call" | custom-call | flops 5637144576 | bytes 25821184 | tf_op jit(solution)/shard_map/pallas_call | solution.py:134
  269.5 13.6 %shard_map.105.q_ref = bf16[2048,256]{1,0:T(8,128)(2,1)S(1)} custom-call(s32[4]{0:T(128)S(1)} %and_select_fusion.source_ref, bf16[4,2048,1344]{2,1,0:T(8,128)(2,1)} %shard_map.100.x_ref, bf16[1344,256]{1,0:T(8,128)(2,1)S(1)} %copy-done.7, bf16[1344,256]{1,0:T(8,128)(2,1)} %collective-permute-done.16.refs_1_, ...), custom_call_target="tpu_custom_call" | custom-call | flops 5637144576 | bytes 25821184 | tf_op jit(solution)/shard_map/pallas_call | solution.py:134
  283.2 13.7 %shard_map.101.q_ref = bf16[2048,256]{1,0:T(8,128)(2,1)S(1)} custom-call(s32[4]{0:T(128)S(1)} %and_select_fusion.source_ref, bf16[4,2048,1344]{2,1,0:T(8,128)(2,1)} %shard_map.100.x_ref, bf16[1344,256]{1,0:T(8,128)(2,1)S(1)} %copy-done.5, bf16[1344,256]{1,0:T(8,128)(2,1)} %collective-permute-done.9.refs_1_, ...), custom_call_target="tpu_custom_call" | custom-call | flops 5637144576 | bytes 25821184 | tf_op jit(solution)/shard_map/pallas_call | solution.py:134
  298.4 15.1 %shard_map.106.refs_1_ = bf16[2048,256]{1,0:T(8,128)(2,1)S(1)} custom-call(s32[2048,1]{1,0:T(8,128)S(1)} %copy-done.8, bf16[2048,256]{1,0:T(8,128)(2,1)S(1)} %shard_map.105.q_ref, bf16[3072,128]{1,0:T(8,128)(2,1)S(1)} %get-tuple-element.34.k_ref, bf16[3072,128]{1,0:T(8,128)(2,1)S(1)} %get-tuple-element.33.v_ref), custom_call_target="tpu_custom_call" | custom-call | flops 2684354560 | bytes 3670016 | tf_op jit(solution)/shard_map/pallas_call | solution.py:180
  315.3 15.2 %shard_map.104.refs_0_ = bf16[2048,256]{1,0:T(8,128)(2,1)S(1)} custom-call(s32[2048,1]{1,0:T(8,128)S(1)} %copy-done.8, bf16[2048,256]{1,0:T(8,128)(2,1)S(1)} %shard_map.101.q_ref, bf16[3072,128]{1,0:T(8,128)(2,1)S(1)} %get-tuple-element.36.k_ref, bf16[3072,128]{1,0:T(8,128)(2,1)S(1)} %get-tuple-element.35.v_ref), custom_call_target="tpu_custom_call" | custom-call | flops 2684354560 | bytes 3670016 | tf_op jit(solution)/shard_map/pallas_call | solution.py:180
  331.4 7.7 %collective-permute-done.22.refs_5_ = bf16[2048,256]{1,0:T(8,128)(2,1)S(1)} collective-permute-done((bf16[2048,256]{1,0:T(8,128)(2,1)S(1)}, bf16[2048,256]{1,0:T(8,128)(2,1)S(1)}, u32[]{:S(2)}, u32[]{:S(2)}) %collective-permute-start.22) | collective-permute-done | bytes 1048608 | tf_op jit(solution)/shard_map/ppermute | solution.py:52
  339.2 16.1 %collective-permute-done.21.refs_4_ = bf16[2048,256]{1,0:T(8,128)(2,1)S(1)} collective-permute-done((bf16[2048,256]{1,0:T(8,128)(2,1)S(1)}, bf16[2048,256]{1,0:T(8,128)(2,1)S(1)}, u32[]{:S(2)}, u32[]{:S(2)}) %collective-permute-start.21) | collective-permute-done | bytes 1048608 | tf_op jit(solution)/shard_map/ppermute | solution.py:52
  355.3 2.2 collective-permute-done.34.refs_8_
  360.5 6.6 %shard_map.107 = bf16[336,2048]{1,0:T(8,128)(2,1)} custom-call(s32[1]{0:T(128)} %bitcast.place_ref, bf16[2048,256]{1,0:T(8,128)(2,1)S(1)} %shard_map.104.refs_0_, bf16[2048,256]{1,0:T(8,128)(2,1)S(1)} %shard_map.106.refs_1_, bf16[2048,256]{1,0:T(8,128)(2,1)S(1)} %collective-permute-done.19.refs_2_, bf16[2048,256]{1,0:T(8,128)(2,1)S(1)} %collective-permute-done.20.refs_3_, ...), custom_call_target="tpu_custom_call" | custom-call | flops 2818572288 | bytes 11141120 | tf_op jit(solution)/shard_map/pallas_call | solution.py:222
  367.1 5.0 collective-permute-start.25
  372.0 6.6 %shard_map.108 = bf16[336,2048]{1,0:T(8,128)(2,1)} custom-call(s32[1]{0:T(128)} %bitcast.place_ref, bf16[2048,256]{1,0:T(8,128)(2,1)S(1)} %shard_map.104.refs_0_, bf16[2048,256]{1,0:T(8,128)(2,1)S(1)} %shard_map.106.refs_1_, bf16[2048,256]{1,0:T(8,128)(2,1)S(1)} %collective-permute-done.19.refs_2_, bf16[2048,256]{1,0:T(8,128)(2,1)S(1)} %collective-permute-done.20.refs_3_, ...), custom_call_target="tpu_custom_call" | custom-call | flops 2818572288 | bytes 11141120 | tf_op jit(solution)/shard_map/pallas_call | solution.py:222
  378.7 2.5 collective-permute-start.30
  386.8 4.5 copy.15
  396.3 6.6 %shard_map.109 = bf16[336,2048]{1,0:T(8,128)(2,1)} custom-call(s32[1]{0:T(128)} %bitcast.place_ref, bf16[2048,256]{1,0:T(8,128)(2,1)S(1)} %shard_map.104.refs_0_, bf16[2048,256]{1,0:T(8,128)(2,1)S(1)} %shard_map.106.refs_1_, bf16[2048,256]{1,0:T(8,128)(2,1)S(1)} %copy-done.3, bf16[2048,256]{1,0:T(8,128)(2,1)S(1)} %copy-done.1, ...), custom_call_target="tpu_custom_call" | custom-call | flops 2818572288 | bytes 11141120 | tf_op jit(solution)/shard_map/pallas_call | solution.py:222
  404.3 6.6 %shard_map.110 = bf16[336,2048]{1,0:T(8,128)(2,1)} custom-call(s32[1]{0:T(128)} %bitcast.place_ref, bf16[2048,256]{1,0:T(8,128)(2,1)S(1)} %shard_map.104.refs_0_, bf16[2048,256]{1,0:T(8,128)(2,1)S(1)} %shard_map.106.refs_1_, bf16[2048,256]{1,0:T(8,128)(2,1)S(1)} %copy-done.3, bf16[2048,256]{1,0:T(8,128)(2,1)S(1)} %copy-done.1, ...), custom_call_target="tpu_custom_call" | custom-call | flops 2818572288 | bytes 11141120 | tf_op jit(solution)/shard_map/pallas_call | solution.py:222
  415.9 13.0 %collective-permute-done.30 = bf16[336,2048]{1,0:T(8,128)(2,1)} collective-permute-done((bf16[336,2048]{1,0:T(8,128)(2,1)}, bf16[336,2048]{1,0:T(8,128)(2,1)}, u32[]{:S(2)}, u32[]{:S(2)}) %collective-permute-start.30) | collective-permute-done | bytes 1376288 | tf_op jit(solution)/shard_map/ppermute | solution.py:352
  431.8 6.5 %collective-permute-done.35 = bf16[336,2048]{1,0:T(8,128)(2,1)S(1)} collective-permute-done((bf16[336,2048]{1,0:T(8,128)(2,1)}, bf16[336,2048]{1,0:T(8,128)(2,1)S(1)}, u32[]{:S(2)}, u32[]{:S(2)}) %collective-permute-start.35) | collective-permute-done | bytes 1376288 | tf_op jit(solution)/shard_map/ppermute | solution.py:352
  439.4 25.7 %collective-permute-done.40 = bf16[336,2048]{1,0:T(8,128)(2,1)S(1)} collective-permute-done((bf16[336,2048]{1,0:T(8,128)(2,1)}, bf16[336,2048]{1,0:T(8,128)(2,1)S(1)}, u32[]{:S(2)}, u32[]{:S(2)}) %collective-permute-start.40) | collective-permute-done | bytes 1376288 | tf_op jit(solution)/shard_map/ppermute | solution.py:352
  469.9 3.0 collective-permute-start.37
  473.0 2.7 collective-permute-start.36
  475.7 2.6 collective-permute-start.43
  478.4 2.8 collective-permute-start.42
  481.3 2.1 collective-permute-start.41
  483.5 3.4 collective-permute-done.37
  487.1 14.6 %collective-permute-done.42 = bf16[336,512]{1,0:T(8,128)(2,1)S(1)} collective-permute-done((bf16[336,512]{1,0:T(8,128)(2,1)S(1)}, bf16[336,512]{1,0:T(8,128)(2,1)S(1)}, u32[]{:S(2)}, u32[]{:S(2)}) %collective-permute-start.42) | collective-permute-done | bytes 344096 | tf_op jit(solution)/shard_map/ppermute | solution.py:357
  503.3 2.8 collective-permute-done.44
  507.4 2.9 copy.18
  (194 shorter events, 50.3 us)
Async XLA Ops:
  6.5 215.7 %all-gather.3.cloned.1.call-start = ((), (), s32[]{:S(2)}) async-start(), calls=%async_computation | async-start | bytes 24772608 | tf_op jit(solution)/shard_map/all_gather | solution.py:283
  8.2 20.9 %collective-permute-start.4 = (bf16[2,336,512]{2,1,0:T(8,128)(2,1)S(1)}, bf16[2,336,512]{2,1,0:T(8,128)(2,1)S(1)}, u32[]{:S(2)}, u32[]{:S(2)}) collective-permute-start(bf16[2,336,512]{2,1,0:T(8,128)(2,1)S(1)} %pad_maximum_fusion.5), channel_id=1, source_target_pairs={{0,4},{2,6},{4,0},{6,2},{1,5},{3,7},{5,1},{7,3},{8,12},{10,14},{12... | collective-permute-start | bytes 2064392 | tf_op jit(solution)/shard_map/ppermute | solution.py:52
  29.4 3.7 collective-permute-start.5
  30.6 33.2 %collective-permute-start.2 = (bf16[2,336,512]{2,1,0:T(8,128)(2,1)S(1)}, bf16[2,336,512]{2,1,0:T(8,128)(2,1)}, u32[]{:S(2)}, u32[]{:S(2)}) collective-permute-start(bf16[2,336,512]{2,1,0:T(8,128)(2,1)S(1)} %pad_maximum_fusion.4), channel_id=1, source_target_pairs={{0,4},{2,6},{4,0},{6,2},{1,5},{3,7},{5,1},{7,3},{8,12},{10,14},{12... | collective-permute-start | bytes 2064392 | tf_op jit(solution)/shard_map/ppermute | solution.py:52
  34.8 30.7 %collective-permute-start.12 = (bf16[1344,256]{1,0:T(8,128)(2,1)S(1)}, bf16[1344,256]{1,0:T(8,128)(2,1)S(1)}, u32[]{:S(2)}, u32[]{:S(2)}) collective-permute-start(bf16[1344,256]{1,0:T(8,128)(2,1)S(1)} %get-tuple-element.51.refs_0_), channel_id=1, source_target_pairs={{0,8},{8,16},{16,24},{24,0},{1,9},{9,17},{17,25},{25,1},{2,10},{10... | collective-permute-start | bytes 2064392 | tf_op jit(solution)/shard_map/ppermute | solution.py:61
  35.0 31.2 %collective-permute-start.6 = (bf16[1344,256]{1,0:T(8,128)(2,1)S(1)}, bf16[1344,256]{1,0:T(8,128)(2,1)S(1)}, u32[]{:S(2)}, u32[]{:S(2)}) collective-permute-start(bf16[1344,256]{1,0:T(8,128)(2,1)S(1)} %get-tuple-element.52.refs_0_), channel_id=1, source_target_pairs={{0,8},{8,16},{16,24},{24,0},{1,9},{9,17},{17,25},{25,1},{2,10},{10... | collective-permute-start | bytes 2064392 | tf_op jit(solution)/shard_map/ppermute | solution.py:61
  65.4 33.3 %collective-permute-start.13 = (bf16[1344,256]{1,0:T(8,128)(2,1)S(1)}, bf16[1344,256]{1,0:T(8,128)(2,1)S(1)}, u32[]{:S(2)}, u32[]{:S(2)}) collective-permute-start(bf16[1344,256]{1,0:T(8,128)(2,1)S(1)} %collective-permute-done.12.refs_1_), channel_id=1, source_target_pairs={{0,8},{8,16},{16,24},{24,0},{1,9},{9,17},{17,25},{25,1},{2,10},{10... | collective-permute-start | bytes 2064392 | tf_op jit(solution)/shard_map/ppermute | solution.py:61
  66.2 30.4 %collective-permute-start.7 = (bf16[1344,256]{1,0:T(8,128)(2,1)S(1)}, bf16[1344,256]{1,0:T(8,128)(2,1)S(1)}, u32[]{:S(2)}, u32[]{:S(2)}) collective-permute-start(bf16[1344,256]{1,0:T(8,128)(2,1)S(1)} %collective-permute-done.6.refs_1_), channel_id=1, source_target_pairs={{0,8},{8,16},{16,24},{24,0},{1,9},{9,17},{17,25},{25,1},{2,10},{10... | collective-permute-start | bytes 2064392 | tf_op jit(solution)/shard_map/ppermute | solution.py:61
  68.4 30.4 %collective-permute-start.3 = (bf16[2,336,512]{2,1,0:T(8,128)(2,1)S(1)}, bf16[2,336,512]{2,1,0:T(8,128)(2,1)S(1)}, u32[]{:S(2)}, u32[]{:S(2)}) collective-permute-start(bf16[2,336,512]{2,1,0:T(8,128)(2,1)S(1)} %get-tuple-element.56), channel_id=1, source_target_pairs={{0,2},{2,0},{4,6},{6,4},{1,3},{3,1},{5,7},{7,5},{8,10},{10,8},{12,... | collective-permute-start | bytes 2064392 | tf_op jit(solution)/shard_map/ppermute | solution.py:52
  96.6 18.4 %collective-permute-start.8 = (bf16[1344,256]{1,0:T(8,128)(2,1)S(1)}, bf16[1344,256]{1,0:T(8,128)(2,1)S(1)}, u32[]{:S(2)}, u32[]{:S(2)}) collective-permute-start(bf16[1344,256]{1,0:T(8,128)(2,1)S(1)} %collective-permute-done.7.refs_2_), channel_id=1, source_target_pairs={{0,8},{8,16},{16,24},{24,0},{1,9},{9,17},{17,25},{25,1},{2,10},{10... | collective-permute-start | bytes 2064392 | tf_op jit(solution)/shard_map/ppermute | solution.py:61
  98.7 31.0 %collective-permute-start.14 = (bf16[1344,256]{1,0:T(8,128)(2,1)S(1)}, bf16[1344,256]{1,0:T(8,128)(2,1)S(1)}, u32[]{:S(2)}, u32[]{:S(2)}) collective-permute-start(bf16[1344,256]{1,0:T(8,128)(2,1)S(1)} %collective-permute-done.13.refs_2_), channel_id=1, source_target_pairs={{0,8},{8,16},{16,24},{24,0},{1,9},{9,17},{17,25},{25,1},{2,10},{10... | collective-permute-start | bytes 2064392 | tf_op jit(solution)/shard_map/ppermute | solution.py:61
  99.6 67.4 %copy-start.4 = (bf16[1344,256]{1,0:T(8,128)(2,1)}, bf16[1344,256]{1,0:T(8,128)(2,1)S(1)}, u32[]{:S(2)}) copy-start(bf16[1344,256]{1,0:T(8,128)(2,1)S(1)} %get-tuple-element.21.refs_0_) | copy-start | bytes 2064388
  99.6 67.4 %copy-start.6 = (bf16[1344,256]{1,0:T(8,128)(2,1)}, bf16[1344,256]{1,0:T(8,128)(2,1)S(1)}, u32[]{:S(2)}) copy-start(bf16[1344,256]{1,0:T(8,128)(2,1)S(1)} %get-tuple-element.26.refs_0_) | copy-start | bytes 2064388
  115.9 28.7 %collective-permute-start.9 = (bf16[1344,256]{1,0:T(8,128)(2,1)S(1)}, bf16[1344,256]{1,0:T(8,128)(2,1)}, u32[]{:S(2)}, u32[]{:S(2)}) collective-permute-start(bf16[1344,256]{1,0:T(8,128)(2,1)S(1)} %get-tuple-element.21.refs_0_), channel_id=1, source_target_pairs={{0,8},{8,16},{16,24},{24,0},{1,9},{9,17},{17,25},{25,1},{2,10},{10... | collective-permute-start | bytes 2064392 | tf_op jit(solution)/shard_map/ppermute | solution.py:61
  130.6 28.7 %collective-permute-start.16 = (bf16[1344,256]{1,0:T(8,128)(2,1)S(1)}, bf16[1344,256]{1,0:T(8,128)(2,1)}, u32[]{:S(2)}, u32[]{:S(2)}) collective-permute-start(bf16[1344,256]{1,0:T(8,128)(2,1)S(1)} %get-tuple-element.26.refs_0_), channel_id=1, source_target_pairs={{0,8},{8,16},{16,24},{24,0},{1,9},{9,17},{17,25},{25,1},{2,10},{10... | collective-permute-start | bytes 2064392 | tf_op jit(solution)/shard_map/ppermute | solution.py:61
  134.5 3.6 collective-permute-start
  136.1 194.7 %collective-permute-start.29 = (bf16[336,2048]{1,0:T(8,128)(2,1)}, bf16[336,2048]{1,0:T(8,128)(2,1)}, u32[]{:S(2)}, u32[]{:S(2)}) collective-permute-start(bf16[336,2048]{1,0:T(8,128)(2,1)} %bitcast.33.refs_8_), channel_id=1, source_target_pairs={{0,8},{8,16},{16,24},{24,0},{1,9},{9,17},{17,25},{25,1},{2,10},{10... | collective-permute-start | bytes 4128776 | tf_op jit(solution)/shard_map/ppermute | solution.py:61
  138.1 1.2 collective-permute-start.1
  144.6 59.0 %collective-permute-start.10 = (bf16[1344,256]{1,0:T(8,128)(2,1)}, bf16[1344,256]{1,0:T(8,128)(2,1)}, u32[]{:S(2)}, u32[]{:S(2)}) collective-permute-start(bf16[1344,256]{1,0:T(8,128)(2,1)} %collective-permute-done.9.refs_1_), channel_id=1, source_target_pairs={{0,8},{8,16},{16,24},{24,0},{1,9},{9,17},{17,25},{25,1},{2,10},{10... | collective-permute-start | bytes 2064392 | tf_op jit(solution)/shard_map/ppermute | solution.py:61
  159.3 59.0 %collective-permute-start.17 = (bf16[1344,256]{1,0:T(8,128)(2,1)}, bf16[1344,256]{1,0:T(8,128)(2,1)}, u32[]{:S(2)}, u32[]{:S(2)}) collective-permute-start(bf16[1344,256]{1,0:T(8,128)(2,1)} %collective-permute-done.16.refs_1_), channel_id=1, source_target_pairs={{0,8},{8,16},{16,24},{24,0},{1,9},{9,17},{17,25},{25,1},{2,10},{10... | collective-permute-start | bytes 2064392 | tf_op jit(solution)/shard_map/ppermute | solution.py:61
  203.6 79.6 %collective-permute-start.11 = (bf16[1344,256]{1,0:T(8,128)(2,1)}, bf16[1344,256]{1,0:T(8,128)(2,1)}, u32[]{:S(2)}, u32[]{:S(2)}) collective-permute-start(bf16[1344,256]{1,0:T(8,128)(2,1)} %collective-permute-done.10.refs_2_), channel_id=1, source_target_pairs={{0,8},{8,16},{16,24},{24,0},{1,9},{9,17},{17,25},{25,1},{2,10},{10... | collective-permute-start | bytes 2064392 | tf_op jit(solution)/shard_map/ppermute | solution.py:61
  218.3 51.2 %collective-permute-start.18 = (bf16[1344,256]{1,0:T(8,128)(2,1)}, bf16[1344,256]{1,0:T(8,128)(2,1)}, u32[]{:S(2)}, u32[]{:S(2)}) collective-permute-start(bf16[1344,256]{1,0:T(8,128)(2,1)} %collective-permute-done.17.refs_2_), channel_id=1, source_target_pairs={{0,8},{8,16},{16,24},{24,0},{1,9},{9,17},{17,25},{25,1},{2,10},{10... | collective-permute-start | bytes 2064392 | tf_op jit(solution)/shard_map/ppermute | solution.py:61
  268.1 28.9 %collective-permute-start.15 = (bf16[1024,512]{1,0:T(8,128)(2,1)S(1)}, bf16[1024,512]{1,0:T(8,128)(2,1)S(1)}, u32[]{:S(2)}, u32[]{:S(2)}) collective-permute-start(bf16[1024,512]{1,0:T(8,128)(2,1)S(1)} %pad_maximum_fusion), channel_id=1, source_target_pairs={{0,8},{8,16},{16,24},{1,9},{9,17},{17,25},{2,10},{10,18},{18,26},{... | collective-permute-start | bytes 3145736 | tf_op jit(solution)/shard_map/ppermute | solution.py:326
  313.5 25.6 %collective-permute-start.22 = (bf16[2048,256]{1,0:T(8,128)(2,1)S(1)}, bf16[2048,256]{1,0:T(8,128)(2,1)S(1)}, u32[]{:S(2)}, u32[]{:S(2)}) collective-permute-start(bf16[2048,256]{1,0:T(8,128)(2,1)S(1)} %shard_map.106.refs_1_), channel_id=1, source_target_pairs={{0,4},{2,6},{4,0},{6,2},{1,5},{3,7},{5,1},{7,3},{8,12},{10,14},{12... | collective-permute-start | bytes 3145736 | tf_op jit(solution)/shard_map/ppermute | solution.py:52
  330.4 24.9 %collective-permute-start.21 = (bf16[2048,256]{1,0:T(8,128)(2,1)S(1)}, bf16[2048,256]{1,0:T(8,128)(2,1)S(1)}, u32[]{:S(2)}, u32[]{:S(2)}) collective-permute-start(bf16[2048,256]{1,0:T(8,128)(2,1)S(1)} %shard_map.104.refs_0_), channel_id=1, source_target_pairs={{0,4},{2,6},{4,0},{6,2},{1,5},{3,7},{5,1},{7,3},{8,12},{10,14},{12... | collective-permute-start | bytes 3145736 | tf_op jit(solution)/shard_map/ppermute | solution.py:52
  330.9 26.6 %collective-permute-start.34 = (bf16[336,2048]{1,0:T(8,128)(2,1)}, bf16[336,2048]{1,0:T(8,128)(2,1)}, u32[]{:S(2)}, u32[]{:S(2)}) collective-permute-start(bf16[336,2048]{1,0:T(8,128)(2,1)} %collective-permute-done.29.refs_8_), channel_id=1, source_target_pairs={{0,8},{8,16},{16,24},{24,0},{1,9},{9,17},{17,25},{25,1},{2,10},{10... | collective-permute-start | bytes 4128776 | tf_op jit(solution)/shard_map/ppermute | solution.py:61
  330.9 28.1 %collective-permute-start.20 = (bf16[2048,256]{1,0:T(8,128)(2,1)S(1)}, bf16[2048,256]{1,0:T(8,128)(2,1)S(1)}, u32[]{:S(2)}, u32[]{:S(2)}) collective-permute-start(bf16[2048,256]{1,0:T(8,128)(2,1)S(1)} %shard_map.106.refs_1_), channel_id=1, source_target_pairs={{0,2},{2,0},{4,6},{6,4},{1,3},{3,1},{5,7},{7,5},{8,10},{10,8},{12,... | collective-permute-start | bytes 3145736 | tf_op jit(solution)/shard_map/ppermute | solution.py:52
  330.9 28.1 %collective-permute-start.19 = (bf16[2048,256]{1,0:T(8,128)(2,1)S(1)}, bf16[2048,256]{1,0:T(8,128)(2,1)S(1)}, u32[]{:S(2)}, u32[]{:S(2)}) collective-permute-start(bf16[2048,256]{1,0:T(8,128)(2,1)S(1)} %shard_map.104.refs_0_), channel_id=1, source_target_pairs={{0,2},{2,0},{4,6},{6,4},{1,3},{3,1},{5,7},{7,5},{8,10},{10,8},{12,... | collective-permute-start | bytes 3145736 | tf_op jit(solution)/shard_map/ppermute | solution.py:52
  339.2 19.9 %collective-permute-start.24 = (bf16[2048,256]{1,0:T(8,128)(2,1)S(1)}, bf16[2048,256]{1,0:T(8,128)(2,1)S(1)}, u32[]{:S(2)}, u32[]{:S(2)}) collective-permute-start(bf16[2048,256]{1,0:T(8,128)(2,1)S(1)} %collective-permute-done.22.refs_5_), channel_id=1, source_target_pairs={{0,2},{2,0},{4,6},{6,4},{1,3},{3,1},{5,7},{7,5},{8,10},{10,8},{12,... | collective-permute-start | bytes 3145736 | tf_op jit(solution)/shard_map/ppermute | solution.py:52
  355.3 3.8 collective-permute-start.23
  357.5 46.8 %collective-permute-start.39 = (bf16[336,2048]{1,0:T(8,128)(2,1)}, bf16[336,2048]{1,0:T(8,128)(2,1)}, u32[]{:S(2)}, u32[]{:S(2)}) collective-permute-start(bf16[336,2048]{1,0:T(8,128)(2,1)} %collective-permute-done.34.refs_8_), channel_id=1, source_target_pairs={{0,8},{8,16},{16,24},{24,0},{1,9},{9,17},{17,25},{25,1},{2,10},{10... | collective-permute-start | bytes 4128776 | tf_op jit(solution)/shard_map/ppermute | solution.py:61
  367.1 45.5 %collective-permute-start.25 = (bf16[336,2048]{1,0:T(8,128)(2,1)}, bf16[336,2048]{1,0:T(8,128)(2,1)}, u32[]{:S(2)}, u32[]{:S(2)}) collective-permute-start(bf16[336,2048]{1,0:T(8,128)(2,1)} %shard_map.107), channel_id=1, source_target_pairs={{1,0},{3,2},{5,4},{7,6},{9,8},{11,10},{13,12},{15,14},{16,17},{18,... | collective-permute-start | bytes 4128776 | tf_op jit(solution)/shard_map/ppermute | solution.py:352
  378.7 50.3 %collective-permute-start.30 = (bf16[336,2048]{1,0:T(8,128)(2,1)}, bf16[336,2048]{1,0:T(8,128)(2,1)}, u32[]{:S(2)}, u32[]{:S(2)}) collective-permute-start(bf16[336,2048]{1,0:T(8,128)(2,1)} %shard_map.108), channel_id=1, source_target_pairs={{0,1},{2,3},{4,5},{6,7},{9,8},{11,10},{13,12},{15,14},{17,16},{19,... | collective-permute-start | bytes 4128776 | tf_op jit(solution)/shard_map/ppermute | solution.py:352
  402.9 35.3 %collective-permute-start.35 = (bf16[336,2048]{1,0:T(8,128)(2,1)}, bf16[336,2048]{1,0:T(8,128)(2,1)S(1)}, u32[]{:S(2)}, u32[]{:S(2)}) collective-permute-start(bf16[336,2048]{1,0:T(8,128)(2,1)} %shard_map.109), channel_id=1, source_target_pairs={{0,1},{2,3},{4,5},{6,7},{8,9},{10,11},{12,13},{14,15},{17,16},{19,... | collective-permute-start | bytes 4128776 | tf_op jit(solution)/shard_map/ppermute | solution.py:352
  411.0 54.2 %collective-permute-start.40 = (bf16[336,2048]{1,0:T(8,128)(2,1)}, bf16[336,2048]{1,0:T(8,128)(2,1)S(1)}, u32[]{:S(2)}, u32[]{:S(2)}) collective-permute-start(bf16[336,2048]{1,0:T(8,128)(2,1)} %shard_map.110), channel_id=1, source_target_pairs={{1,0},{3,2},{5,4},{7,6},{8,9},{10,11},{12,13},{14,15},{16,17},{18,... | collective-permute-start | bytes 4128776 | tf_op jit(solution)/shard_map/ppermute | solution.py:352
  414.6 55.3 %collective-permute-start.28 = (bf16[336,512]{1,0:T(8,128)(2,1)S(1)}, bf16[336,512]{1,0:T(8,128)(2,1)S(1)}, u32[]{:S(2)}, u32[]{:S(2)}) collective-permute-start(bf16[336,512]{1,0:T(8,128)(2,1)S(1)} %get-tuple-element.46), channel_id=1, source_target_pairs={{0,6},{2,4},{4,2},{6,0},{8,14},{10,12},{12,10},{14,8},{17,23},{19,... | collective-permute-start | bytes 1032200 | tf_op jit(solution)/shard_map/ppermute | solution.py:357
  415.3 52.6 %collective-permute-start.27 = (bf16[336,512]{1,0:T(8,128)(2,1)S(1)}, bf16[336,512]{1,0:T(8,128)(2,1)S(1)}, u32[]{:S(2)}, u32[]{:S(2)}) collective-permute-start(bf16[336,512]{1,0:T(8,128)(2,1)S(1)} %get-tuple-element.47), channel_id=1, source_target_pairs={{0,4},{2,6},{4,0},{6,2},{8,12},{10,14},{12,8},{14,10},{17,21},{19,... | collective-permute-start | bytes 1032200 | tf_op jit(solution)/shard_map/ppermute | solution.py:357
  429.0 38.2 %collective-permute-start.26 = (bf16[336,512]{1,0:T(8,128)(2,1)S(1)}, bf16[336,512]{1,0:T(8,128)(2,1)S(1)}, u32[]{:S(2)}, u32[]{:S(2)}) collective-permute-start(bf16[336,512]{1,0:T(8,128)(2,1)S(1)} %get-tuple-element.48), channel_id=1, source_target_pairs={{0,2},{2,0},{4,6},{6,4},{8,10},{10,8},{12,14},{14,12},{17,19},{19,... | collective-permute-start | bytes 1032200 | tf_op jit(solution)/shard_map/ppermute | solution.py:357
  438.3 40.1 %collective-permute-start.33 = (bf16[336,512]{1,0:T(8,128)(2,1)S(1)}, bf16[336,512]{1,0:T(8,128)(2,1)S(1)}, u32[]{:S(2)}, u32[]{:S(2)}) collective-permute-start(bf16[336,512]{1,0:T(8,128)(2,1)S(1)} %get-tuple-element.43), channel_id=1, source_target_pairs={{1,7},{3,5},{5,3},{7,1},{8,14},{10,12},{12,10},{14,8},{16,22},{18,... | collective-permute-start | bytes 1032200 | tf_op jit(solution)/shard_map/ppermute | solution.py:357
  465.1 10.5 %collective-permute-start.32 = (bf16[336,512]{1,0:T(8,128)(2,1)S(1)}, bf16[336,512]{1,0:T(8,128)(2,1)S(1)}, u32[]{:S(2)}, u32[]{:S(2)}) collective-permute-start(bf16[336,512]{1,0:T(8,128)(2,1)S(1)} %get-tuple-element.44), channel_id=1, source_target_pairs={{1,5},{3,7},{5,1},{7,3},{8,12},{10,14},{12,8},{14,10},{16,20},{18,... | collective-permute-start | bytes 1032200 | tf_op jit(solution)/shard_map/ppermute | solution.py:357
  467.2 5.8 %collective-permute-start.31 = (bf16[336,512]{1,0:T(8,128)(2,1)S(1)}, bf16[336,512]{1,0:T(8,128)(2,1)S(1)}, u32[]{:S(2)}, u32[]{:S(2)}) collective-permute-start(bf16[336,512]{1,0:T(8,128)(2,1)S(1)} %get-tuple-element.45), channel_id=1, source_target_pairs={{1,3},{3,1},{5,7},{7,5},{8,10},{10,8},{12,14},{14,12},{16,18},{18,... | collective-permute-start | bytes 1032200 | tf_op jit(solution)/shard_map/ppermute | solution.py:357
  467.9 19.1 %collective-permute-start.38 = (bf16[336,512]{1,0:T(8,128)(2,1)S(1)}, bf16[336,512]{1,0:T(8,128)(2,1)S(1)}, u32[]{:S(2)}, u32[]{:S(2)}) collective-permute-start(bf16[336,512]{1,0:T(8,128)(2,1)S(1)} %get-tuple-element.40), channel_id=1, source_target_pairs={{1,7},{3,5},{5,3},{7,1},{9,15},{11,13},{13,11},{15,9},{16,22},{18,... | collective-permute-start | bytes 1032200 | tf_op jit(solution)/shard_map/ppermute | solution.py:357
  469.9 17.0 %collective-permute-start.37 = (bf16[336,512]{1,0:T(8,128)(2,1)S(1)}, bf16[336,512]{1,0:T(8,128)(2,1)S(1)}, u32[]{:S(2)}, u32[]{:S(2)}) collective-permute-start(bf16[336,512]{1,0:T(8,128)(2,1)S(1)} %get-tuple-element.41), channel_id=1, source_target_pairs={{1,5},{3,7},{5,1},{7,3},{9,13},{11,15},{13,9},{15,11},{16,20},{18,... | collective-permute-start | bytes 1032200 | tf_op jit(solution)/shard_map/ppermute | solution.py:357
  473.0 8.3 %collective-permute-start.36 = (bf16[336,512]{1,0:T(8,128)(2,1)S(1)}, bf16[336,512]{1,0:T(8,128)(2,1)S(1)}, u32[]{:S(2)}, u32[]{:S(2)}) collective-permute-start(bf16[336,512]{1,0:T(8,128)(2,1)S(1)} %get-tuple-element.42), channel_id=1, source_target_pairs={{1,3},{3,1},{5,7},{7,5},{9,11},{11,9},{13,15},{15,13},{16,18},{18,... | collective-permute-start | bytes 1032200 | tf_op jit(solution)/shard_map/ppermute | solution.py:357
  475.7 26.0 %collective-permute-start.43 = (bf16[336,512]{1,0:T(8,128)(2,1)S(1)}, bf16[336,512]{1,0:T(8,128)(2,1)S(1)}, u32[]{:S(2)}, u32[]{:S(2)}) collective-permute-start(bf16[336,512]{1,0:T(8,128)(2,1)S(1)} %get-tuple-element.37), channel_id=1, source_target_pairs={{0,6},{2,4},{4,2},{6,0},{9,15},{11,13},{13,11},{15,9},{17,23},{19,... | collective-permute-start | bytes 1032200 | tf_op jit(solution)/shard_map/ppermute | solution.py:357
  478.4 23.3 %collective-permute-start.42 = (bf16[336,512]{1,0:T(8,128)(2,1)S(1)}, bf16[336,512]{1,0:T(8,128)(2,1)S(1)}, u32[]{:S(2)}, u32[]{:S(2)}) collective-permute-start(bf16[336,512]{1,0:T(8,128)(2,1)S(1)} %get-tuple-element.38), channel_id=1, source_target_pairs={{0,4},{2,6},{4,0},{6,2},{9,13},{11,15},{13,9},{15,11},{17,21},{19,... | collective-permute-start | bytes 1032200 | tf_op jit(solution)/shard_map/ppermute | solution.py:357
  481.3 5.7 %collective-permute-start.41 = (bf16[336,512]{1,0:T(8,128)(2,1)S(1)}, bf16[336,512]{1,0:T(8,128)(2,1)S(1)}, u32[]{:S(2)}, u32[]{:S(2)}) collective-permute-start(bf16[336,512]{1,0:T(8,128)(2,1)S(1)} %get-tuple-element.39), channel_id=1, source_target_pairs={{0,2},{2,0},{4,6},{6,4},{9,11},{11,9},{13,15},{15,13},{17,19},{19,... | collective-permute-start | bytes 1032200 | tf_op jit(solution)/shard_map/ppermute | solution.py:357
  502.4 3.7 collective-permute-start.44
  (35 other events, 405.9 us)
Sparse Core Ops, SparseCore 0:
  9.2 130.9 all-gather.2

commit v4 on v3

--- a/solution.py
+++ b/solution.py
@@ -151,89 +151,92 @@
     )(source, normed, *weights, *extra)
 
 
-def attend_kernel(pos_ref, q_ref, k_ref, v_ref, o_ref):
-    start = pl.multiple_of(pl.program_id(0) * QUERY_BLOCK, QUERY_BLOCK)
+def attend_kernel(part, pos_ref, *refs):
+    queries, (kv_ref, o_ref) = refs[:-2], refs[-2:]
+    start = pl.multiple_of((pl.program_id(0) * 2 + part) * QUERY_BLOCK, QUERY_BLOCK)
     window = VISIBLE_SPAN + QUERY_BLOCK
-    keys = k_ref[pl.ds(start, window), :]
-    values = v_ref[pl.ds(start, window), :]
     shape = (QUERY_BLOCK, window)
     last = lax.broadcasted_iota(jnp.int32, shape, 0) + VISIBLE_SPAN
     column = lax.broadcasted_iota(jnp.int32, shape, 1)
     first = last - jnp.minimum(pos_ref[...], VISIBLE_SPAN - 1)
     allowed = (column <= last) & (column >= first)
-    for head in range(q_ref.shape[1] // HEAD_SIZE):
-        span = slice(head * HEAD_SIZE, (head + 1) * HEAD_SIZE)
-        scores = lax.dot_general(
-            q_ref[:, span], keys, (((1,), (1,)), ((), ())), preferred_element_type=jnp.float32
-        )
-        scores = jnp.where(allowed, scores, MASKED)
-        expo = jnp.exp(scores - jnp.max(scores, axis=-1, keepdims=True))
-        weights = (expo / jnp.sum(expo, axis=-1, keepdims=True)).astype(jnp.bfloat16)
-        mixed = jnp.dot(weights, values, preferred_element_type=jnp.float32)
-        o_ref[:, span] = mixed.astype(jnp.bfloat16)
-
-
-def attend(position, queries, keys, values):
-    tokens, cols = queries.shape
+    kv_heads = len(queries)
+    for kv_head, q_ref in enumerate(queries):
+        keys = kv_ref[pl.ds(start, window), pl.ds(kv_head * HEAD_SIZE, HEAD_SIZE)]
+        values = kv_ref[pl.ds(start, window), pl.ds((kv_heads + kv_head) * HEAD_SIZE, HEAD_SIZE)]
+        group = q_ref.shape[1] // HEAD_SIZE
+        for head in range(group):
+            span = slice(head * HEAD_SIZE, (head + 1) * HEAD_SIZE)
+            scores = lax.dot_general(
+                q_ref[:, span], keys, (((1,), (1,)), ((), ())), preferred_element_type=jnp.float32
+            )
+            scores = jnp.where(allowed, scores, MASKED)
+            expo = jnp.exp(scores - jnp.max(scores, axis=-1, keepdims=True))
+            weights = (expo / jnp.sum(expo, axis=-1, keepdims=True)).astype(jnp.bfloat16)
+            mixed = jnp.dot(weights, values, preferred_element_type=jnp.float32)
+            place = (kv_head * group + head) * HEAD_SIZE
+            o_ref[:, place : place + HEAD_SIZE] = mixed.astype(jnp.bfloat16)
+
+
+def attend(part, position, queries, all_kv):
+    tokens, cols = queries[0].shape
     window = VISIBLE_SPAN + QUERY_BLOCK
-    heads = cols // HEAD_SIZE
+    width = cols * len(queries)
+    half = tokens // 2
     return pl.pallas_call(
-        attend_kernel,
-        grid=(tokens // QUERY_BLOCK,),
-        in_specs=[
-            pl.BlockSpec((QUERY_BLOCK, 1), lambda b: (b, 0)),
-            pl.BlockSpec((QUERY_BLOCK, cols), lambda b: (b, 0)),
-            pl.BlockSpec(keys.shape, lambda b: (0, 0)),
-            pl.BlockSpec(values.shape, lambda b: (0, 0)),
-        ],
-        out_specs=pl.BlockSpec((QUERY_BLOCK, cols), lambda b: (b, 0)),
-        out_shape=jax.ShapeDtypeStruct((tokens, cols), jnp.bfloat16),
+        functools.partial(attend_kernel, part),
+        grid=(half // QUERY_BLOCK,),
+        in_specs=[pl.BlockSpec((QUERY_BLOCK, 1), lambda b: (2 * b + part, 0))]
+        + [pl.BlockSpec((QUERY_BLOCK, cols), lambda b: (2 * b + part, 0)) for _ in queries]
+        + [pl.BlockSpec(all_kv.shape, lambda b: (0, 0))],
+        out_specs=pl.BlockSpec((QUERY_BLOCK, width), lambda b: (b, 0)),
+        out_shape=jax.ShapeDtypeStruct((half, width), jnp.bfloat16),
         compiler_params=pltpu.CompilerParams(vmem_limit_bytes=VMEM),
         cost_estimate=pl.CostEstimate(
-            flops=4 * tokens * window * cols,
-            bytes_accessed=4 * tokens * cols + 4 * keys.shape[0] * HEAD_SIZE,
-            transcendentals=heads * tokens * window,
+            flops=4 * half * window * width,
+            bytes_accessed=4 * half * width + 2 * all_kv.size,
+            transcendentals=half * window * width // HEAD_SIZE,
         ),
-    )(position, queries, keys, values)
-
-
-def group_kernel(inner, pieces, place_ref, *refs):
-    lefts, weight_ref, o_ref = refs[: inner * pieces], refs[-2], refs[-1]
+    )(position, *queries, all_kv)
+
+
+def group_kernel(inner, place_ref, source_ref, *refs):
+    lefts, weights, o_ref = refs[:inner], refs[inner:-1], refs[-1]
     place = place_ref[0]
     depth = lefts[0].shape[1]
-    total = None
-    for m in range(inner):
-        for piece in range(pieces):
-            row = pl.multiple_of(((place ^ m) * pieces + piece) * depth, depth)
+    for d, weight_ref in enumerate(weights):
+        total = None
+        for m in range(inner):
+            row = pl.multiple_of((place ^ m) * depth, depth)
             term = lax.dot_general(
                 weight_ref[:, pl.ds(row, depth)],
-                lefts[m * pieces + piece][...],
+                lefts[m][...],
                 (((1,), (1,)), ((), ())),
                 preferred_element_type=jnp.float32,
             )
             total = term if total is None else total + term
-    o_ref[...] = total.astype(jnp.bfloat16)
-
-
-def group_product(place, attended, weight):
-    lefts = [piece for pieces in attended for piece in pieces]
-    tokens, depth = lefts[0].shape
-    cols, rows = weight.shape
+        o_ref[source_ref[d]] = total.astype(jnp.bfloat16)
+
+
+def group_product(place, source, attended, weights):
+    tokens, depth = attended[0].shape
+    cols, rows = weights[0].shape
+    blocks = len(weights)
     return pl.pallas_call(
-        functools.partial(group_kernel, len(attended), len(attended[0])),
+        functools.partial(group_kernel, len(attended)),
         grid=(tokens // TOKEN_BLOCK,),
-        in_specs=[pl.BlockSpec(memory_space=pltpu.SMEM)]
-        + [pl.BlockSpec((TOKEN_BLOCK, depth), lambda b: (b, 0)) for _ in lefts]
-        + [pl.BlockSpec((cols, rows), lambda b: (0, 0))],
-        out_specs=pl.BlockSpec((cols, TOKEN_BLOCK), lambda b: (0, b)),
-        out_shape=jax.ShapeDtypeStruct((cols, tokens), jnp.bfloat16),
+        in_specs=[pl.BlockSpec(memory_space=pltpu.SMEM)] * 2
+        + [pl.BlockSpec((TOKEN_BLOCK, depth), lambda b: (b, 0)) for _ in attended]
+        + [pl.BlockSpec((cols, rows), lambda b: (0, 0)) for _ in weights],
+        out_specs=pl.BlockSpec((blocks, cols, TOKEN_BLOCK), lambda b: (0, 0, b)),
+        out_shape=jax.ShapeDtypeStruct((blocks, cols, tokens), jnp.bfloat16),
         compiler_params=pltpu.CompilerParams(vmem_limit_bytes=VMEM),
         cost_estimate=pl.CostEstimate(
-            flops=2 * tokens * rows * cols,
-            bytes_accessed=2 * (tokens * rows + rows * cols + tokens * cols),
+            flops=2 * tokens * rows * cols * blocks,
+            bytes_accessed=2 * (tokens * rows + (rows + tokens) * cols * blocks),
             transcendentals=0,
         ),
-    )(jnp.reshape(place, (1,)), *lefts, weight)
+    )(jnp.reshape(place, (1,)), source, *attended, *weights)
 
 
 def shuffle_start(weights, place):
@@ -296,18 +299,19 @@
     hop("o")
     pos_x = in_order(place // 2 == 0, positions, swap(positions, 2))
     q_on_way = shuffle_start([after(q_weight, kv_on_way[0])], place)
-    kv = shuffle_end(*kv_on_way, place)
+    kv = shuffle_end(kv_on_way[0], after(kv_on_way[1], hops["o"][1]), place)
     kv_half = kv.shape[1] // 2
     hops["k"], hops["v"] = [kv[:, :kv_half]], [kv[:, kv_half:]]
     pos = in_order(place % 2 == 0, pos_x, swap(pos_x, 1)).transpose(1, 0, 2).reshape(-1)
     hop("k")
     hop("v")
-    q = shuffle_end(*q_on_way, place)
+    q = shuffle_end(q_on_way[0], after(q_on_way[1], hops["k"][1]), place)
     q_half = q.shape[1] // 2
     hops["qa"], hops["qb"] = [q[:, :q_half]], [q[:, q_half:]]
-    order = ["k", "v"] * (planes - 2) + ["qa", "qb"] * (planes - 1) + ["o"] * (planes - 2)
-    for name in order:
+    for name in ["k", "v"] * (planes - 2):
         hop(name, previous[-2])
+    hop("qa", previous[-2])
+    hop("qb", previous[-2])
 
     half = HEAD_SIZE // 2
     frequency = ROPE_BASE ** (-jnp.arange(half, dtype=jnp.float32) / half)
@@ -318,52 +322,53 @@
         jnp.concatenate([-sine, sine], axis=1),
     )
 
-    normed = norm_by_blocks(gathered, in_gain, planes)
-    keys = project(normed, source, hops["k"], key_norm_gain, turn)
-    values = project(normed, source, hops["v"])
+    normed = norm_by_blocks(after(gathered, hops["v"][-1], *turn), in_gain, planes)
+    hop("qa", normed)
+    hop("qb", normed)
+    keys = project(after(normed, hops["qb"][-2]), source, hops["k"], key_norm_gain, turn)
+    for _ in range(planes - 3):
+        hop("qa", keys)
+        hop("qb", keys)
+    values = project(after(normed, hops["qa"][-2], keys), source, hops["v"])
     up = [(c, c + 1) for c in range(planes - 1)]
     own_kv = jnp.concatenate([keys, values], axis=1)
     halo = lax.ppermute(own_kv[plane_tokens - VISIBLE_SPAN :], "z", up)
     all_kv = jnp.concatenate([halo, own_kv], axis=0)
+    for _ in range(planes - 2):
+        hop("o", previous[-2])
 
     factor = (MODEL_WIDTH // QUERY_HEADS) ** (-0.5)
-    attended = [[] for _ in range(INNER)]
-    for index, name in enumerate(("qa", "qb")):
-        queries = project(normed, source, hops[name], q_gain, turn, factor)
-        spans = [
-            slice(n * HEAD_SIZE, (n + 1) * HEAD_SIZE) for n in (index, index + kv_half // HEAD_SIZE)
-        ]
-        own = attend(pos[:, None], queries, all_kv[:, spans[0]], all_kv[:, spans[1]])
-        far = swap(own, 2)
-        for mask, piece in zip(range(INNER), (own, swap(own, 1), far, swap(far, 1))):
-            attended[mask].append(piece)
-
-    axes = ("z", "i", "tp")
-    cols = out_rows.shape[0]
+    queries = [
+        project(after(normed, values), source, hops[name], q_gain, turn, factor)
+        for name in ("qa", "qb")
+    ]
+
+    own = [attend(0, pos[:, None], queries, all_kv)]
+    own.append(attend(1, after(pos, own[0], hops["o"][-2])[:, None], queries, all_kv))
+    here = place // 2, place % 2
     per_side = planes // 2
-    slots = jnp.zeros((planes, INNER, cols, tok_rows), jnp.bfloat16)
-    for d in range(planes):
-        term = group_product(place, attended, hops["o"][d])
-        across, inside = [], []
-        for c in range(planes * INNER):
-            home = ((c // INNER - d) % planes) // per_side
-            across.append((2 * c + 1 - home, 2 * c + home))
-            inside.append(2 * c + home)
-        other = lax.ppermute(term, axes, across)
-        total = (term.astype(jnp.float32) + other.astype(jnp.float32)).astype(jnp.bfloat16)
-        for mask in range(INNER):
-            block = lax.dynamic_slice_in_dim(total, (place ^ mask) * tok_rows, tok_rows, axis=1)
-            if mask:
-                block = lax.ppermute(block, axes, [(n, n ^ (2 * mask)) for n in inside])
-            slots = lax.dynamic_update_slice(
-                slots, block[None, None], (source[d], place ^ mask, 0, 0)
-            )
-    mine = lax.dynamic_slice_in_dim(slots, side * per_side, per_side, axis=0)
-    share = mine.reshape(-1, tok_rows).astype(jnp.float32)
-    own_squares = jnp.sum(share * share, axis=0)
-    squares = own_squares + swap_tp(own_squares)
-    branch = share * lax.rsqrt(squares / MODEL_WIDTH + EPS)[None, :] * post_gain[:, None]
-    return (inputs.astype(jnp.float32) + branch.T).astype(jnp.bfloat16)
+    results = []
+    for part in range(2):
+        far = swap(own[part], 2)
+        attended = [own[part], swap(own[part], 1), far, swap(far, 1)]
+        if part == 0:
+            attended[0] = after(own[0], own[1])
+        terms = group_product(place, source, attended, hops["o"])
+        keep = lax.dynamic_slice_in_dim(terms, side * per_side, per_side, axis=0)
+        give = lax.dynamic_slice_in_dim(terms, (1 - side) * per_side, per_side, axis=0)
+        sums = (keep.astype(jnp.float32) + swap_tp(give).astype(jnp.float32)).astype(jnp.bfloat16)
+        for bit, mask in ((0, 2), (1, 1)):
+            width = sums.shape[-1] // 2
+            keep = lax.dynamic_slice_in_dim(sums, here[bit] * width, width, axis=-1)
+            give = lax.dynamic_slice_in_dim(sums, (1 - here[bit]) * width, width, axis=-1)
+            sums = in_order(here[bit] == 0, keep, swap(give, mask))
+        share = sums.transpose(2, 1, 0, 3, 4).reshape(-1, sums.shape[-1]).astype(jnp.float32)
+        own_squares = jnp.sum(share * share, axis=0)
+        squares = own_squares + swap_tp(own_squares)
+        branch = share * lax.rsqrt(squares / MODEL_WIDTH + EPS)[None, :] * post_gain[:, None]
+        rows = inputs[part * QUERY_BLOCK : (part + 1) * QUERY_BLOCK].astype(jnp.float32)
+        results.append((rows + branch.T).astype(jnp.bfloat16))
+    return jnp.concatenate(results, axis=0)
 
 
 def from_behind(x, axis, by):

time: 519 us -> 462 us (0.89)
  the two profiles are of different devices: /device:TPU:24 before, /device:TPU:2 now
where the time goes in v4:
time: 462 us; the launch traced here: 458 us
  waiting for transfers between devices  233 us (50%)
  Pallas kernels  126 us (27%)
  local copies, waits for them, and re-layouts  34.4 us (7%)
  starting transfers between devices  29.5 us (6%)
  other arithmetic  20.5 us (4%)
  between operations  14.3 us (3%)
    ppermute x15, waiting for transfers between devices, ring_step(): return lax.ppermute(x, 'z', [(c, (c + 1) % size) for c in range(size)])  131 us
    ppermute x16, waiting for transfers between devices, swap(): return lax.ppermute(x, 'i', [(c, c ^ mask) for c in range(INNER)])  57 us
    pallas_call x4, Pallas kernels, project(): pl.pallas_call(functools.partial(project_kernel, factor), grid=(tokens //...  51.3 us
    ppermute x4, waiting for transfers between devices, swap_tp(): return lax.ppermute(x, 'tp', [(0, 1), (1, 0)])  42.7 us
    pallas_call x2, Pallas kernels, attend(): pl.pallas_call(functools.partial(attend_kernel, part), grid=(half // QUER...  32.5 us
    pallas_call x1, Pallas kernels, norm_by_blocks(): pl.pallas_call(norm_kernel, grid=(inner, per_place), in_specs=[pl.BlockSp...  21.4 us
    pallas_call x2, Pallas kernels, group_product(): pl.pallas_call(functools.partial(group_kernel, len(attended)), grid=(toke...  20.4 us
    unnamed x77, local copies, waits for them, and re-layouts  17.9 us
  transfers between devices with their start and end apart: 37, of which 22 were waited for; matrix products, arithmetic and copies ran while one was open for 8% of the time, Pallas kernels for 27%

profile of v4, /device:TPU:2, one launch (start us, length us, event | category | flops | bytes accessed | tf_op | source)
XLA Modules:
  0.0 457.8 jit_solution(1998272915360029075)
XLA Ops:
  7.9 1.6 collective-permute-start.3
  10.5 22.5 %collective-permute-done.2 = bf16[2,336,512]{2,1,0:T(8,128)(2,1)S(1)} collective-permute-done((bf16[2,336,512]{2,1,0:T(8,128)(2,1)S(1)}, bf16[2,336,512]{2,1,0:T(8,128)(2,1)S(1)}, u32[]{:S(2)}, u32[]{:S(2)}) %collective-permute-start.2) | collective-permute-done | bytes 688160 | tf_op jit(solution)/shard_map/ppermute | solution.py:52
  33.0 8.8 %collective-permute-done.3.refs_5_ = bf16[336,2048]{1,0:T(8,128)(2,1)} collective-permute-done((bf16[336,2048]{1,0:T(8,128)(2,1)S(1)}, bf16[336,2048]{1,0:T(8,128)(2,1)}, u32[]{:S(2)}, u32[]{:S(2)}) %collective-permute-start.3) | collective-permute-done | bytes 1376288 | tf_op jit(solution)/shard_map/ppermute | solution.py:61
  47.0 18.0 %collective-permute-done.5.refs_1_ = bf16[1344,256]{1,0:T(8,128)(2,1)S(1)} collective-permute-done((bf16[1344,256]{1,0:T(8,128)(2,1)S(1)}, bf16[1344,256]{1,0:T(8,128)(2,1)S(1)}, u32[]{:S(2)}, u32[]{:S(2)}) %collective-permute-start.5) | collective-permute-done | bytes 688160 | tf_op jit(solution)/shard_map/ppermute | solution.py:61
  65.0 6.0 %collective-permute-done.8 = bf16[2,336,512]{2,1,0:T(8,128)(2,1)S(1)} collective-permute-done((bf16[2,336,512]{2,1,0:T(8,128)(2,1)S(1)}, bf16[2,336,512]{2,1,0:T(8,128)(2,1)S(1)}, u32[]{:S(2)}, u32[]{:S(2)}) %collective-permute-start.8) | collective-permute-done | bytes 688160 | tf_op jit(solution)/shard_map/ppermute | solution.py:52
  71.0 8.8 %collective-permute-done.9.refs_1_ = bf16[1344,256]{1,0:T(8,128)(2,1)S(1)} collective-permute-done((bf16[1344,256]{1,0:T(8,128)(2,1)S(1)}, bf16[1344,256]{1,0:T(8,128)(2,1)S(1)}, u32[]{:S(2)}, u32[]{:S(2)}) %collective-permute-start.9) | collective-permute-done | bytes 688160 | tf_op jit(solution)/shard_map/ppermute | solution.py:61
  82.2 3.0 collective-permute-done
  86.4 8.0 %collective-permute-done.6.refs_2_ = bf16[1344,256]{1,0:T(8,128)(2,1)S(1)} collective-permute-done((bf16[1344,256]{1,0:T(8,128)(2,1)S(1)}, bf16[1344,256]{1,0:T(8,128)(2,1)S(1)}, u32[]{:S(2)}, u32[]{:S(2)}) %collective-permute-start.6) | collective-permute-done | bytes 688160 | tf_op jit(solution)/shard_map/ppermute | solution.py:61
  94.5 14.8 %collective-permute-done.11.refs_2_ = bf16[1344,256]{1,0:T(8,128)(2,1)} collective-permute-done((bf16[1344,256]{1,0:T(8,128)(2,1)S(1)}, bf16[1344,256]{1,0:T(8,128)(2,1)}, u32[]{:S(2)}, u32[]{:S(2)}) %collective-permute-start.11) | collective-permute-done | bytes 688160 | tf_op jit(solution)/shard_map/ppermute | solution.py:61
  109.4 1.7 maximum_select_fusion.2
  111.2 26.7 %collective-permute-done.12.refs_3_ = bf16[1344,256]{1,0:T(8,128)(2,1)S(1)} collective-permute-done((bf16[1344,256]{1,0:T(8,128)(2,1)}, bf16[1344,256]{1,0:T(8,128)(2,1)S(1)}, u32[]{:S(2)}, u32[]{:S(2)}) %collective-permute-start.12) | collective-permute-done | bytes 688160 | tf_op jit(solution)/shard_map/ppermute | solution.py:61
  138.0 3.7 fusion.6
  142.4 21.4 %shard_map.100.x_ref = bf16[4,2048,1344]{2,1,0:T(8,128)(2,1)} custom-call(bf16[4,2,512,2688]{3,2,1,0:T(8,128)(2,1)} %bitcast.100, f32[2,1,2688]{2,1,0:T(1,128)S(1)} %reshape.108.gain_ref), custom_call_target="tpu_custom_call" | custom-call | flops 55050240 | bytes 44040192 | tf_op jit(solution)/shard_map/pallas_call | solution.py:89
  164.8 8.1 %collective-permute-done.15.refs_1_ = bf16[1344,256]{1,0:T(8,128)(2,1)} collective-permute-done((bf16[1344,256]{1,0:T(8,128)(2,1)S(1)}, bf16[1344,256]{1,0:T(8,128)(2,1)}, u32[]{:S(2)}, u32[]{:S(2)}) %collective-permute-start.15) | collective-permute-done | bytes 688160 | tf_op jit(solution)/shard_map/ppermute | solution.py:61
  176.5 13.1 %shard_map.101 = bf16[2048,256]{1,0:T(8,128)(2,1)S(1)} custom-call(s32[4]{0:T(128)S(1)} %and_select_fusion.source_ref, bf16[4,2048,1344]{2,1,0:T(8,128)(2,1)} %shard_map.100.x_ref, bf16[1344,256]{1,0:T(8,128)(2,1)S(1)} %copy-done.3, bf16[1344,256]{1,0:T(8,128)(2,1)S(1)} %copy-done.20, bf16[1344,256]{1,0:T(8,128)(2,1)} %collective-permute-done.11.refs_2_, ...), custom_call_target="tpu_custom_call" | custom-call | flops 5637144576 | bytes 25821184 | tf_op jit(solution)/shard_map/pallas_call | solution.py:134
  189.7 1.9 broadcast_in_dim_reshape.7.pos_ref
  191.7 10.8 %collective-permute-done.17.refs_2_ = bf16[1344,256]{1,0:T(8,128)(2,1)} collective-permute-done((bf16[1344,256]{1,0:T(8,128)(2,1)}, bf16[1344,256]{1,0:T(8,128)(2,1)}, u32[]{:S(2)}, u32[]{:S(2)}) %collective-permute-start.17) | collective-permute-done | bytes 688160 | tf_op jit(solution)/shard_map/ppermute | solution.py:61
  206.8 10.9 %shard_map.102 = bf16[2048,256]{1,0:T(8,128)(2,1)S(1)} custom-call(s32[4]{0:T(128)S(1)} %and_select_fusion.source_ref, bf16[4,2048,1344]{2,1,0:T(8,128)(2,1)} %shard_map.100.x_ref, bf16[1344,256]{1,0:T(8,128)(2,1)S(1)} %copy-done.1, bf16[1344,256]{1,0:T(8,128)(2,1)S(1)} %copy-done.14, bf16[1344,256]{1,0:T(8,128)(2,1)S(1)} %copy-done.16, ...), custom_call_target="tpu_custom_call" | custom-call | flops 5637144576 | bytes 25821184 | tf_op jit(solution)/shard_map/pallas_call | solution.py:134
  217.8 1.8 collective-permute-start.19
  220.6 13.6 %shard_map.103.refs_0_ = bf16[2048,256]{1,0:T(8,128)(2,1)S(1)} custom-call(s32[4]{0:T(128)S(1)} %and_select_fusion.source_ref, bf16[4,2048,1344]{2,1,0:T(8,128)(2,1)} %shard_map.100.x_ref, bf16[1344,256]{1,0:T(8,128)(2,1)S(1)} %copy-done.7, bf16[1344,256]{1,0:T(8,128)(2,1)} %collective-permute-done.13.refs_1_, ...), custom_call_target="tpu_custom_call" | custom-call | flops 5637144576 | bytes 25821184 | tf_op jit(solution)/shard_map/pallas_call | solution.py:134
  234.3 13.7 %shard_map.104.refs_1_ = bf16[2048,256]{1,0:T(8,128)(2,1)S(1)} custom-call(s32[4]{0:T(128)S(1)} %and_select_fusion.source_ref, bf16[4,2048,1344]{2,1,0:T(8,128)(2,1)} %shard_map.100.x_ref, bf16[1344,256]{1,0:T(8,128)(2,1)S(1)} %copy-done.5, bf16[1344,256]{1,0:T(8,128)(2,1)} %collective-permute-done.15.refs_1_, ...), custom_call_target="tpu_custom_call" | custom-call | flops 5637144576 | bytes 25821184 | tf_op jit(solution)/shard_map/pallas_call | solution.py:134
  248.0 2.0 collective-permute-done.19
  250.0 1.9 maximum_maximum_fusion.refs_2_
  251.9 16.2 %shard_map.105.refs_0_ = bf16[1024,512]{1,0:T(8,128)(2,1)} custom-call(s32[2048,1]{1,0:T(8,128)S(1)} %copy-done.12, bf16[2048,256]{1,0:T(8,128)(2,1)S(1)} %shard_map.103.refs_0_, bf16[2048,256]{1,0:T(8,128)(2,1)S(1)} %shard_map.104.refs_1_, bf16[3072,512]{1,0:T(8,128)(2,1)} %maximum_maximum_fusion.refs_2_), custom_call_target="tpu_custom_call" | custom-call | flops 2684354560 | bytes 5242880 | tf_op jit(solution)/shard_map/pallas_call | solution.py:186
  268.6 9.5 %collective-permute-done.20.refs_6_ = bf16[336,2048]{1,0:T(8,128)(2,1)} collective-permute-done((bf16[336,2048]{1,0:T(8,128)(2,1)}, bf16[336,2048]{1,0:T(8,128)(2,1)}, u32[]{:S(2)}, u32[]{:S(2)}) %collective-permute-start.20) | collective-permute-done | bytes 1376288 | tf_op jit(solution)/shard_map/ppermute | solution.py:61
  281.0 16.3 %shard_map.106.refs_0_ = bf16[1024,512]{1,0:T(8,128)(2,1)} custom-call(s32[2048,1]{1,0:T(8,128)S(1)} %copy.23.pos_ref, bf16[2048,256]{1,0:T(8,128)(2,1)S(1)} %copy-done.9, bf16[2048,256]{1,0:T(8,128)(2,1)S(1)} %copy-done.11, bf16[3072,512]{1,0:T(8,128)(2,1)} %maximum_maximum_fusion.refs_2_), custom_call_target="tpu_custom_call" | custom-call | flops 2684354560 | bytes 5242880 | tf_op jit(solution)/shard_map/pallas_call | solution.py:186
  297.9 10.8 %collective-permute-start.24 = (bf16[336,2048]{1,0:T(8,128)(2,1)}, bf16[336,2048]{1,0:T(8,128)(2,1)}, u32[]{:S(2)}, u32[]{:S(2)}) collective-permute-start(bf16[336,2048]{1,0:T(8,128)(2,1)} %collective-permute-done.20.refs_6_), channel_id=1, source_target_pairs={{0,8},{8,16},{16,24},{24,0},{1,9},{9,17},{17,25},{25,1},{2,10},{10... | collective-permute-start | bytes 4128776 | tf_op jit(solution)/shard_map/ppermute | solution.py:61
  309.1 12.2 %collective-permute-done.30.refs_2_ = bf16[1024,512]{1,0:T(8,128)(2,1)S(1)} collective-permute-done((bf16[1024,512]{1,0:T(8,128)(2,1)}, bf16[1024,512]{1,0:T(8,128)(2,1)S(1)}, u32[]{:S(2)}, u32[]{:S(2)}) %collective-permute-start.30) | collective-permute-done | bytes 1048608 | tf_op jit(solution)/shard_map/ppermute | solution.py:52
  321.3 17.4 %collective-permute-done.24.refs_7_ = bf16[336,2048]{1,0:T(8,128)(2,1)} collective-permute-done((bf16[336,2048]{1,0:T(8,128)(2,1)}, bf16[336,2048]{1,0:T(8,128)(2,1)}, u32[]{:S(2)}, u32[]{:S(2)}) %collective-permute-start.24) | collective-permute-done | bytes 1376288 | tf_op jit(solution)/shard_map/ppermute | solution.py:61
  338.8 10.2 %shard_map.107 = bf16[4,336,1024]{2,1,0:T(8,128)(2,1)} custom-call(s32[1]{0:T(128)} %bitcast.place_ref, s32[4]{0:T(128)S(1)} %and_select_fusion.source_ref, bf16[1024,512]{1,0:T(8,128)(2,1)} %shard_map.105.refs_0_, bf16[1024,512]{1,0:T(8,128)(2,1)} %collective-permute-done.21.refs_1_, bf16[1024,512]{1,0:T(8,128)(2,1)} %collective-permute-done.22.refs_2_, ...), custom_call_target="tpu_custom_call" | custom-call | flops 5637144576 | bytes 12451840 | tf_op jit(solution)/shard_map/pallas_call | solution.py:225
  349.0 2.6 constant_dynamic-slice_fusion.5
  353.1 10.2 %shard_map.108 = bf16[4,336,1024]{2,1,0:T(8,128)(2,1)} custom-call(s32[1]{0:T(128)} %bitcast.place_ref, s32[4]{0:T(128)S(1)} %and_select_fusion.source_ref, bf16[1024,512]{1,0:T(8,128)(2,1)} %shard_map.106.refs_0_, bf16[1024,512]{1,0:T(8,128)(2,1)} %collective-permute-done.29.refs_1_, bf16[1024,512]{1,0:T(8,128)(2,1)S(1)} %collective-permute-done.30.refs_2_, ...), custom_call_target="tpu_custom_call" | custom-call | flops 5637144576 | bytes 12451840 | tf_op jit(solution)/shard_map/pallas_call | solution.py:225
  363.3 2.8 constant_dynamic-slice_fusion.2
  366.6 18.4 %collective-permute-done.25 = bf16[2,336,1024]{2,1,0:T(8,128)(2,1)} collective-permute-done((bf16[2,336,1024]{2,1,0:T(8,128)(2,1)}, bf16[2,336,1024]{2,1,0:T(8,128)(2,1)}, u32[]{:S(2)}, u32[]{:S(2)}) %collective-permute-start.25) | collective-permute-done | bytes 1376288 | tf_op jit(solution)/shard_map/ppermute | solution.py:56
  385.0 1.9 add_convert_fusion.1
  387.1 1.6 collective-permute-start.26
  388.6 22.3 %collective-permute-done.32 = bf16[2,336,1024]{2,1,0:T(8,128)(2,1)} collective-permute-done((bf16[2,336,1024]{2,1,0:T(8,128)(2,1)}, bf16[2,336,1024]{2,1,0:T(8,128)(2,1)}, u32[]{:S(2)}, u32[]{:S(2)}) %collective-permute-start.32) | collective-permute-done | bytes 1376288 | tf_op jit(solution)/shard_map/ppermute | solution.py:56
  410.9 1.9 add_convert_fusion
  413.0 1.6 collective-permute-start.33
  415.8 11.3 %collective-permute-done.33 = bf16[2,336,512]{2,1,0:T(8,128)(2,1)} collective-permute-done((bf16[2,336,512]{2,1,0:T(8,128)(2,1)S(1)}, bf16[2,336,512]{2,1,0:T(8,128)(2,1)}, u32[]{:S(2)}, u32[]{:S(2)}) %collective-permute-start.33) | collective-permute-done | bytes 688160 | tf_op jit(solution)/shard_map/ppermute | solution.py:52
  427.1 1.6 maximum_select_fusion.5
  430.7 1.7 fusion.11
  432.5 1.8 copy.28
  434.3 2.5 copy.29
  436.8 1.8 fusion
  440.1 1.6 convert_bitcast_fusion.1
  444.6 1.6 collective-permute-done.35
  447.9 2.9 copy.27
  (168 shorter events, 38.0 us)
Async XLA Ops:
  6.5 135.9 %all-gather.3.cloned.1.call-start = ((), (), s32[]{:S(2)}) async-start(), calls=%async_computation | async-start | bytes 24772608 | tf_op jit(solution)/shard_map/all_gather | solution.py:286
  7.9 33.9 %collective-permute-start.3 = (bf16[336,2048]{1,0:T(8,128)(2,1)S(1)}, bf16[336,2048]{1,0:T(8,128)(2,1)}, u32[]{:S(2)}, u32[]{:S(2)}) collective-permute-start(bf16[336,2048]{1,0:T(8,128)(2,1)S(1)} %bitcast.97), channel_id=1, source_target_pairs={{0,8},{8,16},{16,24},{24,0},{1,9},{9,17},{17,25},{25,1},{2,10},{10... | collective-permute-start | bytes 4128776 | tf_op jit(solution)/shard_map/ppermute | solution.py:61
  9.8 23.2 %collective-permute-start.2 = (bf16[2,336,512]{2,1,0:T(8,128)(2,1)S(1)}, bf16[2,336,512]{2,1,0:T(8,128)(2,1)S(1)}, u32[]{:S(2)}, u32[]{:S(2)}) collective-permute-start(bf16[2,336,512]{2,1,0:T(8,128)(2,1)S(1)} %pad_maximum_fusion.8), channel_id=1, source_target_pairs={{0,4},{2,6},{4,0},{6,2},{1,5},{3,7},{5,1},{7,3},{8,12},{10,14},{12... | collective-permute-start | bytes 2064392 | tf_op jit(solution)/shard_map/ppermute | solution.py:52
  42.1 2.2 collective-permute-start.4
  44.9 20.1 %collective-permute-start.5 = (bf16[1344,256]{1,0:T(8,128)(2,1)S(1)}, bf16[1344,256]{1,0:T(8,128)(2,1)S(1)}, u32[]{:S(2)}, u32[]{:S(2)}) collective-permute-start(bf16[1344,256]{1,0:T(8,128)(2,1)S(1)} %get-tuple-element.67.refs_0_), channel_id=1, source_target_pairs={{0,8},{8,16},{16,24},{24,0},{1,9},{9,17},{17,25},{25,1},{2,10},{10... | collective-permute-start | bytes 2064392 | tf_op jit(solution)/shard_map/ppermute | solution.py:61
  45.0 26.0 %collective-permute-start.8 = (bf16[2,336,512]{2,1,0:T(8,128)(2,1)S(1)}, bf16[2,336,512]{2,1,0:T(8,128)(2,1)S(1)}, u32[]{:S(2)}, u32[]{:S(2)}) collective-permute-start(bf16[2,336,512]{2,1,0:T(8,128)(2,1)S(1)} %pad_maximum_fusion.9), channel_id=1, source_target_pairs={{0,4},{2,6},{4,0},{6,2},{1,5},{3,7},{5,1},{7,3},{8,12},{10,14},{12... | collective-permute-start | bytes 2064392 | tf_op jit(solution)/shard_map/ppermute | solution.py:52
  45.6 34.1 %collective-permute-start.9 = (bf16[1344,256]{1,0:T(8,128)(2,1)S(1)}, bf16[1344,256]{1,0:T(8,128)(2,1)S(1)}, u32[]{:S(2)}, u32[]{:S(2)}) collective-permute-start(bf16[1344,256]{1,0:T(8,128)(2,1)S(1)} %get-tuple-element.66.refs_0_), channel_id=1, source_target_pairs={{0,8},{8,16},{16,24},{24,0},{1,9},{9,17},{17,25},{25,1},{2,10},{10... | collective-permute-start | bytes 2064392 | tf_op jit(solution)/shard_map/ppermute | solution.py:61
  65.0 15.0 %copy-start.13 = (bf16[1344,256]{1,0:T(8,128)(2,1)}, bf16[1344,256]{1,0:T(8,128)(2,1)S(1)}, u32[]{:S(2)}) copy-start(bf16[1344,256]{1,0:T(8,128)(2,1)S(1)} %collective-permute-done.5.refs_1_) | copy-start | bytes 2064388
  65.0 29.5 %collective-permute-start.6 = (bf16[1344,256]{1,0:T(8,128)(2,1)S(1)}, bf16[1344,256]{1,0:T(8,128)(2,1)S(1)}, u32[]{:S(2)}, u32[]{:S(2)}) collective-permute-start(bf16[1344,256]{1,0:T(8,128)(2,1)S(1)} %collective-permute-done.5.refs_1_), channel_id=1, source_target_pairs={{0,8},{8,16},{16,24},{24,0},{1,9},{9,17},{17,25},{25,1},{2,10},{10... | collective-permute-start | bytes 2064392 | tf_op jit(solution)/shard_map/ppermute | solution.py:61
  79.7 29.6 %collective-permute-start.11 = (bf16[1344,256]{1,0:T(8,128)(2,1)S(1)}, bf16[1344,256]{1,0:T(8,128)(2,1)}, u32[]{:S(2)}, u32[]{:S(2)}) collective-permute-start(bf16[1344,256]{1,0:T(8,128)(2,1)S(1)} %collective-permute-done.9.refs_1_), channel_id=1, source_target_pairs={{0,8},{8,16},{16,24},{24,0},{1,9},{9,17},{17,25},{25,1},{2,10},{10... | collective-permute-start | bytes 2064392 | tf_op jit(solution)/shard_map/ppermute | solution.py:61
  81.6 27.8 %collective-permute-start.10 = (bf16[2,336,512]{2,1,0:T(8,128)(2,1)}, bf16[2,336,512]{2,1,0:T(8,128)(2,1)}, u32[]{:S(2)}, u32[]{:S(2)}) collective-permute-start(bf16[2,336,512]{2,1,0:T(8,128)(2,1)} %get-tuple-element.61), channel_id=1, source_target_pairs={{0,2},{2,0},{4,6},{6,4},{1,3},{3,1},{5,7},{7,5},{8,10},{10,8},{12,... | collective-permute-start | bytes 2064392 | tf_op jit(solution)/shard_map/ppermute | solution.py:52
  81.6 3.6 collective-permute-start
  85.2 1.2 collective-permute-start.1
  94.5 16.6 %copy-start.15 = (bf16[1344,256]{1,0:T(8,128)(2,1)}, bf16[1344,256]{1,0:T(8,128)(2,1)S(1)}, u32[]{:S(2)}) copy-start(bf16[1344,256]{1,0:T(8,128)(2,1)S(1)} %collective-permute-done.6.refs_2_) | copy-start | bytes 2064388
  94.5 43.4 %collective-permute-start.7 = (bf16[1344,256]{1,0:T(8,128)(2,1)S(1)}, bf16[1344,256]{1,0:T(8,128)(2,1)S(1)}, u32[]{:S(2)}, u32[]{:S(2)}) collective-permute-start(bf16[1344,256]{1,0:T(8,128)(2,1)S(1)} %collective-permute-done.6.refs_2_), channel_id=1, source_target_pairs={{0,8},{8,16},{16,24},{24,0},{1,9},{9,17},{17,25},{25,1},{2,10},{10... | collective-permute-start | bytes 2064392 | tf_op jit(solution)/shard_map/ppermute | solution.py:61
  109.3 28.6 %collective-permute-start.12 = (bf16[1344,256]{1,0:T(8,128)(2,1)}, bf16[1344,256]{1,0:T(8,128)(2,1)S(1)}, u32[]{:S(2)}, u32[]{:S(2)}) collective-permute-start(bf16[1344,256]{1,0:T(8,128)(2,1)} %collective-permute-done.11.refs_2_), channel_id=1, source_target_pairs={{0,8},{8,16},{16,24},{24,0},{1,9},{9,17},{17,25},{25,1},{2,10},{10... | collective-permute-start | bytes 2064392 | tf_op jit(solution)/shard_map/ppermute | solution.py:61
  111.2 30.5 %copy-start.4 = (bf16[1344,256]{1,0:T(8,128)(2,1)}, bf16[1344,256]{1,0:T(8,128)(2,1)S(1)}, u32[]{:S(2)}) copy-start(bf16[1344,256]{1,0:T(8,128)(2,1)S(1)} %get-tuple-element.36.refs_0_) | copy-start | bytes 2064388
  111.2 30.5 %copy-start.6 = (bf16[1344,256]{1,0:T(8,128)(2,1)}, bf16[1344,256]{1,0:T(8,128)(2,1)S(1)}, u32[]{:S(2)}) copy-start(bf16[1344,256]{1,0:T(8,128)(2,1)S(1)} %get-tuple-element.34.refs_0_) | copy-start | bytes 2064388
  137.9 25.9 %collective-permute-start.13 = (bf16[1344,256]{1,0:T(8,128)(2,1)S(1)}, bf16[1344,256]{1,0:T(8,128)(2,1)}, u32[]{:S(2)}, u32[]{:S(2)}) collective-permute-start(bf16[1344,256]{1,0:T(8,128)(2,1)S(1)} %get-tuple-element.34.refs_0_), channel_id=1, source_target_pairs={{0,8},{8,16},{16,24},{24,0},{1,9},{9,17},{17,25},{25,1},{2,10},{10... | collective-permute-start | bytes 2064392 | tf_op jit(solution)/shard_map/ppermute | solution.py:61
  137.9 35.0 %collective-permute-start.15 = (bf16[1344,256]{1,0:T(8,128)(2,1)S(1)}, bf16[1344,256]{1,0:T(8,128)(2,1)}, u32[]{:S(2)}, u32[]{:S(2)}) collective-permute-start(bf16[1344,256]{1,0:T(8,128)(2,1)S(1)} %get-tuple-element.36.refs_0_), channel_id=1, source_target_pairs={{0,8},{8,16},{16,24},{24,0},{1,9},{9,17},{17,25},{25,1},{2,10},{10... | collective-permute-start | bytes 2064392 | tf_op jit(solution)/shard_map/ppermute | solution.py:61
  142.4 30.8 %copy-start.24 = (f32[128]{0:T(128)S(1)}, f32[128]{0:T(128)}, u32[]{:S(2)}) copy-start(f32[128]{0:T(128)} %param.17) | copy-start | bytes 1540
  163.8 25.9 %collective-permute-start.14 = (bf16[1344,256]{1,0:T(8,128)(2,1)}, bf16[1344,256]{1,0:T(8,128)(2,1)}, u32[]{:S(2)}, u32[]{:S(2)}) collective-permute-start(bf16[1344,256]{1,0:T(8,128)(2,1)} %collective-permute-done.13.refs_1_), channel_id=1, source_target_pairs={{0,8},{8,16},{16,24},{24,0},{1,9},{9,17},{17,25},{25,1},{2,10},{10... | collective-permute-start | bytes 2064392 | tf_op jit(solution)/shard_map/ppermute | solution.py:61
  172.9 29.5 %collective-permute-start.17 = (bf16[1344,256]{1,0:T(8,128)(2,1)}, bf16[1344,256]{1,0:T(8,128)(2,1)}, u32[]{:S(2)}, u32[]{:S(2)}) collective-permute-start(bf16[1344,256]{1,0:T(8,128)(2,1)} %collective-permute-done.15.refs_1_), channel_id=1, source_target_pairs={{0,8},{8,16},{16,24},{24,0},{1,9},{9,17},{17,25},{25,1},{2,10},{10... | collective-permute-start | bytes 2064392 | tf_op jit(solution)/shard_map/ppermute | solution.py:61
  189.7 29.9 %collective-permute-start.16 = (bf16[1344,256]{1,0:T(8,128)(2,1)}, bf16[1344,256]{1,0:T(8,128)(2,1)}, u32[]{:S(2)}, u32[]{:S(2)}) collective-permute-start(bf16[1344,256]{1,0:T(8,128)(2,1)} %collective-permute-done.14.refs_2_), channel_id=1, source_target_pairs={{0,8},{8,16},{16,24},{24,0},{1,9},{9,17},{17,25},{25,1},{2,10},{10... | collective-permute-start | bytes 2064392 | tf_op jit(solution)/shard_map/ppermute | solution.py:61
  202.4 31.8 %collective-permute-start.18 = (bf16[1344,256]{1,0:T(8,128)(2,1)}, bf16[1344,256]{1,0:T(8,128)(2,1)S(1)}, u32[]{:S(2)}, u32[]{:S(2)}) collective-permute-start(bf16[1344,256]{1,0:T(8,128)(2,1)} %collective-permute-done.17.refs_2_), channel_id=1, source_target_pairs={{0,8},{8,16},{16,24},{24,0},{1,9},{9,17},{17,25},{25,1},{2,10},{10... | collective-permute-start | bytes 2064392 | tf_op jit(solution)/shard_map/ppermute | solution.py:61
  217.8 32.2 %collective-permute-start.19 = (bf16[1024,512]{1,0:T(8,128)(2,1)S(1)}, bf16[1024,512]{1,0:T(8,128)(2,1)S(1)}, u32[]{:S(2)}, u32[]{:S(2)}) collective-permute-start(bf16[1024,512]{1,0:T(8,128)(2,1)S(1)} %pad_maximum_fusion.4), channel_id=1, source_target_pairs={{0,8},{8,16},{16,24},{1,9},{9,17},{17,25},{2,10},{10,18},{18,26},{... | collective-permute-start | bytes 3145736 | tf_op jit(solution)/shard_map/ppermute | solution.py:335
  219.6 58.6 %collective-permute-start.20 = (bf16[336,2048]{1,0:T(8,128)(2,1)}, bf16[336,2048]{1,0:T(8,128)(2,1)}, u32[]{:S(2)}, u32[]{:S(2)}) collective-permute-start(bf16[336,2048]{1,0:T(8,128)(2,1)} %collective-permute-done.3.refs_5_), channel_id=1, source_target_pairs={{0,8},{8,16},{16,24},{24,0},{1,9},{9,17},{17,25},{25,1},{2,10},{10... | collective-permute-start | bytes 4128776 | tf_op jit(solution)/shard_map/ppermute | solution.py:61
  220.6 13.6 %copy-start.5 = (bf16[1344,256]{1,0:T(8,128)(2,1)S(1)}, bf16[1344,256]{1,0:T(8,128)(2,1)}, u32[]{:S(2)}) copy-start(bf16[1344,256]{1,0:T(8,128)(2,1)} %copy-done.4) | copy-start | bytes 2064388
  234.2 17.6 %copy-start.8 = (bf16[2048,256]{1,0:T(8,128)(2,1)}, bf16[2048,256]{1,0:T(8,128)(2,1)S(1)}, u32[]{:S(2)}) copy-start(bf16[2048,256]{1,0:T(8,128)(2,1)S(1)} %shard_map.103.refs_0_) | copy-start | bytes 3145732
  248.0 3.9 copy-start.10
  268.1 40.5 %collective-permute-start.22 = (bf16[1024,512]{1,0:T(8,128)(2,1)}, bf16[1024,512]{1,0:T(8,128)(2,1)}, u32[]{:S(2)}, u32[]{:S(2)}) collective-permute-start(bf16[1024,512]{1,0:T(8,128)(2,1)} %shard_map.105.refs_0_), channel_id=1, source_target_pairs={{0,4},{2,6},{4,0},{6,2},{1,5},{3,7},{5,1},{7,3},{8,12},{10,14},{12... | collective-permute-start | bytes 3145736 | tf_op jit(solution)/shard_map/ppermute | solution.py:52
  281.0 57.8 %copy-start.26 = (bf16[2048,336]{0,1:T(8,128)(2,1)S(1)}, bf16[2048,336]{0,1:T(8,128)(2,1)}, u32[]{:S(2)}) copy-start(bf16[2048,336]{0,1:T(8,128)(2,1)} %param.18) | copy-start | bytes 4128772
  297.3 24.0 %collective-permute-start.30 = (bf16[1024,512]{1,0:T(8,128)(2,1)}, bf16[1024,512]{1,0:T(8,128)(2,1)S(1)}, u32[]{:S(2)}, u32[]{:S(2)}) collective-permute-start(bf16[1024,512]{1,0:T(8,128)(2,1)} %shard_map.106.refs_0_), channel_id=1, source_target_pairs={{0,4},{2,6},{4,0},{6,2},{1,5},{3,7},{5,1},{7,3},{8,12},{10,14},{12... | collective-permute-start | bytes 3145736 | tf_op jit(solution)/shard_map/ppermute | solution.py:52
  297.9 40.9 %collective-permute-start.24 = (bf16[336,2048]{1,0:T(8,128)(2,1)}, bf16[336,2048]{1,0:T(8,128)(2,1)}, u32[]{:S(2)}, u32[]{:S(2)}) collective-permute-start(bf16[336,2048]{1,0:T(8,128)(2,1)} %collective-permute-done.20.refs_6_), channel_id=1, source_target_pairs={{0,8},{8,16},{16,24},{24,0},{1,9},{9,17},{17,25},{25,1},{2,10},{10... | collective-permute-start | bytes 4128776 | tf_op jit(solution)/shard_map/ppermute | solution.py:61
  308.6 12.7 %collective-permute-start.21 = (bf16[1024,512]{1,0:T(8,128)(2,1)}, bf16[1024,512]{1,0:T(8,128)(2,1)}, u32[]{:S(2)}, u32[]{:S(2)}) collective-permute-start(bf16[1024,512]{1,0:T(8,128)(2,1)} %shard_map.105.refs_0_), channel_id=1, source_target_pairs={{0,2},{2,0},{4,6},{6,4},{1,3},{3,1},{5,7},{7,5},{8,10},{10,8},{12,... | collective-permute-start | bytes 3145736 | tf_op jit(solution)/shard_map/ppermute | solution.py:52
  308.6 12.7 %collective-permute-start.23 = (bf16[1024,512]{1,0:T(8,128)(2,1)}, bf16[1024,512]{1,0:T(8,128)(2,1)}, u32[]{:S(2)}, u32[]{:S(2)}) collective-permute-start(bf16[1024,512]{1,0:T(8,128)(2,1)} %collective-permute-done.22.refs_2_), channel_id=1, source_target_pairs={{0,2},{2,0},{4,6},{6,4},{1,3},{3,1},{5,7},{7,5},{8,10},{10,8},{12,... | collective-permute-start | bytes 3145736 | tf_op jit(solution)/shard_map/ppermute | solution.py:52
  309.1 43.9 %collective-permute-start.29 = (bf16[1024,512]{1,0:T(8,128)(2,1)}, bf16[1024,512]{1,0:T(8,128)(2,1)}, u32[]{:S(2)}, u32[]{:S(2)}) collective-permute-start(bf16[1024,512]{1,0:T(8,128)(2,1)} %shard_map.106.refs_0_), channel_id=1, source_target_pairs={{0,2},{2,0},{4,6},{6,4},{1,3},{3,1},{5,7},{7,5},{8,10},{10,8},{12,... | collective-permute-start | bytes 3145736 | tf_op jit(solution)/shard_map/ppermute | solution.py:52
  321.3 31.8 %collective-permute-start.31 = (bf16[1024,512]{1,0:T(8,128)(2,1)S(1)}, bf16[1024,512]{1,0:T(8,128)(2,1)}, u32[]{:S(2)}, u32[]{:S(2)}) collective-permute-start(bf16[1024,512]{1,0:T(8,128)(2,1)S(1)} %collective-permute-done.30.refs_2_), channel_id=1, source_target_pairs={{0,2},{2,0},{4,6},{6,4},{1,3},{3,1},{5,7},{7,5},{8,10},{10,8},{12,... | collective-permute-start | bytes 3145736 | tf_op jit(solution)/shard_map/ppermute | solution.py:52
  351.5 33.4 %collective-permute-start.25 = (bf16[2,336,1024]{2,1,0:T(8,128)(2,1)}, bf16[2,336,1024]{2,1,0:T(8,128)(2,1)}, u32[]{:S(2)}, u32[]{:S(2)}) collective-permute-start(bf16[2,336,1024]{2,1,0:T(8,128)(2,1)} %constant_dynamic-slice_fusion.5), channel_id=1, source_target_pairs={{0,1},{1,0},{2,3},{3,2},{4,5},{5,4},{6,7},{7,6},{8,9},{9,8},{10,11... | collective-permute-start | bytes 4128776 | tf_op jit(solution)/shard_map/ppermute | solution.py:56
  363.3 21.7 %copy-start.29 = (bf16[4,336,1024]{2,1,0:T(8,128)(2,1)S(1)}, bf16[4,336,1024]{2,1,0:T(8,128)(2,1)}, u32[]{:S(2)}) copy-start(bf16[4,336,1024]{2,1,0:T(8,128)(2,1)} %shard_map.107) | copy-start | bytes 8257540
  366.1 44.9 %collective-permute-start.32 = (bf16[2,336,1024]{2,1,0:T(8,128)(2,1)}, bf16[2,336,1024]{2,1,0:T(8,128)(2,1)}, u32[]{:S(2)}, u32[]{:S(2)}) collective-permute-start(bf16[2,336,1024]{2,1,0:T(8,128)(2,1)} %constant_dynamic-slice_fusion.2), channel_id=1, source_target_pairs={{0,1},{1,0},{2,3},{3,2},{4,5},{5,4},{6,7},{7,6},{8,9},{9,8},{10,11... | collective-permute-start | bytes 4128776 | tf_op jit(solution)/shard_map/ppermute | solution.py:56
  386.9 24.1 %copy-start.30 = (bf16[4,336,1024]{2,1,0:T(8,128)(2,1)S(1)}, bf16[4,336,1024]{2,1,0:T(8,128)(2,1)}, u32[]{:S(2)}) copy-start(bf16[4,336,1024]{2,1,0:T(8,128)(2,1)} %shard_map.108) | copy-start | bytes 8257540
  387.1 27.5 %collective-permute-start.26 = (bf16[2,336,512]{2,1,0:T(8,128)(2,1)S(1)}, bf16[2,336,512]{2,1,0:T(8,128)(2,1)S(1)}, u32[]{:S(2)}, u32[]{:S(2)}) collective-permute-start(bf16[2,336,512]{2,1,0:T(8,128)(2,1)S(1)} %get-tuple-element.52), channel_id=1, source_target_pairs={{0,4},{2,6},{4,0},{6,2},{1,5},{3,7},{5,1},{7,3},{8,12},{10,14},{12... | collective-permute-start | bytes 2064392 | tf_op jit(solution)/shard_map/ppermute | solution.py:52
  413.0 14.1 %collective-permute-start.33 = (bf16[2,336,512]{2,1,0:T(8,128)(2,1)S(1)}, bf16[2,336,512]{2,1,0:T(8,128)(2,1)}, u32[]{:S(2)}, u32[]{:S(2)}) collective-permute-start(bf16[2,336,512]{2,1,0:T(8,128)(2,1)S(1)} %get-tuple-element.56), channel_id=1, source_target_pairs={{0,4},{2,6},{4,0},{6,2},{1,5},{3,7},{5,1},{7,3},{8,12},{10,14},{12... | collective-permute-start | bytes 2064392 | tf_op jit(solution)/shard_map/ppermute | solution.py:52
  415.8 21.0 %collective-permute-start.27 = (bf16[2,2,336,256]{3,2,1,0:T(8,128)(2,1)}, bf16[2,2,336,256]{3,2,1,0:T(8,128)(2,1)}, u32[]{:S(2)}, u32[]{:S(2)}) collective-permute-start(bf16[2,2,336,256]{3,2,1,0:T(8,128)(2,1)} %get-tuple-element.49), channel_id=1, source_target_pairs={{0,2},{2,0},{4,6},{6,4},{1,3},{3,1},{5,7},{7,5},{8,10},{10,8},{12,... | collective-permute-start | bytes 2064392 | tf_op jit(solution)/shard_map/ppermute | solution.py:52
  429.7 12.5 %collective-permute-start.34 = (bf16[2,2,336,256]{3,2,1,0:T(8,128)(2,1)}, bf16[2,2,336,256]{3,2,1,0:T(8,128)(2,1)S(1)}, u32[]{:S(2)}, u32[]{:S(2)}) collective-permute-start(bf16[2,2,336,256]{3,2,1,0:T(8,128)(2,1)} %get-tuple-element.53), channel_id=1, source_target_pairs={{0,2},{2,0},{4,6},{6,4},{1,3},{3,1},{5,7},{7,5},{8,10},{10,8},{12,... | collective-permute-start | bytes 2064392 | tf_op jit(solution)/shard_map/ppermute | solution.py:52
  438.6 3.6 collective-permute-start.28
  442.6 3.6 collective-permute-start.35
  (26 other events, 49.4 us)
Sparse Core Ops, SparseCore 0:
  9.2 125.4 all-gather.2

commit v5 on v4

--- a/solution.py
+++ b/solution.py
@@ -20,7 +20,11 @@
 INNER = 4
 QUERY_BLOCK = 256
 TOKEN_BLOCK = 512
-VMEM = 48 * 2**20
+MIB = 2**20
+
+
+def lasting(microseconds):
+    return pl.CostEstimate(flops=int(microseconds * 1e9), bytes_accessed=0, transcendentals=0)
 
 
 def rms_scale(values, gain):
@@ -69,86 +73,60 @@
     return jnp.where(first, jnp.stack([mine, other]), jnp.stack([other, mine]))
 
 
-def norm_kernel(x_ref, gain_ref, o_ref):
-    sides = [x_ref[0, side].astype(jnp.float32) for side in range(2)]
-    squares = sum(jnp.sum(x * x, axis=-1, keepdims=True) for x in sides)
-    scale = lax.rsqrt(squares / MODEL_WIDTH + EPS)
-    per_side = o_ref.shape[0] // 2
-    cols = o_ref.shape[2]
-    for side, x in enumerate(sides):
-        normed = (x * scale * gain_ref[side]).astype(jnp.bfloat16)
-        for part in range(per_side):
-            o_ref[side * per_side + part] = normed[:, part * cols : (part + 1) * cols]
-
-
-def norm_by_blocks(gathered, in_gain, blocks):
-    inner, sides, rows, cols = gathered.shape
-    width = sides * cols // blocks
-    step = 256
-    per_place = rows // step
-    return pl.pallas_call(
-        norm_kernel,
-        grid=(inner, per_place),
-        in_specs=[
-            pl.BlockSpec((1, sides, step, cols), lambda i, r: (i, 0, r, 0)),
-            pl.BlockSpec((sides, 1, cols), lambda i, r: (0, 0, 0)),
-        ],
-        out_specs=pl.BlockSpec((blocks, step, width), lambda i, r: (0, i * per_place + r, 0)),
-        out_shape=jax.ShapeDtypeStruct((blocks, inner * rows, width), jnp.bfloat16),
-        compiler_params=pltpu.CompilerParams(vmem_limit_bytes=VMEM),
-        cost_estimate=pl.CostEstimate(
-            flops=5 * gathered.size, bytes_accessed=4 * gathered.size, transcendentals=0
-        ),
-    )(gathered, in_gain.reshape(sides, 1, cols))
-
-
-def project_kernel(factor, source_ref, x_ref, *refs):
-    blocks = x_ref.shape[0]
-    weights, rest, o_ref = refs[:blocks], refs[blocks:-1], refs[-1]
+def project_kernel(factor, turned_cols, blocks, source_ref, x_ref, *refs):
+    o_ref, whole_ref = refs[-2:]
+    gain_ref, cos_ref, sin_ref = refs[-5:-2]
+    weights = refs[:-5]
+
+    @pl.when(pl.program_id(0) == 0)
+    def _():
+        for n, weight_ref in enumerate(weights):
+            height, width = weight_ref.shape
+            row = pl.multiple_of(source_ref[n % blocks] * height, 64)
+            col = n // blocks * width
+            whole_ref[pl.ds(row, height), col : col + width] = weight_ref[...]
+
+    depth = x_ref.shape[-1]
     total = None
-    for d in range(blocks):
-        term = jnp.dot(x_ref[source_ref[d]], weights[d][...], preferred_element_type=jnp.float32)
+    for side in range(x_ref.shape[1]):
+        term = jnp.dot(
+            x_ref[0, side],
+            whole_ref[side * depth : (side + 1) * depth, :],
+            preferred_element_type=jnp.float32,
+        )
         total = term if total is None else total + term
-    if not rest:
-        o_ref[...] = total.astype(jnp.bfloat16)
-        return
-    gain_ref, cos_ref, sin_ref = rest
-    for head in range(total.shape[1] // HEAD_SIZE):
+    for head in range(turned_cols // HEAD_SIZE):
         span = slice(head * HEAD_SIZE, (head + 1) * HEAD_SIZE)
-        values = total[:, span]
-        values = rms_scale(values, gain_ref[...])
+        values = rms_scale(total[:, span], gain_ref[...])
         turned = pltpu.roll(values, HEAD_SIZE // 2, 1)
         values = values * cos_ref[...] + turned * sin_ref[...]
         o_ref[:, span] = (values * factor).astype(jnp.bfloat16)
-
-
-def project(normed, source, weights, gain=None, turn=None, factor=1.0):
-    blocks, tokens, width = normed.shape
-    cols = weights[0].shape[1]
-    extra, extra_specs = [], []
-    if gain is not None:
-        extra = [gain.reshape(1, HEAD_SIZE), *turn]
-        extra_specs = [pl.BlockSpec((1, HEAD_SIZE), lambda b: (0, 0))] + [
-            pl.BlockSpec((TOKEN_BLOCK, HEAD_SIZE), lambda b: (b, 0))
-        ] * 2
+    if turned_cols < total.shape[1]:
+        o_ref[:, turned_cols:] = total[:, turned_cols:].astype(jnp.bfloat16)
+
+
+def project(normed, source, groups, turned_groups, gain, turn, factor=1.0):
+    inner, sides, rows, depth = normed.shape
+    height, width = groups[0][0].shape
+    cols = width * len(groups)
+    weights = [block for group in groups for block in group]
+    tokens = inner * rows
     return pl.pallas_call(
-        functools.partial(project_kernel, factor),
-        grid=(tokens // TOKEN_BLOCK,),
+        functools.partial(project_kernel, factor, turned_groups * width, len(groups[0])),
+        grid=(inner,),
         in_specs=[
             pl.BlockSpec(memory_space=pltpu.SMEM),
-            pl.BlockSpec((blocks, TOKEN_BLOCK, width), lambda b: (0, b, 0)),
+            pl.BlockSpec((1, sides, rows, depth), lambda b: (b, 0, 0, 0)),
         ]
-        + [pl.BlockSpec((width, cols), lambda b: (0, 0))] * blocks
-        + extra_specs,
-        out_specs=pl.BlockSpec((TOKEN_BLOCK, cols), lambda b: (b, 0)),
+        + [pl.BlockSpec((height, width), lambda b: (0, 0)) for _ in weights]
+        + [pl.BlockSpec((1, HEAD_SIZE), lambda b: (0, 0))]
+        + [pl.BlockSpec((rows, HEAD_SIZE), lambda b: (b, 0)) for _ in turn],
+        out_specs=pl.BlockSpec((rows, cols), lambda b: (b, 0)),
         out_shape=jax.ShapeDtypeStruct((tokens, cols), jnp.bfloat16),
-        compiler_params=pltpu.CompilerParams(vmem_limit_bytes=VMEM),
-        cost_estimate=pl.CostEstimate(
-            flops=2 * normed.size * cols,
-            bytes_accessed=2 * (normed.size + blocks * width * cols + tokens * cols),
-            transcendentals=0,
-        ),
-    )(source, normed, *weights, *extra)
+        scratch_shapes=[pltpu.VMEM((sides * depth, cols), jnp.bfloat16)],
+        compiler_params=pltpu.CompilerParams(vmem_limit_bytes=36 * MIB),
+        cost_estimate=lasting(width / 26),
+    )(source, normed, *weights, gain.reshape(1, HEAD_SIZE), *turn)
 
 
 def attend_kernel(part, pos_ref, *refs):
@@ -191,20 +169,17 @@
         + [pl.BlockSpec(all_kv.shape, lambda b: (0, 0))],
         out_specs=pl.BlockSpec((QUERY_BLOCK, width), lambda b: (b, 0)),
         out_shape=jax.ShapeDtypeStruct((half, width), jnp.bfloat16),
-        compiler_params=pltpu.CompilerParams(vmem_limit_bytes=VMEM),
-        cost_estimate=pl.CostEstimate(
-            flops=4 * half * window * width,
-            bytes_accessed=4 * half * width + 2 * all_kv.size,
-            transcendentals=half * window * width // HEAD_SIZE,
-        ),
+        compiler_params=pltpu.CompilerParams(vmem_limit_bytes=20 * MIB),
+        cost_estimate=lasting(14.5),
     )(position, *queries, all_kv)
 
 
-def group_kernel(inner, place_ref, source_ref, *refs):
-    lefts, weights, o_ref = refs[:inner], refs[inner:-1], refs[-1]
+def group_kernel(inner, place_ref, kept_ref, *refs):
+    pairs = kept_ref.shape[0]
+    lefts, weights, outs = refs[:inner], refs[inner : inner + 2 * pairs], refs[inner + 2 * pairs :]
     place = place_ref[0]
     depth = lefts[0].shape[1]
-    for d, weight_ref in enumerate(weights):
+    for n, weight_ref in enumerate(weights):
         total = None
         for m in range(inner):
             row = pl.multiple_of((place ^ m) * depth, depth)
@@ -215,28 +190,81 @@
                 preferred_element_type=jnp.float32,
             )
             total = term if total is None else total + term
-        o_ref[source_ref[d]] = total.astype(jnp.bfloat16)
-
-
-def group_product(place, source, attended, weights):
+        total = total.astype(jnp.bfloat16)
+        kept = kept_ref[n // 2]
+        for out, which in zip(outs[n // 2 * 2 : n // 2 * 2 + 2], (kept, 1 - kept)):
+
+            @pl.when(which == n % 2)
+            def _():
+                out[...] = total
+
+
+def group_product(place, kept, attended, weights):
     tokens, depth = attended[0].shape
     cols, rows = weights[0].shape
-    blocks = len(weights)
+    shape = jax.ShapeDtypeStruct((cols, tokens), jnp.bfloat16)
     return pl.pallas_call(
         functools.partial(group_kernel, len(attended)),
         grid=(tokens // TOKEN_BLOCK,),
         in_specs=[pl.BlockSpec(memory_space=pltpu.SMEM)] * 2
         + [pl.BlockSpec((TOKEN_BLOCK, depth), lambda b: (b, 0)) for _ in attended]
         + [pl.BlockSpec((cols, rows), lambda b: (0, 0)) for _ in weights],
-        out_specs=pl.BlockSpec((blocks, cols, TOKEN_BLOCK), lambda b: (0, 0, b)),
-        out_shape=jax.ShapeDtypeStruct((blocks, cols, tokens), jnp.bfloat16),
-        compiler_params=pltpu.CompilerParams(vmem_limit_bytes=VMEM),
-        cost_estimate=pl.CostEstimate(
-            flops=2 * tokens * rows * cols * blocks,
-            bytes_accessed=2 * (tokens * rows + (rows + tokens) * cols * blocks),
-            transcendentals=0,
-        ),
-    )(jnp.reshape(place, (1,)), source, *attended, *weights)
+        out_specs=[pl.BlockSpec((cols, TOKEN_BLOCK), lambda b: (0, b))] * len(weights),
+        out_shape=[shape] * len(weights),
+        compiler_params=pltpu.CompilerParams(vmem_limit_bytes=24 * MIB),
+        cost_estimate=lasting(2.9 * len(weights)),
+    )(jnp.reshape(place, (1,)), jnp.stack(kept).astype(jnp.int32), *attended, *weights)
+
+
+def squares_kernel(*refs):
+    total = None
+    for ref in refs[:-1]:
+        values = ref[...].astype(jnp.float32)
+        term = jnp.sum(values * values, axis=0, keepdims=True)
+        total = term if total is None else total + term
+    refs[-1][...] = total
+
+
+def squares_of(blocks):
+    return pl.pallas_call(
+        squares_kernel,
+        out_shape=jax.ShapeDtypeStruct((1, blocks[0].shape[1]), jnp.float32),
+        compiler_params=pltpu.CompilerParams(vmem_limit_bytes=8 * MIB),
+    )(*blocks)
+
+
+def finish_kernel(count, slots_ref, own_ref, other_ref, gain_ref, input_ref, *refs):
+    blocks, (o_ref, share_ref) = refs[:count], refs[-2:]
+    height = blocks[0].shape[0]
+    for n, block in enumerate(blocks):
+        row = pl.multiple_of(slots_ref[n] * height, 16)
+        share_ref[pl.ds(row, height), :] = block[...]
+    scale = lax.rsqrt((own_ref[...] + other_ref[...]) / MODEL_WIDTH + EPS)
+    for col in range(0, share_ref.shape[0], HEAD_SIZE):
+        span = slice(col, col + HEAD_SIZE)
+        branch = (share_ref[span, :].astype(jnp.float32) * scale).T * gain_ref[:, span]
+        o_ref[:, span] = (input_ref[:, span].astype(jnp.float32) + branch).astype(jnp.bfloat16)
+
+
+def finish(part, slots, own, other, gain, inputs, blocks, so_far):
+    rows, cols = inputs.shape
+    step = blocks[0].shape[1]
+    whole = lambda x: pl.BlockSpec(x.shape, lambda b: (0, 0))
+    extra = [] if so_far is None else [so_far]
+    operands = [slots, own, other, gain.reshape(1, cols), inputs, *blocks, *extra]
+    return pl.pallas_call(
+        functools.partial(finish_kernel, len(blocks)),
+        grid=(1,),
+        in_specs=[pl.BlockSpec(memory_space=pltpu.SMEM), whole(own), whole(other), whole(operands[3])]
+        + [pl.BlockSpec((step, cols), lambda b: (part, 0))]
+        + [whole(block) for block in blocks]
+        + [pl.BlockSpec(memory_space=pl.ANY) for _ in extra],
+        out_specs=pl.BlockSpec((step, cols), lambda b: (part, 0)),
+        out_shape=jax.ShapeDtypeStruct((rows, cols), jnp.bfloat16),
+        scratch_shapes=[pltpu.VMEM((cols, step), jnp.bfloat16)],
+        input_output_aliases={len(operands) - 1: 0} if extra else {},
+        compiler_params=pltpu.CompilerParams(vmem_limit_bytes=16 * MIB),
+    )(*operands)
 
 
 def shuffle_start(weights, place):
@@ -283,9 +311,6 @@
     plane_tokens = INNER * tok_rows
     source = ((plane - jnp.arange(planes)) % planes).astype(jnp.int32)
 
-    gathered = lax.all_gather(inputs, ("i", "tp"), axis=0, tiled=False)
-    gathered = gathered.reshape(INNER, 2, *inputs.shape)
-
     kv_on_way = shuffle_start([key_matrix, value_matrix], place)
     out_rows = out_weight.T
     hops = {"o": [out_rows]}
@@ -297,8 +322,16 @@
         previous.append(hops[name][-1])
 
     hop("o")
+    values = inputs.astype(jnp.float32)
+    squares = jnp.sum(values * values, axis=-1)
+    scale = lax.rsqrt((squares + swap_tp(squares)) / MODEL_WIDTH + EPS)
+    gain = lax.dynamic_slice_in_dim(in_gain, side * inputs.shape[1], inputs.shape[1])
+    normed = (values * scale[:, None] * gain).astype(jnp.bfloat16)
+    normed = lax.all_gather(normed, ("i", "tp"), axis=0, tiled=False)
+    normed = normed.reshape(INNER, 2, *inputs.shape)
+
     pos_x = in_order(place // 2 == 0, positions, swap(positions, 2))
-    q_on_way = shuffle_start([after(q_weight, kv_on_way[0])], place)
+    q_on_way = shuffle_start([after(q_weight, kv_on_way[1])], place)
     kv = shuffle_end(kv_on_way[0], after(kv_on_way[1], hops["o"][1]), place)
     kv_half = kv.shape[1] // 2
     hops["k"], hops["v"] = [kv[:, :kv_half]], [kv[:, kv_half:]]
@@ -322,53 +355,73 @@
         jnp.concatenate([-sine, sine], axis=1),
     )
 
-    normed = norm_by_blocks(after(gathered, hops["v"][-1], *turn), in_gain, planes)
-    hop("qa", normed)
-    hop("qb", normed)
-    keys = project(after(normed, hops["qb"][-2]), source, hops["k"], key_norm_gain, turn)
-    for _ in range(planes - 3):
-        hop("qa", keys)
-        hop("qb", keys)
-    values = project(after(normed, hops["qa"][-2], keys), source, hops["v"])
+    own_kv = project(
+        after(normed, *turn),
+        source,
+        [hops["k"], hops["v"]],
+        1,
+        key_norm_gain,
+        turn,
+    )
+    for n in range(planes - 2):
+        hop("qa", own_kv)
+        hop("qb", own_kv)
     up = [(c, c + 1) for c in range(planes - 1)]
-    own_kv = jnp.concatenate([keys, values], axis=1)
     halo = lax.ppermute(own_kv[plane_tokens - VISIBLE_SPAN :], "z", up)
     all_kv = jnp.concatenate([halo, own_kv], axis=0)
-    for _ in range(planes - 2):
+    for _ in range(planes - 3):
         hop("o", previous[-2])
 
     factor = (MODEL_WIDTH // QUERY_HEADS) ** (-0.5)
     queries = [
-        project(after(normed, values), source, hops[name], q_gain, turn, factor)
+        project(after(normed, own_kv), source, [hops[name]], 1, q_gain, turn, factor)
         for name in ("qa", "qb")
     ]
 
     own = [attend(0, pos[:, None], queries, all_kv)]
-    own.append(attend(1, after(pos, own[0], hops["o"][-2])[:, None], queries, all_kv))
-    here = place // 2, place % 2
+    own.append(attend(1, after(pos[:, None], own[0]), queries, all_kv))
+    hop("o", own[0])
     per_side = planes // 2
-    results = []
+    kept, slots = [], []
+    for d in range(per_side):
+        near, opposite = source[d], source[d + per_side]
+        kept.append(jnp.where(near // per_side == side, 0, 1))
+        which = jnp.where(kept[d] == 0, near, opposite) % per_side
+        slots += [which * INNER + (place ^ mask) for mask in range(INNER)]
+    slots = jnp.stack(slots).astype(jnp.int32)
+    keeps, arrived = [], []
+    pairs = [block for d in range(per_side) for block in (hops["o"][d], hops["o"][d + per_side])]
     for part in range(2):
         far = swap(own[part], 2)
-        attended = [own[part], swap(own[part], 1), far, swap(far, 1)]
+        first = after(own[0], own[1]) if part == 0 else after(own[1], keeps[-1])
+        across = after(far, own[1]) if part == 0 else after(far, keeps[-1], arrived[0])
+        attended = [first, swap(own[part], 1), far, swap(across, 1)]
+        terms = group_product(place, kept, attended, pairs)
+        keeps += terms[::2]
+        arrived += [swap_tp(give) for give in terms[1::2]]
+
+    output = None
+    for part in range(2):
+        sums = []
+        for n in range(part * per_side, (part + 1) * per_side):
+            theirs = after(arrived[n], keeps[-1]) if part == 0 else arrived[n]
+            total = keeps[n].astype(jnp.float32) + theirs.astype(jnp.float32)
+            sums.append(total.astype(jnp.bfloat16))
+        shipped = [jnp.concatenate(sums, axis=0)] if part == 0 else sums
+        blocks = []
+        for total in shipped:
+            for mask in range(INNER):
+                at = (place ^ mask) * QUERY_BLOCK
+                block = lax.dynamic_slice_in_dim(total, at, QUERY_BLOCK, axis=1)
+                blocks.append(swap(block, mask) if mask else block)
         if part == 0:
-            attended[0] = after(own[0], own[1])
-        terms = group_product(place, source, attended, hops["o"])
-        keep = lax.dynamic_slice_in_dim(terms, side * per_side, per_side, axis=0)
-        give = lax.dynamic_slice_in_dim(terms, (1 - side) * per_side, per_side, axis=0)
-        sums = (keep.astype(jnp.float32) + swap_tp(give).astype(jnp.float32)).astype(jnp.bfloat16)
-        for bit, mask in ((0, 2), (1, 1)):
-            width = sums.shape[-1] // 2
-            keep = lax.dynamic_slice_in_dim(sums, here[bit] * width, width, axis=-1)
-            give = lax.dynamic_slice_in_dim(sums, (1 - here[bit]) * width, width, axis=-1)
-            sums = in_order(here[bit] == 0, keep, swap(give, mask))
-        share = sums.transpose(2, 1, 0, 3, 4).reshape(-1, sums.shape[-1]).astype(jnp.float32)
-        own_squares = jnp.sum(share * share, axis=0)
-        squares = own_squares + swap_tp(own_squares)
-        branch = share * lax.rsqrt(squares / MODEL_WIDTH + EPS)[None, :] * post_gain[:, None]
-        rows = inputs[part * QUERY_BLOCK : (part + 1) * QUERY_BLOCK].astype(jnp.float32)
-        results.append((rows + branch.T).astype(jnp.bfloat16))
-    return jnp.concatenate(results, axis=0)
+            height = sums[0].shape[0]
+            blocks = [block[n * height : (n + 1) * height] for n in range(per_side) for block in blocks]
+        squares = squares_of(blocks)
+        output = finish(
+            part, slots, squares, swap_tp(squares), post_gain, inputs, blocks, output
+        )
+    return output
 
 
 def from_behind(x, axis, by):

time: 462 us -> 451 us (0.976)
  Pallas kernels: 126 us -> 101 us
  waiting for transfers between devices: 233 us -> 224 us
  starting transfers between devices: 29.5 us -> 38.4 us
  between operations: 14.3 us -> 22 us
  local copies, waits for them, and re-layouts: 34.4 us -> 41.5 us
    pallas_call x5 -> x7, Pallas kernels: 72.7 us -> 50.4 us  [the longest x3 45.2 us: project(): pl.pallas_call(functools.partial(project_kernel, factor, turned_groups *...]
    ppermute x15, waiting for transfers between devices: 131 us -> 144 us  [ring_step(): return lax.ppermute(x, 'z', [(c, (c + 1) % size) for c in range(size)])]
    unnamed x77 -> x141, local copies, waits for them, and re-layouts: 17.9 us -> 29 us
    ppermute x4 -> x7, waiting for transfers between devices: 42.7 us -> 31.7 us  [swap_tp(): return lax.ppermute(x, 'tp', [(0, 1), (1, 0)])]
    ppermute x16 -> x21, waiting for transfers between devices: 57 us -> 48.2 us  [swap(): return lax.ppermute(x, 'i', [(c, c ^ mask) for c in range(INNER)])]
    dynamic_slice x4 -> x3, local copies, waits for them, and re-layouts: 7.26 us -> 0.99 us  [the longest x1 0.79 us: by_planes(): lax.dynamic_slice_in_dim(in_gain, side * inputs.shape[1], inputs.shape[1])]
    ppermute x4 -> x7, starting transfers between devices: 5.12 us -> 9.78 us  [swap_tp(): return lax.ppermute(x, 'tp', [(0, 1), (1, 0)])]
    ppermute x16 -> x21, starting transfers between devices: 6.58 us -> 9.32 us  [swap(): return lax.ppermute(x, 'i', [(c, c ^ mask) for c in range(INNER)])]
  transfers between devices with their start and end apart: 37 -> 45, of which waited for: 22 -> 24; matrix products, arithmetic and copies ran while one was open for 8% -> 6% of each run, Pallas kernels for 27% -> 22%
where the time goes in v5:
time: 451 us; the launch traced here: 447 us
  waiting for transfers between devices  224 us (50%)
  Pallas kernels  101 us (22%)
  local copies, waits for them, and re-layouts  41.5 us (9%)
  starting transfers between devices  38.4 us (9%)
  between operations  22 us (5%)
  other arithmetic  20.1 us (4%)
    ppermute x15, waiting for transfers between devices, ring_step(): return lax.ppermute(x, 'z', [(c, (c + 1) % size) for c in range(size)])  144 us
    ppermute x21, waiting for transfers between devices, swap(): return lax.ppermute(x, 'i', [(c, c ^ mask) for c in range(INNER)])  48.2 us
    pallas_call x3, Pallas kernels, project(): pl.pallas_call(functools.partial(project_kernel, factor, turned_groups *...  45.2 us
    ppermute x7, waiting for transfers between devices, swap_tp(): return lax.ppermute(x, 'tp', [(0, 1), (1, 0)])  31.7 us
    unnamed x141, local copies, waits for them, and re-layouts  29 us
    pallas_call x2, Pallas kernels, attend(): pl.pallas_call(functools.partial(attend_kernel, part), grid=(half // QUER...  28.8 us
    pallas_call x2, Pallas kernels, group_product(): pl.pallas_call(functools.partial(group_kernel, len(attended)), grid=(toke...  21.8 us
    ppermute x15, starting transfers between devices, ring_step(): return lax.ppermute(x, 'z', [(c, (c + 1) % size) for c in range(size)])  16 us
  transfers between devices with their start and end apart: 45, of which 24 were waited for; matrix products, arithmetic and copies ran while one was open for 6% of the time, Pallas kernels for 22%

profile of v5, /device:TPU:2, one launch (start us, length us, event | category | flops | bytes accessed | tf_op | source)
XLA Modules:
  0.0 447.1 jit_solution(4033490994918951675)
XLA Ops:
  6.5 2.5 fusion
  9.1 1.6 collective-permute-start.2
  12.7 2.2 fusion.2
  15.0 1.6 collective-permute-start.4
  16.6 2.1 constant_dynamic-slice_fusion.14
  22.4 23.8 %collective-permute-done.3 = bf16[2,336,512]{2,1,0:T(8,128)(2,1)S(1)} collective-permute-done((bf16[2,336,512]{2,1,0:T(8,128)(2,1)}, bf16[2,336,512]{2,1,0:T(8,128)(2,1)S(1)}, u32[]{:S(2)}, u32[]{:S(2)}) %collective-permute-start.3) | collective-permute-done | bytes 688160 | tf_op jit(solution)/shard_map/ppermute | solution.py:56
  46.1 1.9 collective-permute-done.4.refs_6_
  52.8 1.6 maximum_select_fusion.1
  57.2 17.4 %collective-permute-done.6.refs_1_ = bf16[1344,256]{1,0:T(8,128)(2,1)S(1)} collective-permute-done((bf16[1344,256]{1,0:T(8,128)(2,1)S(1)}, bf16[1344,256]{1,0:T(8,128)(2,1)S(1)}, u32[]{:S(2)}, u32[]{:S(2)}) %collective-permute-start.6) | collective-permute-done | bytes 688160 | tf_op jit(solution)/shard_map/ppermute | solution.py:65
  74.7 14.7 %collective-permute-done.9.refs_5_ = bf16[1344,256]{1,0:T(8,128)(2,1)S(1)} collective-permute-done((bf16[1344,256]{1,0:T(8,128)(2,1)S(1)}, bf16[1344,256]{1,0:T(8,128)(2,1)S(1)}, u32[]{:S(2)}, u32[]{:S(2)}) %collective-permute-start.9) | collective-permute-done | bytes 688160 | tf_op jit(solution)/shard_map/ppermute | solution.py:65
  90.4 3.7 fusion.7
  94.2 10.0 %collective-permute-done.7.refs_2_ = bf16[1344,256]{1,0:T(8,128)(2,1)S(1)} collective-permute-done((bf16[1344,256]{1,0:T(8,128)(2,1)S(1)}, bf16[1344,256]{1,0:T(8,128)(2,1)S(1)}, u32[]{:S(2)}, u32[]{:S(2)}) %collective-permute-start.7) | collective-permute-done | bytes 688160 | tf_op jit(solution)/shard_map/ppermute | solution.py:65
  104.2 14.7 %collective-permute-done.10.refs_6_ = bf16[1344,256]{1,0:T(8,128)(2,1)S(1)} collective-permute-done((bf16[1344,256]{1,0:T(8,128)(2,1)S(1)}, bf16[1344,256]{1,0:T(8,128)(2,1)S(1)}, u32[]{:S(2)}, u32[]{:S(2)}) %collective-permute-start.10) | collective-permute-done | bytes 688160 | tf_op jit(solution)/shard_map/ppermute | solution.py:65
  118.9 1.9 pad_maximum_fusion.1
  122.2 11.4 %collective-permute-done.8.refs_3_ = bf16[1344,256]{1,0:T(8,128)(2,1)S(1)} collective-permute-done((bf16[1344,256]{1,0:T(8,128)(2,1)S(1)}, bf16[1344,256]{1,0:T(8,128)(2,1)S(1)}, u32[]{:S(2)}, u32[]{:S(2)}) %collective-permute-start.8) | collective-permute-done | bytes 688160 | tf_op jit(solution)/shard_map/ppermute | solution.py:65
  134.6 13.8 %collective-permute-done.11.refs_7_ = bf16[1344,256]{1,0:T(8,128)(2,1)S(1)} collective-permute-done((bf16[1344,256]{1,0:T(8,128)(2,1)S(1)}, bf16[1344,256]{1,0:T(8,128)(2,1)S(1)}, u32[]{:S(2)}, u32[]{:S(2)}) %collective-permute-start.11) | collective-permute-done | bytes 688160 | tf_op jit(solution)/shard_map/ppermute | solution.py:65
  159.4 18.7 %shard_map.100 = bf16[2048,512]{1,0:T(8,128)(2,1)S(1)} custom-call(s32[4]{0:T(128)S(1)} %and_select_fusion.source_ref, bf16[4,2,512,2688]{3,2,1,0:T(8,128)(2,1)} %bitcast.83, bf16[1344,256]{1,0:T(8,128)(2,1)S(1)} %copy-done.27, bf16[1344,256]{1,0:T(8,128)(2,1)S(1)} %copy-done.47, bf16[1344,256]{1,0:T(8,128)(2,1)S(1)} %copy-done.51, ...), custom_call_target="tpu_custom_call" | custom-call | flops 9846154240 | tf_op jit(solution)/shard_map/pallas_call | solution.py:114
  180.5 3.3 collective-permute-start.20
  184.4 3.0 collective-permute-start.18
  187.4 34.0 %collective-permute-done.15.refs_2_ = bf16[1344,256]{1,0:T(8,128)(2,1)} collective-permute-done((bf16[1344,256]{1,0:T(8,128)(2,1)}, bf16[1344,256]{1,0:T(8,128)(2,1)}, u32[]{:S(2)}, u32[]{:S(2)}) %collective-permute-start.15) | collective-permute-done | bytes 688160 | tf_op jit(solution)/shard_map/ppermute | solution.py:65
  221.4 2.5 collective-permute-start.16
  225.3 10.9 %collective-permute-done.18.refs_2_ = bf16[1344,256]{1,0:T(8,128)(2,1)S(1)} collective-permute-done((bf16[1344,256]{1,0:T(8,128)(2,1)}, bf16[1344,256]{1,0:T(8,128)(2,1)S(1)}, u32[]{:S(2)}, u32[]{:S(2)}) %collective-permute-start.18) | collective-permute-done | bytes 688160 | tf_op jit(solution)/shard_map/ppermute | solution.py:65
  236.1 2.4 collective-permute-start.19
  238.5 2.1 pad_maximum_fusion.refs_2_
  240.6 10.3 %collective-permute-done.16.refs_3_ = bf16[1344,256]{1,0:T(8,128)(2,1)} collective-permute-done((bf16[1344,256]{1,0:T(8,128)(2,1)}, bf16[1344,256]{1,0:T(8,128)(2,1)}, u32[]{:S(2)}, u32[]{:S(2)}) %collective-permute-start.16) | collective-permute-done | bytes 688160 | tf_op jit(solution)/shard_map/ppermute | solution.py:65
  250.9 2.5 collective-permute-start.24
  253.4 13.2 %shard_map.101.refs_0_ = bf16[2048,256]{1,0:T(8,128)(2,1)S(1)} custom-call(s32[4]{0:T(128)S(1)} %and_select_fusion.source_ref, bf16[4,2,512,2688]{3,2,1,0:T(8,128)(2,1)} %bitcast.84, bf16[1344,256]{1,0:T(8,128)(2,1)} %get-tuple-element.46.refs_0_, bf16[1344,256]{1,0:T(8,128)(2,1)} %collective-permute-done.14.refs_1_, ...), custom_call_target="tpu_custom_call" | custom-call | flops 9846154240 | tf_op jit(solution)/shard_map/pallas_call | solution.py:114
  266.7 13.2 %shard_map.102.refs_1_ = bf16[2048,256]{1,0:T(8,128)(2,1)S(1)} custom-call(s32[4]{0:T(128)S(1)} %and_select_fusion.source_ref, bf16[4,2,512,2688]{3,2,1,0:T(8,128)(2,1)} %bitcast.85, bf16[1344,256]{1,0:T(8,128)(2,1)} %get-tuple-element.49.refs_0_, bf16[1344,256]{1,0:T(8,128)(2,1)} %collective-permute-done.17.refs_1_, ...), custom_call_target="tpu_custom_call" | custom-call | flops 9846154240 | tf_op jit(solution)/shard_map/pallas_call | solution.py:114
  279.9 14.5 %shard_map.103.refs_0_ = bf16[1024,512]{1,0:T(8,128)(2,1)} custom-call(s32[2048,1]{1,0:T(8,128)S(1)} %copy-done.20, bf16[2048,256]{1,0:T(8,128)(2,1)S(1)} %shard_map.101.refs_0_, bf16[2048,256]{1,0:T(8,128)(2,1)S(1)} %shard_map.102.refs_1_, bf16[3072,512]{1,0:T(8,128)(2,1)S(1)} %pad_maximum_fusion.refs_2_), custom_call_target="tpu_custom_call" | custom-call | flops 14499999744 | tf_op jit(solution)/shard_map/pallas_call | solution.py:164
  296.4 2.1 collective-permute-start.25
  298.5 1.9 copy-done.3
  304.1 14.3 %shard_map.104.refs_0_ = bf16[1024,512]{1,0:T(8,128)(2,1)} custom-call(s32[2048,1]{1,0:T(8,128)S(1)} %copy-done.21, bf16[2048,256]{1,0:T(8,128)(2,1)S(1)} %copy-done.62, bf16[2048,256]{1,0:T(8,128)(2,1)S(1)} %copy-done.64, bf16[3072,512]{1,0:T(8,128)(2,1)S(1)} %copy-done.3), custom_call_target="tpu_custom_call" | custom-call | flops 14499999744 | tf_op jit(solution)/shard_map/pallas_call | solution.py:164
  318.4 2.0 collective-permute-done.22.refs_2_
  326.8 4.9 %collective-permute-done.25.refs_7_ = bf16[336,2048]{1,0:T(8,128)(2,1)} collective-permute-done((bf16[336,2048]{1,0:T(8,128)(2,1)}, bf16[336,2048]{1,0:T(8,128)(2,1)}, u32[]{:S(2)}, u32[]{:S(2)}) %collective-permute-start.25) | collective-permute-done | bytes 1376288 | tf_op jit(solution)/shard_map/ppermute | solution.py:65
  333.0 10.8 %shard_map.105 = (bf16[336,1024]{1,0:T(8,128)(2,1)S(1)}, bf16[336,1024]{1,0:T(8,128)(2,1)S(1)}, bf16[336,1024]{1,0:T(8,128)(2,1)S(1)}, bf16[336,1024]{1,0:T(8,128)(2,1)S(1)}) custom-call(s32[1]{0:T(128)} %bitcast.12.place_ref, s32[2]{0:T(128)S(1)} %pad_add_fusion.kept_ref, bf16[1024,512]{1,0:T(8,128)(2,1)} %shard_map.103.refs_0_, ...), custom_call_target="tpu_custom_call" | custom-call | flops 11600000000 | tf_op jit(solution)/shard_map/pallas_call | solution.py:206
  347.1 5.0 %collective-permute-done.27.refs_2_ = bf16[1024,512]{1,0:T(8,128)(2,1)} collective-permute-done((bf16[1024,512]{1,0:T(8,128)(2,1)}, bf16[1024,512]{1,0:T(8,128)(2,1)}, u32[]{:S(2)}, u32[]{:S(2)}) %collective-permute-start.27) | collective-permute-done | bytes 1048608 | tf_op jit(solution)/shard_map/ppermute | solution.py:56
  352.1 10.5 %collective-permute-done.28 = bf16[336,1024]{1,0:T(8,128)(2,1)S(1)} collective-permute-done((bf16[336,1024]{1,0:T(8,128)(2,1)S(1)}, bf16[336,1024]{1,0:T(8,128)(2,1)S(1)}, u32[]{:S(2)}, u32[]{:S(2)}) %collective-permute-start.28) | collective-permute-done | bytes 688160 | tf_op jit(solution)/shard_map/ppermute | solution.py:60
  367.9 11.0 %shard_map.106 = (bf16[336,1024]{1,0:T(8,128)(2,1)S(1)}, bf16[336,1024]{1,0:T(8,128)(2,1)S(1)}, bf16[336,1024]{1,0:T(8,128)(2,1)S(1)}, bf16[336,1024]{1,0:T(8,128)(2,1)S(1)}) custom-call(s32[1]{0:T(128)} %bitcast.12.place_ref, s32[2]{0:T(128)S(1)} %pad_add_fusion.kept_ref, bf16[1024,512]{1,0:T(8,128)(2,1)} %shard_map.104.refs_0_, ...), custom_call_target="tpu_custom_call" | custom-call | flops 11600000000 | tf_op jit(solution)/shard_map/pallas_call | solution.py:206
  378.9 2.6 collective-permute-done.39
  385.8 1.6 collective-permute-start.30
  390.5 8.5 %collective-permute-done.41 = bf16[672,256]{1,0:T(8,128)(2,1)S(1)} collective-permute-done((bf16[672,256]{1,0:T(8,128)(2,1)}, bf16[672,256]{1,0:T(8,128)(2,1)S(1)}, u32[]{:S(2)}, u32[]{:S(2)}) %collective-permute-start.41) | collective-permute-done | bytes 344096 | tf_op jit(solution)/shard_map/ppermute | solution.py:56
  399.1 5.2 %collective-permute-done.30 = bf16[336,1024]{1,0:T(8,128)(2,1)S(1)} collective-permute-done((bf16[336,1024]{1,0:T(8,128)(2,1)}, bf16[336,1024]{1,0:T(8,128)(2,1)S(1)}, u32[]{:S(2)}, u32[]{:S(2)}) %collective-permute-start.30) | collective-permute-done | bytes 688160 | tf_op jit(solution)/shard_map/ppermute | solution.py:60
  406.7 12.0 %collective-permute-done.34 = bf16[336,1024]{1,0:T(8,128)(2,1)S(1)} collective-permute-done((bf16[336,1024]{1,0:T(8,128)(2,1)}, bf16[336,1024]{1,0:T(8,128)(2,1)S(1)}, u32[]{:S(2)}, u32[]{:S(2)}) %collective-permute-start.34) | collective-permute-done | bytes 688160 | tf_op jit(solution)/shard_map/ppermute | solution.py:60
  421.3 1.6 collective-permute-start.43
  422.9 3.5 collective-permute-done.36.refs_6_
  426.4 2.8 collective-permute-done.37.refs_7_
  435.2 2.5 shard_map.109.refs_8_
  437.8 2.5 shard_map.110
  (245 shorter events, 64.1 us)
Async XLA Ops:
  6.5 142.7 %all-gather.3.cloned.1.call-start = ((), (), s32[]{:S(2)}) async-start(), calls=%async_computation | async-start | bytes 24772608 | tf_op jit(solution)/shard_map/all_gather | solution.py:330
  9.1 3.6 collective-permute-start.2
  15.0 33.0 %collective-permute-start.4 = (bf16[336,2048]{1,0:T(8,128)(2,1)}, bf16[336,2048]{1,0:T(8,128)(2,1)}, u32[]{:S(2)}, u32[]{:S(2)}) collective-permute-start(bf16[336,2048]{1,0:T(8,128)(2,1)} %bitcast.67), channel_id=1, source_target_pairs={{0,8},{8,16},{16,24},{24,0},{1,9},{9,17},{17,25},{25,1},{2,10},{10... | collective-permute-start | bytes 4128776 | tf_op jit(solution)/shard_map/ppermute | solution.py:65
  19.7 26.4 %collective-permute-start.3 = (bf16[2,336,512]{2,1,0:T(8,128)(2,1)}, bf16[2,336,512]{2,1,0:T(8,128)(2,1)S(1)}, u32[]{:S(2)}, u32[]{:S(2)}) collective-permute-start(bf16[2,336,512]{2,1,0:T(8,128)(2,1)} %pad_maximum_fusion.3), channel_id=1, source_target_pairs={{0,4},{2,6},{4,0},{6,2},{1,5},{3,7},{5,1},{7,3},{8,12},{10,14},{12... | collective-permute-start | bytes 2064392 | tf_op jit(solution)/shard_map/ppermute | solution.py:56
  49.2 3.6 collective-permute-start.5
  49.2 6.7 %collective-permute-start = (s32[512]{0:T(512)S(1)}, s32[512]{0:T(512)S(1)}, u32[]{:S(2)}, u32[]{:S(2)}) collective-permute-start(s32[512]{0:T(512)S(1)} %copy-done.69), channel_id=1, source_target_pairs={{0,4},{2,6},{4,0},{6,2},{1,5},{3,7},{5,1},{7,3},{8,12},{10,14},{12... | collective-permute-start | bytes 6152 | tf_op jit(solution)/shard_map/ppermute | solution.py:56
  51.2 38.2 %collective-permute-start.12 = (bf16[2,336,512]{2,1,0:T(8,128)(2,1)S(1)}, bf16[2,336,512]{2,1,0:T(8,128)(2,1)S(1)}, u32[]{:S(2)}, u32[]{:S(2)}) collective-permute-start(bf16[2,336,512]{2,1,0:T(8,128)(2,1)S(1)} %pad_maximum_fusion.4), channel_id=1, source_target_pairs={{0,4},{2,6},{4,0},{6,2},{1,5},{3,7},{5,1},{7,3},{8,12},{10,14},{12... | collective-permute-start | bytes 2064392 | tf_op jit(solution)/shard_map/ppermute | solution.py:56
  54.5 34.9 %copy-start.26 = (bf16[1344,256]{1,0:T(8,128)(2,1)}, bf16[1344,256]{1,0:T(8,128)(2,1)S(1)}, u32[]{:S(2)}) copy-start(bf16[1344,256]{1,0:T(8,128)(2,1)S(1)} %get-tuple-element.84.refs_0_) | copy-start | bytes 2064388
  54.5 20.2 %collective-permute-start.6 = (bf16[1344,256]{1,0:T(8,128)(2,1)S(1)}, bf16[1344,256]{1,0:T(8,128)(2,1)S(1)}, u32[]{:S(2)}, u32[]{:S(2)}) collective-permute-start(bf16[1344,256]{1,0:T(8,128)(2,1)S(1)} %get-tuple-element.84.refs_0_), channel_id=1, source_target_pairs={{0,8},{8,16},{16,24},{24,0},{1,9},{9,17},{17,25},{25,1},{2,10},{10... | collective-permute-start | bytes 2064392 | tf_op jit(solution)/shard_map/ppermute | solution.py:65
  54.6 34.8 %collective-permute-start.9 = (bf16[1344,256]{1,0:T(8,128)(2,1)S(1)}, bf16[1344,256]{1,0:T(8,128)(2,1)S(1)}, u32[]{:S(2)}, u32[]{:S(2)}) collective-permute-start(bf16[1344,256]{1,0:T(8,128)(2,1)S(1)} %get-tuple-element.83.refs_4_), channel_id=1, source_target_pairs={{0,8},{8,16},{16,24},{24,0},{1,9},{9,17},{17,25},{25,1},{2,10},{10... | collective-permute-start | bytes 2064392 | tf_op jit(solution)/shard_map/ppermute | solution.py:65
  55.9 1.2 collective-permute-start.1
  74.7 29.5 %collective-permute-start.7 = (bf16[1344,256]{1,0:T(8,128)(2,1)S(1)}, bf16[1344,256]{1,0:T(8,128)(2,1)S(1)}, u32[]{:S(2)}, u32[]{:S(2)}) collective-permute-start(bf16[1344,256]{1,0:T(8,128)(2,1)S(1)} %collective-permute-done.6.refs_1_), channel_id=1, source_target_pairs={{0,8},{8,16},{16,24},{24,0},{1,9},{9,17},{17,25},{25,1},{2,10},{10... | collective-permute-start | bytes 2064392 | tf_op jit(solution)/shard_map/ppermute | solution.py:65
  89.4 29.5 %collective-permute-start.10 = (bf16[1344,256]{1,0:T(8,128)(2,1)S(1)}, bf16[1344,256]{1,0:T(8,128)(2,1)S(1)}, u32[]{:S(2)}, u32[]{:S(2)}) collective-permute-start(bf16[1344,256]{1,0:T(8,128)(2,1)S(1)} %collective-permute-done.9.refs_5_), channel_id=1, source_target_pairs={{0,8},{8,16},{16,24},{24,0},{1,9},{9,17},{17,25},{25,1},{2,10},{10... | collective-permute-start | bytes 2064392 | tf_op jit(solution)/shard_map/ppermute | solution.py:65
  90.4 30.5 %collective-permute-start.13 = (bf16[2,336,512]{2,1,0:T(8,128)(2,1)S(1)}, bf16[2,336,512]{2,1,0:T(8,128)(2,1)S(1)}, u32[]{:S(2)}, u32[]{:S(2)}) collective-permute-start(bf16[2,336,512]{2,1,0:T(8,128)(2,1)S(1)} %get-tuple-element.78), channel_id=1, source_target_pairs={{0,2},{2,0},{4,6},{6,4},{1,3},{3,1},{5,7},{7,5},{8,10},{10,8},{12,... | collective-permute-start | bytes 2064392 | tf_op jit(solution)/shard_map/ppermute | solution.py:56
  104.2 29.5 %collective-permute-start.8 = (bf16[1344,256]{1,0:T(8,128)(2,1)S(1)}, bf16[1344,256]{1,0:T(8,128)(2,1)S(1)}, u32[]{:S(2)}, u32[]{:S(2)}) collective-permute-start(bf16[1344,256]{1,0:T(8,128)(2,1)S(1)} %collective-permute-done.7.refs_2_), channel_id=1, source_target_pairs={{0,8},{8,16},{16,24},{24,0},{1,9},{9,17},{17,25},{25,1},{2,10},{10... | collective-permute-start | bytes 2064392 | tf_op jit(solution)/shard_map/ppermute | solution.py:65
  118.9 29.5 %collective-permute-start.11 = (bf16[1344,256]{1,0:T(8,128)(2,1)S(1)}, bf16[1344,256]{1,0:T(8,128)(2,1)S(1)}, u32[]{:S(2)}, u32[]{:S(2)}) collective-permute-start(bf16[1344,256]{1,0:T(8,128)(2,1)S(1)} %collective-permute-done.10.refs_6_), channel_id=1, source_target_pairs={{0,8},{8,16},{16,24},{24,0},{1,9},{9,17},{17,25},{25,1},{2,10},{10... | collective-permute-start | bytes 2064392 | tf_op jit(solution)/shard_map/ppermute | solution.py:65
  121.0 28.2 %copy-start.59 = (f32[128]{0:T(128)S(1)}, f32[128]{0:T(128)}, u32[]{:S(2)}) copy-start(f32[128]{0:T(128)} %param.17) | copy-start | bytes 1540
  134.6 49.3 %collective-permute-start.14 = (bf16[1344,256]{1,0:T(8,128)(2,1)}, bf16[1344,256]{1,0:T(8,128)(2,1)}, u32[]{:S(2)}, u32[]{:S(2)}) collective-permute-start(bf16[1344,256]{1,0:T(8,128)(2,1)} %get-tuple-element.46.refs_0_), channel_id=1, source_target_pairs={{0,8},{8,16},{16,24},{24,0},{1,9},{9,17},{17,25},{25,1},{2,10},{10... | collective-permute-start | bytes 2064392 | tf_op jit(solution)/shard_map/ppermute | solution.py:65
  149.3 35.1 %collective-permute-start.17 = (bf16[1344,256]{1,0:T(8,128)(2,1)}, bf16[1344,256]{1,0:T(8,128)(2,1)}, u32[]{:S(2)}, u32[]{:S(2)}) collective-permute-start(bf16[1344,256]{1,0:T(8,128)(2,1)} %get-tuple-element.49.refs_0_), channel_id=1, source_target_pairs={{0,8},{8,16},{16,24},{24,0},{1,9},{9,17},{17,25},{25,1},{2,10},{10... | collective-permute-start | bytes 2064392 | tf_op jit(solution)/shard_map/ppermute | solution.py:65
  180.5 58.0 %collective-permute-start.20 = (bf16[1024,512]{1,0:T(8,128)(2,1)}, bf16[1024,512]{1,0:T(8,128)(2,1)}, u32[]{:S(2)}, u32[]{:S(2)}) collective-permute-start(bf16[1024,512]{1,0:T(8,128)(2,1)} %slice.72), channel_id=1, source_target_pairs={{0,8},{8,16},{16,24},{1,9},{9,17},{17,25},{2,10},{10,18},{18,26},{... | collective-permute-start | bytes 3145736 | tf_op jit(solution)/shard_map/ppermute | solution.py:370
  183.9 37.5 %collective-permute-start.15 = (bf16[1344,256]{1,0:T(8,128)(2,1)}, bf16[1344,256]{1,0:T(8,128)(2,1)}, u32[]{:S(2)}, u32[]{:S(2)}) collective-permute-start(bf16[1344,256]{1,0:T(8,128)(2,1)} %collective-permute-done.14.refs_1_), channel_id=1, source_target_pairs={{0,8},{8,16},{16,24},{24,0},{1,9},{9,17},{17,25},{25,1},{2,10},{10... | collective-permute-start | bytes 2064392 | tf_op jit(solution)/shard_map/ppermute | solution.py:65
  184.4 51.7 %collective-permute-start.18 = (bf16[1344,256]{1,0:T(8,128)(2,1)}, bf16[1344,256]{1,0:T(8,128)(2,1)S(1)}, u32[]{:S(2)}, u32[]{:S(2)}) collective-permute-start(bf16[1344,256]{1,0:T(8,128)(2,1)} %collective-permute-done.17.refs_1_), channel_id=1, source_target_pairs={{0,8},{8,16},{16,24},{24,0},{1,9},{9,17},{17,25},{25,1},{2,10},{10... | collective-permute-start | bytes 2064392 | tf_op jit(solution)/shard_map/ppermute | solution.py:65
  221.4 29.5 %collective-permute-start.16 = (bf16[1344,256]{1,0:T(8,128)(2,1)}, bf16[1344,256]{1,0:T(8,128)(2,1)}, u32[]{:S(2)}, u32[]{:S(2)}) collective-permute-start(bf16[1344,256]{1,0:T(8,128)(2,1)} %collective-permute-done.15.refs_2_), channel_id=1, source_target_pairs={{0,8},{8,16},{16,24},{24,0},{1,9},{9,17},{17,25},{25,1},{2,10},{10... | collective-permute-start | bytes 2064392 | tf_op jit(solution)/shard_map/ppermute | solution.py:65
  236.1 30.5 %collective-permute-start.19 = (bf16[1344,256]{1,0:T(8,128)(2,1)S(1)}, bf16[1344,256]{1,0:T(8,128)(2,1)S(1)}, u32[]{:S(2)}, u32[]{:S(2)}) collective-permute-start(bf16[1344,256]{1,0:T(8,128)(2,1)S(1)} %collective-permute-done.18.refs_2_), channel_id=1, source_target_pairs={{0,8},{8,16},{16,24},{24,0},{1,9},{9,17},{17,25},{25,1},{2,10},{10... | collective-permute-start | bytes 2064392 | tf_op jit(solution)/shard_map/ppermute | solution.py:65
  240.6 39.3 %copy-start.2 = (bf16[3072,512]{1,0:T(8,128)(2,1)}, bf16[3072,512]{1,0:T(8,128)(2,1)S(1)}, u32[]{:S(2)}) copy-start(bf16[3072,512]{1,0:T(8,128)(2,1)S(1)} %pad_maximum_fusion.refs_2_) | copy-start | bytes 9437188
  250.9 45.5 %collective-permute-start.24 = (bf16[336,2048]{1,0:T(8,128)(2,1)}, bf16[336,2048]{1,0:T(8,128)(2,1)}, u32[]{:S(2)}, u32[]{:S(2)}) collective-permute-start(bf16[336,2048]{1,0:T(8,128)(2,1)} %collective-permute-done.4.refs_6_), channel_id=1, source_target_pairs={{0,8},{8,16},{16,24},{24,0},{1,9},{9,17},{17,25},{25,1},{2,10},{10... | collective-permute-start | bytes 4128776 | tf_op jit(solution)/shard_map/ppermute | solution.py:65
  294.5 32.3 %collective-permute-start.21 = (bf16[1024,512]{1,0:T(8,128)(2,1)}, bf16[1024,512]{1,0:T(8,128)(2,1)}, u32[]{:S(2)}, u32[]{:S(2)}) collective-permute-start(bf16[1024,512]{1,0:T(8,128)(2,1)} %shard_map.103.refs_0_), channel_id=1, source_target_pairs={{0,2},{2,0},{4,6},{6,4},{1,3},{3,1},{5,7},{7,5},{8,10},{10,8},{12,... | collective-permute-start | bytes 3145736 | tf_op jit(solution)/shard_map/ppermute | solution.py:56
  294.5 25.9 %collective-permute-start.22 = (bf16[1024,512]{1,0:T(8,128)(2,1)}, bf16[1024,512]{1,0:T(8,128)(2,1)}, u32[]{:S(2)}, u32[]{:S(2)}) collective-permute-start(bf16[1024,512]{1,0:T(8,128)(2,1)} %shard_map.103.refs_0_), channel_id=1, source_target_pairs={{0,4},{2,6},{4,0},{6,2},{1,5},{3,7},{5,1},{7,3},{8,12},{10,14},{12... | collective-permute-start | bytes 3145736 | tf_op jit(solution)/shard_map/ppermute | solution.py:56
  296.4 35.3 %collective-permute-start.25 = (bf16[336,2048]{1,0:T(8,128)(2,1)}, bf16[336,2048]{1,0:T(8,128)(2,1)}, u32[]{:S(2)}, u32[]{:S(2)}) collective-permute-start(bf16[336,2048]{1,0:T(8,128)(2,1)} %collective-permute-done.24.refs_5_), channel_id=1, source_target_pairs={{0,8},{8,16},{16,24},{24,0},{1,9},{9,17},{17,25},{25,1},{2,10},{10... | collective-permute-start | bytes 4128776 | tf_op jit(solution)/shard_map/ppermute | solution.py:65
  320.4 6.4 %collective-permute-start.23 = (bf16[1024,512]{1,0:T(8,128)(2,1)}, bf16[1024,512]{1,0:T(8,128)(2,1)}, u32[]{:S(2)}, u32[]{:S(2)}) collective-permute-start(bf16[1024,512]{1,0:T(8,128)(2,1)} %collective-permute-done.22.refs_2_), channel_id=1, source_target_pairs={{0,2},{2,0},{4,6},{6,4},{1,3},{3,1},{5,7},{7,5},{8,10},{10,8},{12,... | collective-permute-start | bytes 3145736 | tf_op jit(solution)/shard_map/ppermute | solution.py:56
  326.2 25.9 %collective-permute-start.27 = (bf16[1024,512]{1,0:T(8,128)(2,1)}, bf16[1024,512]{1,0:T(8,128)(2,1)}, u32[]{:S(2)}, u32[]{:S(2)}) collective-permute-start(bf16[1024,512]{1,0:T(8,128)(2,1)} %shard_map.104.refs_0_), channel_id=1, source_target_pairs={{0,4},{2,6},{4,0},{6,2},{1,5},{3,7},{5,1},{7,3},{8,12},{10,14},{12... | collective-permute-start | bytes 3145736 | tf_op jit(solution)/shard_map/ppermute | solution.py:56
  345.6 17.1 %collective-permute-start.28 = (bf16[336,1024]{1,0:T(8,128)(2,1)S(1)}, bf16[336,1024]{1,0:T(8,128)(2,1)S(1)}, u32[]{:S(2)}, u32[]{:S(2)}) collective-permute-start(bf16[336,1024]{1,0:T(8,128)(2,1)S(1)} %get-tuple-element.59), channel_id=1, source_target_pairs={{0,1},{1,0},{2,3},{3,2},{4,5},{5,4},{6,7},{7,6},{8,9},{9,8},{10,11... | collective-permute-start | bytes 2064392 | tf_op jit(solution)/shard_map/ppermute | solution.py:60
  347.1 18.0 %collective-permute-start.26 = (bf16[1024,512]{1,0:T(8,128)(2,1)}, bf16[1024,512]{1,0:T(8,128)(2,1)}, u32[]{:S(2)}, u32[]{:S(2)}) collective-permute-start(bf16[1024,512]{1,0:T(8,128)(2,1)} %shard_map.104.refs_0_), channel_id=1, source_target_pairs={{0,2},{2,0},{4,6},{6,4},{1,3},{3,1},{5,7},{7,5},{8,10},{10,8},{12,... | collective-permute-start | bytes 3145736 | tf_op jit(solution)/shard_map/ppermute | solution.py:56
  363.5 3.0 collective-permute-start.29
  363.5 18.1 %collective-permute-start.39 = (bf16[336,1024]{1,0:T(8,128)(2,1)}, bf16[336,1024]{1,0:T(8,128)(2,1)S(1)}, u32[]{:S(2)}, u32[]{:S(2)}) collective-permute-start(bf16[336,1024]{1,0:T(8,128)(2,1)} %copy-done.54), channel_id=1, source_target_pairs={{0,1},{1,0},{2,3},{3,2},{4,5},{5,4},{6,7},{7,6},{8,9},{9,8},{10,11... | collective-permute-start | bytes 2064392 | tf_op jit(solution)/shard_map/ppermute | solution.py:60
  383.2 6.3 %collective-permute-start.40 = (bf16[672,256]{1,0:T(8,128)(2,1)}, bf16[672,256]{1,0:T(8,128)(2,1)}, u32[]{:S(2)}, u32[]{:S(2)}) collective-permute-start(bf16[672,256]{1,0:T(8,128)(2,1)} %get-tuple-element.73), channel_id=1, source_target_pairs={{0,2},{2,0},{4,6},{6,4},{1,3},{3,1},{5,7},{7,5},{8,10},{10,8},{12,... | collective-permute-start | bytes 1032200 | tf_op jit(solution)/shard_map/ppermute | solution.py:56
  385.8 18.5 %collective-permute-start.30 = (bf16[336,1024]{1,0:T(8,128)(2,1)}, bf16[336,1024]{1,0:T(8,128)(2,1)S(1)}, u32[]{:S(2)}, u32[]{:S(2)}) collective-permute-start(bf16[336,1024]{1,0:T(8,128)(2,1)} %copy-done.45), channel_id=1, source_target_pairs={{0,1},{1,0},{2,3},{3,2},{4,5},{5,4},{6,7},{7,6},{8,9},{9,8},{10,11... | collective-permute-start | bytes 2064392 | tf_op jit(solution)/shard_map/ppermute | solution.py:60
  387.4 31.3 %collective-permute-start.34 = (bf16[336,1024]{1,0:T(8,128)(2,1)}, bf16[336,1024]{1,0:T(8,128)(2,1)S(1)}, u32[]{:S(2)}, u32[]{:S(2)}) collective-permute-start(bf16[336,1024]{1,0:T(8,128)(2,1)} %copy-done.44), channel_id=1, source_target_pairs={{0,1},{1,0},{2,3},{3,2},{4,5},{5,4},{6,7},{7,6},{8,9},{9,8},{10,11... | collective-permute-start | bytes 2064392 | tf_op jit(solution)/shard_map/ppermute | solution.py:60
  387.9 11.1 %collective-permute-start.41 = (bf16[672,256]{1,0:T(8,128)(2,1)}, bf16[672,256]{1,0:T(8,128)(2,1)S(1)}, u32[]{:S(2)}, u32[]{:S(2)}) collective-permute-start(bf16[672,256]{1,0:T(8,128)(2,1)} %get-tuple-element.74), channel_id=1, source_target_pairs={{0,4},{2,6},{4,0},{6,2},{1,5},{3,7},{5,1},{7,3},{8,12},{10,14},{12... | collective-permute-start | bytes 1032200 | tf_op jit(solution)/shard_map/ppermute | solution.py:56
  389.4 29.7 %collective-permute-start.42 = (bf16[672,256]{1,0:T(8,128)(2,1)}, bf16[672,256]{1,0:T(8,128)(2,1)S(1)}, u32[]{:S(2)}, u32[]{:S(2)}) collective-permute-start(bf16[672,256]{1,0:T(8,128)(2,1)} %get-tuple-element.71), channel_id=1, source_target_pairs={{0,6},{2,4},{4,2},{6,0},{1,7},{3,5},{5,3},{7,1},{8,14},{10,12},{12... | collective-permute-start | bytes 1032200 | tf_op jit(solution)/shard_map/ppermute | solution.py:56
  404.7 16.0 %collective-permute-start.31 = (bf16[336,256]{1,0:T(8,128)(2,1)S(1)}, bf16[336,256]{1,0:T(8,128)(2,1)S(1)}, u32[]{:S(2)}, u32[]{:S(2)}) collective-permute-start(bf16[336,256]{1,0:T(8,128)(2,1)S(1)} %get-tuple-element.93), channel_id=1, source_target_pairs={{0,2},{2,0},{4,6},{6,4},{1,3},{3,1},{5,7},{7,5},{8,10},{10,8},{12,... | collective-permute-start | bytes 516104 | tf_op jit(solution)/shard_map/ppermute | solution.py:56
  404.8 16.5 %collective-permute-start.32 = (bf16[336,256]{1,0:T(8,128)(2,1)S(1)}, bf16[336,256]{1,0:T(8,128)(2,1)S(1)}, u32[]{:S(2)}, u32[]{:S(2)}) collective-permute-start(bf16[336,256]{1,0:T(8,128)(2,1)S(1)} %get-tuple-element.92), channel_id=1, source_target_pairs={{0,4},{2,6},{4,0},{6,2},{1,5},{3,7},{5,1},{7,3},{8,12},{10,14},{12... | collective-permute-start | bytes 516104 | tf_op jit(solution)/shard_map/ppermute | solution.py:56
  406.3 16.5 %collective-permute-start.33 = (bf16[336,256]{1,0:T(8,128)(2,1)S(1)}, bf16[336,256]{1,0:T(8,128)(2,1)S(1)}, u32[]{:S(2)}, u32[]{:S(2)}) collective-permute-start(bf16[336,256]{1,0:T(8,128)(2,1)S(1)} %get-tuple-element.91), channel_id=1, source_target_pairs={{0,6},{2,4},{4,2},{6,0},{1,7},{3,5},{5,3},{7,1},{8,14},{10,12},{12... | collective-permute-start | bytes 516104 | tf_op jit(solution)/shard_map/ppermute | solution.py:56
  419.1 3.8 collective-permute-start.35
  419.2 7.2 %collective-permute-start.36 = (bf16[336,256]{1,0:T(8,128)(2,1)S(1)}, bf16[336,256]{1,0:T(8,128)(2,1)S(1)}, u32[]{:S(2)}, u32[]{:S(2)}) collective-permute-start(bf16[336,256]{1,0:T(8,128)(2,1)S(1)} %get-tuple-element.88), channel_id=1, source_target_pairs={{0,4},{2,6},{4,0},{6,2},{1,5},{3,7},{5,1},{7,3},{8,12},{10,14},{12... | collective-permute-start | bytes 516104 | tf_op jit(solution)/shard_map/ppermute | solution.py:56
  420.7 8.5 %collective-permute-start.37 = (bf16[336,256]{1,0:T(8,128)(2,1)S(1)}, bf16[336,256]{1,0:T(8,128)(2,1)S(1)}, u32[]{:S(2)}, u32[]{:S(2)}) collective-permute-start(bf16[336,256]{1,0:T(8,128)(2,1)S(1)} %get-tuple-element.87), channel_id=1, source_target_pairs={{0,6},{2,4},{4,2},{6,0},{1,7},{3,5},{5,3},{7,1},{8,14},{10,12},{12... | collective-permute-start | bytes 516104 | tf_op jit(solution)/shard_map/ppermute | solution.py:56
  421.3 10.2 %collective-permute-start.43 = (f32[1,256]{1,0:T(1,128)S(1)}, f32[1,256]{1,0:T(1,128)S(1)}, u32[]{:S(2)}, u32[]{:S(2)}) collective-permute-start(f32[1,256]{1,0:T(1,128)S(1)} %shard_map.108.own_ref), channel_id=1, source_target_pairs={{0,1},{1,0},{2,3},{3,2},{4,5},{5,4},{6,7},{7,6},{8,9},{9,8},{10,11... | collective-permute-start | bytes 3080 | tf_op jit(solution)/shard_map/ppermute | solution.py:60
  429.8 7.9 %collective-permute-start.38 = (f32[1,256]{1,0:T(1,128)S(1)}, f32[1,256]{1,0:T(1,128)S(1)}, u32[]{:S(2)}, u32[]{:S(2)}) collective-permute-start(f32[1,256]{1,0:T(1,128)S(1)} %shard_map.107.own_ref), channel_id=1, source_target_pairs={{0,1},{1,0},{2,3},{3,2},{4,5},{5,4},{6,7},{7,6},{8,9},{9,8},{10,11... | collective-permute-start | bytes 3080 | tf_op jit(solution)/shard_map/ppermute | solution.py:60
  (67 other events, 422.5 us)
Sparse Core Ops, SparseCore 0:
  15.1 133.0 all-gather.2

commit v6 on v5

--- a/solution.py
+++ b/solution.py
@@ -138,22 +138,26 @@
     column = lax.broadcasted_iota(jnp.int32, shape, 1)
     first = last - jnp.minimum(pos_ref[...], VISIBLE_SPAN - 1)
     allowed = (column <= last) & (column >= first)
+    bias = jnp.where(allowed, 0.0, MASKED)
+    tall = jnp.concatenate([bias, bias], axis=0)
     kv_heads = len(queries)
     for kv_head, q_ref in enumerate(queries):
         keys = kv_ref[pl.ds(start, window), pl.ds(kv_head * HEAD_SIZE, HEAD_SIZE)]
         values = kv_ref[pl.ds(start, window), pl.ds((kv_heads + kv_head) * HEAD_SIZE, HEAD_SIZE)]
         group = q_ref.shape[1] // HEAD_SIZE
+        stacked = jnp.concatenate(
+            [q_ref[:, h * HEAD_SIZE : (h + 1) * HEAD_SIZE] for h in range(group)], axis=0
+        )
+        scores = lax.dot_general(
+            stacked, keys, (((1,), (1,)), ((), ())), preferred_element_type=jnp.float32
+        )
+        scores = scores + tall
+        expo = jnp.exp(scores - jnp.max(scores, axis=-1, keepdims=True))
+        weights = (expo * (1.0 / jnp.sum(expo, axis=-1, keepdims=True))).astype(jnp.bfloat16)
+        mixed = jnp.dot(weights, values, preferred_element_type=jnp.float32).astype(jnp.bfloat16)
         for head in range(group):
-            span = slice(head * HEAD_SIZE, (head + 1) * HEAD_SIZE)
-            scores = lax.dot_general(
-                q_ref[:, span], keys, (((1,), (1,)), ((), ())), preferred_element_type=jnp.float32
-            )
-            scores = jnp.where(allowed, scores, MASKED)
-            expo = jnp.exp(scores - jnp.max(scores, axis=-1, keepdims=True))
-            weights = (expo / jnp.sum(expo, axis=-1, keepdims=True)).astype(jnp.bfloat16)
-            mixed = jnp.dot(weights, values, preferred_element_type=jnp.float32)
             place = (kv_head * group + head) * HEAD_SIZE
-            o_ref[:, place : place + HEAD_SIZE] = mixed.astype(jnp.bfloat16)
+            o_ref[:, place : place + HEAD_SIZE] = mixed[head * QUERY_BLOCK : (head + 1) * QUERY_BLOCK]
 
 
 def attend(part, position, queries, all_kv):
@@ -327,12 +331,12 @@
     scale = lax.rsqrt((squares + swap_tp(squares)) / MODEL_WIDTH + EPS)
     gain = lax.dynamic_slice_in_dim(in_gain, side * inputs.shape[1], inputs.shape[1])
     normed = (values * scale[:, None] * gain).astype(jnp.bfloat16)
-    normed = lax.all_gather(normed, ("i", "tp"), axis=0, tiled=False)
-    normed = normed.reshape(INNER, 2, *inputs.shape)
 
     pos_x = in_order(place // 2 == 0, positions, swap(positions, 2))
     q_on_way = shuffle_start([after(q_weight, kv_on_way[1])], place)
-    kv = shuffle_end(kv_on_way[0], after(kv_on_way[1], hops["o"][1]), place)
+    kv = shuffle_end(*kv_on_way, place)
+    normed = lax.all_gather(after(normed, hops["o"][1], kv), ("i", "tp"), axis=0, tiled=False)
+    normed = normed.reshape(INNER, 2, *inputs.shape)
     kv_half = kv.shape[1] // 2
     hops["k"], hops["v"] = [kv[:, :kv_half]], [kv[:, kv_half:]]
     pos = in_order(place % 2 == 0, pos_x, swap(pos_x, 1)).transpose(1, 0, 2).reshape(-1)
@@ -364,8 +368,8 @@
         turn,
     )
     for n in range(planes - 2):
-        hop("qa", own_kv)
-        hop("qb", own_kv)
+        hop("qa", *[own_kv][:n])
+        hop("qb", *[own_kv][:n])
     up = [(c, c + 1) for c in range(planes - 1)]
     halo = lax.ppermute(own_kv[plane_tokens - VISIBLE_SPAN :], "z", up)
     all_kv = jnp.concatenate([halo, own_kv], axis=0)

time: 451 us -> 423 us (0.938)
  starting transfers between devices: 38.4 us -> 26.4 us
  local copies, waits for them, and re-layouts: 41.5 us -> 33 us
    ppermute x15, starting transfers between devices: 16 us -> 6.54 us  [ring_step(): return lax.ppermute(x, 'z', [(c, (c + 1) % size) for c in range(size)])]
    unnamed x141 -> x133, local copies, waits for them, and re-layouts: 29 us -> 21.4 us
    ppermute x7, waiting for transfers between devices: 31.7 us -> 26.2 us  [swap_tp(): return lax.ppermute(x, 'tp', [(0, 1), (1, 0)])]
    ppermute x1, waiting for transfers between devices: 0.01 us -> 5.19 us  [by_planes(): halo = lax.ppermute(own_kv[plane_tokens - VISIBLE_SPAN:], 'z', up)]
  transfers between devices with their start and end apart: 45 -> 45, of which waited for: 24 -> 27; matrix products, arithmetic and copies ran while one was open for 6% -> 6% of each run, Pallas kernels for 22% -> 23%
where the time goes in v6:
time: 423 us; the launch traced here: 419 us
  waiting for transfers between devices  220 us (52%)
  Pallas kernels  100 us (24%)
  local copies, waits for them, and re-layouts  33 us (8%)
  starting transfers between devices  26.4 us (6%)
  between operations  21.6 us (5%)
  other arithmetic  18.5 us (4%)
    ppermute x15, waiting for transfers between devices, ring_step(): return lax.ppermute(x, 'z', [(c, (c + 1) % size) for c in range(size)])  143 us
    pallas_call x3, Pallas kernels, project(): pl.pallas_call(functools.partial(project_kernel, factor, turned_groups *...  45.5 us
    ppermute x21, waiting for transfers between devices, swap(): return lax.ppermute(x, 'i', [(c, c ^ mask) for c in range(INNER)])  45.3 us
    pallas_call x2, Pallas kernels, attend(): pl.pallas_call(functools.partial(attend_kernel, part), grid=(half // QUER...  26.5 us
    ppermute x7, waiting for transfers between devices, swap_tp(): return lax.ppermute(x, 'tp', [(0, 1), (1, 0)])  26.2 us
    pallas_call x2, Pallas kernels, group_product(): pl.pallas_call(functools.partial(group_kernel, len(attended)), grid=(toke...  22.7 us
    unnamed x133, local copies, waits for them, and re-layouts  21.4 us
  transfers between devices with their start and end apart: 45, of which 27 were waited for; matrix products, arithmetic and copies ran while one was open for 6% of the time, Pallas kernels for 23%

profile of v6, /device:TPU:2, one launch (start us, length us, event | category | flops | bytes accessed | tf_op | source)
XLA Modules:
  0.0 419.2 jit_solution(16745484833907279483)
XLA Ops:
  6.5 1.5 constant_dynamic-slice_fusion.14
  10.7 1.6 collective-permute-start.2
  12.3 1.6 collective-permute-start.3
  14.7 11.9 %collective-permute-done.4 = bf16[2,336,512]{2,1,0:T(8,128)(2,1)} collective-permute-done((bf16[2,336,512]{2,1,0:T(8,128)(2,1)}, bf16[2,336,512]{2,1,0:T(8,128)(2,1)}, u32[]{:S(2)}, u32[]{:S(2)}) %collective-permute-start.4) | collective-permute-done | bytes 688160 | tf_op jit(solution)/shard_map/ppermute | solution.py:56
  26.5 1.5 maximum_select_fusion
  29.0 2.2 fusion.2
  31.5 2.6 maximum_select_fusion.1
  34.2 11.9 %collective-permute-done.3.refs_6_ = bf16[336,2048]{1,0:T(8,128)(2,1)} collective-permute-done((bf16[336,2048]{1,0:T(8,128)(2,1)}, bf16[336,2048]{1,0:T(8,128)(2,1)}, u32[]{:S(2)}, u32[]{:S(2)}) %collective-permute-start.3) | collective-permute-done | bytes 1376288 | tf_op jit(solution)/shard_map/ppermute | solution.py:65
  46.2 1.5 dynamic-slice_bitcast_fusion.7
  50.3 18.1 %collective-permute-done.6.refs_1_ = bf16[1344,256]{1,0:T(8,128)(2,1)} collective-permute-done((bf16[1344,256]{1,0:T(8,128)(2,1)S(1)}, bf16[1344,256]{1,0:T(8,128)(2,1)}, u32[]{:S(2)}, u32[]{:S(2)}) %collective-permute-start.6) | collective-permute-done | bytes 688160 | tf_op jit(solution)/shard_map/ppermute | solution.py:65
  68.4 14.7 %collective-permute-done.9.refs_5_ = bf16[1344,256]{1,0:T(8,128)(2,1)} collective-permute-done((bf16[1344,256]{1,0:T(8,128)(2,1)S(1)}, bf16[1344,256]{1,0:T(8,128)(2,1)}, u32[]{:S(2)}, u32[]{:S(2)}) %collective-permute-start.9) | collective-permute-done | bytes 688160 | tf_op jit(solution)/shard_map/ppermute | solution.py:65
  85.3 2.9 collective-permute-done
  89.4 8.4 %collective-permute-done.7.refs_2_ = bf16[1344,256]{1,0:T(8,128)(2,1)} collective-permute-done((bf16[1344,256]{1,0:T(8,128)(2,1)}, bf16[1344,256]{1,0:T(8,128)(2,1)}, u32[]{:S(2)}, u32[]{:S(2)}) %collective-permute-start.7) | collective-permute-done | bytes 688160 | tf_op jit(solution)/shard_map/ppermute | solution.py:65
  97.8 14.7 %collective-permute-done.10.refs_6_ = bf16[1344,256]{1,0:T(8,128)(2,1)} collective-permute-done((bf16[1344,256]{1,0:T(8,128)(2,1)}, bf16[1344,256]{1,0:T(8,128)(2,1)}, u32[]{:S(2)}, u32[]{:S(2)}) %collective-permute-start.10) | collective-permute-done | bytes 688160 | tf_op jit(solution)/shard_map/ppermute | solution.py:65
  112.6 2.0 maximum_select_fusion.3
  114.8 12.5 %collective-permute-done.8.refs_3_ = bf16[1344,256]{1,0:T(8,128)(2,1)S(1)} collective-permute-done((bf16[1344,256]{1,0:T(8,128)(2,1)}, bf16[1344,256]{1,0:T(8,128)(2,1)S(1)}, u32[]{:S(2)}, u32[]{:S(2)}) %collective-permute-start.8) | collective-permute-done | bytes 688160 | tf_op jit(solution)/shard_map/ppermute | solution.py:65
  127.2 14.7 %collective-permute-done.11.refs_7_ = bf16[1344,256]{1,0:T(8,128)(2,1)S(1)} collective-permute-done((bf16[1344,256]{1,0:T(8,128)(2,1)}, bf16[1344,256]{1,0:T(8,128)(2,1)S(1)}, u32[]{:S(2)}, u32[]{:S(2)}) %collective-permute-start.11) | collective-permute-done | bytes 688160 | tf_op jit(solution)/shard_map/ppermute | solution.py:65
  142.0 3.7 fusion.7
  145.8 1.9 pad_maximum_fusion.1
  147.7 9.1 %collective-permute-done.14.refs_1_ = bf16[1344,256]{1,0:T(8,128)(2,1)} collective-permute-done((bf16[1344,256]{1,0:T(8,128)(2,1)S(1)}, bf16[1344,256]{1,0:T(8,128)(2,1)}, u32[]{:S(2)}, u32[]{:S(2)}) %collective-permute-start.14) | collective-permute-done | bytes 688160 | tf_op jit(solution)/shard_map/ppermute | solution.py:65
  156.8 14.7 %collective-permute-done.17.refs_1_ = bf16[1344,256]{1,0:T(8,128)(2,1)} collective-permute-done((bf16[1344,256]{1,0:T(8,128)(2,1)S(1)}, bf16[1344,256]{1,0:T(8,128)(2,1)}, u32[]{:S(2)}, u32[]{:S(2)}) %collective-permute-start.17) | collective-permute-done | bytes 688160 | tf_op jit(solution)/shard_map/ppermute | solution.py:65
  177.3 19.5 %shard_map.100 = bf16[2048,512]{1,0:T(8,128)(2,1)S(1)} custom-call(s32[4]{0:T(128)S(1)} %and_select_fusion.source_ref, bf16[4,2,512,2688]{3,2,1,0:T(8,128)(2,1)} %bitcast.78, bf16[1344,256]{1,0:T(8,128)(2,1)S(1)} %copy-done.24, bf16[1344,256]{1,0:T(8,128)(2,1)} %collective-permute-done.6.refs_1_, bf16[1344,256]{1,0:T(8,128)(2,1)} %collective-permute-done.7.refs_2_, ...), custom_call_target="tpu_custom_call" | custom-call | flops 9846154240 | tf_op jit(solution)/shard_map/pallas_call | solution.py:114
  199.5 1.4 slice.72
  202.1 5.8 %collective-permute-start.20 = (bf16[1024,512]{1,0:T(8,128)(2,1)S(1)}, bf16[1024,512]{1,0:T(8,128)(2,1)S(1)}, u32[]{:S(2)}, u32[]{:S(2)}) collective-permute-start(bf16[1024,512]{1,0:T(8,128)(2,1)S(1)} %slice.72), channel_id=1, source_target_pairs={{0,8},{8,16},{16,24},{1,9},{9,17},{17,25},{2,10},{10,18},{18,26},{... | collective-permute-start | bytes 3145736 | tf_op jit(solution)/shard_map/ppermute | solution.py:374
  208.0 10.7 %collective-permute-done.16.refs_3_ = bf16[1344,256]{1,0:T(8,128)(2,1)} collective-permute-done((bf16[1344,256]{1,0:T(8,128)(2,1)}, bf16[1344,256]{1,0:T(8,128)(2,1)}, u32[]{:S(2)}, u32[]{:S(2)}) %collective-permute-start.16) | collective-permute-done | bytes 688160 | tf_op jit(solution)/shard_map/ppermute | solution.py:65
  218.7 13.1 %shard_map.101.refs_0_ = bf16[2048,256]{1,0:T(8,128)(2,1)S(1)} custom-call(s32[4]{0:T(128)S(1)} %and_select_fusion.source_ref, bf16[4,2,512,2688]{3,2,1,0:T(8,128)(2,1)} %bitcast.79, bf16[1344,256]{1,0:T(8,128)(2,1)S(1)} %copy-done.32, bf16[1344,256]{1,0:T(8,128)(2,1)} %collective-permute-done.14.refs_1_, bf16[1344,256]{1,0:T(8,128)(2,1)} %collective-permute-done.15.refs_2_, ...), custom_call_target="tpu_custom_call" | custom-call | flops 9846154240 | tf_op jit(solution)/shard_map/pallas_call | solution.py:114
  231.8 1.5 collective-permute-done.19.refs_3_
  233.3 13.0 %shard_map.102.refs_1_ = bf16[2048,256]{1,0:T(8,128)(2,1)S(1)} custom-call(s32[4]{0:T(128)S(1)} %and_select_fusion.source_ref, bf16[4,2,512,2688]{3,2,1,0:T(8,128)(2,1)} %bitcast.80, bf16[1344,256]{1,0:T(8,128)(2,1)S(1)} %copy-done.30, bf16[1344,256]{1,0:T(8,128)(2,1)} %collective-permute-done.17.refs_1_, bf16[1344,256]{1,0:T(8,128)(2,1)} %collective-permute-done.18.refs_2_, ...), custom_call_target="tpu_custom_call" | custom-call | flops 9846154240 | tf_op jit(solution)/shard_map/pallas_call | solution.py:114
  246.3 5.2 %collective-permute-done.20 = bf16[1024,512]{1,0:T(8,128)(2,1)S(1)} collective-permute-done((bf16[1024,512]{1,0:T(8,128)(2,1)S(1)}, bf16[1024,512]{1,0:T(8,128)(2,1)S(1)}, u32[]{:S(2)}, u32[]{:S(2)}) %collective-permute-start.20) | collective-permute-done | bytes 1048608 | tf_op jit(solution)/shard_map/ppermute | solution.py:374
  251.7 13.4 %shard_map.103.refs_0_ = bf16[1024,512]{1,0:T(8,128)(2,1)} custom-call(s32[2048,1]{1,0:T(8,128)S(1)} %copy-done.21, bf16[2048,256]{1,0:T(8,128)(2,1)S(1)} %shard_map.101.refs_0_, bf16[2048,256]{1,0:T(8,128)(2,1)S(1)} %shard_map.102.refs_1_, bf16[3072,512]{1,0:T(8,128)(2,1)S(1)} %pad_maximum_fusion.refs_2_), custom_call_target="tpu_custom_call" | custom-call | flops 14499999744 | tf_op jit(solution)/shard_map/pallas_call | solution.py:168
  267.2 10.8 %collective-permute-done.24.refs_5_ = bf16[336,2048]{1,0:T(8,128)(2,1)} collective-permute-done((bf16[336,2048]{1,0:T(8,128)(2,1)}, bf16[336,2048]{1,0:T(8,128)(2,1)}, u32[]{:S(2)}, u32[]{:S(2)}) %collective-permute-start.24) | collective-permute-done | bytes 1376288 | tf_op jit(solution)/shard_map/ppermute | solution.py:65
  278.0 2.5 collective-permute-start.25
  280.5 1.9 copy-done.4
  286.0 13.1 %shard_map.104.refs_0_ = bf16[1024,512]{1,0:T(8,128)(2,1)} custom-call(s32[2048,1]{1,0:T(8,128)S(1)} %copy-done.22, bf16[2048,256]{1,0:T(8,128)(2,1)S(1)} %copy-done.57, bf16[2048,256]{1,0:T(8,128)(2,1)S(1)} %copy-done.59, bf16[3072,512]{1,0:T(8,128)(2,1)S(1)} %copy-done.4), custom_call_target="tpu_custom_call" | custom-call | flops 14499999744 | tf_op jit(solution)/shard_map/pallas_call | solution.py:168
  306.4 11.2 %shard_map.105 = (bf16[336,1024]{1,0:T(8,128)(2,1)S(1)}, bf16[336,1024]{1,0:T(8,128)(2,1)S(1)}, bf16[336,1024]{1,0:T(8,128)(2,1)S(1)}, bf16[336,1024]{1,0:T(8,128)(2,1)S(1)}) custom-call(s32[1]{0:T(128)} %bitcast.12.place_ref, s32[2]{0:T(128)S(1)} %pad_add_fusion.kept_ref, bf16[1024,512]{1,0:T(8,128)(2,1)} %shard_map.103.refs_0_, ...), custom_call_target="tpu_custom_call" | custom-call | flops 11600000000 | tf_op jit(solution)/shard_map/pallas_call | solution.py:210
  319.9 10.6 %collective-permute-done.27.refs_2_ = bf16[1024,512]{1,0:T(8,128)(2,1)} collective-permute-done((bf16[1024,512]{1,0:T(8,128)(2,1)}, bf16[1024,512]{1,0:T(8,128)(2,1)}, u32[]{:S(2)}, u32[]{:S(2)}) %collective-permute-start.27) | collective-permute-done | bytes 1048608 | tf_op jit(solution)/shard_map/ppermute | solution.py:56
  330.5 5.4 %collective-permute-done.28 = bf16[336,1024]{1,0:T(8,128)(2,1)S(1)} collective-permute-done((bf16[336,1024]{1,0:T(8,128)(2,1)S(1)}, bf16[336,1024]{1,0:T(8,128)(2,1)S(1)}, u32[]{:S(2)}, u32[]{:S(2)}) %collective-permute-start.28) | collective-permute-done | bytes 688160 | tf_op jit(solution)/shard_map/ppermute | solution.py:60
  337.3 2.5 collective-permute-done.29.refs_3_
  339.8 11.4 %shard_map.106 = (bf16[336,1024]{1,0:T(8,128)(2,1)S(1)}, bf16[336,1024]{1,0:T(8,128)(2,1)S(1)}, bf16[336,1024]{1,0:T(8,128)(2,1)S(1)}, bf16[336,1024]{1,0:T(8,128)(2,1)S(1)}) custom-call(s32[1]{0:T(128)} %bitcast.12.place_ref, s32[2]{0:T(128)S(1)} %pad_add_fusion.kept_ref, bf16[1024,512]{1,0:T(8,128)(2,1)} %shard_map.104.refs_0_, ...), custom_call_target="tpu_custom_call" | custom-call | flops 11600000000 | tf_op jit(solution)/shard_map/pallas_call | solution.py:210
  351.2 3.6 collective-permute-done.39
  359.4 1.5 collective-permute-start.34
  363.4 8.7 %collective-permute-done.41 = bf16[672,256]{1,0:T(8,128)(2,1)S(1)} collective-permute-done((bf16[672,256]{1,0:T(8,128)(2,1)}, bf16[672,256]{1,0:T(8,128)(2,1)S(1)}, u32[]{:S(2)}, u32[]{:S(2)}) %collective-permute-start.41) | collective-permute-done | bytes 344096 | tf_op jit(solution)/shard_map/ppermute | solution.py:56
  372.2 5.2 %collective-permute-done.30 = bf16[336,1024]{1,0:T(8,128)(2,1)S(1)} collective-permute-done((bf16[336,1024]{1,0:T(8,128)(2,1)}, bf16[336,1024]{1,0:T(8,128)(2,1)S(1)}, u32[]{:S(2)}, u32[]{:S(2)}) %collective-permute-start.30) | collective-permute-done | bytes 688160 | tf_op jit(solution)/shard_map/ppermute | solution.py:60
  379.7 12.0 %collective-permute-done.34 = bf16[336,1024]{1,0:T(8,128)(2,1)S(1)} collective-permute-done((bf16[336,1024]{1,0:T(8,128)(2,1)}, bf16[336,1024]{1,0:T(8,128)(2,1)S(1)}, u32[]{:S(2)}, u32[]{:S(2)}) %collective-permute-start.34) | collective-permute-done | bytes 688160 | tf_op jit(solution)/shard_map/ppermute | solution.py:60
  394.9 4.6 %collective-permute-done.36.refs_6_ = bf16[336,256]{1,0:T(8,128)(2,1)S(1)} collective-permute-done((bf16[336,256]{1,0:T(8,128)(2,1)S(1)}, bf16[336,256]{1,0:T(8,128)(2,1)S(1)}, u32[]{:S(2)}, u32[]{:S(2)}) %collective-permute-start.36) | collective-permute-done | bytes 172064 | tf_op jit(solution)/shard_map/ppermute | solution.py:56
  399.5 2.8 collective-permute-done.37.refs_7_
  407.2 2.5 shard_map.109.refs_8_
  409.8 2.5 shard_map.110
  (237 shorter events, 47.3 us)
Async XLA Ops:
  6.5 165.0 %all-gather.3.cloned.1.call-start = ((), (), s32[]{:S(2)}) async-start(), calls=%async_computation | async-start | bytes 24772608 | tf_op jit(solution)/shard_map/all_gather | solution.py:338
  9.1 17.5 %collective-permute-start.4 = (bf16[2,336,512]{2,1,0:T(8,128)(2,1)}, bf16[2,336,512]{2,1,0:T(8,128)(2,1)}, u32[]{:S(2)}, u32[]{:S(2)}) collective-permute-start(bf16[2,336,512]{2,1,0:T(8,128)(2,1)} %pad_maximum_fusion.3), channel_id=1, source_target_pairs={{0,4},{2,6},{4,0},{6,2},{1,5},{3,7},{5,1},{7,3},{8,12},{10,14},{12... | collective-permute-start | bytes 2064392 | tf_op jit(solution)/shard_map/ppermute | solution.py:56
  10.7 4.0 collective-permute-start.2
  12.3 33.8 %collective-permute-start.3 = (bf16[336,2048]{1,0:T(8,128)(2,1)}, bf16[336,2048]{1,0:T(8,128)(2,1)}, u32[]{:S(2)}, u32[]{:S(2)}) collective-permute-start(bf16[336,2048]{1,0:T(8,128)(2,1)} %bitcast.20.refs_4_), channel_id=1, source_target_pairs={{0,8},{8,16},{16,24},{24,0},{1,9},{9,17},{17,25},{25,1},{2,10},{10... | collective-permute-start | bytes 4128776 | tf_op jit(solution)/shard_map/ppermute | solution.py:65
  29.0 2.5 collective-permute-start.5
  48.0 20.3 %collective-permute-start.6 = (bf16[1344,256]{1,0:T(8,128)(2,1)S(1)}, bf16[1344,256]{1,0:T(8,128)(2,1)}, u32[]{:S(2)}, u32[]{:S(2)}) collective-permute-start(bf16[1344,256]{1,0:T(8,128)(2,1)S(1)} %get-tuple-element.80.refs_0_), channel_id=1, source_target_pairs={{0,8},{8,16},{16,24},{24,0},{1,9},{9,17},{17,25},{25,1},{2,10},{10... | collective-permute-start | bytes 2064392 | tf_op jit(solution)/shard_map/ppermute | solution.py:65
  48.1 35.0 %collective-permute-start.9 = (bf16[1344,256]{1,0:T(8,128)(2,1)S(1)}, bf16[1344,256]{1,0:T(8,128)(2,1)}, u32[]{:S(2)}, u32[]{:S(2)}) collective-permute-start(bf16[1344,256]{1,0:T(8,128)(2,1)S(1)} %get-tuple-element.79.refs_4_), channel_id=1, source_target_pairs={{0,8},{8,16},{16,24},{24,0},{1,9},{9,17},{17,25},{25,1},{2,10},{10... | collective-permute-start | bytes 2064392 | tf_op jit(solution)/shard_map/ppermute | solution.py:65
  49.4 33.7 %collective-permute-start.12 = (bf16[2,336,512]{2,1,0:T(8,128)(2,1)S(1)}, bf16[2,336,512]{2,1,0:T(8,128)(2,1)S(1)}, u32[]{:S(2)}, u32[]{:S(2)}) collective-permute-start(bf16[2,336,512]{2,1,0:T(8,128)(2,1)S(1)} %pad_maximum_fusion.4), channel_id=1, source_target_pairs={{0,4},{2,6},{4,0},{6,2},{1,5},{3,7},{5,1},{7,3},{8,12},{10,14},{12... | collective-permute-start | bytes 2064392 | tf_op jit(solution)/shard_map/ppermute | solution.py:56
  68.4 29.5 %collective-permute-start.7 = (bf16[1344,256]{1,0:T(8,128)(2,1)}, bf16[1344,256]{1,0:T(8,128)(2,1)}, u32[]{:S(2)}, u32[]{:S(2)}) collective-permute-start(bf16[1344,256]{1,0:T(8,128)(2,1)} %collective-permute-done.6.refs_1_), channel_id=1, source_target_pairs={{0,8},{8,16},{16,24},{24,0},{1,9},{9,17},{17,25},{25,1},{2,10},{10... | collective-permute-start | bytes 2064392 | tf_op jit(solution)/shard_map/ppermute | solution.py:65
  83.1 29.5 %collective-permute-start.10 = (bf16[1344,256]{1,0:T(8,128)(2,1)}, bf16[1344,256]{1,0:T(8,128)(2,1)}, u32[]{:S(2)}, u32[]{:S(2)}) collective-permute-start(bf16[1344,256]{1,0:T(8,128)(2,1)} %collective-permute-done.9.refs_5_), channel_id=1, source_target_pairs={{0,8},{8,16},{16,24},{24,0},{1,9},{9,17},{17,25},{25,1},{2,10},{10... | collective-permute-start | bytes 2064392 | tf_op jit(solution)/shard_map/ppermute | solution.py:65
  84.6 28.1 %collective-permute-start.13 = (bf16[2,336,512]{2,1,0:T(8,128)(2,1)}, bf16[2,336,512]{2,1,0:T(8,128)(2,1)}, u32[]{:S(2)}, u32[]{:S(2)}) collective-permute-start(bf16[2,336,512]{2,1,0:T(8,128)(2,1)} %get-tuple-element.74), channel_id=1, source_target_pairs={{0,2},{2,0},{4,6},{6,4},{1,3},{3,1},{5,7},{7,5},{8,10},{10,8},{12,... | collective-permute-start | bytes 2064392 | tf_op jit(solution)/shard_map/ppermute | solution.py:56
  84.6 3.6 collective-permute-start
  88.2 1.2 collective-permute-start.1
  97.8 29.4 %collective-permute-start.8 = (bf16[1344,256]{1,0:T(8,128)(2,1)}, bf16[1344,256]{1,0:T(8,128)(2,1)S(1)}, u32[]{:S(2)}, u32[]{:S(2)}) collective-permute-start(bf16[1344,256]{1,0:T(8,128)(2,1)} %collective-permute-done.7.refs_2_), channel_id=1, source_target_pairs={{0,8},{8,16},{16,24},{24,0},{1,9},{9,17},{17,25},{25,1},{2,10},{10... | collective-permute-start | bytes 2064392 | tf_op jit(solution)/shard_map/ppermute | solution.py:65
  112.6 29.4 %collective-permute-start.11 = (bf16[1344,256]{1,0:T(8,128)(2,1)}, bf16[1344,256]{1,0:T(8,128)(2,1)S(1)}, u32[]{:S(2)}, u32[]{:S(2)}) collective-permute-start(bf16[1344,256]{1,0:T(8,128)(2,1)} %collective-permute-done.10.refs_6_), channel_id=1, source_target_pairs={{0,8},{8,16},{16,24},{24,0},{1,9},{9,17},{17,25},{25,1},{2,10},{10... | collective-permute-start | bytes 2064392 | tf_op jit(solution)/shard_map/ppermute | solution.py:65
  114.7 31.0 %copy-start.29 = (bf16[1344,256]{1,0:T(8,128)(2,1)}, bf16[1344,256]{1,0:T(8,128)(2,1)S(1)}, u32[]{:S(2)}) copy-start(bf16[1344,256]{1,0:T(8,128)(2,1)S(1)} %get-tuple-element.46.refs_0_) | copy-start | bytes 2064388
  114.7 31.0 %copy-start.31 = (bf16[1344,256]{1,0:T(8,128)(2,1)}, bf16[1344,256]{1,0:T(8,128)(2,1)S(1)}, u32[]{:S(2)}) copy-start(bf16[1344,256]{1,0:T(8,128)(2,1)S(1)} %get-tuple-element.44.refs_0_) | copy-start | bytes 2064388
  127.2 29.6 %collective-permute-start.14 = (bf16[1344,256]{1,0:T(8,128)(2,1)S(1)}, bf16[1344,256]{1,0:T(8,128)(2,1)}, u32[]{:S(2)}, u32[]{:S(2)}) collective-permute-start(bf16[1344,256]{1,0:T(8,128)(2,1)S(1)} %get-tuple-element.44.refs_0_), channel_id=1, source_target_pairs={{0,8},{8,16},{16,24},{24,0},{1,9},{9,17},{17,25},{25,1},{2,10},{10... | collective-permute-start | bytes 2064392 | tf_op jit(solution)/shard_map/ppermute | solution.py:65
  142.0 29.6 %collective-permute-start.17 = (bf16[1344,256]{1,0:T(8,128)(2,1)S(1)}, bf16[1344,256]{1,0:T(8,128)(2,1)}, u32[]{:S(2)}, u32[]{:S(2)}) collective-permute-start(bf16[1344,256]{1,0:T(8,128)(2,1)S(1)} %get-tuple-element.46.refs_0_), channel_id=1, source_target_pairs={{0,8},{8,16},{16,24},{24,0},{1,9},{9,17},{17,25},{25,1},{2,10},{10... | collective-permute-start | bytes 2064392 | tf_op jit(solution)/shard_map/ppermute | solution.py:65
  145.7 25.8 %copy-start.54 = (f32[128]{0:T(128)S(1)}, f32[128]{0:T(128)}, u32[]{:S(2)}) copy-start(f32[128]{0:T(128)} %param.17) | copy-start | bytes 1540
  156.8 41.3 %collective-permute-start.15 = (bf16[1344,256]{1,0:T(8,128)(2,1)}, bf16[1344,256]{1,0:T(8,128)(2,1)}, u32[]{:S(2)}, u32[]{:S(2)}) collective-permute-start(bf16[1344,256]{1,0:T(8,128)(2,1)} %collective-permute-done.14.refs_1_), channel_id=1, source_target_pairs={{0,8},{8,16},{16,24},{24,0},{1,9},{9,17},{17,25},{25,1},{2,10},{10... | collective-permute-start | bytes 2064392 | tf_op jit(solution)/shard_map/ppermute | solution.py:65
  171.6 29.4 %collective-permute-start.18 = (bf16[1344,256]{1,0:T(8,128)(2,1)}, bf16[1344,256]{1,0:T(8,128)(2,1)}, u32[]{:S(2)}, u32[]{:S(2)}) collective-permute-start(bf16[1344,256]{1,0:T(8,128)(2,1)} %collective-permute-done.17.refs_1_), channel_id=1, source_target_pairs={{0,8},{8,16},{16,24},{24,0},{1,9},{9,17},{17,25},{25,1},{2,10},{10... | collective-permute-start | bytes 2064392 | tf_op jit(solution)/shard_map/ppermute | solution.py:65
  198.1 20.5 %collective-permute-start.16 = (bf16[1344,256]{1,0:T(8,128)(2,1)}, bf16[1344,256]{1,0:T(8,128)(2,1)}, u32[]{:S(2)}, u32[]{:S(2)}) collective-permute-start(bf16[1344,256]{1,0:T(8,128)(2,1)} %collective-permute-done.15.refs_2_), channel_id=1, source_target_pairs={{0,8},{8,16},{16,24},{24,0},{1,9},{9,17},{17,25},{25,1},{2,10},{10... | collective-permute-start | bytes 2064392 | tf_op jit(solution)/shard_map/ppermute | solution.py:65
  201.0 32.3 %collective-permute-start.19 = (bf16[1344,256]{1,0:T(8,128)(2,1)}, bf16[1344,256]{1,0:T(8,128)(2,1)S(1)}, u32[]{:S(2)}, u32[]{:S(2)}) collective-permute-start(bf16[1344,256]{1,0:T(8,128)(2,1)} %collective-permute-done.18.refs_2_), channel_id=1, source_target_pairs={{0,8},{8,16},{16,24},{24,0},{1,9},{9,17},{17,25},{25,1},{2,10},{10... | collective-permute-start | bytes 2064392 | tf_op jit(solution)/shard_map/ppermute | solution.py:65
  202.1 49.4 %collective-permute-start.20 = (bf16[1024,512]{1,0:T(8,128)(2,1)S(1)}, bf16[1024,512]{1,0:T(8,128)(2,1)S(1)}, u32[]{:S(2)}, u32[]{:S(2)}) collective-permute-start(bf16[1024,512]{1,0:T(8,128)(2,1)S(1)} %slice.72), channel_id=1, source_target_pairs={{0,8},{8,16},{16,24},{1,9},{9,17},{17,25},{2,10},{10,18},{18,26},{... | collective-permute-start | bytes 3145736 | tf_op jit(solution)/shard_map/ppermute | solution.py:374
  218.6 59.3 %collective-permute-start.24 = (bf16[336,2048]{1,0:T(8,128)(2,1)}, bf16[336,2048]{1,0:T(8,128)(2,1)}, u32[]{:S(2)}, u32[]{:S(2)}) collective-permute-start(bf16[336,2048]{1,0:T(8,128)(2,1)} %collective-permute-done.3.refs_6_), channel_id=1, source_target_pairs={{0,8},{8,16},{16,24},{24,0},{1,9},{9,17},{17,25},{25,1},{2,10},{10... | collective-permute-start | bytes 4128776 | tf_op jit(solution)/shard_map/ppermute | solution.py:65
  265.1 40.2 %collective-permute-start.21 = (bf16[1024,512]{1,0:T(8,128)(2,1)}, bf16[1024,512]{1,0:T(8,128)(2,1)}, u32[]{:S(2)}, u32[]{:S(2)}) collective-permute-start(bf16[1024,512]{1,0:T(8,128)(2,1)} %shard_map.103.refs_0_), channel_id=1, source_target_pairs={{0,2},{2,0},{4,6},{6,4},{1,3},{3,1},{5,7},{7,5},{8,10},{10,8},{12,... | collective-permute-start | bytes 3145736 | tf_op jit(solution)/shard_map/ppermute | solution.py:56
  265.1 34.0 %collective-permute-start.22 = (bf16[1024,512]{1,0:T(8,128)(2,1)}, bf16[1024,512]{1,0:T(8,128)(2,1)}, u32[]{:S(2)}, u32[]{:S(2)}) collective-permute-start(bf16[1024,512]{1,0:T(8,128)(2,1)} %shard_map.103.refs_0_), channel_id=1, source_target_pairs={{0,4},{2,6},{4,0},{6,2},{1,5},{3,7},{5,1},{7,3},{8,12},{10,14},{12... | collective-permute-start | bytes 3145736 | tf_op jit(solution)/shard_map/ppermute | solution.py:56
  278.0 28.5 %collective-permute-start.25 = (bf16[336,2048]{1,0:T(8,128)(2,1)}, bf16[336,2048]{1,0:T(8,128)(2,1)}, u32[]{:S(2)}, u32[]{:S(2)}) collective-permute-start(bf16[336,2048]{1,0:T(8,128)(2,1)} %collective-permute-done.24.refs_5_), channel_id=1, source_target_pairs={{0,8},{8,16},{16,24},{24,0},{1,9},{9,17},{17,25},{25,1},{2,10},{10... | collective-permute-start | bytes 4128776 | tf_op jit(solution)/shard_map/ppermute | solution.py:65
  299.1 6.2 %collective-permute-start.23 = (bf16[1024,512]{1,0:T(8,128)(2,1)}, bf16[1024,512]{1,0:T(8,128)(2,1)}, u32[]{:S(2)}, u32[]{:S(2)}) collective-permute-start(bf16[1024,512]{1,0:T(8,128)(2,1)} %collective-permute-done.22.refs_2_), channel_id=1, source_target_pairs={{0,2},{2,0},{4,6},{6,4},{1,3},{3,1},{5,7},{7,5},{8,10},{10,8},{12,... | collective-permute-start | bytes 3145736 | tf_op jit(solution)/shard_map/ppermute | solution.py:56
  304.6 25.9 %collective-permute-start.27 = (bf16[1024,512]{1,0:T(8,128)(2,1)}, bf16[1024,512]{1,0:T(8,128)(2,1)}, u32[]{:S(2)}, u32[]{:S(2)}) collective-permute-start(bf16[1024,512]{1,0:T(8,128)(2,1)} %shard_map.104.refs_0_), channel_id=1, source_target_pairs={{0,4},{2,6},{4,0},{6,2},{1,5},{3,7},{5,1},{7,3},{8,12},{10,14},{12... | collective-permute-start | bytes 3145736 | tf_op jit(solution)/shard_map/ppermute | solution.py:56
  319.4 16.5 %collective-permute-start.28 = (bf16[336,1024]{1,0:T(8,128)(2,1)S(1)}, bf16[336,1024]{1,0:T(8,128)(2,1)S(1)}, u32[]{:S(2)}, u32[]{:S(2)}) collective-permute-start(bf16[336,1024]{1,0:T(8,128)(2,1)S(1)} %get-tuple-element.55), channel_id=1, source_target_pairs={{0,1},{1,0},{2,3},{3,2},{4,5},{5,4},{6,7},{7,6},{8,9},{9,8},{10,11... | collective-permute-start | bytes 2064392 | tf_op jit(solution)/shard_map/ppermute | solution.py:60
  319.9 17.4 %collective-permute-start.26 = (bf16[1024,512]{1,0:T(8,128)(2,1)}, bf16[1024,512]{1,0:T(8,128)(2,1)}, u32[]{:S(2)}, u32[]{:S(2)}) collective-permute-start(bf16[1024,512]{1,0:T(8,128)(2,1)} %shard_map.104.refs_0_), channel_id=1, source_target_pairs={{0,2},{2,0},{4,6},{6,4},{1,3},{3,1},{5,7},{7,5},{8,10},{10,8},{12,... | collective-permute-start | bytes 3145736 | tf_op jit(solution)/shard_map/ppermute | solution.py:56
  336.8 3.0 collective-permute-start.29
  336.8 18.1 %collective-permute-start.39 = (bf16[336,1024]{1,0:T(8,128)(2,1)}, bf16[336,1024]{1,0:T(8,128)(2,1)S(1)}, u32[]{:S(2)}, u32[]{:S(2)}) collective-permute-start(bf16[336,1024]{1,0:T(8,128)(2,1)} %copy-done.49), channel_id=1, source_target_pairs={{0,1},{1,0},{2,3},{3,2},{4,5},{5,4},{6,7},{7,6},{8,9},{9,8},{10,11... | collective-permute-start | bytes 2064392 | tf_op jit(solution)/shard_map/ppermute | solution.py:60
  356.5 5.9 %collective-permute-start.40 = (bf16[672,256]{1,0:T(8,128)(2,1)}, bf16[672,256]{1,0:T(8,128)(2,1)}, u32[]{:S(2)}, u32[]{:S(2)}) collective-permute-start(bf16[672,256]{1,0:T(8,128)(2,1)} %get-tuple-element.69), channel_id=1, source_target_pairs={{0,2},{2,0},{4,6},{6,4},{1,3},{3,1},{5,7},{7,5},{8,10},{10,8},{12,... | collective-permute-start | bytes 1032200 | tf_op jit(solution)/shard_map/ppermute | solution.py:56
  358.9 18.5 %collective-permute-start.30 = (bf16[336,1024]{1,0:T(8,128)(2,1)}, bf16[336,1024]{1,0:T(8,128)(2,1)S(1)}, u32[]{:S(2)}, u32[]{:S(2)}) collective-permute-start(bf16[336,1024]{1,0:T(8,128)(2,1)} %copy-done.48), channel_id=1, source_target_pairs={{0,1},{1,0},{2,3},{3,2},{4,5},{5,4},{6,7},{7,6},{8,9},{9,8},{10,11... | collective-permute-start | bytes 2064392 | tf_op jit(solution)/shard_map/ppermute | solution.py:60
  359.4 32.3 %collective-permute-start.34 = (bf16[336,1024]{1,0:T(8,128)(2,1)}, bf16[336,1024]{1,0:T(8,128)(2,1)S(1)}, u32[]{:S(2)}, u32[]{:S(2)}) collective-permute-start(bf16[336,1024]{1,0:T(8,128)(2,1)} %copy-done.47), channel_id=1, source_target_pairs={{0,1},{1,0},{2,3},{3,2},{4,5},{5,4},{6,7},{7,6},{8,9},{9,8},{10,11... | collective-permute-start | bytes 2064392 | tf_op jit(solution)/shard_map/ppermute | solution.py:60
  361.0 11.1 %collective-permute-start.41 = (bf16[672,256]{1,0:T(8,128)(2,1)}, bf16[672,256]{1,0:T(8,128)(2,1)S(1)}, u32[]{:S(2)}, u32[]{:S(2)}) collective-permute-start(bf16[672,256]{1,0:T(8,128)(2,1)} %get-tuple-element.70), channel_id=1, source_target_pairs={{0,4},{2,6},{4,0},{6,2},{1,5},{3,7},{5,1},{7,3},{8,12},{10,14},{12... | collective-permute-start | bytes 1032200 | tf_op jit(solution)/shard_map/ppermute | solution.py:56
  362.3 29.9 %collective-permute-start.42 = (bf16[672,256]{1,0:T(8,128)(2,1)}, bf16[672,256]{1,0:T(8,128)(2,1)S(1)}, u32[]{:S(2)}, u32[]{:S(2)}) collective-permute-start(bf16[672,256]{1,0:T(8,128)(2,1)} %get-tuple-element.67), channel_id=1, source_target_pairs={{0,6},{2,4},{4,2},{6,0},{1,7},{3,5},{5,3},{7,1},{8,14},{10,12},{12... | collective-permute-start | bytes 1032200 | tf_op jit(solution)/shard_map/ppermute | solution.py:56
  377.8 15.8 %collective-permute-start.31 = (bf16[336,256]{1,0:T(8,128)(2,1)S(1)}, bf16[336,256]{1,0:T(8,128)(2,1)S(1)}, u32[]{:S(2)}, u32[]{:S(2)}) collective-permute-start(bf16[336,256]{1,0:T(8,128)(2,1)S(1)} %get-tuple-element.89), channel_id=1, source_target_pairs={{0,2},{2,0},{4,6},{6,4},{1,3},{3,1},{5,7},{7,5},{8,10},{10,8},{12,... | collective-permute-start | bytes 516104 | tf_op jit(solution)/shard_map/ppermute | solution.py:56
  377.8 16.5 %collective-permute-start.32 = (bf16[336,256]{1,0:T(8,128)(2,1)S(1)}, bf16[336,256]{1,0:T(8,128)(2,1)S(1)}, u32[]{:S(2)}, u32[]{:S(2)}) collective-permute-start(bf16[336,256]{1,0:T(8,128)(2,1)S(1)} %get-tuple-element.88), channel_id=1, source_target_pairs={{0,4},{2,6},{4,0},{6,2},{1,5},{3,7},{5,1},{7,3},{8,12},{10,14},{12... | collective-permute-start | bytes 516104 | tf_op jit(solution)/shard_map/ppermute | solution.py:56
  379.2 15.7 %collective-permute-start.33 = (bf16[336,256]{1,0:T(8,128)(2,1)S(1)}, bf16[336,256]{1,0:T(8,128)(2,1)S(1)}, u32[]{:S(2)}, u32[]{:S(2)}) collective-permute-start(bf16[336,256]{1,0:T(8,128)(2,1)S(1)} %get-tuple-element.87), channel_id=1, source_target_pairs={{0,6},{2,4},{4,2},{6,0},{1,7},{3,5},{5,3},{7,1},{8,14},{10,12},{12... | collective-permute-start | bytes 516104 | tf_op jit(solution)/shard_map/ppermute | solution.py:56
  392.1 2.8 collective-permute-start.35
  392.2 7.2 %collective-permute-start.36 = (bf16[336,256]{1,0:T(8,128)(2,1)S(1)}, bf16[336,256]{1,0:T(8,128)(2,1)S(1)}, u32[]{:S(2)}, u32[]{:S(2)}) collective-permute-start(bf16[336,256]{1,0:T(8,128)(2,1)S(1)} %get-tuple-element.84), channel_id=1, source_target_pairs={{0,4},{2,6},{4,0},{6,2},{1,5},{3,7},{5,1},{7,3},{8,12},{10,14},{12... | collective-permute-start | bytes 516104 | tf_op jit(solution)/shard_map/ppermute | solution.py:56
  393.6 8.6 %collective-permute-start.37 = (bf16[336,256]{1,0:T(8,128)(2,1)S(1)}, bf16[336,256]{1,0:T(8,128)(2,1)S(1)}, u32[]{:S(2)}, u32[]{:S(2)}) collective-permute-start(bf16[336,256]{1,0:T(8,128)(2,1)S(1)} %get-tuple-element.83), channel_id=1, source_target_pairs={{0,6},{2,4},{4,2},{6,0},{1,7},{3,5},{5,3},{7,1},{8,14},{10,12},{12... | collective-permute-start | bytes 516104 | tf_op jit(solution)/shard_map/ppermute | solution.py:56
  394.3 9.2 %collective-permute-start.43 = (f32[1,256]{1,0:T(1,128)S(1)}, f32[1,256]{1,0:T(1,128)S(1)}, u32[]{:S(2)}, u32[]{:S(2)}) collective-permute-start(f32[1,256]{1,0:T(1,128)S(1)} %shard_map.108.own_ref), channel_id=1, source_target_pairs={{0,1},{1,0},{2,3},{3,2},{4,5},{5,4},{6,7},{7,6},{8,9},{9,8},{10,11... | collective-permute-start | bytes 3080 | tf_op jit(solution)/shard_map/ppermute | solution.py:60
  402.9 6.8 %collective-permute-start.38 = (f32[1,256]{1,0:T(1,128)S(1)}, f32[1,256]{1,0:T(1,128)S(1)}, u32[]{:S(2)}, u32[]{:S(2)}) collective-permute-start(f32[1,256]{1,0:T(1,128)S(1)} %shard_map.107.own_ref), channel_id=1, source_target_pairs={{0,1},{1,0},{2,3},{3,2},{4,5},{5,4},{6,7},{7,6},{8,9},{9,8},{10,11... | collective-permute-start | bytes 3080 | tf_op jit(solution)/shard_map/ppermute | solution.py:60
  (63 other events, 437.3 us)
Sparse Core Ops, SparseCore 0:
  46.2 117.5 all-gather.2

commit v7 on v6

--- a/solution.py
+++ b/solution.py
@@ -75,8 +75,8 @@
 
 def project_kernel(factor, turned_cols, blocks, source_ref, x_ref, *refs):
     o_ref, whole_ref = refs[-2:]
-    gain_ref, cos_ref, sin_ref = refs[-5:-2]
-    weights = refs[:-5]
+    gain_ref, turn_ref = refs[-4:-2]
+    weights = refs[:-4]
 
     @pl.when(pl.program_id(0) == 0)
     def _():
@@ -95,11 +95,14 @@
             preferred_element_type=jnp.float32,
         )
         total = term if total is None else total + term
+    here, there = turn_ref[...], pltpu.roll(turn_ref[...], HEAD_SIZE // 2, 1)
+    first = lax.broadcasted_iota(jnp.int32, here.shape, 1) < HEAD_SIZE // 2
+    cosine, sine = jnp.where(first, here, there), jnp.where(first, -there, here)
     for head in range(turned_cols // HEAD_SIZE):
         span = slice(head * HEAD_SIZE, (head + 1) * HEAD_SIZE)
         values = rms_scale(total[:, span], gain_ref[...])
         turned = pltpu.roll(values, HEAD_SIZE // 2, 1)
-        values = values * cos_ref[...] + turned * sin_ref[...]
+        values = values * cosine + turned * sine
         o_ref[:, span] = (values * factor).astype(jnp.bfloat16)
     if turned_cols < total.shape[1]:
         o_ref[:, turned_cols:] = total[:, turned_cols:].astype(jnp.bfloat16)
@@ -120,13 +123,13 @@
         ]
         + [pl.BlockSpec((height, width), lambda b: (0, 0)) for _ in weights]
         + [pl.BlockSpec((1, HEAD_SIZE), lambda b: (0, 0))]
-        + [pl.BlockSpec((rows, HEAD_SIZE), lambda b: (b, 0)) for _ in turn],
+        + [pl.BlockSpec((rows, HEAD_SIZE), lambda b: (b, 0))],
         out_specs=pl.BlockSpec((rows, cols), lambda b: (b, 0)),
         out_shape=jax.ShapeDtypeStruct((tokens, cols), jnp.bfloat16),
         scratch_shapes=[pltpu.VMEM((sides * depth, cols), jnp.bfloat16)],
         compiler_params=pltpu.CompilerParams(vmem_limit_bytes=36 * MIB),
         cost_estimate=lasting(width / 26),
-    )(source, normed, *weights, gain.reshape(1, HEAD_SIZE), *turn)
+    )(source, normed, *weights, gain.reshape(1, HEAD_SIZE), turn)
 
 
 def attend_kernel(part, pos_ref, *refs):
@@ -178,10 +181,9 @@
     )(position, *queries, all_kv)
 
 
-def group_kernel(inner, place_ref, kept_ref, *refs):
-    pairs = kept_ref.shape[0]
-    lefts, weights, outs = refs[:inner], refs[inner : inner + 2 * pairs], refs[inner + 2 * pairs :]
-    place = place_ref[0]
+def group_kernel(inner, planes, pairs, facts_ref, *refs):
+    lefts, weights, outs = refs[:inner], refs[inner : -2 * len(pairs)], refs[-2 * len(pairs) :]
+    place = facts_ref[planes]
     depth = lefts[0].shape[1]
     for n, weight_ref in enumerate(weights):
         total = None
@@ -195,29 +197,31 @@
             )
             total = term if total is None else total + term
         total = total.astype(jnp.bfloat16)
-        kept = kept_ref[n // 2]
-        for out, which in zip(outs[n // 2 * 2 : n // 2 * 2 + 2], (kept, 1 - kept)):
+        kept = facts_ref[planes + 1 + pairs[n // 2]]
+        for out, which in zip(outs[n // 2 * 2 :], (kept, 1 - kept)):
 
             @pl.when(which == n % 2)
             def _():
                 out[...] = total
 
 
-def group_product(place, kept, attended, weights):
+def group_product(facts, attended, blocks, pairs):
     tokens, depth = attended[0].shape
-    cols, rows = weights[0].shape
+    cols, rows = blocks[0].shape
+    weights = [blocks[n] for pair in pairs for n in (pair, pair + len(blocks) // 2)]
     shape = jax.ShapeDtypeStruct((cols, tokens), jnp.bfloat16)
-    return pl.pallas_call(
-        functools.partial(group_kernel, len(attended)),
+    outs = pl.pallas_call(
+        functools.partial(group_kernel, len(attended), len(blocks), pairs),
         grid=(tokens // TOKEN_BLOCK,),
-        in_specs=[pl.BlockSpec(memory_space=pltpu.SMEM)] * 2
+        in_specs=[pl.BlockSpec(memory_space=pltpu.SMEM)]
         + [pl.BlockSpec((TOKEN_BLOCK, depth), lambda b: (b, 0)) for _ in attended]
         + [pl.BlockSpec((cols, rows), lambda b: (0, 0)) for _ in weights],
         out_specs=[pl.BlockSpec((cols, TOKEN_BLOCK), lambda b: (0, b))] * len(weights),
         out_shape=[shape] * len(weights),
         compiler_params=pltpu.CompilerParams(vmem_limit_bytes=24 * MIB),
         cost_estimate=lasting(2.9 * len(weights)),
-    )(jnp.reshape(place, (1,)), jnp.stack(kept).astype(jnp.int32), *attended, *weights)
+    )(facts, *attended, *weights)
+    return outs[::2], outs[1::2]
 
 
 def squares_kernel(*refs):
@@ -237,12 +241,20 @@
     )(*blocks)
 
 
-def finish_kernel(count, slots_ref, own_ref, other_ref, gain_ref, input_ref, *refs):
-    blocks, (o_ref, share_ref) = refs[:count], refs[-2:]
-    height = blocks[0].shape[0]
-    for n, block in enumerate(blocks):
-        row = pl.multiple_of(slots_ref[n] * height, 16)
-        share_ref[pl.ds(row, height), :] = block[...]
+def finish_kernel(inner, planes, facts_ref, own_ref, other_ref, gain_ref, input_ref, *refs):
+    o_ref, share_ref = refs[-2:]
+    place = facts_ref[planes]
+    pairs = planes // 2
+    height = share_ref.shape[0] // (pairs * inner)
+    pair = 0
+    while pair < pairs:
+        spread, refs = refs[:inner], refs[inner:]
+        for m, ref in enumerate(spread):
+            for n in range(ref.shape[0] // height):
+                slot = facts_ref[planes + 1 + pairs + pair + n] * inner + (place ^ m)
+                row = pl.multiple_of(slot * height, 16)
+                share_ref[pl.ds(row, height), :] = ref[n * height : (n + 1) * height, :]
+        pair += spread[0].shape[0] // height
     scale = lax.rsqrt((own_ref[...] + other_ref[...]) / MODEL_WIDTH + EPS)
     for col in range(0, share_ref.shape[0], HEAD_SIZE):
         span = slice(col, col + HEAD_SIZE)
@@ -250,24 +262,26 @@
         o_ref[:, span] = (input_ref[:, span].astype(jnp.float32) + branch).astype(jnp.bfloat16)
 
 
-def finish(part, slots, own, other, gain, inputs, blocks, so_far):
+def finish(part, planes, facts, own, other, gain, inputs, spread, so_far):
     rows, cols = inputs.shape
-    step = blocks[0].shape[1]
+    step = own.shape[1]
     whole = lambda x: pl.BlockSpec(x.shape, lambda b: (0, 0))
     extra = [] if so_far is None else [so_far]
-    operands = [slots, own, other, gain.reshape(1, cols), inputs, *blocks, *extra]
+    gain = gain.reshape(1, cols)
+    operands = [facts, own, other, gain, inputs, *spread, *extra]
     return pl.pallas_call(
-        functools.partial(finish_kernel, len(blocks)),
+        functools.partial(finish_kernel, INNER, planes),
         grid=(1,),
-        in_specs=[pl.BlockSpec(memory_space=pltpu.SMEM), whole(own), whole(other), whole(operands[3])]
+        in_specs=[pl.BlockSpec(memory_space=pltpu.SMEM), whole(own), whole(other), whole(gain)]
         + [pl.BlockSpec((step, cols), lambda b: (part, 0))]
-        + [whole(block) for block in blocks]
+        + [whole(block) for block in spread]
         + [pl.BlockSpec(memory_space=pl.ANY) for _ in extra],
         out_specs=pl.BlockSpec((step, cols), lambda b: (part, 0)),
         out_shape=jax.ShapeDtypeStruct((rows, cols), jnp.bfloat16),
         scratch_shapes=[pltpu.VMEM((cols, step), jnp.bfloat16)],
         input_output_aliases={len(operands) - 1: 0} if extra else {},
         compiler_params=pltpu.CompilerParams(vmem_limit_bytes=16 * MIB),
+        cost_estimate=lasting(2.5),
     )(*operands)
 
 
@@ -313,7 +327,14 @@
     planes = lax.axis_size("z")
     place, plane, side = lax.axis_index("i"), lax.axis_index("z"), lax.axis_index("tp")
     plane_tokens = INNER * tok_rows
-    source = ((plane - jnp.arange(planes)) % planes).astype(jnp.int32)
+    per_side = planes // 2
+    source = [(plane - d) % planes for d in range(planes)]
+    kept, slots = [], []
+    for d in range(per_side):
+        near, opposite = source[d], source[d + per_side]
+        kept.append(jnp.where(near // per_side == side, 0, 1))
+        slots.append(jnp.where(kept[d] == 0, near, opposite) % per_side)
+    facts = jnp.stack([*source, place, *kept, *slots]).astype(jnp.int32)
 
     kv_on_way = shuffle_start([key_matrix, value_matrix], place)
     out_rows = out_weight.T
@@ -353,15 +374,11 @@
     half = HEAD_SIZE // 2
     frequency = ROPE_BASE ** (-jnp.arange(half, dtype=jnp.float32) / half)
     angles = pos.astype(jnp.float32)[:, None] * frequency[None, :]
-    cosine, sine = jnp.cos(angles), jnp.sin(angles)
-    turn = (
-        jnp.concatenate([cosine, cosine], axis=1),
-        jnp.concatenate([-sine, sine], axis=1),
-    )
+    turn = jnp.concatenate([jnp.cos(angles), jnp.sin(angles)], axis=1)
 
     own_kv = project(
-        after(normed, *turn),
-        source,
+        after(normed, turn),
+        facts,
         [hops["k"], hops["v"]],
         1,
         key_norm_gain,
@@ -378,52 +395,48 @@
 
     factor = (MODEL_WIDTH // QUERY_HEADS) ** (-0.5)
     queries = [
-        project(after(normed, own_kv), source, [hops[name]], 1, q_gain, turn, factor)
+        project(after(normed, own_kv), facts, [hops[name]], 1, q_gain, turn, factor)
         for name in ("qa", "qb")
     ]
 
     own = [attend(0, pos[:, None], queries, all_kv)]
-    own.append(attend(1, after(pos[:, None], own[0]), queries, all_kv))
+    own.append(attend(1, pos[:, None], [after(queries[0], own[0], hops["o"][planes - 2]), queries[1]], all_kv))
     hop("o", own[0])
-    per_side = planes // 2
-    kept, slots = [], []
-    for d in range(per_side):
-        near, opposite = source[d], source[d + per_side]
-        kept.append(jnp.where(near // per_side == side, 0, 1))
-        which = jnp.where(kept[d] == 0, near, opposite) % per_side
-        slots += [which * INNER + (place ^ mask) for mask in range(INNER)]
-    slots = jnp.stack(slots).astype(jnp.int32)
     keeps, arrived = [], []
-    pairs = [block for d in range(per_side) for block in (hops["o"][d], hops["o"][d + per_side])]
     for part in range(2):
         far = swap(own[part], 2)
         first = after(own[0], own[1]) if part == 0 else after(own[1], keeps[-1])
-        across = after(far, own[1]) if part == 0 else after(far, keeps[-1], arrived[0])
+        across = after(far, own[1] if part == 0 else keeps[-1])
         attended = [first, swap(own[part], 1), far, swap(across, 1)]
-        terms = group_product(place, kept, attended, pairs)
-        keeps += terms[::2]
-        arrived += [swap_tp(give) for give in terms[1::2]]
+        for pairs in [range(per_side)]:
+            kept_terms, given_terms = group_product(facts, attended, hops["o"], tuple(pairs))
+            keeps += kept_terms
+            arrived += [swap_tp(term) for term in given_terms]
+
+    def to_tokens(total):
+        blocks = []
+        for mask in range(INNER):
+            at = (place ^ mask) * QUERY_BLOCK
+            block = lax.dynamic_slice_in_dim(total, at, QUERY_BLOCK, axis=1)
+            blocks.append(swap(block, mask) if mask else block)
+        return blocks
 
     output = None
     for part in range(2):
-        sums = []
+        sums, spread = [], []
         for n in range(part * per_side, (part + 1) * per_side):
-            theirs = after(arrived[n], keeps[-1]) if part == 0 else arrived[n]
+            theirs = after(arrived[n], *(keeps[-1:] if part == 0 else spread[-INNER + 1 :]))
             total = keeps[n].astype(jnp.float32) + theirs.astype(jnp.float32)
             sums.append(total.astype(jnp.bfloat16))
-        shipped = [jnp.concatenate(sums, axis=0)] if part == 0 else sums
-        blocks = []
-        for total in shipped:
-            for mask in range(INNER):
-                at = (place ^ mask) * QUERY_BLOCK
-                block = lax.dynamic_slice_in_dim(total, at, QUERY_BLOCK, axis=1)
-                blocks.append(swap(block, mask) if mask else block)
+            if part == 1:
+                spread += to_tokens(sums[-1])
         if part == 0:
-            height = sums[0].shape[0]
-            blocks = [block[n * height : (n + 1) * height] for n in range(per_side) for block in blocks]
-        squares = squares_of(blocks)
+            spread = to_tokens(jnp.concatenate(sums, axis=0))
+        if output is not None:
+            spread[-1] = after(spread[-1], output)
+        squares = squares_of(spread)
         output = finish(
-            part, slots, squares, swap_tp(squares), post_gain, inputs, blocks, output
+            part, planes, facts, squares, swap_tp(squares), post_gain, inputs, spread, output
         )
     return output
 

time: 423 us -> 407 us (0.962)
  local copies, waits for them, and re-layouts: 33 us -> 22.2 us
  between operations: 21.6 us -> 13.9 us
  waiting for transfers between devices: 220 us -> 226 us
    ppermute x21, waiting for transfers between devices: 45.3 us -> 26.7 us  [swap(): return lax.ppermute(x, 'i', [(c, c ^ mask) for c in range(INNER)])]
    ppermute x7, waiting for transfers between devices: 26.2 us -> 40.2 us  [swap_tp(): return lax.ppermute(x, 'tp', [(0, 1), (1, 0)])]
    ppermute x15, waiting for transfers between devices: 143 us -> 154 us  [ring_step(): return lax.ppermute(x, 'z', [(c, (c + 1) % size) for c in range(size)])]
    unnamed x133 -> x61, local copies, waits for them, and re-layouts: 21.4 us -> 13.1 us
where the time goes in v7:
time: 407 us; the launch traced here: 405 us
  waiting for transfers between devices  226 us (56%)
  Pallas kernels  97.4 us (24%)
  starting transfers between devices  28.2 us (7%)
  local copies, waits for them, and re-layouts  22.2 us (5%)
  other arithmetic  17.3 us (4%)
  between operations  13.9 us (3%)
    ppermute x15, waiting for transfers between devices, ring_step(): return lax.ppermute(x, 'z', [(c, (c + 1) % size) for c in range(size)])  154 us
    pallas_call x3, Pallas kernels, project(): pl.pallas_call(functools.partial(project_kernel, factor, turned_groups *...  45.4 us
    ppermute x7, waiting for transfers between devices, swap_tp(): return lax.ppermute(x, 'tp', [(0, 1), (1, 0)])  40.2 us
    ppermute x21, waiting for transfers between devices, swap(): return lax.ppermute(x, 'i', [(c, c ^ mask) for c in range(INNER)])  26.7 us
    pallas_call x2, Pallas kernels, attend(): pl.pallas_call(functools.partial(attend_kernel, part), grid=(half // QUER...  26.1 us
    pallas_call x2, Pallas kernels, group_product(): pl.pallas_call(functools.partial(group_kernel, len(attended), len(blocks)...  20.6 us
    unnamed x61, local copies, waits for them, and re-layouts  13.1 us
    ppermute x21, starting transfers between devices, swap(): return lax.ppermute(x, 'i', [(c, c ^ mask) for c in range(INNER)])  9.41 us
  transfers between devices with their start and end apart: 45, of which 27 were waited for; matrix products, arithmetic and copies ran while one was open for 6% of the time, Pallas kernels for 23%

profile of v7, /device:TPU:2, one launch (start us, length us, event | category | flops | bytes accessed | tf_op | source)
XLA Modules:
  0.0 405.3 jit_solution(5622768782093292469)
XLA Ops:
  6.5 1.5 constant_dynamic-slice_fusion.14
  10.7 1.6 collective-permute-start.2
  12.3 1.6 collective-permute-start.3
  14.7 11.9 %collective-permute-done.4 = bf16[2,336,512]{2,1,0:T(8,128)(2,1)} collective-permute-done((bf16[2,336,512]{2,1,0:T(8,128)(2,1)}, bf16[2,336,512]{2,1,0:T(8,128)(2,1)}, u32[]{:S(2)}, u32[]{:S(2)}) %collective-permute-start.4) | collective-permute-done | bytes 688160 | tf_op jit(solution)/shard_map/ppermute | solution.py:56
  26.5 1.6 maximum_select_fusion
  29.1 2.2 fusion.2
  31.6 2.8 maximum_select_fusion.1
  34.4 11.8 %collective-permute-done.3.refs_6_ = bf16[336,2048]{1,0:T(8,128)(2,1)} collective-permute-done((bf16[336,2048]{1,0:T(8,128)(2,1)}, bf16[336,2048]{1,0:T(8,128)(2,1)}, u32[]{:S(2)}, u32[]{:S(2)}) %collective-permute-start.3) | collective-permute-done | bytes 1376288 | tf_op jit(solution)/shard_map/ppermute | solution.py:65
  46.2 1.5 dynamic-slice_bitcast_fusion.7
  50.3 18.1 %collective-permute-done.6.refs_1_ = bf16[1344,256]{1,0:T(8,128)(2,1)} collective-permute-done((bf16[1344,256]{1,0:T(8,128)(2,1)S(1)}, bf16[1344,256]{1,0:T(8,128)(2,1)}, u32[]{:S(2)}, u32[]{:S(2)}) %collective-permute-start.6) | collective-permute-done | bytes 688160 | tf_op jit(solution)/shard_map/ppermute | solution.py:65
  68.4 14.7 %collective-permute-done.9.refs_5_ = bf16[1344,256]{1,0:T(8,128)(2,1)} collective-permute-done((bf16[1344,256]{1,0:T(8,128)(2,1)S(1)}, bf16[1344,256]{1,0:T(8,128)(2,1)}, u32[]{:S(2)}, u32[]{:S(2)}) %collective-permute-start.9) | collective-permute-done | bytes 688160 | tf_op jit(solution)/shard_map/ppermute | solution.py:65
  85.4 2.8 collective-permute-done
  89.4 8.4 %collective-permute-done.7.refs_2_ = bf16[1344,256]{1,0:T(8,128)(2,1)} collective-permute-done((bf16[1344,256]{1,0:T(8,128)(2,1)}, bf16[1344,256]{1,0:T(8,128)(2,1)}, u32[]{:S(2)}, u32[]{:S(2)}) %collective-permute-start.7) | collective-permute-done | bytes 688160 | tf_op jit(solution)/shard_map/ppermute | solution.py:65
  97.8 14.7 %collective-permute-done.10.refs_6_ = bf16[1344,256]{1,0:T(8,128)(2,1)} collective-permute-done((bf16[1344,256]{1,0:T(8,128)(2,1)}, bf16[1344,256]{1,0:T(8,128)(2,1)}, u32[]{:S(2)}, u32[]{:S(2)}) %collective-permute-start.10) | collective-permute-done | bytes 688160 | tf_op jit(solution)/shard_map/ppermute | solution.py:65
  112.6 2.1 maximum_select_fusion.3
  114.9 12.3 %collective-permute-done.8.refs_3_ = bf16[1344,256]{1,0:T(8,128)(2,1)S(1)} collective-permute-done((bf16[1344,256]{1,0:T(8,128)(2,1)}, bf16[1344,256]{1,0:T(8,128)(2,1)S(1)}, u32[]{:S(2)}, u32[]{:S(2)}) %collective-permute-start.8) | collective-permute-done | bytes 688160 | tf_op jit(solution)/shard_map/ppermute | solution.py:65
  127.2 14.7 %collective-permute-done.11.refs_7_ = bf16[1344,256]{1,0:T(8,128)(2,1)S(1)} collective-permute-done((bf16[1344,256]{1,0:T(8,128)(2,1)}, bf16[1344,256]{1,0:T(8,128)(2,1)S(1)}, u32[]{:S(2)}, u32[]{:S(2)}) %collective-permute-start.11) | collective-permute-done | bytes 688160 | tf_op jit(solution)/shard_map/ppermute | solution.py:65
  142.0 3.7 multiply_cosine_fusion
  147.1 9.7 %collective-permute-done.14.refs_1_ = bf16[1344,256]{1,0:T(8,128)(2,1)} collective-permute-done((bf16[1344,256]{1,0:T(8,128)(2,1)S(1)}, bf16[1344,256]{1,0:T(8,128)(2,1)}, u32[]{:S(2)}, u32[]{:S(2)}) %collective-permute-start.14) | collective-permute-done | bytes 688160 | tf_op jit(solution)/shard_map/ppermute | solution.py:65
  156.8 14.7 %collective-permute-done.17.refs_1_ = bf16[1344,256]{1,0:T(8,128)(2,1)} collective-permute-done((bf16[1344,256]{1,0:T(8,128)(2,1)S(1)}, bf16[1344,256]{1,0:T(8,128)(2,1)}, u32[]{:S(2)}, u32[]{:S(2)}) %collective-permute-start.17) | collective-permute-done | bytes 688160 | tf_op jit(solution)/shard_map/ppermute | solution.py:65
  176.1 19.4 %shard_map.100 = bf16[2048,512]{1,0:T(8,128)(2,1)S(1)} custom-call(s32[9]{0:T(128)S(1)} %stack.165.source_ref.facts_ref, bf16[4,2,512,2688]{3,2,1,0:T(8,128)(2,1)} %bitcast.72, bf16[1344,256]{1,0:T(8,128)(2,1)S(1)} %copy-done.7, bf16[1344,256]{1,0:T(8,128)(2,1)} %collective-permute-done.6.refs_1_, bf16[1344,256]{1,0:T(8,128)(2,1)} %collective-permute-done.7.refs_2_, ...), custom_call_target="tpu_custom_call" | custom-call | flops 9846154240 | tf_op jit(solution)/shard_map/pallas_call | solution.py:117
  196.8 1.9 broadcast_in_dim_reshape.5.pos_ref
  201.3 5.8 %collective-permute-start.20 = (bf16[1024,512]{1,0:T(8,128)(2,1)S(1)}, bf16[1024,512]{1,0:T(8,128)(2,1)S(1)}, u32[]{:S(2)}, u32[]{:S(2)}) collective-permute-start(bf16[1024,512]{1,0:T(8,128)(2,1)S(1)} %slice.24), channel_id=1, source_target_pairs={{0,8},{8,16},{16,24},{1,9},{9,17},{17,25},{2,10},{10,18},{18,26},{... | collective-permute-start | bytes 3145736 | tf_op jit(solution)/shard_map/ppermute | solution.py:391
  207.1 10.2 %collective-permute-done.16.refs_3_ = bf16[1344,256]{1,0:T(8,128)(2,1)} collective-permute-done((bf16[1344,256]{1,0:T(8,128)(2,1)}, bf16[1344,256]{1,0:T(8,128)(2,1)}, u32[]{:S(2)}, u32[]{:S(2)}) %collective-permute-start.16) | collective-permute-done | bytes 688160 | tf_op jit(solution)/shard_map/ppermute | solution.py:65
  217.3 13.1 %shard_map.101.refs_0_ = bf16[2048,256]{1,0:T(8,128)(2,1)S(1)} custom-call(s32[9]{0:T(128)S(1)} %stack.165.source_ref.facts_ref, bf16[4,2,512,2688]{3,2,1,0:T(8,128)(2,1)} %bitcast.73, bf16[1344,256]{1,0:T(8,128)(2,1)S(1)} %copy-done.13, bf16[1344,256]{1,0:T(8,128)(2,1)} %collective-permute-done.14.refs_1_, ...), custom_call_target="tpu_custom_call" | custom-call | flops 9846154240 | tf_op jit(solution)/shard_map/pallas_call | solution.py:117
  230.4 1.5 collective-permute-done.19.refs_3_
  232.0 13.0 %shard_map.102.refs_1_ = bf16[2048,256]{1,0:T(8,128)(2,1)S(1)} custom-call(s32[9]{0:T(128)S(1)} %stack.165.source_ref.facts_ref, bf16[4,2,512,2688]{3,2,1,0:T(8,128)(2,1)} %bitcast.74, bf16[1344,256]{1,0:T(8,128)(2,1)S(1)} %copy-done.11, bf16[1344,256]{1,0:T(8,128)(2,1)} %collective-permute-done.17.refs_1_, ...), custom_call_target="tpu_custom_call" | custom-call | flops 9846154240 | tf_op jit(solution)/shard_map/pallas_call | solution.py:117
  244.9 5.2 %collective-permute-done.20 = bf16[1024,512]{1,0:T(8,128)(2,1)S(1)} collective-permute-done((bf16[1024,512]{1,0:T(8,128)(2,1)S(1)}, bf16[1024,512]{1,0:T(8,128)(2,1)S(1)}, u32[]{:S(2)}, u32[]{:S(2)}) %collective-permute-start.20) | collective-permute-done | bytes 1048608 | tf_op jit(solution)/shard_map/ppermute | solution.py:391
  250.4 12.7 %shard_map.103.refs_0_ = bf16[1024,512]{1,0:T(8,128)(2,1)S(1)} custom-call(s32[2048,1]{1,0:T(8,128)S(1)} %copy-done.5, bf16[2048,256]{1,0:T(8,128)(2,1)S(1)} %shard_map.101.refs_0_, bf16[2048,256]{1,0:T(8,128)(2,1)S(1)} %shard_map.102.refs_1_, bf16[3072,512]{1,0:T(8,128)(2,1)S(1)} %pad_maximum_fusion.refs_2_), custom_call_target="tpu_custom_call" | custom-call | flops 14499999744 | tf_op jit(solution)/shard_map/pallas_call | solution.py:171
  263.9 13.1 %collective-permute-done.21.refs_5_ = bf16[336,2048]{1,0:T(8,128)(2,1)S(1)} collective-permute-done((bf16[336,2048]{1,0:T(8,128)(2,1)}, bf16[336,2048]{1,0:T(8,128)(2,1)S(1)}, u32[]{:S(2)}, u32[]{:S(2)}) %collective-permute-start.21) | collective-permute-done | bytes 1376288 | tf_op jit(solution)/shard_map/ppermute | solution.py:65
  277.0 2.4 collective-permute-start.25
  279.3 13.4 %shard_map.104.refs_0_ = bf16[1024,512]{1,0:T(8,128)(2,1)} custom-call(s32[2048,1]{1,0:T(8,128)S(1)} %copy-done.5, bf16[2048,256]{1,0:T(8,128)(2,1)S(1)} %shard_map.101.refs_0_, bf16[2048,256]{1,0:T(8,128)(2,1)S(1)} %shard_map.102.refs_1_, bf16[3072,512]{1,0:T(8,128)(2,1)S(1)} %pad_maximum_fusion.refs_2_), custom_call_target="tpu_custom_call" | custom-call | flops 14499999744 | tf_op jit(solution)/shard_map/pallas_call | solution.py:171
  294.0 2.9 collective-permute-done.24.refs_3_
  296.9 9.8 %collective-permute-done.25.refs_7_ = bf16[336,2048]{1,0:T(8,128)(2,1)S(1)} collective-permute-done((bf16[336,2048]{1,0:T(8,128)(2,1)S(1)}, bf16[336,2048]{1,0:T(8,128)(2,1)S(1)}, u32[]{:S(2)}, u32[]{:S(2)}) %collective-permute-start.25) | collective-permute-done | bytes 1376288 | tf_op jit(solution)/shard_map/ppermute | solution.py:65
  306.7 10.0 %shard_map.105 = (bf16[336,1024]{1,0:T(8,128)(2,1)S(1)}, bf16[336,1024]{1,0:T(8,128)(2,1)S(1)}, bf16[336,1024]{1,0:T(8,128)(2,1)S(1)}, bf16[336,1024]{1,0:T(8,128)(2,1)S(1)}) custom-call(s32[9]{0:T(128)S(1)} %stack.165.source_ref.facts_ref, bf16[1024,512]{1,0:T(8,128)(2,1)S(1)} %shard_map.103.refs_0_, bf16[1024,512]{1,0:T(8,128)(2,1)S(1)} %collective-permute-done.22.refs_1_, ...), custom_call_target="tpu_custom_call" | custom-call | flops 11600000000 | tf_op jit(solution)/shard_map/pallas_call | solution.py:213
  319.9 1.5 collective-permute-start.38
  325.0 10.6 %shard_map.106 = (bf16[336,1024]{1,0:T(8,128)(2,1)S(1)}, bf16[336,1024]{1,0:T(8,128)(2,1)S(1)}, bf16[336,1024]{1,0:T(8,128)(2,1)S(1)}, bf16[336,1024]{1,0:T(8,128)(2,1)S(1)}) custom-call(s32[9]{0:T(128)S(1)} %stack.165.source_ref.facts_ref, bf16[1024,512]{1,0:T(8,128)(2,1)} %shard_map.104.refs_0_, bf16[1024,512]{1,0:T(8,128)(2,1)} %collective-permute-done.26.refs_1_, ...), custom_call_target="tpu_custom_call" | custom-call | flops 11600000000 | tf_op jit(solution)/shard_map/pallas_call | solution.py:213
  336.2 1.6 collective-permute-start.33
  337.8 14.7 %collective-permute-done.38 = bf16[336,1024]{1,0:T(8,128)(2,1)S(1)} collective-permute-done((bf16[336,1024]{1,0:T(8,128)(2,1)}, bf16[336,1024]{1,0:T(8,128)(2,1)S(1)}, u32[]{:S(2)}, u32[]{:S(2)}) %collective-permute-start.38) | collective-permute-done | bytes 688160 | tf_op jit(solution)/shard_map/ppermute | solution.py:60
  353.5 1.7 collective-permute-start.41
  355.2 12.1 %collective-permute-done.29 = bf16[336,1024]{1,0:T(8,128)(2,1)S(1)} collective-permute-done((bf16[336,1024]{1,0:T(8,128)(2,1)S(1)}, bf16[336,1024]{1,0:T(8,128)(2,1)S(1)}, u32[]{:S(2)}, u32[]{:S(2)}) %collective-permute-start.29) | collective-permute-done | bytes 688160 | tf_op jit(solution)/shard_map/ppermute | solution.py:60
  367.9 1.7 collective-permute-start.32
  371.4 10.2 %collective-permute-done.33 = bf16[336,1024]{1,0:T(8,128)(2,1)S(1)} collective-permute-done((bf16[336,1024]{1,0:T(8,128)(2,1)S(1)}, bf16[336,1024]{1,0:T(8,128)(2,1)S(1)}, u32[]{:S(2)}, u32[]{:S(2)}) %collective-permute-start.33) | collective-permute-done | bytes 688160 | tf_op jit(solution)/shard_map/ppermute | solution.py:60
  382.3 1.7 collective-permute-start.36
  384.0 2.5 shard_map.108.refs_8_
  386.5 5.7 %collective-permute-done.36.refs_7_ = bf16[336,256]{1,0:T(8,128)(2,1)S(1)} collective-permute-done((bf16[336,256]{1,0:T(8,128)(2,1)S(1)}, bf16[336,256]{1,0:T(8,128)(2,1)S(1)}, u32[]{:S(2)}, u32[]{:S(2)}) %collective-permute-start.36) | collective-permute-done | bytes 172064 | tf_op jit(solution)/shard_map/ppermute | solution.py:56
  392.9 3.1 collective-permute-done.43.other_ref
  395.9 2.5 shard_map.110
  (156 shorter events, 34.9 us)
Async XLA Ops:
  6.5 165.0 %all-gather.3.cloned.1.call-start = ((), (), s32[]{:S(2)}) async-start(), calls=%async_computation | async-start | bytes 24772608 | tf_op jit(solution)/shard_map/all_gather | solution.py:359
  9.1 17.5 %collective-permute-start.4 = (bf16[2,336,512]{2,1,0:T(8,128)(2,1)}, bf16[2,336,512]{2,1,0:T(8,128)(2,1)}, u32[]{:S(2)}, u32[]{:S(2)}) collective-permute-start(bf16[2,336,512]{2,1,0:T(8,128)(2,1)} %pad_maximum_fusion.2), channel_id=1, source_target_pairs={{0,4},{2,6},{4,0},{6,2},{1,5},{3,7},{5,1},{7,3},{8,12},{10,14},{12... | collective-permute-start | bytes 2064392 | tf_op jit(solution)/shard_map/ppermute | solution.py:56
  10.7 4.0 collective-permute-start.2
  12.3 33.8 %collective-permute-start.3 = (bf16[336,2048]{1,0:T(8,128)(2,1)}, bf16[336,2048]{1,0:T(8,128)(2,1)}, u32[]{:S(2)}, u32[]{:S(2)}) collective-permute-start(bf16[336,2048]{1,0:T(8,128)(2,1)} %bitcast.14.refs_4_), channel_id=1, source_target_pairs={{0,8},{8,16},{16,24},{24,0},{1,9},{9,17},{17,25},{25,1},{2,10},{10... | collective-permute-start | bytes 4128776 | tf_op jit(solution)/shard_map/ppermute | solution.py:65
  29.1 2.5 collective-permute-start.5
  48.0 20.3 %collective-permute-start.6 = (bf16[1344,256]{1,0:T(8,128)(2,1)S(1)}, bf16[1344,256]{1,0:T(8,128)(2,1)}, u32[]{:S(2)}, u32[]{:S(2)}) collective-permute-start(bf16[1344,256]{1,0:T(8,128)(2,1)S(1)} %get-tuple-element.84.refs_0_), channel_id=1, source_target_pairs={{0,8},{8,16},{16,24},{24,0},{1,9},{9,17},{17,25},{25,1},{2,10},{10... | collective-permute-start | bytes 2064392 | tf_op jit(solution)/shard_map/ppermute | solution.py:65
  48.1 35.0 %collective-permute-start.9 = (bf16[1344,256]{1,0:T(8,128)(2,1)S(1)}, bf16[1344,256]{1,0:T(8,128)(2,1)}, u32[]{:S(2)}, u32[]{:S(2)}) collective-permute-start(bf16[1344,256]{1,0:T(8,128)(2,1)S(1)} %get-tuple-element.83.refs_4_), channel_id=1, source_target_pairs={{0,8},{8,16},{16,24},{24,0},{1,9},{9,17},{17,25},{25,1},{2,10},{10... | collective-permute-start | bytes 2064392 | tf_op jit(solution)/shard_map/ppermute | solution.py:65
  49.4 33.7 %collective-permute-start.12 = (bf16[2,336,512]{2,1,0:T(8,128)(2,1)S(1)}, bf16[2,336,512]{2,1,0:T(8,128)(2,1)S(1)}, u32[]{:S(2)}, u32[]{:S(2)}) collective-permute-start(bf16[2,336,512]{2,1,0:T(8,128)(2,1)S(1)} %pad_maximum_fusion.3), channel_id=1, source_target_pairs={{0,4},{2,6},{4,0},{6,2},{1,5},{3,7},{5,1},{7,3},{8,12},{10,14},{12... | collective-permute-start | bytes 2064392 | tf_op jit(solution)/shard_map/ppermute | solution.py:56
  68.4 29.5 %collective-permute-start.7 = (bf16[1344,256]{1,0:T(8,128)(2,1)}, bf16[1344,256]{1,0:T(8,128)(2,1)}, u32[]{:S(2)}, u32[]{:S(2)}) collective-permute-start(bf16[1344,256]{1,0:T(8,128)(2,1)} %collective-permute-done.6.refs_1_), channel_id=1, source_target_pairs={{0,8},{8,16},{16,24},{24,0},{1,9},{9,17},{17,25},{25,1},{2,10},{10... | collective-permute-start | bytes 2064392 | tf_op jit(solution)/shard_map/ppermute | solution.py:65
  83.1 29.5 %collective-permute-start.10 = (bf16[1344,256]{1,0:T(8,128)(2,1)}, bf16[1344,256]{1,0:T(8,128)(2,1)}, u32[]{:S(2)}, u32[]{:S(2)}) collective-permute-start(bf16[1344,256]{1,0:T(8,128)(2,1)} %collective-permute-done.9.refs_5_), channel_id=1, source_target_pairs={{0,8},{8,16},{16,24},{24,0},{1,9},{9,17},{17,25},{25,1},{2,10},{10... | collective-permute-start | bytes 2064392 | tf_op jit(solution)/shard_map/ppermute | solution.py:65
  84.6 28.0 %collective-permute-start.13 = (bf16[2,336,512]{2,1,0:T(8,128)(2,1)}, bf16[2,336,512]{2,1,0:T(8,128)(2,1)}, u32[]{:S(2)}, u32[]{:S(2)}) collective-permute-start(bf16[2,336,512]{2,1,0:T(8,128)(2,1)} %get-tuple-element.78), channel_id=1, source_target_pairs={{0,2},{2,0},{4,6},{6,4},{1,3},{3,1},{5,7},{7,5},{8,10},{10,8},{12,... | collective-permute-start | bytes 2064392 | tf_op jit(solution)/shard_map/ppermute | solution.py:56
  84.6 3.6 collective-permute-start
  88.2 1.2 collective-permute-start.1
  97.8 29.4 %collective-permute-start.8 = (bf16[1344,256]{1,0:T(8,128)(2,1)}, bf16[1344,256]{1,0:T(8,128)(2,1)S(1)}, u32[]{:S(2)}, u32[]{:S(2)}) collective-permute-start(bf16[1344,256]{1,0:T(8,128)(2,1)} %collective-permute-done.7.refs_2_), channel_id=1, source_target_pairs={{0,8},{8,16},{16,24},{24,0},{1,9},{9,17},{17,25},{25,1},{2,10},{10... | collective-permute-start | bytes 2064392 | tf_op jit(solution)/shard_map/ppermute | solution.py:65
  112.6 29.4 %collective-permute-start.11 = (bf16[1344,256]{1,0:T(8,128)(2,1)}, bf16[1344,256]{1,0:T(8,128)(2,1)S(1)}, u32[]{:S(2)}, u32[]{:S(2)}) collective-permute-start(bf16[1344,256]{1,0:T(8,128)(2,1)} %collective-permute-done.10.refs_6_), channel_id=1, source_target_pairs={{0,8},{8,16},{16,24},{24,0},{1,9},{9,17},{17,25},{25,1},{2,10},{10... | collective-permute-start | bytes 2064392 | tf_op jit(solution)/shard_map/ppermute | solution.py:65
  114.9 32.2 %copy-start.10 = (bf16[1344,256]{1,0:T(8,128)(2,1)}, bf16[1344,256]{1,0:T(8,128)(2,1)S(1)}, u32[]{:S(2)}) copy-start(bf16[1344,256]{1,0:T(8,128)(2,1)S(1)} %get-tuple-element.48.refs_0_) | copy-start | bytes 2064388
  114.9 32.2 %copy-start.12 = (bf16[1344,256]{1,0:T(8,128)(2,1)}, bf16[1344,256]{1,0:T(8,128)(2,1)S(1)}, u32[]{:S(2)}) copy-start(bf16[1344,256]{1,0:T(8,128)(2,1)S(1)} %get-tuple-element.46.refs_0_) | copy-start | bytes 2064388
  127.2 29.6 %collective-permute-start.14 = (bf16[1344,256]{1,0:T(8,128)(2,1)S(1)}, bf16[1344,256]{1,0:T(8,128)(2,1)}, u32[]{:S(2)}, u32[]{:S(2)}) collective-permute-start(bf16[1344,256]{1,0:T(8,128)(2,1)S(1)} %get-tuple-element.46.refs_0_), channel_id=1, source_target_pairs={{0,8},{8,16},{16,24},{24,0},{1,9},{9,17},{17,25},{25,1},{2,10},{10... | collective-permute-start | bytes 2064392 | tf_op jit(solution)/shard_map/ppermute | solution.py:65
  142.0 29.6 %collective-permute-start.17 = (bf16[1344,256]{1,0:T(8,128)(2,1)S(1)}, bf16[1344,256]{1,0:T(8,128)(2,1)}, u32[]{:S(2)}, u32[]{:S(2)}) collective-permute-start(bf16[1344,256]{1,0:T(8,128)(2,1)S(1)} %get-tuple-element.48.refs_0_), channel_id=1, source_target_pairs={{0,8},{8,16},{16,24},{24,0},{1,9},{9,17},{17,25},{25,1},{2,10},{10... | collective-permute-start | bytes 2064392 | tf_op jit(solution)/shard_map/ppermute | solution.py:65
  156.8 40.0 %collective-permute-start.15 = (bf16[1344,256]{1,0:T(8,128)(2,1)}, bf16[1344,256]{1,0:T(8,128)(2,1)}, u32[]{:S(2)}, u32[]{:S(2)}) collective-permute-start(bf16[1344,256]{1,0:T(8,128)(2,1)} %collective-permute-done.14.refs_1_), channel_id=1, source_target_pairs={{0,8},{8,16},{16,24},{24,0},{1,9},{9,17},{17,25},{25,1},{2,10},{10... | collective-permute-start | bytes 2064392 | tf_op jit(solution)/shard_map/ppermute | solution.py:65
  171.6 28.9 %collective-permute-start.18 = (bf16[1344,256]{1,0:T(8,128)(2,1)}, bf16[1344,256]{1,0:T(8,128)(2,1)}, u32[]{:S(2)}, u32[]{:S(2)}) collective-permute-start(bf16[1344,256]{1,0:T(8,128)(2,1)} %collective-permute-done.17.refs_1_), channel_id=1, source_target_pairs={{0,8},{8,16},{16,24},{24,0},{1,9},{9,17},{17,25},{25,1},{2,10},{10... | collective-permute-start | bytes 2064392 | tf_op jit(solution)/shard_map/ppermute | solution.py:65
  196.8 20.5 %collective-permute-start.16 = (bf16[1344,256]{1,0:T(8,128)(2,1)}, bf16[1344,256]{1,0:T(8,128)(2,1)}, u32[]{:S(2)}, u32[]{:S(2)}) collective-permute-start(bf16[1344,256]{1,0:T(8,128)(2,1)} %collective-permute-done.15.refs_2_), channel_id=1, source_target_pairs={{0,8},{8,16},{16,24},{24,0},{1,9},{9,17},{17,25},{25,1},{2,10},{10... | collective-permute-start | bytes 2064392 | tf_op jit(solution)/shard_map/ppermute | solution.py:65
  200.4 31.5 %collective-permute-start.19 = (bf16[1344,256]{1,0:T(8,128)(2,1)}, bf16[1344,256]{1,0:T(8,128)(2,1)S(1)}, u32[]{:S(2)}, u32[]{:S(2)}) collective-permute-start(bf16[1344,256]{1,0:T(8,128)(2,1)} %collective-permute-done.18.refs_2_), channel_id=1, source_target_pairs={{0,8},{8,16},{16,24},{24,0},{1,9},{9,17},{17,25},{25,1},{2,10},{10... | collective-permute-start | bytes 2064392 | tf_op jit(solution)/shard_map/ppermute | solution.py:65
  201.3 48.9 %collective-permute-start.20 = (bf16[1024,512]{1,0:T(8,128)(2,1)S(1)}, bf16[1024,512]{1,0:T(8,128)(2,1)S(1)}, u32[]{:S(2)}, u32[]{:S(2)}) collective-permute-start(bf16[1024,512]{1,0:T(8,128)(2,1)S(1)} %slice.24), channel_id=1, source_target_pairs={{0,8},{8,16},{16,24},{1,9},{9,17},{17,25},{2,10},{10,18},{18,26},{... | collective-permute-start | bytes 3145736 | tf_op jit(solution)/shard_map/ppermute | solution.py:391
  217.3 59.7 %collective-permute-start.21 = (bf16[336,2048]{1,0:T(8,128)(2,1)}, bf16[336,2048]{1,0:T(8,128)(2,1)S(1)}, u32[]{:S(2)}, u32[]{:S(2)}) collective-permute-start(bf16[336,2048]{1,0:T(8,128)(2,1)} %collective-permute-done.3.refs_6_), channel_id=1, source_target_pairs={{0,8},{8,16},{16,24},{24,0},{1,9},{9,17},{17,25},{25,1},{2,10},{10... | collective-permute-start | bytes 4128776 | tf_op jit(solution)/shard_map/ppermute | solution.py:65
  263.0 30.9 %collective-permute-start.22 = (bf16[1024,512]{1,0:T(8,128)(2,1)S(1)}, bf16[1024,512]{1,0:T(8,128)(2,1)S(1)}, u32[]{:S(2)}, u32[]{:S(2)}) collective-permute-start(bf16[1024,512]{1,0:T(8,128)(2,1)S(1)} %shard_map.103.refs_0_), channel_id=1, source_target_pairs={{0,2},{2,0},{4,6},{6,4},{1,3},{3,1},{5,7},{7,5},{8,10},{10,8},{12,... | collective-permute-start | bytes 3145736 | tf_op jit(solution)/shard_map/ppermute | solution.py:56
  263.1 29.6 %collective-permute-start.23 = (bf16[1024,512]{1,0:T(8,128)(2,1)S(1)}, bf16[1024,512]{1,0:T(8,128)(2,1)S(1)}, u32[]{:S(2)}, u32[]{:S(2)}) collective-permute-start(bf16[1024,512]{1,0:T(8,128)(2,1)S(1)} %shard_map.103.refs_0_), channel_id=1, source_target_pairs={{0,4},{2,6},{4,0},{6,2},{1,5},{3,7},{5,1},{7,3},{8,12},{10,14},{12... | collective-permute-start | bytes 3145736 | tf_op jit(solution)/shard_map/ppermute | solution.py:56
  277.0 29.7 %collective-permute-start.25 = (bf16[336,2048]{1,0:T(8,128)(2,1)S(1)}, bf16[336,2048]{1,0:T(8,128)(2,1)S(1)}, u32[]{:S(2)}, u32[]{:S(2)}) collective-permute-start(bf16[336,2048]{1,0:T(8,128)(2,1)S(1)} %collective-permute-done.21.refs_5_), channel_id=1, source_target_pairs={{0,8},{8,16},{16,24},{24,0},{1,9},{9,17},{17,25},{25,1},{2,10},{10... | collective-permute-start | bytes 4128776 | tf_op jit(solution)/shard_map/ppermute | solution.py:65
  292.7 4.1 %collective-permute-start.24 = (bf16[1024,512]{1,0:T(8,128)(2,1)S(1)}, bf16[1024,512]{1,0:T(8,128)(2,1)S(1)}, u32[]{:S(2)}, u32[]{:S(2)}) collective-permute-start(bf16[1024,512]{1,0:T(8,128)(2,1)S(1)} %collective-permute-done.23.refs_2_), channel_id=1, source_target_pairs={{0,2},{2,0},{4,6},{6,4},{1,3},{3,1},{5,7},{7,5},{8,10},{10,8},{12,... | collective-permute-start | bytes 3145736 | tf_op jit(solution)/shard_map/ppermute | solution.py:56
  292.7 28.7 %collective-permute-start.26 = (bf16[1024,512]{1,0:T(8,128)(2,1)}, bf16[1024,512]{1,0:T(8,128)(2,1)}, u32[]{:S(2)}, u32[]{:S(2)}) collective-permute-start(bf16[1024,512]{1,0:T(8,128)(2,1)} %shard_map.104.refs_0_), channel_id=1, source_target_pairs={{0,2},{2,0},{4,6},{6,4},{1,3},{3,1},{5,7},{7,5},{8,10},{10,8},{12,... | collective-permute-start | bytes 3145736 | tf_op jit(solution)/shard_map/ppermute | solution.py:56
  293.2 26.1 %collective-permute-start.27 = (bf16[1024,512]{1,0:T(8,128)(2,1)}, bf16[1024,512]{1,0:T(8,128)(2,1)}, u32[]{:S(2)}, u32[]{:S(2)}) collective-permute-start(bf16[1024,512]{1,0:T(8,128)(2,1)} %shard_map.104.refs_0_), channel_id=1, source_target_pairs={{0,4},{2,6},{4,0},{6,2},{1,5},{3,7},{5,1},{7,3},{8,12},{10,14},{12... | collective-permute-start | bytes 3145736 | tf_op jit(solution)/shard_map/ppermute | solution.py:56
  319.4 3.0 collective-permute-start.28
  319.4 18.4 %collective-permute-start.37 = (bf16[336,1024]{1,0:T(8,128)(2,1)}, bf16[336,1024]{1,0:T(8,128)(2,1)S(1)}, u32[]{:S(2)}, u32[]{:S(2)}) collective-permute-start(bf16[336,1024]{1,0:T(8,128)(2,1)} %copy-done.19), channel_id=1, source_target_pairs={{0,1},{1,0},{2,3},{3,2},{4,5},{5,4},{6,7},{7,6},{8,9},{9,8},{10,11... | collective-permute-start | bytes 2064392 | tf_op jit(solution)/shard_map/ppermute | solution.py:60
  319.9 32.7 %copy-start.9 = (bf16[336,1024]{1,0:T(8,128)(2,1)S(1)}, bf16[336,1024]{1,0:T(8,128)(2,1)}, u32[]{:S(2)}) copy-start(bf16[336,1024]{1,0:T(8,128)(2,1)} %copy-done.8) | copy-start | bytes 2064388
  319.9 32.7 %collective-permute-start.38 = (bf16[336,1024]{1,0:T(8,128)(2,1)}, bf16[336,1024]{1,0:T(8,128)(2,1)S(1)}, u32[]{:S(2)}, u32[]{:S(2)}) collective-permute-start(bf16[336,1024]{1,0:T(8,128)(2,1)} %copy-done.18), channel_id=1, source_target_pairs={{0,1},{1,0},{2,3},{3,2},{4,5},{5,4},{6,7},{7,6},{8,9},{9,8},{10,11... | collective-permute-start | bytes 2064392 | tf_op jit(solution)/shard_map/ppermute | solution.py:60
  335.7 31.6 %collective-permute-start.29 = (bf16[336,1024]{1,0:T(8,128)(2,1)S(1)}, bf16[336,1024]{1,0:T(8,128)(2,1)S(1)}, u32[]{:S(2)}, u32[]{:S(2)}) collective-permute-start(bf16[336,1024]{1,0:T(8,128)(2,1)S(1)} %get-tuple-element.59), channel_id=1, source_target_pairs={{0,1},{1,0},{2,3},{3,2},{4,5},{5,4},{6,7},{7,6},{8,9},{9,8},{10,11... | collective-permute-start | bytes 2064392 | tf_op jit(solution)/shard_map/ppermute | solution.py:60
  336.2 45.4 %collective-permute-start.33 = (bf16[336,1024]{1,0:T(8,128)(2,1)S(1)}, bf16[336,1024]{1,0:T(8,128)(2,1)S(1)}, u32[]{:S(2)}, u32[]{:S(2)}) collective-permute-start(bf16[336,1024]{1,0:T(8,128)(2,1)S(1)} %get-tuple-element.61), channel_id=1, source_target_pairs={{0,1},{1,0},{2,3},{3,2},{4,5},{5,4},{6,7},{7,6},{8,9},{9,8},{10,11... | collective-permute-start | bytes 2064392 | tf_op jit(solution)/shard_map/ppermute | solution.py:60
  353.2 14.5 %collective-permute-start.39 = (bf16[672,256]{1,0:T(8,128)(2,1)S(1)}, bf16[672,256]{1,0:T(8,128)(2,1)S(1)}, u32[]{:S(2)}, u32[]{:S(2)}) collective-permute-start(bf16[672,256]{1,0:T(8,128)(2,1)S(1)} %get-tuple-element.73), channel_id=1, source_target_pairs={{0,2},{2,0},{4,6},{6,4},{1,3},{3,1},{5,7},{7,5},{8,10},{10,8},{12,... | collective-permute-start | bytes 1032200 | tf_op jit(solution)/shard_map/ppermute | solution.py:56
  353.3 14.6 %collective-permute-start.40 = (bf16[672,256]{1,0:T(8,128)(2,1)S(1)}, bf16[672,256]{1,0:T(8,128)(2,1)S(1)}, u32[]{:S(2)}, u32[]{:S(2)}) collective-permute-start(bf16[672,256]{1,0:T(8,128)(2,1)S(1)} %get-tuple-element.74), channel_id=1, source_target_pairs={{0,4},{2,6},{4,0},{6,2},{1,5},{3,7},{5,1},{7,3},{8,12},{10,14},{12... | collective-permute-start | bytes 1032200 | tf_op jit(solution)/shard_map/ppermute | solution.py:56
  353.5 17.2 %collective-permute-start.41 = (bf16[672,256]{1,0:T(8,128)(2,1)S(1)}, bf16[672,256]{1,0:T(8,128)(2,1)S(1)}, u32[]{:S(2)}, u32[]{:S(2)}) collective-permute-start(bf16[672,256]{1,0:T(8,128)(2,1)S(1)} %get-tuple-element.71), channel_id=1, source_target_pairs={{0,6},{2,4},{4,2},{6,0},{1,7},{3,5},{5,3},{7,1},{8,14},{10,12},{12... | collective-permute-start | bytes 1032200 | tf_op jit(solution)/shard_map/ppermute | solution.py:56
  367.7 14.0 %collective-permute-start.30 = (bf16[336,256]{1,0:T(8,128)(2,1)S(1)}, bf16[336,256]{1,0:T(8,128)(2,1)S(1)}, u32[]{:S(2)}, u32[]{:S(2)}) collective-permute-start(bf16[336,256]{1,0:T(8,128)(2,1)S(1)} %get-tuple-element.93), channel_id=1, source_target_pairs={{0,2},{2,0},{4,6},{6,4},{1,3},{3,1},{5,7},{7,5},{8,10},{10,8},{12,... | collective-permute-start | bytes 516104 | tf_op jit(solution)/shard_map/ppermute | solution.py:56
  367.7 13.9 %collective-permute-start.31 = (bf16[336,256]{1,0:T(8,128)(2,1)S(1)}, bf16[336,256]{1,0:T(8,128)(2,1)S(1)}, u32[]{:S(2)}, u32[]{:S(2)}) collective-permute-start(bf16[336,256]{1,0:T(8,128)(2,1)S(1)} %get-tuple-element.92), channel_id=1, source_target_pairs={{0,4},{2,6},{4,0},{6,2},{1,5},{3,7},{5,1},{7,3},{8,12},{10,14},{12... | collective-permute-start | bytes 516104 | tf_op jit(solution)/shard_map/ppermute | solution.py:56
  367.9 13.8 %collective-permute-start.32 = (bf16[336,256]{1,0:T(8,128)(2,1)S(1)}, bf16[336,256]{1,0:T(8,128)(2,1)S(1)}, u32[]{:S(2)}, u32[]{:S(2)}) collective-permute-start(bf16[336,256]{1,0:T(8,128)(2,1)S(1)} %get-tuple-element.91), channel_id=1, source_target_pairs={{0,6},{2,4},{4,2},{6,0},{1,7},{3,5},{5,3},{7,1},{8,14},{10,12},{12... | collective-permute-start | bytes 516104 | tf_op jit(solution)/shard_map/ppermute | solution.py:56
  370.8 13.1 %collective-permute-start.42 = (f32[1,256]{1,0:T(1,128)S(1)}, f32[1,256]{1,0:T(1,128)S(1)}, u32[]{:S(2)}, u32[]{:S(2)}) collective-permute-start(f32[1,256]{1,0:T(1,128)S(1)} %shard_map.107.own_ref), channel_id=1, source_target_pairs={{0,1},{1,0},{2,3},{3,2},{4,5},{5,4},{6,7},{7,6},{8,9},{9,8},{10,11... | collective-permute-start | bytes 3080 | tf_op jit(solution)/shard_map/ppermute | solution.py:60
  382.0 10.1 %collective-permute-start.34 = (bf16[336,256]{1,0:T(8,128)(2,1)S(1)}, bf16[336,256]{1,0:T(8,128)(2,1)S(1)}, u32[]{:S(2)}, u32[]{:S(2)}) collective-permute-start(bf16[336,256]{1,0:T(8,128)(2,1)S(1)} %get-tuple-element.89), channel_id=1, source_target_pairs={{0,2},{2,0},{4,6},{6,4},{1,3},{3,1},{5,7},{7,5},{8,10},{10,8},{12,... | collective-permute-start | bytes 516104 | tf_op jit(solution)/shard_map/ppermute | solution.py:56
  382.1 10.0 %collective-permute-start.35 = (bf16[336,256]{1,0:T(8,128)(2,1)S(1)}, bf16[336,256]{1,0:T(8,128)(2,1)S(1)}, u32[]{:S(2)}, u32[]{:S(2)}) collective-permute-start(bf16[336,256]{1,0:T(8,128)(2,1)S(1)} %get-tuple-element.88), channel_id=1, source_target_pairs={{0,4},{2,6},{4,0},{6,2},{1,5},{3,7},{5,1},{7,3},{8,12},{10,14},{12... | collective-permute-start | bytes 516104 | tf_op jit(solution)/shard_map/ppermute | solution.py:56
  382.3 9.9 %collective-permute-start.36 = (bf16[336,256]{1,0:T(8,128)(2,1)S(1)}, bf16[336,256]{1,0:T(8,128)(2,1)S(1)}, u32[]{:S(2)}, u32[]{:S(2)}) collective-permute-start(bf16[336,256]{1,0:T(8,128)(2,1)S(1)} %get-tuple-element.87), channel_id=1, source_target_pairs={{0,6},{2,4},{4,2},{6,0},{1,7},{3,5},{5,3},{7,1},{8,14},{10,12},{12... | collective-permute-start | bytes 516104 | tf_op jit(solution)/shard_map/ppermute | solution.py:56
  392.3 3.6 collective-permute-start.43
  (27 other events, 210.0 us)
Sparse Core Ops, SparseCore 0:
  46.2 117.5 all-gather.2

commit v8 on v7

--- a/solution.py
+++ b/solution.py
@@ -177,7 +177,7 @@
         out_specs=pl.BlockSpec((QUERY_BLOCK, width), lambda b: (b, 0)),
         out_shape=jax.ShapeDtypeStruct((half, width), jnp.bfloat16),
         compiler_params=pltpu.CompilerParams(vmem_limit_bytes=20 * MIB),
-        cost_estimate=lasting(14.5),
+        cost_estimate=lasting(0.1 if part else 14.5),
     )(position, *queries, all_kv)
 
 
@@ -219,7 +219,7 @@
         out_specs=[pl.BlockSpec((cols, TOKEN_BLOCK), lambda b: (0, b))] * len(weights),
         out_shape=[shape] * len(weights),
         compiler_params=pltpu.CompilerParams(vmem_limit_bytes=24 * MIB),
-        cost_estimate=lasting(2.9 * len(weights)),
+        cost_estimate=lasting(5.8 if pairs == (1,) else 0.1),
     )(facts, *attended, *weights)
     return outs[::2], outs[1::2]
 
@@ -347,7 +347,7 @@
         previous.append(hops[name][-1])
 
     hop("o")
-    values = inputs.astype(jnp.float32)
+    values = after(inputs, kv_on_way[1]).astype(jnp.float32)
     squares = jnp.sum(values * values, axis=-1)
     scale = lax.rsqrt((squares + swap_tp(squares)) / MODEL_WIDTH + EPS)
     gain = lax.dynamic_slice_in_dim(in_gain, side * inputs.shape[1], inputs.shape[1])
@@ -406,12 +406,13 @@
     for part in range(2):
         far = swap(own[part], 2)
         first = after(own[0], own[1]) if part == 0 else after(own[1], keeps[-1])
-        across = after(far, own[1] if part == 0 else keeps[-1])
+        across = after(far, *([own[1]] if part == 0 else [keeps[-1], arrived[0]]))
         attended = [first, swap(own[part], 1), far, swap(across, 1)]
-        for pairs in [range(per_side)]:
+        for pairs in [[n] for n in range(per_side)] if part == 0 else [range(per_side)]:
             kept_terms, given_terms = group_product(facts, attended, hops["o"], tuple(pairs))
             keeps += kept_terms
             arrived += [swap_tp(term) for term in given_terms]
+            attended = [after(attended[0], keeps[-1]), *attended[1:]]
 
     def to_tokens(total):
         blocks = []

time: 407 us -> 393 us (0.966)
  waiting for transfers between devices: 226 us -> 202 us
  starting transfers between devices: 28.2 us -> 35 us
    ppermute x7, waiting for transfers between devices: 40.2 us -> 24.6 us  [swap_tp(): return lax.ppermute(x, 'tp', [(0, 1), (1, 0)])]
    ppermute x15, waiting for transfers between devices: 154 us -> 143 us  [ring_step(): return lax.ppermute(x, 'z', [(c, (c + 1) % size) for c in range(size)])]
    pallas_call x2 -> x3, Pallas kernels: 20.6 us -> 22.4 us  [group_product(): pl.pallas_call(functools.partial(group_kernel, len(attended), len(blocks)...]
  transfers between devices with their start and end apart: 45 -> 45, of which waited for: 27 -> 27; matrix products, arithmetic and copies ran while one was open for 6% -> 7% of each run, Pallas kernels for 23% -> 25%
where the time goes in v8:
time: 393 us; the launch traced here: 390 us
  waiting for transfers between devices  202 us (51%)
  Pallas kernels  99.5 us (25%)
  starting transfers between devices  35 us (9%)
  local copies, waits for them, and re-layouts  20.5 us (5%)
  other arithmetic  19.1 us (5%)
  between operations  13.9 us (4%)
    ppermute x15, waiting for transfers between devices, ring_step(): return lax.ppermute(x, 'z', [(c, (c + 1) % size) for c in range(size)])  143 us
    pallas_call x3, Pallas kernels, project(): pl.pallas_call(functools.partial(project_kernel, factor, turned_groups *...  45.4 us
    ppermute x21, waiting for transfers between devices, swap(): return lax.ppermute(x, 'i', [(c, c ^ mask) for c in range(INNER)])  29.1 us
    pallas_call x2, Pallas kernels, attend(): pl.pallas_call(functools.partial(attend_kernel, part), grid=(half // QUER...  26.5 us
    ppermute x7, waiting for transfers between devices, swap_tp(): return lax.ppermute(x, 'tp', [(0, 1), (1, 0)])  24.6 us
    pallas_call x3, Pallas kernels, group_product(): pl.pallas_call(functools.partial(group_kernel, len(attended), len(blocks)...  22.4 us
    ppermute x21, starting transfers between devices, swap(): return lax.ppermute(x, 'i', [(c, c ^ mask) for c in range(INNER)])  12.5 us
    unnamed x61, local copies, waits for them, and re-layouts  10.6 us
  transfers between devices with their start and end apart: 45, of which 27 were waited for; matrix products, arithmetic and copies ran while one was open for 7% of the time, Pallas kernels for 25%

profile of v8, /device:TPU:2, one launch (start us, length us, event | category | flops | bytes accessed | tf_op | source)
XLA Modules:
  0.0 390.1 jit_solution(9940047651040793925)
XLA Ops:
  6.5 2.3 constant_dynamic-slice_fusion.10
  9.8 2.1 collective-permute-start.4
  14.3 12.9 %collective-permute-done.2 = bf16[2,336,512]{2,1,0:T(8,128)(2,1)S(1)} collective-permute-done((bf16[2,336,512]{2,1,0:T(8,128)(2,1)}, bf16[2,336,512]{2,1,0:T(8,128)(2,1)S(1)}, u32[]{:S(2)}, u32[]{:S(2)}) %collective-permute-start.2) | collective-permute-done | bytes 688160 | tf_op jit(solution)/shard_map/ppermute | solution.py:56
  27.8 1.6 collective-permute-start.3
  31.5 2.2 fusion.2
  33.7 2.7 maximum_select_fusion.1
  36.4 7.7 %collective-permute-done.4.refs_4_.refs_6_ = bf16[336,2048]{1,0:T(8,128)(2,1)} collective-permute-done((bf16[336,2048]{1,0:T(8,128)(2,1)}, bf16[336,2048]{1,0:T(8,128)(2,1)}, u32[]{:S(2)}, u32[]{:S(2)}) %collective-permute-start.4) | collective-permute-done | bytes 1376288 | tf_op jit(solution)/shard_map/ppermute | solution.py:65
  47.5 1.6 collective-permute-start.12
  49.1 17.3 %collective-permute-done.6.refs_1_ = bf16[1344,256]{1,0:T(8,128)(2,1)} collective-permute-done((bf16[1344,256]{1,0:T(8,128)(2,1)S(1)}, bf16[1344,256]{1,0:T(8,128)(2,1)}, u32[]{:S(2)}, u32[]{:S(2)}) %collective-permute-start.6) | collective-permute-done | bytes 688160 | tf_op jit(solution)/shard_map/ppermute | solution.py:65
  66.4 14.7 %collective-permute-done.9.refs_5_ = bf16[1344,256]{1,0:T(8,128)(2,1)} collective-permute-done((bf16[1344,256]{1,0:T(8,128)(2,1)S(1)}, bf16[1344,256]{1,0:T(8,128)(2,1)}, u32[]{:S(2)}, u32[]{:S(2)}) %collective-permute-start.9) | collective-permute-done | bytes 688160 | tf_op jit(solution)/shard_map/ppermute | solution.py:65
  84.2 2.0 collective-permute-done
  87.5 8.4 %collective-permute-done.7.refs_2_ = bf16[1344,256]{1,0:T(8,128)(2,1)} collective-permute-done((bf16[1344,256]{1,0:T(8,128)(2,1)}, bf16[1344,256]{1,0:T(8,128)(2,1)}, u32[]{:S(2)}, u32[]{:S(2)}) %collective-permute-start.7) | collective-permute-done | bytes 688160 | tf_op jit(solution)/shard_map/ppermute | solution.py:65
  95.9 14.7 %collective-permute-done.10.refs_6_ = bf16[1344,256]{1,0:T(8,128)(2,1)} collective-permute-done((bf16[1344,256]{1,0:T(8,128)(2,1)}, bf16[1344,256]{1,0:T(8,128)(2,1)}, u32[]{:S(2)}, u32[]{:S(2)}) %collective-permute-start.10) | collective-permute-done | bytes 688160 | tf_op jit(solution)/shard_map/ppermute | solution.py:65
  110.7 2.1 maximum_select_fusion.3
  112.9 12.4 %collective-permute-done.8.refs_3_ = bf16[1344,256]{1,0:T(8,128)(2,1)S(1)} collective-permute-done((bf16[1344,256]{1,0:T(8,128)(2,1)}, bf16[1344,256]{1,0:T(8,128)(2,1)S(1)}, u32[]{:S(2)}, u32[]{:S(2)}) %collective-permute-start.8) | collective-permute-done | bytes 688160 | tf_op jit(solution)/shard_map/ppermute | solution.py:65
  125.3 14.7 %collective-permute-done.11.refs_7_ = bf16[1344,256]{1,0:T(8,128)(2,1)S(1)} collective-permute-done((bf16[1344,256]{1,0:T(8,128)(2,1)}, bf16[1344,256]{1,0:T(8,128)(2,1)S(1)}, u32[]{:S(2)}, u32[]{:S(2)}) %collective-permute-start.11) | collective-permute-done | bytes 688160 | tf_op jit(solution)/shard_map/ppermute | solution.py:65
  140.0 3.7 multiply_cosine_fusion
  145.2 9.7 %collective-permute-done.14.refs_1_ = bf16[1344,256]{1,0:T(8,128)(2,1)} collective-permute-done((bf16[1344,256]{1,0:T(8,128)(2,1)S(1)}, bf16[1344,256]{1,0:T(8,128)(2,1)}, u32[]{:S(2)}, u32[]{:S(2)}) %collective-permute-start.14) | collective-permute-done | bytes 688160 | tf_op jit(solution)/shard_map/ppermute | solution.py:65
  154.9 14.7 %collective-permute-done.17.refs_1_ = bf16[1344,256]{1,0:T(8,128)(2,1)} collective-permute-done((bf16[1344,256]{1,0:T(8,128)(2,1)S(1)}, bf16[1344,256]{1,0:T(8,128)(2,1)}, u32[]{:S(2)}, u32[]{:S(2)}) %collective-permute-start.17) | collective-permute-done | bytes 688160 | tf_op jit(solution)/shard_map/ppermute | solution.py:65
  174.2 19.4 %shard_map.100 = bf16[2048,512]{1,0:T(8,128)(2,1)S(1)} custom-call(s32[9]{0:T(128)S(1)} %stack.165.source_ref.facts_ref, bf16[4,2,512,2688]{3,2,1,0:T(8,128)(2,1)} %bitcast.73, bf16[1344,256]{1,0:T(8,128)(2,1)S(1)} %copy-done.11, bf16[1344,256]{1,0:T(8,128)(2,1)} %collective-permute-done.6.refs_1_, bf16[1344,256]{1,0:T(8,128)(2,1)} %collective-permute-done.7.refs_2_, ...), custom_call_target="tpu_custom_call" | custom-call | flops 9846154240 | tf_op jit(solution)/shard_map/pallas_call | solution.py:117
  194.9 1.9 broadcast_in_dim_reshape.5.pos_ref
  199.3 5.8 %collective-permute-start.20 = (bf16[1024,512]{1,0:T(8,128)(2,1)S(1)}, bf16[1024,512]{1,0:T(8,128)(2,1)S(1)}, u32[]{:S(2)}, u32[]{:S(2)}) collective-permute-start(bf16[1024,512]{1,0:T(8,128)(2,1)S(1)} %slice.24), channel_id=1, source_target_pairs={{0,8},{8,16},{16,24},{1,9},{9,17},{17,25},{2,10},{10,18},{18,26},{... | collective-permute-start | bytes 3145736 | tf_op jit(solution)/shard_map/ppermute | solution.py:391
  205.2 10.2 %collective-permute-done.16.refs_3_ = bf16[1344,256]{1,0:T(8,128)(2,1)} collective-permute-done((bf16[1344,256]{1,0:T(8,128)(2,1)}, bf16[1344,256]{1,0:T(8,128)(2,1)}, u32[]{:S(2)}, u32[]{:S(2)}) %collective-permute-start.16) | collective-permute-done | bytes 688160 | tf_op jit(solution)/shard_map/ppermute | solution.py:65
  215.4 13.1 %shard_map.101.refs_0_ = bf16[2048,256]{1,0:T(8,128)(2,1)S(1)} custom-call(s32[9]{0:T(128)S(1)} %stack.165.source_ref.facts_ref, bf16[4,2,512,2688]{3,2,1,0:T(8,128)(2,1)} %bitcast.74, bf16[1344,256]{1,0:T(8,128)(2,1)S(1)} %copy-done.17, bf16[1344,256]{1,0:T(8,128)(2,1)} %collective-permute-done.14.refs_1_, ...), custom_call_target="tpu_custom_call" | custom-call | flops 9846154240 | tf_op jit(solution)/shard_map/pallas_call | solution.py:117
  230.0 13.0 %shard_map.102.refs_1_ = bf16[2048,256]{1,0:T(8,128)(2,1)S(1)} custom-call(s32[9]{0:T(128)S(1)} %stack.165.source_ref.facts_ref, bf16[4,2,512,2688]{3,2,1,0:T(8,128)(2,1)} %bitcast.75, bf16[1344,256]{1,0:T(8,128)(2,1)S(1)} %copy-done.15, bf16[1344,256]{1,0:T(8,128)(2,1)} %collective-permute-done.17.refs_1_, ...), custom_call_target="tpu_custom_call" | custom-call | flops 9846154240 | tf_op jit(solution)/shard_map/pallas_call | solution.py:117
  243.0 5.2 %collective-permute-done.20 = bf16[1024,512]{1,0:T(8,128)(2,1)S(1)} collective-permute-done((bf16[1024,512]{1,0:T(8,128)(2,1)S(1)}, bf16[1024,512]{1,0:T(8,128)(2,1)S(1)}, u32[]{:S(2)}, u32[]{:S(2)}) %collective-permute-start.20) | collective-permute-done | bytes 1048608 | tf_op jit(solution)/shard_map/ppermute | solution.py:391
  248.4 12.9 %shard_map.103.refs_0_ = bf16[1024,512]{1,0:T(8,128)(2,1)S(1)} custom-call(s32[2048,1]{1,0:T(8,128)S(1)} %copy-done.5, bf16[2048,256]{1,0:T(8,128)(2,1)S(1)} %shard_map.101.refs_0_, bf16[2048,256]{1,0:T(8,128)(2,1)S(1)} %shard_map.102.refs_1_, bf16[3072,512]{1,0:T(8,128)(2,1)S(1)} %pad_maximum_fusion.refs_2_), custom_call_target="tpu_custom_call" | custom-call | flops 14499999744 | tf_op jit(solution)/shard_map/pallas_call | solution.py:171
  261.3 1.6 collective-permute-start.23
  262.9 12.2 %collective-permute-done.21.refs_5_ = bf16[336,2048]{1,0:T(8,128)(2,1)S(1)} collective-permute-done((bf16[336,2048]{1,0:T(8,128)(2,1)}, bf16[336,2048]{1,0:T(8,128)(2,1)S(1)}, u32[]{:S(2)}, u32[]{:S(2)}) %collective-permute-start.21) | collective-permute-done | bytes 1376288 | tf_op jit(solution)/shard_map/ppermute | solution.py:65
  275.0 2.4 collective-permute-start.25
  277.4 13.6 %shard_map.104.refs_0_ = bf16[1024,512]{1,0:T(8,128)(2,1)} custom-call(s32[2048,1]{1,0:T(8,128)S(1)} %copy-done.5, bf16[2048,256]{1,0:T(8,128)(2,1)S(1)} %shard_map.101.refs_0_, bf16[2048,256]{1,0:T(8,128)(2,1)S(1)} %shard_map.102.refs_1_, bf16[3072,512]{1,0:T(8,128)(2,1)S(1)} %pad_maximum_fusion.refs_2_), custom_call_target="tpu_custom_call" | custom-call | flops 100000000 | tf_op jit(solution)/shard_map/pallas_call | solution.py:171
  293.8 5.2 %shard_map.105 = (bf16[336,1024]{1,0:T(8,128)(2,1)S(1)}, bf16[336,1024]{1,0:T(8,128)(2,1)S(1)}) custom-call(s32[9]{0:T(128)S(1)} %stack.165.source_ref.facts_ref, bf16[1024,512]{1,0:T(8,128)(2,1)S(1)} %shard_map.103.refs_0_, bf16[1024,512]{1,0:T(8,128)(2,1)S(1)} %collective-permute-done.22.refs_1_, bf16[1024,512]{1,0:T(8,128)(2,1)S(1)} %collective-permute-done.23.refs_2_, ...), custom_call_target="tpu_custom_call" | custom-call | flops 100000000 | tf_op jit(solution)/shard_map/pallas_call | solution.py:213
  299.0 1.6 collective-permute-start.28
  300.7 4.5 %collective-permute-done.25.refs_5_.refs_7_ = bf16[336,2048]{1,0:T(8,128)(2,1)S(1)} collective-permute-done((bf16[336,2048]{1,0:T(8,128)(2,1)S(1)}, bf16[336,2048]{1,0:T(8,128)(2,1)S(1)}, u32[]{:S(2)}, u32[]{:S(2)}) %collective-permute-start.25) | collective-permute-done | bytes 1376288 | tf_op jit(solution)/shard_map/ppermute | solution.py:65
  305.3 6.5 %shard_map.106 = (bf16[336,1024]{1,0:T(8,128)(2,1)S(1)}, bf16[336,1024]{1,0:T(8,128)(2,1)}) custom-call(s32[9]{0:T(128)S(1)} %stack.165.source_ref.facts_ref, bf16[1024,512]{1,0:T(8,128)(2,1)S(1)} %shard_map.103.refs_0_, bf16[1024,512]{1,0:T(8,128)(2,1)S(1)} %collective-permute-done.22.refs_1_, bf16[1024,512]{1,0:T(8,128)(2,1)S(1)} %collective-permute-done.23.refs_2_, ...), custom_call_target="tpu_custom_call" | custom-call | flops 5800000000 | tf_op jit(solution)/shard_map/pallas_call | solution.py:213
  312.6 4.3 %collective-permute-done.27.refs_2_ = bf16[1024,512]{1,0:T(8,128)(2,1)} collective-permute-done((bf16[1024,512]{1,0:T(8,128)(2,1)}, bf16[1024,512]{1,0:T(8,128)(2,1)}, u32[]{:S(2)}, u32[]{:S(2)}) %collective-permute-start.27) | collective-permute-done | bytes 1048608 | tf_op jit(solution)/shard_map/ppermute | solution.py:56
  323.5 10.7 %shard_map.107 = (bf16[336,1024]{1,0:T(8,128)(2,1)S(1)}, bf16[336,1024]{1,0:T(8,128)(2,1)S(1)}, bf16[336,1024]{1,0:T(8,128)(2,1)S(1)}, bf16[336,1024]{1,0:T(8,128)(2,1)S(1)}) custom-call(s32[9]{0:T(128)S(1)} %stack.165.source_ref.facts_ref, bf16[1024,512]{1,0:T(8,128)(2,1)} %shard_map.104.refs_0_, bf16[1024,512]{1,0:T(8,128)(2,1)} %collective-permute-done.26.refs_1_, ...), custom_call_target="tpu_custom_call" | custom-call | flops 100000000 | tf_op jit(solution)/shard_map/pallas_call | solution.py:213
  334.2 1.6 collective-permute-start.30
  338.2 1.6 collective-permute-start.40
  340.0 12.5 %collective-permute-done.30 = bf16[336,1024]{1,0:T(8,128)(2,1)S(1)} collective-permute-done((bf16[336,1024]{1,0:T(8,128)(2,1)S(1)}, bf16[336,1024]{1,0:T(8,128)(2,1)S(1)}, u32[]{:S(2)}, u32[]{:S(2)}) %collective-permute-start.30) | collective-permute-done | bytes 688160 | tf_op jit(solution)/shard_map/ppermute | solution.py:60
  355.7 1.6 collective-permute-start.42
  357.3 9.2 %collective-permute-done.34 = bf16[336,1024]{1,0:T(8,128)(2,1)S(1)} collective-permute-done((bf16[336,1024]{1,0:T(8,128)(2,1)S(1)}, bf16[336,1024]{1,0:T(8,128)(2,1)S(1)}, u32[]{:S(2)}, u32[]{:S(2)}) %collective-permute-start.34) | collective-permute-done | bytes 688160 | tf_op jit(solution)/shard_map/ppermute | solution.py:60
  366.9 1.6 collective-permute-start.36
  368.8 2.5 shard_map.109.refs_8_
  371.3 5.7 %collective-permute-done.37.refs_7_ = bf16[336,256]{1,0:T(8,128)(2,1)S(1)} collective-permute-done((bf16[336,256]{1,0:T(8,128)(2,1)S(1)}, bf16[336,256]{1,0:T(8,128)(2,1)S(1)}, u32[]{:S(2)}, u32[]{:S(2)}) %collective-permute-start.37) | collective-permute-done | bytes 172064 | tf_op jit(solution)/shard_map/ppermute | solution.py:56
  377.1 1.6 collective-permute-start.43
  378.7 2.0 collective-permute-done.43.other_ref
  380.7 2.5 shard_map.111
  (157 shorter events, 42.2 us)
Async XLA Ops:
  6.5 163.1 %all-gather.3.cloned.1.call-start = ((), (), s32[]{:S(2)}) async-start(), calls=%async_computation | async-start | bytes 24772608 | tf_op jit(solution)/shard_map/all_gather | solution.py:359
  9.8 17.4 %collective-permute-start.2 = (bf16[2,336,512]{2,1,0:T(8,128)(2,1)}, bf16[2,336,512]{2,1,0:T(8,128)(2,1)S(1)}, u32[]{:S(2)}, u32[]{:S(2)}) collective-permute-start(bf16[2,336,512]{2,1,0:T(8,128)(2,1)} %pad_maximum_fusion.2), channel_id=1, source_target_pairs={{0,4},{2,6},{4,0},{6,2},{1,5},{3,7},{5,1},{7,3},{8,12},{10,14},{12... | collective-permute-start | bytes 2064392 | tf_op jit(solution)/shard_map/ppermute | solution.py:56
  9.8 34.3 %collective-permute-start.4 = (bf16[336,2048]{1,0:T(8,128)(2,1)}, bf16[336,2048]{1,0:T(8,128)(2,1)}, u32[]{:S(2)}, u32[]{:S(2)}) collective-permute-start(bf16[336,2048]{1,0:T(8,128)(2,1)} %bitcast.16.refs_4_), channel_id=1, source_target_pairs={{0,8},{8,16},{16,24},{24,0},{1,9},{9,17},{17,25},{25,1},{2,10},{10... | collective-permute-start | bytes 4128776 | tf_op jit(solution)/shard_map/ppermute | solution.py:65
  27.8 3.6 collective-permute-start.3
  30.6 3.1 collective-permute-start.5
  46.1 20.3 %collective-permute-start.6 = (bf16[1344,256]{1,0:T(8,128)(2,1)S(1)}, bf16[1344,256]{1,0:T(8,128)(2,1)}, u32[]{:S(2)}, u32[]{:S(2)}) collective-permute-start(bf16[1344,256]{1,0:T(8,128)(2,1)S(1)} %get-tuple-element.88.refs_0_), channel_id=1, source_target_pairs={{0,8},{8,16},{16,24},{24,0},{1,9},{9,17},{17,25},{25,1},{2,10},{10... | collective-permute-start | bytes 2064392 | tf_op jit(solution)/shard_map/ppermute | solution.py:65
  46.2 35.0 %collective-permute-start.9 = (bf16[1344,256]{1,0:T(8,128)(2,1)S(1)}, bf16[1344,256]{1,0:T(8,128)(2,1)}, u32[]{:S(2)}, u32[]{:S(2)}) collective-permute-start(bf16[1344,256]{1,0:T(8,128)(2,1)S(1)} %get-tuple-element.87.refs_4_), channel_id=1, source_target_pairs={{0,8},{8,16},{16,24},{24,0},{1,9},{9,17},{17,25},{25,1},{2,10},{10... | collective-permute-start | bytes 2064392 | tf_op jit(solution)/shard_map/ppermute | solution.py:65
  47.5 33.7 %collective-permute-start.12 = (bf16[2,336,512]{2,1,0:T(8,128)(2,1)S(1)}, bf16[2,336,512]{2,1,0:T(8,128)(2,1)S(1)}, u32[]{:S(2)}, u32[]{:S(2)}) collective-permute-start(bf16[2,336,512]{2,1,0:T(8,128)(2,1)S(1)} %pad_maximum_fusion.3), channel_id=1, source_target_pairs={{0,4},{2,6},{4,0},{6,2},{1,5},{3,7},{5,1},{7,3},{8,12},{10,14},{12... | collective-permute-start | bytes 2064392 | tf_op jit(solution)/shard_map/ppermute | solution.py:56
  66.4 29.5 %collective-permute-start.7 = (bf16[1344,256]{1,0:T(8,128)(2,1)}, bf16[1344,256]{1,0:T(8,128)(2,1)}, u32[]{:S(2)}, u32[]{:S(2)}) collective-permute-start(bf16[1344,256]{1,0:T(8,128)(2,1)} %collective-permute-done.6.refs_1_), channel_id=1, source_target_pairs={{0,8},{8,16},{16,24},{24,0},{1,9},{9,17},{17,25},{25,1},{2,10},{10... | collective-permute-start | bytes 2064392 | tf_op jit(solution)/shard_map/ppermute | solution.py:65
  81.2 29.5 %collective-permute-start.10 = (bf16[1344,256]{1,0:T(8,128)(2,1)}, bf16[1344,256]{1,0:T(8,128)(2,1)}, u32[]{:S(2)}, u32[]{:S(2)}) collective-permute-start(bf16[1344,256]{1,0:T(8,128)(2,1)} %collective-permute-done.9.refs_5_), channel_id=1, source_target_pairs={{0,8},{8,16},{16,24},{24,0},{1,9},{9,17},{17,25},{25,1},{2,10},{10... | collective-permute-start | bytes 2064392 | tf_op jit(solution)/shard_map/ppermute | solution.py:65
  82.6 28.0 %collective-permute-start.13 = (bf16[2,336,512]{2,1,0:T(8,128)(2,1)}, bf16[2,336,512]{2,1,0:T(8,128)(2,1)}, u32[]{:S(2)}, u32[]{:S(2)}) collective-permute-start(bf16[2,336,512]{2,1,0:T(8,128)(2,1)} %get-tuple-element.82), channel_id=1, source_target_pairs={{0,2},{2,0},{4,6},{6,4},{1,3},{3,1},{5,7},{7,5},{8,10},{10,8},{12,... | collective-permute-start | bytes 2064392 | tf_op jit(solution)/shard_map/ppermute | solution.py:56
  82.7 3.6 collective-permute-start
  86.3 1.2 collective-permute-start.1
  95.9 29.4 %collective-permute-start.8 = (bf16[1344,256]{1,0:T(8,128)(2,1)}, bf16[1344,256]{1,0:T(8,128)(2,1)S(1)}, u32[]{:S(2)}, u32[]{:S(2)}) collective-permute-start(bf16[1344,256]{1,0:T(8,128)(2,1)} %collective-permute-done.7.refs_2_), channel_id=1, source_target_pairs={{0,8},{8,16},{16,24},{24,0},{1,9},{9,17},{17,25},{25,1},{2,10},{10... | collective-permute-start | bytes 2064392 | tf_op jit(solution)/shard_map/ppermute | solution.py:65
  110.7 29.4 %collective-permute-start.11 = (bf16[1344,256]{1,0:T(8,128)(2,1)}, bf16[1344,256]{1,0:T(8,128)(2,1)S(1)}, u32[]{:S(2)}, u32[]{:S(2)}) collective-permute-start(bf16[1344,256]{1,0:T(8,128)(2,1)} %collective-permute-done.10.refs_6_), channel_id=1, source_target_pairs={{0,8},{8,16},{16,24},{24,0},{1,9},{9,17},{17,25},{25,1},{2,10},{10... | collective-permute-start | bytes 2064392 | tf_op jit(solution)/shard_map/ppermute | solution.py:65
  112.9 32.2 %copy-start.14 = (bf16[1344,256]{1,0:T(8,128)(2,1)}, bf16[1344,256]{1,0:T(8,128)(2,1)S(1)}, u32[]{:S(2)}) copy-start(bf16[1344,256]{1,0:T(8,128)(2,1)S(1)} %get-tuple-element.51.refs_0_) | copy-start | bytes 2064388
  112.9 32.2 %copy-start.16 = (bf16[1344,256]{1,0:T(8,128)(2,1)}, bf16[1344,256]{1,0:T(8,128)(2,1)S(1)}, u32[]{:S(2)}) copy-start(bf16[1344,256]{1,0:T(8,128)(2,1)S(1)} %get-tuple-element.49.refs_0_) | copy-start | bytes 2064388
  125.3 29.6 %collective-permute-start.14 = (bf16[1344,256]{1,0:T(8,128)(2,1)S(1)}, bf16[1344,256]{1,0:T(8,128)(2,1)}, u32[]{:S(2)}, u32[]{:S(2)}) collective-permute-start(bf16[1344,256]{1,0:T(8,128)(2,1)S(1)} %get-tuple-element.49.refs_0_), channel_id=1, source_target_pairs={{0,8},{8,16},{16,24},{24,0},{1,9},{9,17},{17,25},{25,1},{2,10},{10... | collective-permute-start | bytes 2064392 | tf_op jit(solution)/shard_map/ppermute | solution.py:65
  140.0 29.6 %collective-permute-start.17 = (bf16[1344,256]{1,0:T(8,128)(2,1)S(1)}, bf16[1344,256]{1,0:T(8,128)(2,1)}, u32[]{:S(2)}, u32[]{:S(2)}) collective-permute-start(bf16[1344,256]{1,0:T(8,128)(2,1)S(1)} %get-tuple-element.51.refs_0_), channel_id=1, source_target_pairs={{0,8},{8,16},{16,24},{24,0},{1,9},{9,17},{17,25},{25,1},{2,10},{10... | collective-permute-start | bytes 2064392 | tf_op jit(solution)/shard_map/ppermute | solution.py:65
  143.7 25.9 %copy-start.22 = (f32[128]{0:T(128)S(1)}, f32[128]{0:T(128)}, u32[]{:S(2)}) copy-start(f32[128]{0:T(128)} %param.17) | copy-start | bytes 1540
  154.9 40.0 %collective-permute-start.15 = (bf16[1344,256]{1,0:T(8,128)(2,1)}, bf16[1344,256]{1,0:T(8,128)(2,1)}, u32[]{:S(2)}, u32[]{:S(2)}) collective-permute-start(bf16[1344,256]{1,0:T(8,128)(2,1)} %collective-permute-done.14.refs_1_), channel_id=1, source_target_pairs={{0,8},{8,16},{16,24},{24,0},{1,9},{9,17},{17,25},{25,1},{2,10},{10... | collective-permute-start | bytes 2064392 | tf_op jit(solution)/shard_map/ppermute | solution.py:65
  169.6 28.9 %collective-permute-start.18 = (bf16[1344,256]{1,0:T(8,128)(2,1)}, bf16[1344,256]{1,0:T(8,128)(2,1)}, u32[]{:S(2)}, u32[]{:S(2)}) collective-permute-start(bf16[1344,256]{1,0:T(8,128)(2,1)} %collective-permute-done.17.refs_1_), channel_id=1, source_target_pairs={{0,8},{8,16},{16,24},{24,0},{1,9},{9,17},{17,25},{25,1},{2,10},{10... | collective-permute-start | bytes 2064392 | tf_op jit(solution)/shard_map/ppermute | solution.py:65
  194.9 20.5 %collective-permute-start.16 = (bf16[1344,256]{1,0:T(8,128)(2,1)}, bf16[1344,256]{1,0:T(8,128)(2,1)}, u32[]{:S(2)}, u32[]{:S(2)}) collective-permute-start(bf16[1344,256]{1,0:T(8,128)(2,1)} %collective-permute-done.15.refs_2_), channel_id=1, source_target_pairs={{0,8},{8,16},{16,24},{24,0},{1,9},{9,17},{17,25},{25,1},{2,10},{10... | collective-permute-start | bytes 2064392 | tf_op jit(solution)/shard_map/ppermute | solution.py:65
  198.5 31.5 %collective-permute-start.19 = (bf16[1344,256]{1,0:T(8,128)(2,1)}, bf16[1344,256]{1,0:T(8,128)(2,1)S(1)}, u32[]{:S(2)}, u32[]{:S(2)}) collective-permute-start(bf16[1344,256]{1,0:T(8,128)(2,1)} %collective-permute-done.18.refs_2_), channel_id=1, source_target_pairs={{0,8},{8,16},{16,24},{24,0},{1,9},{9,17},{17,25},{25,1},{2,10},{10... | collective-permute-start | bytes 2064392 | tf_op jit(solution)/shard_map/ppermute | solution.py:65
  199.3 48.9 %collective-permute-start.20 = (bf16[1024,512]{1,0:T(8,128)(2,1)S(1)}, bf16[1024,512]{1,0:T(8,128)(2,1)S(1)}, u32[]{:S(2)}, u32[]{:S(2)}) collective-permute-start(bf16[1024,512]{1,0:T(8,128)(2,1)S(1)} %slice.24), channel_id=1, source_target_pairs={{0,8},{8,16},{16,24},{1,9},{9,17},{17,25},{2,10},{10,18},{18,26},{... | collective-permute-start | bytes 3145736 | tf_op jit(solution)/shard_map/ppermute | solution.py:391
  215.4 59.7 %collective-permute-start.21 = (bf16[336,2048]{1,0:T(8,128)(2,1)}, bf16[336,2048]{1,0:T(8,128)(2,1)S(1)}, u32[]{:S(2)}, u32[]{:S(2)}) collective-permute-start(bf16[336,2048]{1,0:T(8,128)(2,1)} %collective-permute-done.4.refs_4_.refs_6_), channel_id=1, source_target_pairs={{0,8},{8,16},{16,24},{24,0},{1,9},{9,17},{17,25},{25,1},{2,10},{10... | collective-permute-start | bytes 4128776 | tf_op jit(solution)/shard_map/ppermute | solution.py:65
  261.3 29.7 %collective-permute-start.23 = (bf16[1024,512]{1,0:T(8,128)(2,1)S(1)}, bf16[1024,512]{1,0:T(8,128)(2,1)S(1)}, u32[]{:S(2)}, u32[]{:S(2)}) collective-permute-start(bf16[1024,512]{1,0:T(8,128)(2,1)S(1)} %shard_map.103.refs_0_), channel_id=1, source_target_pairs={{0,4},{2,6},{4,0},{6,2},{1,5},{3,7},{5,1},{7,3},{8,12},{10,14},{12... | collective-permute-start | bytes 3145736 | tf_op jit(solution)/shard_map/ppermute | solution.py:56
  275.0 30.2 %collective-permute-start.25 = (bf16[336,2048]{1,0:T(8,128)(2,1)S(1)}, bf16[336,2048]{1,0:T(8,128)(2,1)S(1)}, u32[]{:S(2)}, u32[]{:S(2)}) collective-permute-start(bf16[336,2048]{1,0:T(8,128)(2,1)S(1)} %collective-permute-done.21.refs_5_), channel_id=1, source_target_pairs={{0,8},{8,16},{16,24},{24,0},{1,9},{9,17},{17,25},{25,1},{2,10},{10... | collective-permute-start | bytes 4128776 | tf_op jit(solution)/shard_map/ppermute | solution.py:65
  277.4 15.6 %collective-permute-start.22 = (bf16[1024,512]{1,0:T(8,128)(2,1)S(1)}, bf16[1024,512]{1,0:T(8,128)(2,1)S(1)}, u32[]{:S(2)}, u32[]{:S(2)}) collective-permute-start(bf16[1024,512]{1,0:T(8,128)(2,1)S(1)} %shard_map.103.refs_0_), channel_id=1, source_target_pairs={{0,2},{2,0},{4,6},{6,4},{1,3},{3,1},{5,7},{7,5},{8,10},{10,8},{12,... | collective-permute-start | bytes 3145736 | tf_op jit(solution)/shard_map/ppermute | solution.py:56
  291.0 2.8 collective-permute-start.24
  291.5 25.4 %collective-permute-start.27 = (bf16[1024,512]{1,0:T(8,128)(2,1)}, bf16[1024,512]{1,0:T(8,128)(2,1)}, u32[]{:S(2)}, u32[]{:S(2)}) collective-permute-start(bf16[1024,512]{1,0:T(8,128)(2,1)} %shard_map.104.refs_0_), channel_id=1, source_target_pairs={{0,4},{2,6},{4,0},{6,2},{1,5},{3,7},{5,1},{7,3},{8,12},{10,14},{12... | collective-permute-start | bytes 3145736 | tf_op jit(solution)/shard_map/ppermute | solution.py:56
  299.0 17.8 %collective-permute-start.28 = (bf16[336,1024]{1,0:T(8,128)(2,1)S(1)}, bf16[336,1024]{1,0:T(8,128)(2,1)S(1)}, u32[]{:S(2)}, u32[]{:S(2)}) collective-permute-start(bf16[336,1024]{1,0:T(8,128)(2,1)S(1)} %get-tuple-element.62), channel_id=1, source_target_pairs={{0,1},{1,0},{2,3},{3,2},{4,5},{5,4},{6,7},{7,6},{8,9},{9,8},{10,11... | collective-permute-start | bytes 2064392 | tf_op jit(solution)/shard_map/ppermute | solution.py:60
  300.7 18.7 %collective-permute-start.26 = (bf16[1024,512]{1,0:T(8,128)(2,1)}, bf16[1024,512]{1,0:T(8,128)(2,1)}, u32[]{:S(2)}, u32[]{:S(2)}) collective-permute-start(bf16[1024,512]{1,0:T(8,128)(2,1)} %shard_map.104.refs_0_), channel_id=1, source_target_pairs={{0,2},{2,0},{4,6},{6,4},{1,3},{3,1},{5,7},{7,5},{8,10},{10,8},{12,... | collective-permute-start | bytes 3145736 | tf_op jit(solution)/shard_map/ppermute | solution.py:56
  317.8 3.0 collective-permute-start.29
  317.8 18.5 %collective-permute-start.38 = (bf16[336,1024]{1,0:T(8,128)(2,1)}, bf16[336,1024]{1,0:T(8,128)(2,1)}, u32[]{:S(2)}, u32[]{:S(2)}) collective-permute-start(bf16[336,1024]{1,0:T(8,128)(2,1)} %get-tuple-element.70), channel_id=1, source_target_pairs={{0,1},{1,0},{2,3},{3,2},{4,5},{5,4},{6,7},{7,6},{8,9},{9,8},{10,11... | collective-permute-start | bytes 2064392 | tf_op jit(solution)/shard_map/ppermute | solution.py:60
  334.2 18.3 %collective-permute-start.30 = (bf16[336,1024]{1,0:T(8,128)(2,1)S(1)}, bf16[336,1024]{1,0:T(8,128)(2,1)S(1)}, u32[]{:S(2)}, u32[]{:S(2)}) collective-permute-start(bf16[336,1024]{1,0:T(8,128)(2,1)S(1)} %get-tuple-element.65), channel_id=1, source_target_pairs={{0,1},{1,0},{2,3},{3,2},{4,5},{5,4},{6,7},{7,6},{8,9},{9,8},{10,11... | collective-permute-start | bytes 2064392 | tf_op jit(solution)/shard_map/ppermute | solution.py:60
  335.8 30.7 %collective-permute-start.34 = (bf16[336,1024]{1,0:T(8,128)(2,1)S(1)}, bf16[336,1024]{1,0:T(8,128)(2,1)S(1)}, u32[]{:S(2)}, u32[]{:S(2)}) collective-permute-start(bf16[336,1024]{1,0:T(8,128)(2,1)S(1)} %get-tuple-element.67), channel_id=1, source_target_pairs={{0,1},{1,0},{2,3},{3,2},{4,5},{5,4},{6,7},{7,6},{8,9},{9,8},{10,11... | collective-permute-start | bytes 2064392 | tf_op jit(solution)/shard_map/ppermute | solution.py:60
  338.1 14.9 %collective-permute-start.39 = (bf16[672,256]{1,0:T(8,128)(2,1)S(1)}, bf16[672,256]{1,0:T(8,128)(2,1)S(1)}, u32[]{:S(2)}, u32[]{:S(2)}) collective-permute-start(bf16[672,256]{1,0:T(8,128)(2,1)S(1)} %get-tuple-element.77), channel_id=1, source_target_pairs={{0,2},{2,0},{4,6},{6,4},{1,3},{3,1},{5,7},{7,5},{8,10},{10,8},{12,... | collective-permute-start | bytes 1032200 | tf_op jit(solution)/shard_map/ppermute | solution.py:56
  338.2 16.4 %collective-permute-start.40 = (bf16[672,256]{1,0:T(8,128)(2,1)S(1)}, bf16[672,256]{1,0:T(8,128)(2,1)S(1)}, u32[]{:S(2)}, u32[]{:S(2)}) collective-permute-start(bf16[672,256]{1,0:T(8,128)(2,1)S(1)} %get-tuple-element.78), channel_id=1, source_target_pairs={{0,4},{2,6},{4,0},{6,2},{1,5},{3,7},{5,1},{7,3},{8,12},{10,14},{12... | collective-permute-start | bytes 1032200 | tf_op jit(solution)/shard_map/ppermute | solution.py:56
  339.7 15.8 %collective-permute-start.41 = (bf16[672,256]{1,0:T(8,128)(2,1)S(1)}, bf16[672,256]{1,0:T(8,128)(2,1)S(1)}, u32[]{:S(2)}, u32[]{:S(2)}) collective-permute-start(bf16[672,256]{1,0:T(8,128)(2,1)S(1)} %get-tuple-element.75), channel_id=1, source_target_pairs={{0,6},{2,4},{4,2},{6,0},{1,7},{3,5},{5,3},{7,1},{8,14},{10,12},{12... | collective-permute-start | bytes 1032200 | tf_op jit(solution)/shard_map/ppermute | solution.py:56
  352.9 13.6 %collective-permute-start.31 = (bf16[336,256]{1,0:T(8,128)(2,1)S(1)}, bf16[336,256]{1,0:T(8,128)(2,1)S(1)}, u32[]{:S(2)}, u32[]{:S(2)}) collective-permute-start(bf16[336,256]{1,0:T(8,128)(2,1)S(1)} %get-tuple-element.97), channel_id=1, source_target_pairs={{0,2},{2,0},{4,6},{6,4},{1,3},{3,1},{5,7},{7,5},{8,10},{10,8},{12,... | collective-permute-start | bytes 516104 | tf_op jit(solution)/shard_map/ppermute | solution.py:56
  353.0 13.5 %collective-permute-start.32 = (bf16[336,256]{1,0:T(8,128)(2,1)S(1)}, bf16[336,256]{1,0:T(8,128)(2,1)S(1)}, u32[]{:S(2)}, u32[]{:S(2)}) collective-permute-start(bf16[336,256]{1,0:T(8,128)(2,1)S(1)} %get-tuple-element.96), channel_id=1, source_target_pairs={{0,4},{2,6},{4,0},{6,2},{1,5},{3,7},{5,1},{7,3},{8,12},{10,14},{12... | collective-permute-start | bytes 516104 | tf_op jit(solution)/shard_map/ppermute | solution.py:56
  354.5 12.0 %collective-permute-start.33 = (bf16[336,256]{1,0:T(8,128)(2,1)S(1)}, bf16[336,256]{1,0:T(8,128)(2,1)S(1)}, u32[]{:S(2)}, u32[]{:S(2)}) collective-permute-start(bf16[336,256]{1,0:T(8,128)(2,1)S(1)} %get-tuple-element.95), channel_id=1, source_target_pairs={{0,6},{2,4},{4,2},{6,0},{1,7},{3,5},{5,3},{7,1},{8,14},{10,12},{12... | collective-permute-start | bytes 516104 | tf_op jit(solution)/shard_map/ppermute | solution.py:56
  355.7 13.1 %collective-permute-start.42 = (f32[1,256]{1,0:T(1,128)S(1)}, f32[1,256]{1,0:T(1,128)S(1)}, u32[]{:S(2)}, u32[]{:S(2)}) collective-permute-start(f32[1,256]{1,0:T(1,128)S(1)} %shard_map.108.own_ref), channel_id=1, source_target_pairs={{0,1},{1,0},{2,3},{3,2},{4,5},{5,4},{6,7},{7,6},{8,9},{9,8},{10,11... | collective-permute-start | bytes 3080 | tf_op jit(solution)/shard_map/ppermute | solution.py:60
  366.9 10.1 %collective-permute-start.35 = (bf16[336,256]{1,0:T(8,128)(2,1)S(1)}, bf16[336,256]{1,0:T(8,128)(2,1)S(1)}, u32[]{:S(2)}, u32[]{:S(2)}) collective-permute-start(bf16[336,256]{1,0:T(8,128)(2,1)S(1)} %get-tuple-element.93), channel_id=1, source_target_pairs={{0,2},{2,0},{4,6},{6,4},{1,3},{3,1},{5,7},{7,5},{8,10},{10,8},{12,... | collective-permute-start | bytes 516104 | tf_op jit(solution)/shard_map/ppermute | solution.py:56
  366.9 10.0 %collective-permute-start.36 = (bf16[336,256]{1,0:T(8,128)(2,1)S(1)}, bf16[336,256]{1,0:T(8,128)(2,1)S(1)}, u32[]{:S(2)}, u32[]{:S(2)}) collective-permute-start(bf16[336,256]{1,0:T(8,128)(2,1)S(1)} %get-tuple-element.92), channel_id=1, source_target_pairs={{0,4},{2,6},{4,0},{6,2},{1,5},{3,7},{5,1},{7,3},{8,12},{10,14},{12... | collective-permute-start | bytes 516104 | tf_op jit(solution)/shard_map/ppermute | solution.py:56
  368.5 8.5 %collective-permute-start.37 = (bf16[336,256]{1,0:T(8,128)(2,1)S(1)}, bf16[336,256]{1,0:T(8,128)(2,1)S(1)}, u32[]{:S(2)}, u32[]{:S(2)}) collective-permute-start(bf16[336,256]{1,0:T(8,128)(2,1)S(1)} %get-tuple-element.91), channel_id=1, source_target_pairs={{0,6},{2,4},{4,2},{6,0},{1,7},{3,5},{5,3},{7,1},{8,14},{10,12},{12... | collective-permute-start | bytes 516104 | tf_op jit(solution)/shard_map/ppermute | solution.py:56
  377.1 3.6 collective-permute-start.43
  (27 other events, 200.1 us)
Sparse Core Ops, SparseCore 0:
  44.3 118.5 all-gather.2
